TPU v7x, 32 devices: a whole 2x2x4 slice. The times are simulated.
32 devices in a mesh: section: 2 (over x), dp: 4 (over z), tensor: 4 (over y, core).
Axes of the slice: x: 2, y: 2, z: 4, core: 2. Of those that a mesh axis runs over, the one named last changes fastest.
Arguments:
- block_input: float32 [2, 1024, 1536], P(None, ('dp', 'tensor')), may hold values from -6 to 6
- segments: int32 [2, 1024], P(None, 'dp'), may hold values from 0 to 4, as said below
- expert_ids: int32 [2, 2, 1024, 4], P('section', None, 'dp'), may hold values from 0 to 15, all different within a row; in each aligned block of 256 rows (0 to 255, 256 to 511, ..., all dimensions but the last counted through in order) at most 72 rows name the same one
- gate_values: float32 [2, 2, 1024, 4], P('section', None, 'dp'), may hold values from 0.15 to 0.45
- cotangent: float32 [2, 2, 1024, 1536], P('section', None, ('dp', 'tensor')), may hold values from -6 to 6
- attn_gain: bfloat16 [2, 1536], P('section', ('dp', 'tensor')), may hold values from 0.5 to 1.5
- query_weight: bfloat16 [2, 1536, 1536], P('section', 'dp', 'tensor'), may hold values from -0.21875 to 0.21875
- kv_weight: bfloat16 [2, 1536, 512], P('section', 'dp', 'tensor'), may hold values from -0.21875 to 0.21875
- out_weight: bfloat16 [2, 1536, 1536], P('section', 'tensor', 'dp'), may hold values from -1.25 to 1.25
- moe_gain: bfloat16 [2, 1536], P('section', ('dp', 'tensor')), may hold values from 0.5 to 1.5
- w_in: bfloat16 [2, 16, 1536, 1536], P('section', 'dp', None, 'tensor'), may hold values from -0.15625 to 0.15625
- w_out: bfloat16 [2, 16, 768, 1536], P('section', 'dp', 'tensor'), may hold values from -0.625 to 0.625
Outputs:
- block_out: float32 [2, 2, 1024, 1536], P('section', None, ('dp', 'tensor'))
- input_grad: float32 [2, 2, 1024, 1536], P('section', None, ('dp', 'tensor'))
- attn_gain_grad: float32 [2, 1536], P('section', ('dp', 'tensor'))
- query_grad: float32 [2, 1536, 1536], P('section', 'dp', 'tensor')
- kv_grad: float32 [2, 1536, 512], P('section', 'dp', 'tensor')
- out_grad: float32 [2, 1536, 1536], P('section', 'tensor', 'dp')
- moe_gain_grad: float32 [2, 1536], P('section', ('dp', 'tensor'))
- w_in_grad: float32 [2, 16, 1536, 1536], P('section', 'dp', None, 'tensor')
- w_out_grad: float32 [2, 16, 768, 1536], P('section', 'dp', 'tensor')
Inputs may be any that keep to these rules, and one draw needn't show every extreme that they name: `segments`: within each sequence of 256 tokens segment numbers never fall from one token to the next and start at 0. `expert_ids`: each token names 4 different experts; within each sequence of 256 tokens of one layer and micro-batch no expert is named by more than 72 tokens.
All inputs are finite; a program needn't handle non-finite values.
Results may differ from a plain program's by a relative error of at most 0.04.
Values may be sent and summed in bfloat16 or wider, within the bound.
No kernel may reach another device: no remote copies, remote signals or barrier semaphores. Data moves between devices by JAX's collectives and lax.ppermute only.
A program may use at most 256 MiB of HBM per device.

v0:
```python
import jax
import jax.numpy as jnp
from jax import lax
from jax.sharding import PartitionSpec as P

H = 12
KVH = 2
HD = 128
E = 16


EPS = 1e-06
THETA = 10000.0


def shifted(array, axis, by):
    size = lax.axis_size(axis)
    pairs = [(i, i + by) for i in range(size) if 0 <= i + by < size]
    return lax.ppermute(array, axis, pairs)


def positions(segment):
    length = segment.shape[0]
    ordinal = jnp.arange(length, dtype=jnp.int32)
    change = jnp.concatenate([jnp.ones((1,), dtype=jnp.bool_), segment[1:] != segment[:-1]])
    starts = lax.cummax(jnp.where(change, ordinal, 0), axis=0)
    return ordinal - starts


def rotate(values, places, sign):
    half_dim = values.shape[-1] // 2
    frequency = THETA ** (-2.0 * jnp.arange(half_dim, dtype=jnp.float32) / values.shape[-1])
    angles = places.astype(jnp.float32)[:, None] * frequency[None, :]
    cosine = jnp.cos(angles)[:, None, :]
    sine_part = sign * jnp.sin(angles)[:, None, :]
    first_half = values[..., :half_dim]
    second_half = values[..., half_dim:]
    return jnp.concatenate(
        [
            first_half * cosine - second_half * sine_part,
            second_half * cosine + first_half * sine_part,
        ],
        axis=-1,
    )


def inverse_rms(layer_rows):
    return lax.rsqrt(jnp.mean(layer_rows * layer_rows, axis=-1, keepdims=True) + EPS)


def norm_backward(layer_rows, factor, weights, upstream):
    weighted = upstream * weights
    projected = jnp.mean(weighted * layer_rows, axis=-1, keepdims=True)
    grad_rows = factor * weighted - layer_rows * (factor * factor * factor) * projected
    return (grad_rows, jnp.sum(upstream * layer_rows * factor, axis=0))


def destinations(chosen, experts, capacity):
    flat_ids = chosen.reshape(-1)
    one_hot = (flat_ids[:, None] == jnp.arange(experts, dtype=jnp.int32)[None, :]).astype(jnp.int32)
    earlier = jnp.cumsum(one_hot, axis=0) - one_hot
    return flat_ids * capacity + jnp.sum(earlier * one_hot, axis=1)


def expert_forward(inputs, piece_in, piece_out):
    gate_up = jnp.einsum("ecd,edf->ecf", inputs, piece_in, preferred_element_type=jnp.float32)
    half_cols = gate_up.shape[2] // 2
    hidden = (jax.nn.silu(gate_up[..., :half_cols]) * gate_up[..., half_cols:]).astype(jnp.bfloat16)
    result = jnp.einsum("ecf,efd->ecd", hidden, piece_out, preferred_element_type=jnp.float32)
    return (gate_up, result)


def expert_backward(inputs, gate_up, grad_out, piece_in, piece_out):
    half_cols = gate_up.shape[2] // 2
    gate_part = gate_up[..., :half_cols]
    up_part = gate_up[..., half_cols:]
    sigmoid_gate = jax.nn.sigmoid(gate_part)
    activated = gate_part * sigmoid_gate
    hidden = (activated * up_part).astype(jnp.bfloat16)
    grad_hidden = jnp.einsum(
        "ecd,efd->ecf", grad_out, piece_out, preferred_element_type=jnp.float32
    )
    grad_gate = grad_hidden * up_part * sigmoid_gate * (1.0 + gate_part * (1.0 - sigmoid_gate))
    grad_up = grad_hidden * activated
    grad_gu = jnp.concatenate([grad_gate, grad_up], axis=-1).astype(jnp.bfloat16)
    grad_win = jnp.einsum("ecd,ecf->edf", inputs, grad_gu, preferred_element_type=jnp.float32)
    grad_wout = jnp.einsum("ecf,ecd->efd", hidden, grad_out, preferred_element_type=jnp.float32)
    grad_inputs = jnp.einsum("ecf,edf->ecd", grad_gu, piece_in, preferred_element_type=jnp.float32)
    return (grad_inputs, grad_win, grad_wout)


def keep_if(stored, fresh_value, position_index, is_valid):
    previous = lax.dynamic_index_in_dim(stored, position_index, 0, keepdims=False)
    return lax.dynamic_update_index_in_dim(
        stored, jnp.where(is_valid, fresh_value, previous), position_index, 0
    )


def per_device(
    block_input,
    segments,
    expert_ids,
    gate_values,
    cotangent,
    attn_gain,
    query_weight,
    kv_weight,
    out_weight,
    moe_gain,
    w_in,
    w_out,
):
    section_index = lax.axis_index("section")
    section_count = lax.axis_size("section")
    group_count = lax.axis_size("dp")
    part_index = lax.axis_index("tensor")
    part_count = lax.axis_size("tensor")
    micro_count = block_input.shape[0]
    tok_rows = block_input.shape[1]
    model_width = block_input.shape[2]
    seq_len = segments.shape[1]
    top_count = expert_ids.shape[3]
    local_heads = query_weight.shape[2] // HD
    ffn_cols = w_out.shape[2]
    capacity = seq_len * top_count * 9 // (8 * E)
    score_scale = HD ** (-0.5)
    kv_head = part_index * local_heads // (H // KVH)
    query_full, out_full = (
        lax.all_gather(query_weight[0], "dp", axis=0, tiled=True),
        lax.all_gather(out_weight[0], "dp", axis=1, tiled=True),
    )
    kv_shard = kv_weight[0][None]
    gain_shard = jnp.stack([attn_gain[0], moe_gain[0]])[None]
    rows_dp = kv_shard.shape[1]
    cols_part = kv_shard.shape[2]
    gain_cols = gain_shard.shape[2]
    kv_all, gain_all = (
        lax.all_gather(kv_shard, ("dp", "tensor"), axis=0, tiled=True),
        lax.all_gather(gain_shard, ("dp", "tensor"), axis=0, tiled=True),
    )
    kv_full = (
        kv_all.reshape(group_count, part_count, rows_dp, cols_part)
        .transpose(0, 2, 1, 3)
        .reshape(model_width, part_count * cols_part)
    )
    gains = gain_all.transpose(1, 0, 2).reshape(2, model_width).astype(jnp.float32)
    gain_attn = gains[0]
    gain_moe = gains[1]
    key_cols = lax.dynamic_slice_in_dim(kv_full, kv_head * HD, HD, 1)
    value_cols = lax.dynamic_slice_in_dim(kv_full, (KVH + kv_head) * HD, HD, 1)
    kv_select = jnp.concatenate([key_cols, value_cols], axis=1)
    placeholder = jnp.zeros((1,), jnp.bfloat16)
    experts_in, experts_out = (
        lax.all_gather(w_in[0], "dp", axis=0, tiled=True),
        lax.all_gather(w_out[0], "dp", axis=0, tiled=True),
    )

    def collect_rows(layer_rows):
        return lax.all_gather(layer_rows, "tensor", axis=0, tiled=True)

    def spread_sum(layer_rows):
        return lax.psum_scatter(
            layer_rows.astype(jnp.bfloat16), "tensor", scatter_dimension=0, tiled=True
        ).astype(jnp.float32)

    def collect_grads(layer_rows):
        return lax.all_gather(layer_rows.astype(jnp.bfloat16), "tensor", axis=0, tiled=True).astype(
            layer_rows.dtype
        )

    def spread_grads(layer_rows):
        return lax.psum_scatter(
            layer_rows.astype(jnp.bfloat16), "tensor", scatter_dimension=0, tiled=True
        ).astype(jnp.float32)

    def run_experts_back(buffer, gate_up, grad_result, acc_in, acc_out):
        grad_buffer, grad_win, grad_wout = expert_backward(
            buffer, gate_up, grad_result, experts_in, experts_out
        )
        return (grad_buffer, acc_in + grad_win, acc_out + grad_wout)

    def attention_scores(queries, key_rows, allowed):
        raw_scores = score_scale * jnp.einsum(
            "qhd,kd->hqk", queries, key_rows, preferred_element_type=jnp.float32
        )
        return jnp.where(allowed[None], raw_scores, -1e30)

    def mask_for(segment):
        ordinal = jnp.arange(seq_len, dtype=jnp.int32)
        return (ordinal[None, :] <= ordinal[:, None]) & (segment[None, :] == segment[:, None])

    def fill_buffer(mixed_in, slot_ids):
        spread_rows = jnp.repeat(mixed_in, top_count, axis=0)
        return (
            jnp.zeros((E * capacity, model_width), jnp.bfloat16)
            .at[slot_ids]
            .set(spread_rows)
            .reshape(E, capacity, model_width)
        )

    def layer_backward(upstream, saved, segment, chosen, gates, accums):
        (
            layer_rows,
            middle,
            normed,
            queries,
            key_rows,
            value_rows,
            log_total,
            attended,
            mixed_in,
            gate_up,
            kept_rows,
        ) = saved
        acc_query, acc_out, acc_kv, acc_gain, acc_in, acc_down = accums
        places = positions(segment)
        slot_ids = destinations(chosen, E, capacity)
        scale_one = inverse_rms(layer_rows)
        scale_two = inverse_rms(middle)
        grad_full = collect_grads(upstream)
        pair_grads = (gates[:, :, None] * grad_full[:, None, :]).reshape(
            seq_len * top_count, model_width
        )
        grad_result = (
            jnp.zeros((E * capacity, model_width), jnp.float32).at[slot_ids].set(pair_grads)
        )
        grad_result = grad_result.astype(jnp.bfloat16).reshape(E, capacity, model_width)
        expert_input = fill_buffer(mixed_in, slot_ids)
        grad_buffer, acc_in, acc_down = run_experts_back(
            expert_input, gate_up, grad_result, acc_in, acc_down
        )
        grad_picked = grad_buffer.reshape(E * capacity, model_width)[slot_ids].reshape(
            seq_len, top_count, model_width
        )
        grad_mixed = spread_grads(jnp.sum(grad_picked, axis=1))
        back_middle, gain_moe_grad = norm_backward(middle, scale_two, gain_moe, grad_mixed)
        grad_middle = upstream + back_middle
        grad_attn = collect_grads(grad_middle).astype(jnp.bfloat16)
        acc_out = acc_out + jnp.einsum(
            "sd,sf->df", grad_attn, attended, preferred_element_type=jnp.float32
        )
        grad_att = jnp.einsum("sd,fd->sf", grad_attn, out_full, preferred_element_type=jnp.float32)
        grad_att = grad_att.astype(jnp.bfloat16).reshape(seq_len, local_heads, HD)
        scores = attention_scores(queries, key_rows, mask_for(segment))
        attention_p = jnp.exp(scores - log_total)
        grad_values = jnp.einsum(
            "hqk,qhd->kd",
            attention_p.astype(jnp.bfloat16),
            grad_att,
            preferred_element_type=jnp.float32,
        )
        grad_probs = jnp.einsum(
            "qhd,kd->hqk", grad_att, value_rows, preferred_element_type=jnp.float32
        )
        row_delta = jnp.sum(attention_p * grad_probs, axis=-1, keepdims=True)
        grad_scores = (attention_p * (grad_probs - row_delta)).astype(jnp.bfloat16)
        grad_query = score_scale * jnp.einsum(
            "hqk,kd->qhd", grad_scores, key_rows, preferred_element_type=jnp.float32
        )
        grad_key = score_scale * jnp.einsum(
            "hqk,qhd->kd", grad_scores, queries, preferred_element_type=jnp.float32
        )
        grad_query_lin = (
            rotate(grad_query, places, -1.0).astype(jnp.bfloat16).reshape(seq_len, local_heads * HD)
        )
        grad_key_lin = rotate(grad_key[:, None, :], places, -1.0)[:, 0, :]
        grad_kv = jnp.concatenate([grad_key_lin, grad_values], axis=1).astype(jnp.bfloat16)
        acc_query = acc_query + jnp.einsum(
            "sd,sf->df", normed, grad_query_lin, preferred_element_type=jnp.float32
        )
        kv_term = jnp.einsum("sd,sf->df", normed, grad_kv, preferred_element_type=jnp.float32)
        key_start = kv_head * HD
        value_start = (KVH + kv_head) * HD
        acc_kv = lax.dynamic_update_slice_in_dim(
            acc_kv,
            lax.dynamic_slice_in_dim(acc_kv, key_start, HD, 1) + kv_term[:, :HD],
            key_start,
            1,
        )
        acc_kv = lax.dynamic_update_slice_in_dim(
            acc_kv,
            lax.dynamic_slice_in_dim(acc_kv, value_start, HD, 1) + kv_term[:, HD:],
            value_start,
            1,
        )
        grad_normed = jnp.einsum(
            "sf,df->sd", grad_query_lin, query_full, preferred_element_type=jnp.float32
        )
        grad_normed = grad_normed + jnp.einsum(
            "sf,df->sd", grad_kv, kv_select, preferred_element_type=jnp.float32
        )
        grad_normed_rows = spread_grads(grad_normed)
        back_input, gain_attn_grad = norm_backward(
            layer_rows, scale_one, gain_attn, grad_normed_rows
        )
        grad_input = grad_middle + back_input
        acc_gain = acc_gain + jnp.stack([gain_attn_grad, gain_moe_grad])
        return (grad_input, (acc_query, acc_out, acc_kv, acc_gain, acc_in, acc_down))

    tick_count = micro_count + section_count - 1
    out_rows = jnp.zeros((micro_count, tok_rows, model_width), jnp.float32)
    incoming = jnp.zeros((tok_rows, model_width), jnp.float32)
    saved_all = None
    for tick_num in range(tick_count):
        batch_index = tick_num - section_index
        is_valid = (batch_index >= 0) & (batch_index < micro_count)
        chosen_batch = jnp.clip(batch_index, 0, micro_count - 1)
        own_input = lax.dynamic_index_in_dim(block_input, chosen_batch, 0, keepdims=False)
        layer_in = jnp.where(section_index == 0, own_input, incoming)
        segment = lax.dynamic_index_in_dim(segments, chosen_batch, 0, keepdims=False)
        chosen = lax.dynamic_index_in_dim(expert_ids[0], chosen_batch, 0, keepdims=False)
        gates = lax.dynamic_index_in_dim(gate_values[0], chosen_batch, 0, keepdims=False)
        layer_places = positions(segment)
        layer_scale_one = inverse_rms(layer_in)
        layer_normed = collect_rows((layer_in * layer_scale_one * gain_attn).astype(jnp.bfloat16))
        query_lin = jnp.dot(layer_normed, query_full, preferred_element_type=jnp.float32).reshape(
            seq_len, local_heads, HD
        )
        layer_queries = rotate(query_lin, layer_places, 1.0).astype(jnp.bfloat16)
        kv_lin = jnp.dot(layer_normed, kv_select, preferred_element_type=jnp.float32)
        layer_key_rows = rotate(kv_lin[:, None, :HD], layer_places, 1.0)[:, 0, :].astype(
            jnp.bfloat16
        )
        layer_value_rows = kv_lin[:, HD:].astype(jnp.bfloat16)
        layer_scores = attention_scores(layer_queries, layer_key_rows, mask_for(segment))
        top_score = jnp.max(layer_scores, axis=-1, keepdims=True)
        layer_log_total = top_score + jnp.log(
            jnp.sum(jnp.exp(layer_scores - top_score), axis=-1, keepdims=True)
        )
        layer_attention_p = jnp.exp(layer_scores - layer_log_total).astype(jnp.bfloat16)
        layer_attended = jnp.einsum(
            "hqk,kd->qhd", layer_attention_p, layer_value_rows, preferred_element_type=jnp.float32
        )
        layer_attended = layer_attended.astype(jnp.bfloat16).reshape(seq_len, local_heads * HD)
        layer_middle = layer_in + spread_sum(
            jnp.dot(layer_attended, out_full, preferred_element_type=jnp.float32)
        )
        layer_scale_two = inverse_rms(layer_middle)
        layer_mixed_in = collect_rows(
            (layer_middle * layer_scale_two * gain_moe).astype(jnp.bfloat16)
        )
        layer_slot_ids = destinations(chosen, E, capacity)
        run_gate_up, result = expert_forward(
            fill_buffer(layer_mixed_in, layer_slot_ids), experts_in, experts_out
        )
        picked = result.reshape(E * capacity, model_width)[layer_slot_ids].reshape(
            seq_len, top_count, model_width
        )
        moe_rows = jnp.sum(gates[:, :, None] * picked, axis=1)
        layer_out = layer_middle + spread_sum(moe_rows)
        layer_saved = (
            layer_in,
            layer_middle,
            layer_normed,
            layer_queries,
            layer_key_rows,
            layer_value_rows,
            layer_log_total,
            layer_attended,
            layer_mixed_in,
            run_gate_up,
            placeholder,
        )
        layer_out, saved = (layer_out, layer_saved)
        if saved_all is None:
            saved_all = jax.tree.map(
                lambda member: jnp.zeros((micro_count,) + member.shape, member.dtype), saved
            )
        saved_all = jax.tree.map(
            lambda stack_all, member: keep_if(stack_all, member, chosen_batch, is_valid),
            saved_all,
            saved,
        )
        out_rows = keep_if(out_rows, layer_out, chosen_batch, is_valid)
        if tick_num + 1 < tick_count:
            incoming = shifted(layer_out.astype(jnp.bfloat16), "section", 1).astype(layer_out.dtype)
    heads_cols = local_heads * HD
    expert_count = E
    accums = (
        jnp.zeros((model_width, heads_cols), jnp.float32),
        jnp.zeros((model_width, heads_cols), jnp.float32),
        jnp.zeros((model_width, part_count * cols_part), jnp.float32),
        jnp.zeros((2, model_width), jnp.float32),
        jnp.zeros((expert_count, model_width, 2 * ffn_cols), jnp.float32),
        jnp.zeros((expert_count, ffn_cols, model_width), jnp.float32),
    )
    grad_rows_all = jnp.zeros((micro_count, tok_rows, model_width), jnp.float32)
    from_next = jnp.zeros((tok_rows, model_width), jnp.float32)
    for tick_num in range(tick_count):
        batch_index = tick_num - (section_count - 1 - section_index)
        is_valid = (batch_index >= 0) & (batch_index < micro_count)
        chosen_batch = jnp.clip(batch_index, 0, micro_count - 1)
        own_grad = lax.dynamic_index_in_dim(cotangent[0], chosen_batch, 0, keepdims=False)
        upstream = own_grad + jnp.where(section_index == section_count - 1, 0.0, from_next)
        upstream = jnp.where(is_valid, upstream, 0.0)
        segment = lax.dynamic_index_in_dim(segments, chosen_batch, 0, keepdims=False)
        chosen = lax.dynamic_index_in_dim(expert_ids[0], chosen_batch, 0, keepdims=False)
        gates = lax.dynamic_index_in_dim(gate_values[0], chosen_batch, 0, keepdims=False)
        saved = jax.tree.map(
            lambda stack_all: lax.dynamic_index_in_dim(stack_all, chosen_batch, 0, keepdims=False),
            saved_all,
        )
        grad_input, accums = layer_backward(upstream, saved, segment, chosen, gates, accums)
        grad_rows_all = keep_if(grad_rows_all, grad_input, chosen_batch, is_valid)
        if tick_num + 1 < tick_count:
            from_next = shifted(grad_input.astype(jnp.bfloat16), "section", -1).astype(
                grad_input.dtype
            )
    acc_query, acc_out, acc_kv, acc_gain, acc_in, acc_down = accums
    grad_query, grad_out_t, grad_in_w, grad_out_w = (
        lax.psum_scatter(
            acc_query.astype(jnp.bfloat16), "dp", scatter_dimension=0, tiled=True
        ).astype(jnp.float32),
        lax.psum_scatter(
            acc_out.astype(jnp.bfloat16), "dp", scatter_dimension=0, tiled=True
        ).astype(jnp.float32),
        lax.psum_scatter(acc_in.astype(jnp.bfloat16), "dp", scatter_dimension=0, tiled=True).astype(
            jnp.float32
        ),
        lax.psum_scatter(
            acc_down.astype(jnp.bfloat16), "dp", scatter_dimension=0, tiled=True
        ).astype(jnp.float32),
    )
    kv_term = (
        acc_kv.reshape(group_count, rows_dp, part_count, cols_part)
        .transpose(0, 2, 1, 3)
        .reshape(group_count * part_count, rows_dp, cols_part)
    )
    gain_term = acc_gain.reshape(2, group_count * part_count, gain_cols).transpose(1, 0, 2)
    grad_kv, grad_gain = (
        lax.psum_scatter(kv_term, ("dp", "tensor"), scatter_dimension=0, tiled=True),
        lax.psum_scatter(gain_term, ("dp", "tensor"), scatter_dimension=0, tiled=True),
    )
    return (
        out_rows[None],
        grad_rows_all[None],
        grad_gain[:, 0, :],
        grad_query[None],
        grad_kv,
        grad_out_t.T[None],
        grad_gain[:, 1, :],
        grad_in_w[None],
        grad_out_w[None],
    )


def solution(mesh):
    return jax.shard_map(
        per_device,
        mesh=mesh,
        in_specs=(
            P(None, ("dp", "tensor"), None),
            P(None, "dp"),
            P("section", None, "dp", None),
            P("section", None, "dp", None),
            P("section", None, ("dp", "tensor"), None),
            P("section", ("dp", "tensor")),
            P("section", "dp", "tensor"),
            P("section", "dp", "tensor"),
            P("section", "tensor", "dp"),
            P("section", ("dp", "tensor")),
            P("section", "dp", None, "tensor"),
            P("section", "dp", "tensor", None),
        ),
        out_specs=(
            P("section", None, ("dp", "tensor"), None),
            P("section", None, ("dp", "tensor"), None),
            P("section", ("dp", "tensor")),
            P("section", "dp", "tensor"),
            P("section", "dp", "tensor"),
            P("section", "tensor", "dp"),
            P("section", ("dp", "tensor")),
            P("section", "dp", None, "tensor"),
            P("section", "dp", "tensor", None),
        ),
        check_vma=False,
    )
```

profile of v0, /device:TPU:9, one launch (start us, length us, event | category | flops | bytes accessed | tf_op | source)
XLA Modules:
  0.0 2071.1 jit_solution(8464944188228301995)
XLA Ops:
  18.0 19.2 all-gather.5
  52.2 29.5 %all-gather.12.cloned.1.call-done = bf16[16,384,128]{2,1,0:T(8,128)(2,1)} async-done(((bf16[1,384,128]{2,1,0:T(8,128)(2,1)}), bf16[16,384,128]{2,1,0:T(8,128)(2,1)}) %all-gather.12.cloned.1.call-update) | async-done | bytes 1572880 | tf_op jit(solution)/shard_map/all_gather | solution.py:138
  87.8 25.1 %all-gather.16.cloned.1.call-done = bf16[1,384,1536]{2,1,0:T(8,128)(2,1)} async-done(((bf16[1,384,384]{2,1,0:T(8,128)(2,1)}), bf16[1,384,1536]{2,1,0:T(8,128)(2,1)}) %all-gather.16.cloned.1.call-update) | async-done | bytes 1179664 | tf_op jit(solution)/shard_map/all_gather | solution.py:130
  142.2 20.2 all_gather.59
  175.1 285.7 %all-gather.18.cloned.1.call-done = bf16[1,16,1536,384]{3,2,0,1:T(8,128)(2,1)} async-done(((bf16[1,4,1536,384]{3,2,0,1:T(8,128)(2,1)}), bf16[1,16,1536,384]{3,2,0,1:T(8,128)(2,1)}) %all-gather.18.cloned.1.call-update) | async-done | bytes 18874384 | tf_op jit(solution)/shard_map/all_gather | solution.py:154
  462.7 9.7 bitcast_dynamic-update-slice_fusion.2
  472.4 154.8 %all-gather.20.cloned.1.call-done = bf16[1,16,192,1536]{3,2,0,1:T(8,128)(2,1)} async-done(((bf16[1,4,192,1536]{3,2,0,1:T(8,128)(2,1)}), bf16[1,16,192,1536]{3,2,0,1:T(8,128)(2,1)}) %all-gather.20.cloned.1.call-update) | async-done | bytes 9437200 | tf_op jit(solution)/shard_map/all_gather | solution.py:155
  627.2 9.3 fusion.22
  636.6 10.9 gather_fusion
  669.7 18.1 reduce-scatter.20.cloned.1.call-done
  698.1 9.5 all_gather.62
  760.0 9.0 scatter_custom_fusion.1
  769.0 11.9 bitcast_dynamic-update-slice_fusion.1
  785.8 10.8 gather_fusion.1
  823.8 9.4 all_gather.66
  844.7 10.0 scatter_custom_fusion.3
  870.1 9.4 all_gather.64
  900.9 10.2 reduce-scatter.26.cloned.1.call-done
  913.5 9.1 all_gather.65
  940.7 12.5 bitcast_dynamic-update-slice_fusion
  962.0 13.8 fusion.4
  975.8 10.8 gather_fusion.3
  1011.5 13.7 reduce-scatter.30.cloned.1.call-done
  1058.3 9.3 reduce-window.146
  1075.9 9.3 reduce-window.116
  1116.4 8.9 all_gather.68
  1136.5 10.4 scatter_custom_fusion.4
  1158.8 13.7 fusion.2
  1172.5 10.8 gather_fusion.4
  1199.7 21.2 %reduce-scatter.34.cloned.1.call-done = bf16[64,1536]{1,0:T(8,128)(2,1)} async-done(((bf16[256,1536]{1,0:T(8,128)(2,1)}), bf16[64,1536]{1,0:T(8,128)(2,1)}) %reduce-scatter.34.cloned.1.call-update) | async-done | bytes 196624 | tf_op jit(solution)/shard_map/reduce_scatter | solution.py:172
  1225.2 8.9 all_gather.69
  1253.1 15.5 reduce-scatter.36.cloned.1.call-done
  1281.1 9.1 all_gather.70
  1301.4 10.2 scatter_custom_fusion.5
  1323.5 13.7 fusion
  1337.2 10.8 gather_fusion.5
  1375.5 10.8 gather_fusion.2
  1406.8 8.8 all_gather.71
  1436.7 10.9 fusion.140
  1451.2 12.1 fusion.141
  1463.2 17.7 add_convert_fusion.1
  1509.0 9.1 scatter_custom_fusion.8
  1535.5 16.8 fusion.161
  1552.3 15.0 fusion.160
  1567.3 33.8 %add_convert_fusion = bf16[16,1536,384]{2,1,0:T(8,128)(2,1)} fusion(f32[16,1536,384]{2,1,0:T(8,128)} %fusion.161, f32[16,1536,384]{2,1,0:T(8,128)} %fusion.160, bf16[16,72,1536]{2,1,0:T(8,128)(2,1)} %bitcast.928, bf16[16,72,192]{2,1,0:T(8,128)(2,1)S(1)} %copy-done.74, bf16[16,72,192]{2,1,0:T(8,128)(2,1)S(1)} %copy-done.72), kind=kOutput, calls=%fused_computation.15 | convolution fusion | flops 1389035520 | bytes 98795520 | tf_op jit(solution)/shard_map/ecd,ecf->edf/dot_general | solution.py:86
  1630.6 51.9 %all-reduce = f32[16,2,96]{2,1,0:T(2,128)S(1)} all-reduce(f32[16,2,96]{2,1,0:T(2,128)S(1)} %fusion.382), channel_id=19, replica_groups=mesh['section'=2,'dp'=4,'tensor'=4] {'dp','tensor'}, use_global_device_ids=true, to_apply=%region_87.88.clone | all-reduce | flops 3072 | bytes 24576
  1693.4 297.1 %reduce-scatter.48.cloned.1.call-done = bf16[4,1536,384]{2,1,0:T(8,128)(2,1)} async-done(((bf16[16,1536,384]{2,1,0:T(8,128)(2,1)}), bf16[4,1536,384]{2,1,0:T(8,128)(2,1)}) %reduce-scatter.48.cloned.1.call-update) | async-done | bytes 4718608 | tf_op jit(solution)/shard_map/reduce_scatter | solution.py:417
  1997.2 66.8 %reduce-scatter.44.cloned.1.call-done = f32[1,384,128]{2,1,0:T(8,128)} async-done(((f32[16,384,128]{2,1,0:T(8,128)}), f32[1,384,128]{2,1,0:T(8,128)}) %reduce-scatter.44.cloned.1.call-update) | async-done | bytes 196624 | tf_op jit(solution)/shard_map/reduce_scatter | solution.py:431
  (911 shorter events, 627.7 us)
Async XLA Ops:
  7.2 42.6 %all-gather.14.cloned.1.call-start = ((), (), s32[]{:S(2)}) async-start(), calls=%async_computation.35 | async-start | bytes 1474560 | tf_op jit(solution)/shard_map/all_gather | solution.py:129
  7.9 73.8 %all-gather.12.cloned.1.call-start = ((), (), s32[]{:S(2)}) async-start(), calls=%async_computation.17 | async-start | bytes 1671168 | tf_op jit(solution)/shard_map/all_gather | solution.py:138
  8.7 104.2 %all-gather.16.cloned.1.call-start = ((), (), s32[]{:S(2)}) async-start(), calls=%async_computation.36 | async-start | bytes 1474560 | tf_op jit(solution)/shard_map/all_gather | solution.py:130
  9.4 129.4 %reduce-scatter.18.cloned.1.call-start = ((), (), s32[]{:S(2)}) async-start(), calls=%async_computation.18 | async-start | bytes 983040 | tf_op jit(solution)/shard_map/reduce_scatter | solution.py:162
  9.5 75.8 %copy-start.168 = (f32[64]{0:T(128)}, f32[64]{0:T(128)S(1)}, u32[]{:S(2)}) copy-start(f32[64]{0:T(128)S(1)} %multiply_power_fusion) | copy-start | bytes 772
  14.4 35.2 %copy-start.187 = (f32[256]{0:T(256)}, f32[256]{0:T(256)S(1)}, u32[]{:S(2)}) copy-start(f32[256]{0:T(256)S(1)} %fusion.403) | copy-start | bytes 3076
  14.7 34.9 %copy-start.189 = (f32[256]{0:T(256)}, f32[256]{0:T(256)S(1)}, u32[]{:S(2)}) copy-start(f32[256]{0:T(256)S(1)} %fusion.404) | copy-start | bytes 3076
  15.7 33.9 %copy-start.191 = (f32[256]{0:T(256)}, f32[256]{0:T(256)S(1)}, u32[]{:S(2)}) copy-start(f32[256]{0:T(256)S(1)} %fusion.405) | copy-start | bytes 3076
  16.0 33.6 %copy-start.193 = (f32[256]{0:T(256)}, f32[256]{0:T(256)S(1)}, u32[]{:S(2)}) copy-start(f32[256]{0:T(256)S(1)} %fusion.406) | copy-start | bytes 3076
  17.0 32.6 %copy-start.195 = (f32[256]{0:T(256)}, f32[256]{0:T(256)S(1)}, u32[]{:S(2)}) copy-start(f32[256]{0:T(256)S(1)} %fusion.407) | copy-start | bytes 3076
  37.4 1233.0 %copy-start.112 = (f32[1536]{0:T(1024)}, f32[1536]{0:T(1024)S(1)}, u32[]{:S(2)}) copy-start(f32[1536]{0:T(1024)S(1)} %mul.1369) | copy-start | bytes 18436
  47.3 37.5 %copy-start.32 = (bf16[256,1536]{1,0:T(8,128)(2,1)}, bf16[256,1536]{1,0:T(8,128)(2,1)S(1)}, u32[]{:S(2)}) copy-start(bf16[256,1536]{1,0:T(8,128)(2,1)S(1)} %all_gather.55) | copy-start | bytes 2359300
  52.2 33.4 %copy-start.93 = (bf16[256,3,64]{2,0,1:T(8,128)(2,1)}, bf16[256,3,64]{2,0,1:T(8,128)(2,1)S(1)}, u32[]{:S(2)}) copy-start(bf16[256,3,64]{2,0,1:T(8,128)(2,1)S(1)} %get-tuple-element.121) | copy-start | bytes 294916
  52.2 33.4 %copy-start.94 = (bf16[256,3,64]{2,0,1:T(8,128)(2,1)}, bf16[256,3,64]{2,0,1:T(8,128)(2,1)S(1)}, u32[]{:S(2)}) copy-start(bf16[256,3,64]{2,0,1:T(8,128)(2,1)S(1)} %get-tuple-element.122) | copy-start | bytes 294916
  85.2 30.4 %copy-start.134 = (f32[256,256]{0,1:T(8,128)}, f32[256,256]{0,1:T(8,128)S(1)}, u32[]{:S(2)}) copy-start(f32[256,256]{0,1:T(8,128)S(1)} %fusion.435) | copy-start | bytes 786436
  85.6 30.1 %copy-start.135 = (bf16[256,1,64]{0,2,1:T(8,128)(2,1)}, bf16[256,1,64]{0,2,1:T(8,128)(2,1)S(1)}, u32[]{:S(2)}) copy-start(bf16[256,1,64]{0,2,1:T(8,128)(2,1)S(1)} %get-tuple-element.146) | copy-start | bytes 98308
  85.6 30.1 %copy-start.136 = (bf16[256,1,64]{0,2,1:T(8,128)(2,1)}, bf16[256,1,64]{0,2,1:T(8,128)(2,1)S(1)}, u32[]{:S(2)}) copy-start(bf16[256,1,64]{0,2,1:T(8,128)(2,1)S(1)} %get-tuple-element.147) | copy-start | bytes 98308
  115.7 345.0 %all-gather.18.cloned.1.call-start = ((), (), s32[]{:S(2)}) async-start(), calls=%async_computation.37 | async-start | bytes 23592960 | tf_op jit(solution)/shard_map/all_gather | solution.py:154
  116.3 510.9 %all-gather.20.cloned.1.call-start = ((), (), s32[]{:S(2)}) async-start(), calls=%async_computation.38 | async-start | bytes 11796480 | tf_op jit(solution)/shard_map/all_gather | solution.py:155
  116.9 571.0 %reduce-scatter.20.cloned.1.call-start = ((), (), s32[]{:S(2)}) async-start(), calls=%async_computation.19 | async-start | bytes 983040 | tf_op jit(solution)/shard_map/reduce_scatter | solution.py:162
  472.4 264.9 %copy-start = (f32[2,16,72,384]{3,2,1,0:T(8,128)}, f32[2,16,72,384]{3,2,1,0:T(8,128)S(1)}, u32[]{:S(2)}) copy-start(f32[2,16,72,384]{3,2,1,0:T(8,128)S(1)} %get-tuple-element.215) | copy-start | bytes 10616836
  663.4 81.0 %reduce-scatter.22.cloned.1.call-start = ((), (), s32[]{:S(2)}) async-start(), calls=%async_computation.20 | async-start | bytes 983040 | tf_op jit(solution)/shard_map/reduce_scatter | solution.py:162
  689.1 6.6 collective-permute-start
  719.6 141.4 %reduce-scatter.24.cloned.1.call-start = ((), (), s32[]{:S(2)}) async-start(), calls=%async_computation.21 | async-start | bytes 983040 | tf_op jit(solution)/shard_map/reduce_scatter | solution.py:162
  746.8 114.1 %copy-start.30 = (f32[64,1536]{1,0:T(8,128)}, f32[64,1536]{1,0:T(8,128)S(1)}, u32[]{:S(2)}) copy-start(f32[64,1536]{1,0:T(8,128)S(1)} %get-tuple-element.92) | copy-start | bytes 1179652
  812.7 98.4 %reduce-scatter.26.cloned.1.call-start = ((), (), s32[]{:S(2)}) async-start(), calls=%async_computation.22 | async-start | bytes 983040 | tf_op jit(solution)/shard_map/reduce_scatter | solution.py:162
  861.9 7.3 collective-permute-start.1
  887.0 138.3 %reduce-scatter.30.cloned.1.call-start = ((), (), s32[]{:S(2)}) async-start(), calls=%async_computation.24 | async-start | bytes 983040 | tf_op jit(solution)/shard_map/reduce_scatter | solution.py:172
  926.0 31.9 %slice-start.3 = ((s8[9437184]{0:T(1024)(128)(4,1)}), s8[1048576]{0:T(1024)(128)(4,1)S(1)}, s32[]{:S(2)}) async-start(s8[9437184]{0:T(1024)(128)(4,1)} %bitcast.924), calls=%async_computation.42 | async-start | bytes 2097152
  1001.9 25.3 %copy-start.56 = (f32[1,2,64,1536]{3,2,1,0:T(8,128)S(1)}, f32[1,2,64,1536]{3,2,1,0:T(8,128)}, u32[]{:S(2)}) copy-start(f32[1,2,64,1536]{3,2,1,0:T(8,128)} %param.16) | copy-start | bytes 2359300
  1001.9 101.6 %reduce-scatter.32.cloned.1.call-start = ((), (), s32[]{:S(2)}) async-start(), calls=%async_computation.25 | async-start | bytes 983040 | tf_op jit(solution)/shard_map/reduce_scatter | solution.py:172
  1006.7 32.1 %copy-start.24 = (bf16[1,384,1536]{2,1,0:T(8,128)(2,1)S(1)}, bf16[1,384,1536]{2,1,0:T(8,128)(2,1)}, u32[]{:S(2)}) copy-start(bf16[1,384,1536]{2,1,0:T(8,128)(2,1)} %all-gather.16.cloned.1.call-done) | copy-start | bytes 3538948
  1009.5 35.1 %copy-start.104 = (bf16[2,256,128]{1,2,0:T(8,128)(2,1)}, bf16[2,256,128]{1,2,0:T(8,128)(2,1)S(1)}, u32[]{:S(2)}) copy-start(bf16[2,256,128]{1,2,0:T(8,128)(2,1)S(1)} %bitcast_dynamic-update-slice_fusion.19) | copy-start | bytes 393220
  1046.0 56.9 %copy-start.8 = (f32[2,64,1536]{2,1,0:T(8,128)S(1)}, f32[2,64,1536]{2,1,0:T(8,128)}, u32[]{:S(2)}) copy-start(f32[2,64,1536]{2,1,0:T(8,128)} %copy-done.7) | copy-start | bytes 2359300
  1047.3 58.0 %copy-start.108 = (f32[64,1536]{1,0:T(8,128)S(1)}, f32[64,1536]{1,0:T(8,128)}, u32[]{:S(2)}) copy-start(f32[64,1536]{1,0:T(8,128)} %get-tuple-element.84) | copy-start | bytes 1179652
  1047.3 173.7 %reduce-scatter.34.cloned.1.call-start = ((), (), s32[]{:S(2)}) async-start(), calls=%async_computation.26 | async-start | bytes 983040 | tf_op jit(solution)/shard_map/reduce_scatter | solution.py:172
  1107.1 8.2 collective-permute-start.2
  1198.4 70.1 %reduce-scatter.36.cloned.1.call-start = ((), (), s32[]{:S(2)}) async-start(), calls=%async_computation.27 | async-start | bytes 983040 | tf_op jit(solution)/shard_map/reduce_scatter | solution.py:172
  1245.3 157.5 %reduce-scatter.38.cloned.1.call-start = ((), (), s32[]{:S(2)}) async-start(), calls=%async_computation.28 | async-start | bytes 983040 | tf_op jit(solution)/shard_map/reduce_scatter | solution.py:172
  1272.3 7.6 collective-permute-start.3
  1363.0 243.1 %reduce-scatter.28.cloned.1.call-start = ((), (), s32[]{:S(2)}) async-start(), calls=%async_computation.23 | async-start | bytes 983040 | tf_op jit(solution)/shard_map/reduce_scatter | solution.py:162
  1402.2 227.1 %reduce-scatter.40.cloned.1.call-start = ((), (), s32[]{:S(2)}) async-start(), calls=%async_computation.29 | async-start | bytes 983040 | tf_op jit(solution)/shard_map/reduce_scatter | solution.py:172
  1424.7 260.1 %reduce-scatter.46.cloned.1.call-start = ((), (), s32[]{:S(2)}) async-start(), calls=%async_computation.32 | async-start | bytes 1474560 | tf_op jit(solution)/shard_map/reduce_scatter | solution.py:414
  1434.5 252.6 %reduce-scatter.42.cloned.1.call-start = ((), (), s32[]{:S(2)}) async-start(), calls=%async_computation.30 | async-start | bytes 1474560 | tf_op jit(solution)/shard_map/reduce_scatter | solution.py:411
  1451.1 237.8 %reduce-scatter.50.cloned.1.call-start = ((), (), s32[]{:S(2)}) async-start(), calls=%async_computation.34 | async-start | bytes 11796480 | tf_op jit(solution)/shard_map/reduce_scatter | solution.py:420
  1481.0 509.6 %reduce-scatter.48.cloned.1.call-start = ((), (), s32[]{:S(2)}) async-start(), calls=%async_computation.33 | async-start | bytes 23592960 | tf_op jit(solution)/shard_map/reduce_scatter | solution.py:417
  1601.3 462.8 %reduce-scatter.44.cloned.1.call-start = ((), (), s32[]{:S(2)}) async-start(), calls=%async_computation.31 | async-start | bytes 3342336 | tf_op jit(solution)/shard_map/reduce_scatter | solution.py:431
  1627.8 55.8 %copy-start.109 = (f32[64,1536]{1,0:T(8,128)S(1)}, f32[64,1536]{1,0:T(8,128)}, u32[]{:S(2)}) copy-start(f32[64,1536]{1,0:T(8,128)} %get-tuple-element.70) | copy-start | bytes 1179652
  (188 other events, 1330.4 us)
Sparse Core Ops, SparseCore 0:
  9.6 30.9 all-gather.13
  42.8 38.8 all-gather.11
  83.4 29.4 all-gather.15
  115.9 22.8 reduce-scatter.17
  140.3 320.4 all-gather.17
  462.2 164.9 all-gather.19
  663.5 24.2 reduce-scatter.19
  719.7 24.6 reduce-scatter.21
  812.9 23.8 reduce-scatter.23
  887.1 24.0 reduce-scatter.25
  1002.0 23.1 reduce-scatter.29
  1047.4 23.1 reduce-scatter.31
  1198.5 22.3 reduce-scatter.33
  1245.4 23.1 reduce-scatter.35
  1363.2 22.7 reduce-scatter.37
  1402.3 22.8 reduce-scatter.27
  1428.3 23.2 reduce-scatter.39
  1453.8 27.1 reduce-scatter.45
  1483.3 27.8 reduce-scatter.41
  1514.0 162.4 reduce-scatter.49
  1678.9 311.6 reduce-scatter.47
  1995.4 68.6 reduce-scatter.43
where the time goes:
time: 2090 us; the launch traced here: 2070 us
  waiting for transfers between devices  972 us (47%)
  local copies, waits for them, and re-layouts  348 us (17%)
  matrix products  275 us (13%)
  other arithmetic  257 us (12%)
  blocking collectives  190 us (9%)
    reduce_scatter x1, waiting for transfers between devices, per_device(): lax.psum_scatter(acc_in.astype(jnp.bfloat16), 'dp', scatter_dimension=0,...  297 us
    all_gather x1, waiting for transfers between devices, per_device(): lax.all_gather(w_in[0], 'dp', axis=0, tiled=True)  286 us
    all_gather x1, waiting for transfers between devices, per_device(): lax.all_gather(w_out[0], 'dp', axis=0, tiled=True)  155 us
    reduce_scatter x1, waiting for transfers between devices, per_device(): lax.psum_scatter(kv_term, ('dp', 'tensor'), scatter_dimension=0, tiled=True)  66.8 us
    dot_general x3, matrix products, expert_backward(): jnp.einsum('ecd,ecf->edf', inputs, grad_gu, preferred_element_type=jnp.fl...  65.7 us
    all_gather x6, blocking collectives, collect_rows(): return lax.all_gather(layer_rows, 'tensor', axis=0, tiled=True)  65.6 us
    all_gather x6, blocking collectives, collect_grads(): lax.all_gather(layer_rows.astype(jnp.bfloat16), 'tensor', axis=0, tiled=T...  53.8 us
    scatter x6, local copies, waits for them, and re-layouts, fill_buffer(): return jnp.zeros((E * capacity, model_width), jnp.bfloat16).at[slot_ids]....  52.6 us
  transfers between devices with their start and end apart: 26, of which 17 were waited for; matrix products, arithmetic and copies ran while one was open for 23% of the time, Pallas kernels for 0%

commit v1 on v0

v1 whole, which is shorter than its diff:
```python
import functools

import jax
import jax.numpy as jnp
from jax import lax
from jax.experimental import pallas as pl
from jax.experimental.pallas import tpu as pltpu
from jax.sharding import PartitionSpec as P

H = 12
KVH = 2
HD = 128
E = 16

EPS = 1e-06
THETA = 10000.0
BF = jnp.bfloat16
F32 = jnp.float32
MIB = 1024 * 1024


def dot(a, b, ca, cb):
    return lax.dot_general(a, b, (((ca,), (cb,)), ((), ())), preferred_element_type=F32)


def by_tensor(value, flip):
    size = lax.axis_size("tensor")
    return lax.ppermute(value, "tensor", [(i, i ^ flip) for i in range(size)])


def by_dp(value, flip):
    size = lax.axis_size("dp")
    return lax.ppermute(value, "dp", [(i, i ^ flip) for i in range(size)])


def by_section(value):
    return lax.ppermute(value, "section", [(0, 1), (1, 0)])


def to_section(value, host):
    return lax.ppermute(value, "section", [(1 - host, host)])


def kv_turn(value):
    return lax.ppermute(value, "tensor", [(0, 0), (1, 2), (2, 1), (3, 3)])


def over_tensor(value):
    across = by_tensor(value, 2)
    core = by_tensor(value, 1)
    return [value, core, across, by_tensor(across, 1)]


def sum_over_tensor(keep, send):
    total = keep + by_tensor(send, 1)
    return total[0], by_tensor(total[1], 2)


def rope(value, cosine, sine):
    return value * cosine + pltpu.roll(value, HD // 2, 1) * sine


def allowed_pairs(idx_row, idx_col, start_col):
    keys = idx_row[...]
    return (keys <= idx_col[...]) & (keys >= start_col[...])


def attn_fwd_kernel(
    heads, rows,
    a0, a1, a2, a3, wq, wkv, wo, cosine, sine, idx_row, idx_col, start_col,
    keep, send, q_out, k_out, v_out, lse_out, o_out, a_all,
):
    for r, ref in enumerate((a0, a1, a2, a3)):
        a_all[r * rows : (r + 1) * rows, :] = ref[...]
    a = a_all[...]
    q = dot(a, wq[...], 1, 0)
    kv = dot(a, wkv[...], 1, 0)
    co, si = cosine[...], sine[...]
    k = rope(kv[:, :HD], co, si).astype(BF)
    v = kv[:, HD:].astype(BF)
    k_out[...] = k
    v_out[...] = v
    allowed = allowed_pairs(idx_row, idx_col, start_col)
    lane = lax.broadcasted_iota(jnp.int32, (q.shape[0], HD), 1)
    lse_all = jnp.zeros((q.shape[0], HD), F32)
    for h in range(heads):
        qh = rope(q[:, h * HD : (h + 1) * HD], co, si).astype(BF)
        q_out[:, h * HD : (h + 1) * HD] = qh
        s = jnp.where(allowed, HD ** (-0.5) * dot(qh, k, 1, 1), -1e30)
        top = jnp.max(s, axis=1, keepdims=True)
        lse = top + jnp.log(jnp.sum(jnp.exp(s - top), axis=1, keepdims=True))
        p = jnp.exp(s - lse).astype(BF)
        o_out[:, h * HD : (h + 1) * HD] = dot(p, v, 1, 0).astype(BF)
        lse_all = jnp.where(lane == h, lse, lse_all)
    lse_out[...] = lse_all
    part = dot(o_out[...], wo[...], 1, 0).astype(BF)
    for r in range(4):
        (send if r % 2 else keep)[r // 2] = part[r * rows : (r + 1) * rows, :]


def attn_bwd_kernel(
    heads, rows,
    d0, d1, d2, d3, q_in, k_in, v_in, lse_in, wq, wkv, wo, cosine, sine, idx_row, idx_col, start_col,
    keep, send, dq_out, dkv_out, d_all,
):
    for r, ref in enumerate((d0, d1, d2, d3)):
        d_all[r * rows : (r + 1) * rows, :] = ref[...]
    do = dot(d_all[...], wo[...], 1, 1).astype(BF)
    co, si = cosine[...], -sine[...]
    k, v = k_in[...], v_in[...]
    allowed = allowed_pairs(idx_row, idx_col, start_col)
    dk = jnp.zeros((do.shape[0], HD), F32)
    dv = jnp.zeros((do.shape[0], HD), F32)
    for h in range(heads):
        qh = q_in[:, h * HD : (h + 1) * HD]
        doh = do[:, h * HD : (h + 1) * HD]
        s = jnp.where(allowed, HD ** (-0.5) * dot(qh, k, 1, 1), -1e30)
        p = jnp.exp(s - lse_in[:, h : h + 1])
        dv = dv + dot(p.astype(BF), doh, 0, 0)
        dp = dot(doh, v, 1, 1)
        ds = (p * (dp - jnp.sum(p * dp, axis=1, keepdims=True))).astype(BF)
        dq = HD ** (-0.5) * dot(ds, k, 1, 0)
        dk = dk + dot(ds, qh, 0, 0)
        dq_out[:, h * HD : (h + 1) * HD] = rope(dq, co, si).astype(BF)
    dkv_out[:, :HD] = rope(HD ** (-0.5) * dk, co, si).astype(BF)
    dkv_out[:, HD:] = dv.astype(BF)
    part = (dot(dq_out[...], wq[...], 1, 1) + dot(dkv_out[...], wkv[...], 1, 1)).astype(BF)
    for r in range(4):
        (send if r % 2 else keep)[r // 2] = part[r * rows : (r + 1) * rows, :]


def attn_wgrad_kernel(
    rows,
    a0, a1, a2, a3, d0, d1, d2, d3, o_in, dq, dkv,
    dwq, dwk, dwv, dwo, a_all, d_all,
):
    for r, ref in enumerate((a0, a1, a2, a3)):
        a_all[r * rows : (r + 1) * rows, :] = ref[...]
    for r, ref in enumerate((d0, d1, d2, d3)):
        d_all[r * rows : (r + 1) * rows, :] = ref[...]
    dwo[...] = dot(o_in[...], d_all[...], 0, 0).astype(BF)
    a = a_all[...]
    dwq[...] = dot(a, dq[...], 0, 0).astype(BF)
    dwk[...] = dot(a, dkv[:, :HD], 0, 0).astype(BF)
    dwv[...] = dot(a, dkv[:, HD:], 0, 0).astype(BF)


def slot_rows(pos_row, s, experts, cap):
    tokens = pos_row.shape[2]
    slot = lax.broadcasted_iota(jnp.int32, (experts * cap, tokens), 0)
    hit = slot == pos_row[s, 0:1, :]
    for e in range(1, experts):
        hit = hit | (slot == pos_row[s, e : e + 1, :])
    return hit


def slot_cols(pos_col, s, experts, cap):
    tokens = pos_col.shape[1]
    slot = lax.broadcasted_iota(jnp.int32, (tokens, experts * cap), 1)
    hit = slot == pos_col[s, :, 0:1]
    for e in range(1, experts):
        hit = hit | (slot == pos_col[s, :, e : e + 1])
    return hit.astype(F32).astype(BF)


def fetch_sequence(blocks, s, into, rows):
    for r in range(4):
        into[r * rows : (r + 1) * rows, :] = blocks[s // 2 * 4 + r][s % 2]


def dispatch(blocks, pos_row, gate_row, into, gates, seq, experts, cap, rows, count, scaled):
    for s in range(count):
        fetch_sequence(blocks, s, seq, rows)
        hit = slot_rows(pos_row, s, experts, cap)
        picked = dot(hit.astype(F32).astype(BF), seq[...], 1, 0)
        own = lax.broadcasted_iota(jnp.int32, hit.shape, 0) // cap
        gate = jnp.zeros(hit.shape, F32)
        for e in range(experts):
            gate = jnp.where(hit & (own == e), gate_row[s, e : e + 1, :], gate)
        gate = jnp.sum(gate, axis=1, keepdims=True)
        if scaled:
            picked = picked * gate
        else:
            gates[s] = gate
        picked = picked.astype(BF)
        for e in range(experts):
            into[e, s * cap : (s + 1) * cap, :] = picked[e * cap : (e + 1) * cap, :]


def combine(values, pos_col, keeps, sends, experts, cap, rows, count):
    for s in range(count):
        total = dot(slot_cols(pos_col, s, experts, cap), values[s], 1, 0).astype(BF)
        for r in range(4):
            (sends if r % 2 else keeps)[s // 2][r // 2, s % 2] = total[r * rows : (r + 1) * rows, :]


def moe_fwd_kernel(experts, cap, rows, count, *refs):
    blocks, refs = refs[: count * 2], refs[count * 2 :]
    pos_row, pos_col, gate_row, w_in, w_out, x_out, gu_out = refs[:7]
    keeps, sends = refs[7 : 7 + count // 2], refs[7 + count // 2 : 7 + count]
    x_all, result, gates, seq = refs[7 + count :]
    step = pl.program_id(0)

    @pl.when(step == 0)
    def _():
        dispatch(blocks, pos_row, gate_row, x_all, gates, seq, experts, cap, rows, count, False)

    x = x_all[step]
    x_out[0] = x
    gu = dot(x, w_in[0], 1, 0)
    gu_out[0] = gu
    half = gu.shape[1] // 2
    gate, up = gu[:, :half], gu[:, half:]
    z = (gate / (1.0 + jnp.exp(-gate)) * up).astype(BF)
    out = dot(z, w_out[0], 1, 0)
    for s in range(count):
        at = pl.ds(pl.multiple_of(step * cap, 16), cap)
        result[s, at, :] = (out[s * cap : (s + 1) * cap, :] * gates[s, at, :]).astype(BF)

    @pl.when(step == experts - 1)
    def _():
        combine(result, pos_col, keeps, sends, experts, cap, rows, count)


def moe_bwd_kernel(experts, cap, rows, count, *refs):
    blocks, refs = refs[: count * 2], refs[count * 2 :]
    pos_row, pos_col, gate_row, gu_in, w_in, w_out, dr_out, z_out, dgu_out = refs[:9]
    keeps, sends = refs[9 : 9 + count // 2], refs[9 + count // 2 : 9 + count]
    dr_all, result, seq = refs[9 + count :]
    step = pl.program_id(0)

    @pl.when(step == 0)
    def _():
        dispatch(blocks, pos_row, gate_row, dr_all, None, seq, experts, cap, rows, count, True)

    dr = dr_all[step]
    dr_out[0] = dr
    gu = gu_in[0]
    half = gu.shape[1] // 2
    gate, up = gu[:, :half], gu[:, half:]
    sg = 1.0 / (1.0 + jnp.exp(-gate))
    act = gate * sg
    z_out[0] = (act * up).astype(BF)
    dz = dot(dr, w_out[0], 1, 1)
    dgu_out[0, :, :half] = (dz * up * sg * (1.0 + gate * (1.0 - sg))).astype(BF)
    dgu_out[0, :, half:] = (dz * act).astype(BF)
    out = dot(dgu_out[0], w_in[0], 1, 1).astype(BF)
    for s in range(count):
        result[s, pl.ds(pl.multiple_of(step * cap, 16), cap), :] = out[s * cap : (s + 1) * cap, :]

    @pl.when(step == experts - 1)
    def _():
        combine(result, pos_col, keeps, sends, experts, cap, rows, count)


def moe_wgrad_kernel(sel, *refs):
    first, second, (dwin, dwout) = refs[:8], refs[8:16], refs[16:]

    def run(x0, x1, dg0, dg1, z0, z1, dr0, dr1):
        dwin[0] = dot(x0[0], dg0[0], 0, 0) + dot(x1[0], dg1[0], 0, 0)
        dwout[0] = dot(z0[0], dr0[0], 0, 0) + dot(z1[0], dr1[0], 0, 0)

    @pl.when(sel[0] == 0)
    def _():
        run(*first)

    @pl.when(sel[0] == 1)
    def _():
        run(*second)


def inverse_rms(rows):
    return lax.rsqrt(jnp.mean(rows * rows, axis=-1, keepdims=True) + EPS)


def norm_backward(rows, factor, gain, upstream):
    weighted = upstream * gain
    projected = jnp.mean(weighted * rows, axis=-1, keepdims=True)
    grad_rows = factor * weighted - rows * (factor * factor * factor) * projected
    return grad_rows, jnp.sum(upstream * rows * factor, axis=0)


def whole(shape):
    return pl.BlockSpec(shape, lambda *_: (0,) * len(shape))


def per_device(
    block_input, segments, expert_ids, gate_values, cotangent, attn_gain,
    query_weight, kv_weight, out_weight, moe_gain, w_in, w_out,
):
    sec = lax.axis_index("section")
    dp = lax.axis_index("dp")
    t = lax.axis_index("tensor")
    n_dp = lax.axis_size("dp")
    n_t = lax.axis_size("tensor")
    first = sec == 0
    core0 = t % 2 == 0
    rows, width = block_input.shape[1], block_input.shape[2]
    seq = segments.shape[1]
    top = expert_ids.shape[3]
    heads = query_weight.shape[2] // HD
    qcols = heads * HD
    experts, ffn = w_in.shape[1], w_out.shape[2]
    cap = -(-(seq * top * 9 // (8 * E)) // 16) * 16
    slots = n_dp * cap
    flips = jnp.arange(n_t, dtype=jnp.int32) ^ t
    groups = n_dp // 2

    gain_all = lax.all_gather(
        jnp.stack([attn_gain[0], moe_gain[0]])[None], ("section", "dp", "tensor"), axis=0, tiled=True
    )
    gain_all = gain_all.reshape(2, n_dp * n_t, 2, -1).transpose(0, 2, 1, 3).reshape(2, 2, 1, width)
    gain_all = gain_all.astype(F32)

    shard = jnp.concatenate([query_weight[0], kv_turn(kv_weight[0])], axis=1)
    shard_far = by_section(shard)
    out_far = by_section(out_weight[0])
    layer_weights = []
    for l in range(2):
        here = sec == l
        qkv = lax.all_gather(jnp.where(here, shard, shard_far), "dp", axis=0, tiled=True)
        wo = lax.all_gather(jnp.where(here, out_weight[0], out_far), "dp", axis=1, tiled=True)
        kv_own = qkv[:, qcols:]
        kv_core = by_tensor(kv_own, 1)
        wkv = jnp.where(
            core0,
            jnp.concatenate([kv_own, kv_core], axis=1),
            jnp.concatenate([kv_core, kv_own], axis=1),
        )
        layer_weights.append((qkv[:, :qcols], wkv, wo))

    segment = jnp.where(first, segments[0], segments[1])
    ordinal = jnp.arange(seq, dtype=jnp.int32)
    start = jnp.sum((segment[None, :] < segment[:, None]).astype(jnp.int32), axis=1)
    places = (ordinal - start).astype(F32)

    def turned(vector):
        return vector.reshape(n_t, rows)[flips].reshape(seq)

    idx = turned(ordinal)
    start_col = turned(start)[:, None]
    frequency = THETA ** (-2.0 * jnp.arange(HD // 2, dtype=F32) / HD)
    angles = turned(places)[:, None] * frequency[None, :]
    cosine = jnp.cos(angles)
    cosine = jnp.concatenate([cosine, cosine], axis=1)
    sine = jnp.sin(angles)
    sine = jnp.concatenate([-sine, sine], axis=1)
    place_args = (cosine, sine, idx[None, :], idx[:, None], start_col)

    routing = jnp.concatenate([expert_ids[0].astype(F32), gate_values[0]], axis=2)
    routing = lax.all_gather(routing[None], "dp", axis=0, tiled=True)
    routing = routing[jnp.arange(n_dp, dtype=jnp.int32) ^ dp]
    routing = routing.reshape(n_dp, 2, n_t, rows, 2 * top)[:, :, flips].reshape(n_dp, 2, seq, 2 * top)
    names = (dp * experts + jnp.arange(experts, dtype=jnp.int32)).astype(F32)
    chosen = routing[:, :, :, :top, None] == names
    member = jnp.sum(chosen.astype(F32), axis=3)
    gates = jnp.sum(jnp.where(chosen, routing[:, :, :, top:, None], 0.0), axis=3)
    lower = (ordinal[:, None] > ordinal[None, :]).astype(BF)
    rank = jnp.einsum("ij,smje->smie", lower, member.astype(BF), preferred_element_type=F32)
    slot = rank + (jnp.arange(experts, dtype=jnp.int32) * cap).astype(F32)
    slot = jnp.where(member > 0.5, slot, -1.0).astype(jnp.int32)
    pos_col = slot.transpose(1, 0, 2, 3)
    pos_row = slot.transpose(1, 0, 3, 2)
    gate_row = gates.transpose(1, 0, 3, 2)

    block = jax.ShapeDtypeStruct((rows, width), BF)
    pair = jax.ShapeDtypeStruct((2, rows, width), BF)
    quad = jax.ShapeDtypeStruct((2, 2, rows, width), BF)

    def shape(*dims, dtype=BF):
        return jax.ShapeDtypeStruct(dims, dtype)

    def params(limit):
        return pltpu.CompilerParams(vmem_limit_bytes=limit * MIB)

    def attn_fwd(a_blocks, weights):
        return pl.pallas_call(
            functools.partial(attn_fwd_kernel, heads, rows),
            out_shape=(
                pair, pair, shape(seq, qcols), shape(seq, HD), shape(seq, HD),
                shape(seq, HD, dtype=F32), shape(seq, qcols),
            ),
            scratch_shapes=[pltpu.VMEM((seq, width), BF)],
            compiler_params=params(40),
            cost_estimate=pl.CostEstimate(
                flops=2 * seq * width * (2 * qcols + 2 * HD), bytes_accessed=6 * MIB, transcendentals=0
            ),
            name="attn_fwd",
        )(*a_blocks, *weights, *place_args)

    def attn_bwd(d_blocks, saved, weights):
        return pl.pallas_call(
            functools.partial(attn_bwd_kernel, heads, rows),
            out_shape=(pair, pair, shape(seq, qcols), shape(seq, 2 * HD)),
            scratch_shapes=[pltpu.VMEM((seq, width), BF)],
            compiler_params=params(40),
            cost_estimate=pl.CostEstimate(
                flops=2 * seq * width * (2 * qcols + 2 * HD), bytes_accessed=6 * MIB, transcendentals=0
            ),
            name="attn_bwd",
        )(*d_blocks, *saved, *weights, *place_args)

    def attn_wgrad(a_blocks, d_blocks, attended, dq, dkv):
        return pl.pallas_call(
            functools.partial(attn_wgrad_kernel, rows),
            out_shape=(shape(width, qcols), shape(width, HD), shape(width, HD), shape(qcols, width)),
            scratch_shapes=[pltpu.VMEM((seq, width), BF), pltpu.VMEM((seq, width), BF)],
            compiler_params=params(40),
            cost_estimate=pl.CostEstimate(
                flops=2 * seq * width * (2 * qcols + 2 * HD), bytes_accessed=6 * MIB, transcendentals=0
            ),
            name="attn_wgrad",
        )(*a_blocks, *d_blocks, attended, dq, dkv)

    def per_expert(*dims):
        return pl.BlockSpec((1,) + dims, lambda e: (e, 0, 0))

    route_specs = [
        whole((n_dp, experts, seq)), whole((n_dp, seq, experts)), whole((n_dp, experts, seq)),
    ]
    block_specs = [whole((2, rows, width))] * (2 * n_dp)
    sum_specs = [whole((2, 2, rows, width))] * n_dp
    seq_scratch = pltpu.VMEM((seq, width), BF)
    moe_flops = 2 * experts * slots * width * 3 * ffn + 4 * n_dp * experts * cap * seq * width

    def moe_fwd(blocks, b):
        out = pl.pallas_call(
            functools.partial(moe_fwd_kernel, experts, cap, rows, n_dp),
            grid=(experts,),
            in_specs=block_specs + route_specs + [per_expert(width, 2 * ffn), per_expert(ffn, width)],
            out_specs=[per_expert(slots, width), per_expert(slots, 2 * ffn)] + sum_specs,
            out_shape=[shape(experts, slots, width), shape(experts, slots, 2 * ffn, dtype=F32)]
            + [quad] * n_dp,
            scratch_shapes=[
                pltpu.VMEM((experts, slots, width), BF),
                pltpu.VMEM((n_dp, experts * cap, width), BF),
                pltpu.VMEM((n_dp, experts * cap, 1), F32),
                seq_scratch,
            ],
            compiler_params=params(56),
            cost_estimate=pl.CostEstimate(flops=moe_flops, bytes_accessed=20 * MIB, transcendentals=0),
            name="moe_fwd",
        )(*blocks, pos_row[b], pos_col[b], gate_row[b], w_in[0], w_out[0])
        return out[0], out[1], out[2 : 2 + groups], out[2 + groups :]

    def moe_bwd(blocks, gu, b):
        out = pl.pallas_call(
            functools.partial(moe_bwd_kernel, experts, cap, rows, n_dp),
            grid=(experts,),
            in_specs=block_specs
            + route_specs
            + [per_expert(slots, 2 * ffn), per_expert(width, 2 * ffn), per_expert(ffn, width)],
            out_specs=[per_expert(slots, width), per_expert(slots, ffn), per_expert(slots, 2 * ffn)]
            + sum_specs,
            out_shape=[
                shape(experts, slots, width), shape(experts, slots, ffn), shape(experts, slots, 2 * ffn),
            ]
            + [quad] * n_dp,
            scratch_shapes=[
                pltpu.VMEM((experts, slots, width), BF),
                pltpu.VMEM((n_dp, experts * cap, width), BF),
                seq_scratch,
            ],
            compiler_params=params(56),
            cost_estimate=pl.CostEstimate(flops=moe_flops, bytes_accessed=20 * MIB, transcendentals=0),
            name="moe_bwd",
        )(*blocks, pos_row[b], pos_col[b], gate_row[b], gu, w_in[0], w_out[0])
        return out[0], out[1], out[2], out[3 : 3 + groups], out[3 + groups :]

    def moe_wgrad(sets):
        def spec(which, *dims):
            return pl.BlockSpec((1,) + dims, lambda e, sel: (jnp.where(sel[0] == which, e, 0), 0, 0))

        in_specs = []
        for which in range(2):
            for dims in ((slots, width), (slots, 2 * ffn), (slots, ffn), (slots, width)):
                in_specs += [spec(which, *dims)] * 2
        return pl.pallas_call(
            moe_wgrad_kernel,
            grid_spec=pltpu.PrefetchScalarGridSpec(
                num_scalar_prefetch=1,
                grid=(experts,),
                in_specs=in_specs,
                out_specs=[
                    pl.BlockSpec((1, width, 2 * ffn), lambda e, sel: (e, 0, 0)),
                    pl.BlockSpec((1, ffn, width), lambda e, sel: (e, 0, 0)),
                ],
            ),
            out_shape=[
                shape(experts, width, 2 * ffn, dtype=F32), shape(experts, ffn, width, dtype=F32),
            ],
            compiler_params=params(56),
            cost_estimate=pl.CostEstimate(flops=2 * moe_flops, bytes_accessed=40 * MIB, transcendentals=0),
            name="moe_wgrad",
        )(sec.astype(jnp.int32)[None], *sets[0], *sets[1])

    def spread_pairs(own):
        parts = [own] + [by_dp(own, k) for k in range(1, n_dp)]
        return [jnp.stack(parts[2 * j : 2 * j + 2]) for j in range(groups)]

    def fill(pairs):
        return [value for pair_rows in pairs for value in over_tensor(pair_rows)]

    def to_host(own, host):
        near = spread_pairs(own)
        far = [to_section(pair_rows, host) for pair_rows in near]
        return fill(near), fill(far)

    def tensor_sums(keeps, sends):
        sums = []
        for keep, send in zip(keeps, sends):
            total = keep + by_tensor(send, 1)
            sums.append(total[0] + by_tensor(total[1], 2))
        return sums

    def from_host(near, far, host):
        here = sec == host
        near, far = tensor_sums(*near), tensor_sums(*far)
        total = None
        for j in reversed(range(groups)):
            back = lax.ppermute(far[j], "section", [(host, 1 - host)])
            mine = jnp.where(here, near[j], back)
            for i in reversed(range(2)):
                k = 2 * j + i
                term = (mine[i] if k == 0 else by_dp(mine[i], k)).astype(F32)
                total = term if total is None else total + term
        return total

    x = jnp.where(first, block_input[0], block_input[1])
    cot_far = by_section(jnp.where(first, cotangent[0, 1], cotangent[0, 0]))
    cot_near = jnp.where(first, cotangent[0, 0], cotangent[0, 1])
    cots = (jnp.where(first, cot_near, cot_far), jnp.where(first, cot_far, cot_near))

    kept = []
    outs = []
    experts_kept = []
    for l in range(2):
        r1 = inverse_rms(x)
        a_blocks = over_tensor((x * r1 * gain_all[l, 0]).astype(BF))
        keep, send, q, k, v, lse, attended = attn_fwd(a_blocks, layer_weights[l])
        part0, part1 = sum_over_tensor(keep, send)
        mid = x + (part0.astype(F32) + part1.astype(F32))
        r2 = inverse_rms(mid)
        m = (mid * r2 * gain_all[l, 1]).astype(BF)
        near, far = to_host(m, l)
        x_near, gu_near, *near_sums = moe_fwd(near, l)
        x_far, gu_far, *far_sums = moe_fwd(far, 1 - l)
        out = mid + from_host(near_sums, far_sums, l)
        kept.append((x, r1, a_blocks, (q, k, v, lse), attended, mid, r2))
        experts_kept.append((x_near, x_far, gu_near, gu_far))
        outs.append(out)
        x = out

    grads = [None, None]
    gain_sums = [None, None]
    in_grads = [None, None]
    sets = [None, None]
    g = cots[1]
    for l in (1, 0):
        x, r1, a_blocks, saved, attended, mid, r2 = kept[l]
        x_near, x_far, gu_near, gu_far = experts_kept[l]
        if l == 1:
            both = cotangent[0].astype(BF)
            parts = [both] + [by_dp(both, k) for k in range(1, n_dp)]
            near, far = (
                fill([jnp.stack([parts[2 * j][b], parts[2 * j + 1][b]]) for j in range(groups)])
                for b in (1, 0)
            )
        else:
            near, far = to_host(g.astype(BF), l)
        dr_near, z_near, dgu_near, *near_sums = moe_bwd(near, gu_near, l)
        dr_far, z_far, dgu_far, *far_sums = moe_bwd(far, gu_far, 1 - l)
        sets[l] = (x_near, x_far, dgu_near, dgu_far, z_near, z_far, dr_near, dr_far)
        dm = from_host(near_sums, far_sums, l)
        back, gain_moe_sum = norm_backward(mid, r2, gain_all[l, 1], dm)
        dmid = g + back
        d_blocks = over_tensor(dmid.astype(BF))
        keep, send, dq, dkv = attn_bwd(d_blocks, saved, layer_weights[l])
        part0, part1 = sum_over_tensor(keep, send)
        da = part0.astype(F32) + part1.astype(F32)
        back, gain_attn_sum = norm_backward(x, r1, gain_all[l, 0], da)
        in_grads[l] = dmid + back
        gain_sums[l] = jnp.stack([gain_attn_sum, gain_moe_sum])
        dwq, dwk, dwv, dwo = attn_wgrad(a_blocks, d_blocks, attended, dq, dkv)
        dwkv = jnp.where(core0, dwk, dwv) + by_tensor(jnp.where(core0, dwv, dwk), 1)
        grads[l] = (jnp.concatenate([dwq, dwkv], axis=1), dwo)
        if l == 1:
            g = cots[0] + in_grads[1]

    dw_in, dw_out = moe_wgrad(sets)

    qrows = query_weight.shape[1]
    ocols = out_weight.shape[2]

    def dp_sum(value, size, axis):
        total = None
        for k in reversed(range(n_dp)):
            piece = lax.dynamic_slice_in_dim(value, (dp ^ k) * size, size, axis)
            term = (piece if k == 0 else by_dp(piece, k)).astype(F32)
            total = term if total is None else total + term
        return total

    reduced = [(dp_sum(grads[l][0], qrows, 0), dp_sum(grads[l][1], ocols, 1)) for l in range(2)]

    def at_home(value0, value1):
        far = by_section(jnp.where(first, value1, value0).astype(BF)).astype(F32)
        return jnp.where(first, value0, value1) + far

    grad_qkv = at_home(reduced[0][0], reduced[1][0])
    grad_out = at_home(reduced[0][1], reduced[1][1])
    grad_kv = kv_turn(grad_qkv[:, qcols:])

    gains = jnp.stack(gain_sums)
    gains = gains + by_tensor(gains, 1)
    gains = gains + by_tensor(gains, 2)
    flip = 1
    while flip < n_dp:
        gains = gains + by_dp(gains, flip)
        flip *= 2
    gains = jnp.where(first, gains[0], gains[1]) + by_section(jnp.where(first, gains[1], gains[0]))
    cols = attn_gain.shape[1]
    gains = lax.dynamic_slice_in_dim(gains, (dp * n_t + t) * cols, cols, 1)

    def both_batches(value0, value1):
        far = by_section(jnp.where(first, value1, value0).astype(BF)).astype(F32)
        near = jnp.where(first, value0, value1)
        return jnp.stack([jnp.where(first, near, far), jnp.where(first, far, near)])[None]

    return (
        both_batches(*outs),
        both_batches(*in_grads),
        gains[0:1],
        grad_qkv[None, :, :qcols],
        grad_kv[None],
        grad_out[None],
        gains[1:2],
        dw_in[None],
        dw_out[None],
    )


def solution(mesh):
    return jax.shard_map(
        per_device,
        mesh=mesh,
        in_specs=(
            P(None, ("dp", "tensor"), None),
            P(None, "dp"),
            P("section", None, "dp", None),
            P("section", None, "dp", None),
            P("section", None, ("dp", "tensor"), None),
            P("section", ("dp", "tensor")),
            P("section", "dp", "tensor"),
            P("section", "dp", "tensor"),
            P("section", "tensor", "dp"),
            P("section", ("dp", "tensor")),
            P("section", "dp", None, "tensor"),
            P("section", "dp", "tensor", None),
        ),
        out_specs=(
            P("section", None, ("dp", "tensor"), None),
            P("section", None, ("dp", "tensor"), None),
            P("section", ("dp", "tensor")),
            P("section", "dp", "tensor"),
            P("section", "dp", "tensor"),
            P("section", "tensor", "dp"),
            P("section", ("dp", "tensor")),
            P("section", "dp", None, "tensor"),
            P("section", "dp", "tensor", None),
        ),
        check_vma=False,
    )
```

time: 2090 us -> 979 us (0.47)
  waiting for transfers between devices: 972 us -> 445 us
  local copies, waits for them, and re-layouts: 348 us -> 53.2 us
  matrix products: 275 us -> 1.38 us
  other arithmetic: 257 us -> 49.6 us
  starting transfers between devices: 10.7 us -> 200 us
  Pallas kernels: 0 us -> 155 us
  blocking collectives: 190 us -> 49.1 us
    all_gather x5 -> x4, waiting for transfers between devices: 495 us -> 39.1 us  [the longest x2 23.1 us: per_device(): lax.all_gather(jnp.where(here, out_weight[0], out_far), 'dp', axis=1, til...]
    reduce_scatter x17 -> x0, waiting for transfers between devices: 456 us -> none  [the longest x1 297 us: per_device(): lax.psum_scatter(acc_in.astype(jnp.bfloat16), 'dp', scatter_dimension=0,...]
    ppermute x4 -> x168, waiting for transfers between devices: 17.5 us -> 406 us  [the longest x38 185 us: by_dp(): return lax.ppermute(value, 'dp', [(i, i ^ flip) for i in range(size)])]
    dot_general x66 -> x1, matrix products: 275 us -> 1.38 us  [per_device(): jnp.einsum('ij,smje->smie', lower, member.astype(BF), preferred_element_t...]
    ppermute x4 -> x168, starting transfers between devices: 8.77 us -> 200 us  [the longest x106 104 us: by_tensor(): return lax.ppermute(value, 'tensor', [(i, i ^ flip) for i in range(size)])]
    pallas_call x0 -> x15, Pallas kernels: none -> 155 us  [the longest x4 64.9 us: moe_bwd(): pl.pallas_call(functools.partial(moe_bwd_kernel, experts, cap, rows, n_dp...]
    all_gather x13 -> x2, blocking collectives: 139 us -> 49.1 us  [the longest x1 37.3 us: per_device(): lax.all_gather(jnp.stack([attn_gain[0], moe_gain[0]])[None], ('section',...]
    reshape x14 -> x3, local copies, waits for them, and re-layouts: 80 us -> 0.26 us  [per_device(): routing.reshape(n_dp, 2, n_t, rows, 2 * top)[:, :, flips]]
  transfers between devices with their start and end apart: 26 -> 172, of which waited for: 17 -> 61; matrix products, arithmetic and copies ran while one was open for 23% -> 8% of each run, Pallas kernels for 0% -> 16%
where the time goes in v1:
time: 979 us; the launch traced here: 970 us
  waiting for transfers between devices  445 us (45%)
  starting transfers between devices  200 us (20%)
  Pallas kernels  155 us (16%)
  local copies, waits for them, and re-layouts  53.2 us (5%)
  other arithmetic  49.6 us (5%)
  blocking collectives  49.1 us (5%)
  between operations  16.5 us (2%)
    ppermute x38, waiting for transfers between devices, by_dp(): return lax.ppermute(value, 'dp', [(i, i ^ flip) for i in range(size)])  185 us
    ppermute x106, waiting for transfers between devices, by_tensor(): return lax.ppermute(value, 'tensor', [(i, i ^ flip) for i in range(size)])  157 us
    ppermute x106, starting transfers between devices, by_tensor(): return lax.ppermute(value, 'tensor', [(i, i ^ flip) for i in range(size)])  104 us
    pallas_call x4, Pallas kernels, moe_bwd(): pl.pallas_call(functools.partial(moe_bwd_kernel, experts, cap, rows, n_dp...  64.9 us
    pallas_call x4, Pallas kernels, moe_fwd(): pl.pallas_call(functools.partial(moe_fwd_kernel, experts, cap, rows, n_dp...  56.8 us
    ppermute x38, starting transfers between devices, by_dp(): return lax.ppermute(value, 'dp', [(i, i ^ flip) for i in range(size)])  48.5 us
    ppermute x8, waiting for transfers between devices, from_host(): back = lax.ppermute(far[j], 'section', [(host, 1 - host)])  39.7 us
    all_gather x1, blocking collectives, per_device(): lax.all_gather(jnp.stack([attn_gain[0], moe_gain[0]])[None], ('section',...  37.3 us
  transfers between devices with their start and end apart: 172, of which 61 were waited for; matrix products, arithmetic and copies ran while one was open for 8% of the time, Pallas kernels for 16%

profile of v1, /device:TPU:9, one launch (start us, length us, event | category | flops | bytes accessed | tf_op | source)
XLA Modules:
  0.0 970.4 jit_solution(13875081291838447527)
XLA Ops:
  16.8 37.3 %all-gather.2 = bf16[32,2,96]{2,1,0:T(2,128)(2,1)S(1)} all-gather(bf16[1,2,96]{2,1,0:T(2,128)(2,1)S(1)} %maximum_bitcast_fusion.4), channel_id=2, replica_groups=mesh['section'=2,'dp'=4,'tensor'=4] {'section','dp','tensor'}, dimensions={0}, use_global_device_ids=true | all-gather | bytes 12672 | tf_op jit(solution)/shard_map/all_gather | solution.py:309
  60.7 11.8 %all-gather.1 = f32[8,256,8]{1,2,0:T(8,128)S(1)} all-gather(f32[2,256,8]{1,2,0:T(8,128)S(1)} %pad_maximum_fusion.14), channel_id=3, replica_groups=mesh['section'=2,'dp'=4,'tensor'=4] {'dp'}, dimensions={0}, use_global_device_ids=true | all-gather | bytes 81920 | tf_op jit(solution)/shard_map/all_gather | solution.py:351
  78.7 15.9 %all-gather.8.cloned.1.call-done = bf16[1536,512]{1,0:T(8,128)(2,1)} async-done(((bf16[384,512]{1,0:T(8,128)(2,1)}), bf16[1536,512]{1,0:T(8,128)(2,1)}) %all-gather.8.cloned.1.call-update) | async-done | bytes 1572880 | tf_op jit(solution)/shard_map/all_gather | solution.py:321
  103.5 23.1 %all-gather.10.cloned.1.call-done.wo = bf16[384,1536]{1,0:T(8,128)(2,1)} async-done(((bf16[384,384]{1,0:T(8,128)(2,1)}), bf16[384,1536]{1,0:T(8,128)(2,1)}) %all-gather.10.cloned.1.call-update) | async-done | bytes 1179664 | tf_op jit(solution)/shard_map/all_gather | solution.py:322
  163.6 10.6 %collective-permute-done.9 = bf16[64,1536]{1,0:T(8,128)(2,1)S(1)} collective-permute-done((bf16[64,1536]{1,0:T(8,128)(2,1)S(1)}, bf16[64,1536]{1,0:T(8,128)(2,1)S(1)}, u32[]{:S(2)}, u32[]{:S(2)}) %collective-permute-start.9) | collective-permute-done | bytes 196640 | tf_op jit(solution)/shard_map/ppermute | solution.py:33
  177.9 19.3 %collective-permute-done.13 = bf16[64,1536]{1,0:T(8,128)(2,1)S(1)} collective-permute-done((bf16[64,1536]{1,0:T(8,128)(2,1)S(1)}, bf16[64,1536]{1,0:T(8,128)(2,1)S(1)}, u32[]{:S(2)}, u32[]{:S(2)}) %collective-permute-start.13) | collective-permute-done | bytes 196640 | tf_op jit(solution)/shard_map/ppermute | solution.py:33
  219.8 14.3 %moe_fwd.4 = (bf16[4,320,1536]{2,1,0:T(8,128)(2,1)}, f32[4,320,384]{2,1,0:T(8,128)}, bf16[2,2,64,1536]{3,2,1,0:T(8,128)(2,1)}, bf16[2,2,64,1536]{3,2,1,0:T(8,128...) custom-call(bf16[2,64,1536]{2,1,0:T(8,128)(2,1)} %pad_maximum_fusion.1.refs_0_, ...), custom_call_target="tpu_custom_call" | custom-call | flops 4278190080 | bytes 20971520 | tf_op jit(solution)/shard_map/moe_fwd/pallas_call | solution.py:427
  246.7 14.1 %moe_fwd.5 = (bf16[4,320,1536]{2,1,0:T(8,128)(2,1)}, f32[4,320,384]{2,1,0:T(8,128)}, bf16[2,2,64,1536]{3,2,1,0:T(8,128)(2,1)}, bf16[2,2,64,1536]{3,2,1,0:T(8,128...) custom-call(bf16[2,64,1536]{2,1,0:T(8,128)(2,1)} %copy-done.127, ...), custom_call_target="tpu_custom_call" | custom-call | flops 4278190080 | bytes 20971520 | tf_op jit(solution)/shard_map/moe_fwd/pallas_call | solution.py:427
  265.9 16.7 %collective-permute-done.36 = bf16[2,64,1536]{2,1,0:T(8,128)(2,1)S(1)} collective-permute-done((bf16[2,64,1536]{2,1,0:T(8,128)(2,1)S(1)}, bf16[2,64,1536]{2,1,0:T(8,128)(2,1)S(1)}, u32[]{:S(2)}, u32[]{:S(2)}) %collective-permute-start.36) | collective-permute-done | bytes 393248 | tf_op jit(solution)/shard_map/ppermute | solution.py:28
  283.0 9.0 collective-permute-done.29
  294.5 5.3 collective-permute-done.37
  314.2 8.4 collective-permute-done.32
  367.3 8.2 collective-permute-done.49
  396.7 5.8 collective-permute-done.47.refs_2_
  405.0 5.9 collective-permute-done.52.refs_6_
  417.0 14.0 %moe_fwd.6 = (bf16[4,320,1536]{2,1,0:T(8,128)(2,1)}, f32[4,320,384]{2,1,0:T(8,128)}, bf16[2,2,64,1536]{3,2,1,0:T(8,128)(2,1)}, bf16[2,2,64,1536]{3,2,1,0:T(8,128...) custom-call(bf16[2,64,1536]{2,1,0:T(8,128)(2,1)} %copy-done.96, ...), custom_call_target="tpu_custom_call" | custom-call | flops 4278190080 | bytes 20971520 | tf_op jit(solution)/shard_map/moe_fwd/pallas_call | solution.py:427
  434.4 15.9 %moe_bwd.4 = (bf16[4,320,1536]{2,1,0:T(8,128)(2,1)}, bf16[4,320,192]{2,1,0:T(8,128)(2,1)}, bf16[4,320,384]{2,1,0:T(8,128)(2,1)}, bf16[2,2,64,1536]{3,2,1,0:T(8,1...) custom-call(bf16[2,64,1536]{2,1,0:T(8,128)(2,1)} %copy-done.94, ...), custom_call_target="tpu_custom_call" | custom-call | flops 4278190080 | bytes 20971520 | tf_op jit(solution)/shard_map/moe_bwd/pallas_call | solution.py:447
  452.2 14.3 %moe_fwd.7 = (bf16[4,320,1536]{2,1,0:T(8,128)(2,1)}, f32[4,320,384]{2,1,0:T(8,128)}, bf16[2,2,64,1536]{3,2,1,0:T(8,128)(2,1)}, bf16[2,2,64,1536]{3,2,1,0:T(8,128...) custom-call(bf16[2,64,1536]{2,1,0:T(8,128)(2,1)} %collective-permute-done.56.refs_0_, ...), custom_call_target="tpu_custom_call" | custom-call | flops 4278190080 | bytes 20971520 | tf_op jit(solution)/shard_map/moe_fwd/pallas_call | solution.py:427
  469.5 16.2 %moe_bwd.5 = (bf16[4,320,1536]{2,1,0:T(8,128)(2,1)}, bf16[4,320,192]{2,1,0:T(8,128)(2,1)}, bf16[4,320,384]{2,1,0:T(8,128)(2,1)}, bf16[2,2,64,1536]{3,2,1,0:T(8,1...) custom-call(bf16[2,64,1536]{2,1,0:T(8,128)(2,1)} %pad_maximum_fusion., ...), custom_call_target="tpu_custom_call" | custom-call | flops 4278190080 | bytes 20971520 | tf_op jit(solution)/shard_map/moe_bwd/pallas_call | solution.py:447
  498.7 31.0 %collective-permute-done.102 = bf16[2,64,1536]{2,1,0:T(8,128)(2,1)S(1)} collective-permute-done((bf16[2,64,1536]{2,1,0:T(8,128)(2,1)S(1)}, bf16[2,64,1536]{2,1,0:T(8,128)(2,1)S(1)}, u32[]{:S(2)}, u32[]{:S(2)}) %collective-permute-start.102) | collective-permute-done | bytes 393248 | tf_op jit(solution)/shard_map/ppermute | solution.py:28
  530.9 8.6 collective-permute-done.95
  540.3 8.0 collective-permute-done.72
  548.8 7.4 collective-permute-done.65
  557.8 7.3 collective-permute-done.103
  567.8 5.8 collective-permute-done.96
  588.6 6.2 collective-permute-start.74
  594.8 6.4 collective-permute-start.105
  601.2 5.5 collective-permute-start.107
  612.5 11.3 %collective-permute-done.68 = bf16[64,1536]{1,0:T(8,128)(2,1)S(1)} collective-permute-done((bf16[64,1536]{1,0:T(8,128)(2,1)S(1)}, bf16[64,1536]{1,0:T(8,128)(2,1)S(1)}, u32[]{:S(2)}, u32[]{:S(2)}) %collective-permute-start.68) | collective-permute-done | bytes 196640 | tf_op jit(solution)/shard_map/ppermute | solution.py:33
  623.8 5.7 collective-permute-done.67
  630.6 4.9 collective-permute-done.75
  643.6 9.8 %collective-permute-done.114 = bf16[64,1536]{1,0:T(8,128)(2,1)S(1)} collective-permute-done((bf16[64,1536]{1,0:T(8,128)(2,1)S(1)}, bf16[64,1536]{1,0:T(8,128)(2,1)S(1)}, u32[]{:S(2)}, u32[]{:S(2)}) %collective-permute-start.114) | collective-permute-done | bytes 196640 | tf_op jit(solution)/shard_map/ppermute | solution.py:33
  667.6 6.8 collective-permute-done.125.refs_4_
  680.4 16.5 %moe_bwd.6 = (bf16[4,320,1536]{2,1,0:T(8,128)(2,1)}, bf16[4,320,192]{2,1,0:T(8,128)(2,1)}, bf16[4,320,384]{2,1,0:T(8,128)(2,1)}, bf16[2,2,64,1536]{3,2,1,0:T(8,1...) custom-call(bf16[2,64,1536]{2,1,0:T(8,128)(2,1)} %pad_maximum_fusion., ...), custom_call_target="tpu_custom_call" | custom-call | flops 4278190080 | bytes 20971520 | tf_op jit(solution)/shard_map/moe_bwd/pallas_call | solution.py:447
  704.3 16.2 %moe_bwd.7 = (bf16[4,320,1536]{2,1,0:T(8,128)(2,1)}, bf16[4,320,192]{2,1,0:T(8,128)(2,1)}, bf16[4,320,384]{2,1,0:T(8,128)(2,1)}, bf16[2,2,64,1536]{3,2,1,0:T(8,1...) custom-call(bf16[2,64,1536]{2,1,0:T(8,128)(2,1)} %collective-permute-, ...), custom_call_target="tpu_custom_call" | custom-call | flops 4278190080 | bytes 20971520 | tf_op jit(solution)/shard_map/moe_bwd/pallas_call | solution.py:447
  726.6 22.0 %collective-permute-done.137 = bf16[2,64,1536]{2,1,0:T(8,128)(2,1)S(1)} collective-permute-done((bf16[2,64,1536]{2,1,0:T(8,128)(2,1)S(1)}, bf16[2,64,1536]{2,1,0:T(8,128)(2,1)S(1)}, u32[]{:S(2)}, u32[]{:S(2)}) %collective-permute-start.137) | collective-permute-done | bytes 393248 | tf_op jit(solution)/shard_map/ppermute | solution.py:28
  750.1 7.9 collective-permute-done.130
  767.1 6.9 collective-permute-done.131
  777.6 17.6 %collective-permute-done.133 = bf16[64,1536]{1,0:T(8,128)(2,1)S(1)} collective-permute-done((bf16[64,1536]{1,0:T(8,128)(2,1)S(1)}, bf16[64,1536]{1,0:T(8,128)(2,1)S(1)}, u32[]{:S(2)}, u32[]{:S(2)}) %collective-permute-start.133) | collective-permute-done | bytes 196640 | tf_op jit(solution)/shard_map/ppermute | solution.py:33
  795.2 5.8 collective-permute-done.132
  815.5 16.9 %moe_wgrad.1 = (f32[4,1536,384]{2,1,0:T(8,128)}, f32[4,192,1536]{2,1,0:T(8,128)}) custom-call(s32[1]{0:T(128)} %bitcast.114.sel, bf16[4,320,1536]{2,1,0:T(8,128)(2,1)} %get-tuple-element.159.refs_0_, bf16[4,320,1536]{2,1,0:T(8,128)(2,1)} %get-tuple-element.160.refs_1_, bf16[4,320,384]{2,1,0:T(8,128)(2,1)} %get-tuple-element.161.refs_2_, ...), custom_call_target="tpu_custom_call" | custom-call | flops 8556380160 | bytes 41943040 | tf_op jit(solution)/shard_map/moe_wgrad/pallas_call | solution.py:478
  847.1 15.4 %collective-permute-done.162 = bf16[384,384]{1,0:T(8,128)(2,1)S(1)} collective-permute-done((bf16[384,384]{1,0:T(8,128)(2,1)S(1)}, bf16[384,384]{1,0:T(8,128)(2,1)S(1)}, u32[]{:S(2)}, u32[]{:S(2)}) %collective-permute-start.162) | collective-permute-done | bytes 294944 | tf_op jit(solution)/shard_map/ppermute | solution.py:33
  863.3 24.0 %collective-permute-done.161 = bf16[384,384]{1,0:T(8,128)(2,1)S(1)} collective-permute-done((bf16[384,384]{1,0:T(8,128)(2,1)S(1)}, bf16[384,384]{1,0:T(8,128)(2,1)S(1)}, u32[]{:S(2)}, u32[]{:S(2)}) %collective-permute-start.161) | collective-permute-done | bytes 294944 | tf_op jit(solution)/shard_map/ppermute | solution.py:33
  898.1 5.6 collective-permute-done.149
  913.2 11.0 %collective-permute-done.154 = bf16[384,512]{1,0:T(8,128)(2,1)S(1)} collective-permute-done((bf16[384,512]{1,0:T(8,128)(2,1)S(1)}, bf16[384,512]{1,0:T(8,128)(2,1)S(1)}, u32[]{:S(2)}, u32[]{:S(2)}) %collective-permute-start.154) | collective-permute-done | bytes 393248 | tf_op jit(solution)/shard_map/ppermute | solution.py:33
  926.5 17.5 %collective-permute-done.152 = bf16[384,512]{1,0:T(8,128)(2,1)S(1)} collective-permute-done((bf16[384,512]{1,0:T(8,128)(2,1)S(1)}, bf16[384,512]{1,0:T(8,128)(2,1)S(1)}, u32[]{:S(2)}, u32[]{:S(2)}) %collective-permute-start.152) | collective-permute-done | bytes 393248 | tf_op jit(solution)/shard_map/ppermute | solution.py:33
  945.8 7.5 collective-permute-done.159
  953.9 5.8 collective-permute-start.160
  (819 shorter events, 366.0 us)
Async XLA Ops:
  7.2 87.4 %all-gather.8.cloned.1.call-start = ((), (), s32[]{:S(2)}) async-start(), calls=%async_computation | async-start | bytes 1966080 | tf_op jit(solution)/shard_map/all_gather | solution.py:321
  14.9 41.2 %collective-permute-start.4 = (bf16[384,512]{1,0:T(8,128)(2,1)S(1)}, bf16[384,512]{1,0:T(8,128)(2,1)S(1)}, u32[]{:S(2)}, u32[]{:S(2)}) collective-permute-start(bf16[384,512]{1,0:T(8,128)(2,1)S(1)} %pad_maximum_fusion), channel_id=1, source_target_pairs={{0,16},{16,0},{1,17},{17,1},{2,18},{18,2},{3,19},{19,3},{4,20},{20... | collective-permute-start | bytes 1179656 | tf_op jit(solution)/shard_map/ppermute | solution.py:37
  57.2 69.4 %all-gather.10.cloned.1.call-start = ((), (), s32[]{:S(2)}) async-start(), calls=%async_computation.1 | async-start | bytes 1474560 | tf_op jit(solution)/shard_map/all_gather | solution.py:322
  58.0 44.1 %collective-permute-start = (bf16[64,1536]{1,0:T(8,128)(2,1)S(1)}, bf16[64,1536]{1,0:T(8,128)(2,1)S(1)}, u32[]{:S(2)}, u32[]{:S(2)}) collective-permute-start(bf16[64,1536]{1,0:T(8,128)(2,1)S(1)} %fusion.46.a0), channel_id=1, source_target_pairs={{0,1},{1,0},{2,3},{3,2},{4,5},{5,4},{6,7},{7,6},{8,9},{9,8},{10,11... | collective-permute-start | bytes 589832 | tf_op jit(solution)/shard_map/ppermute | solution.py:28
  58.3 40.9 %collective-permute-start.1 = (bf16[64,1536]{1,0:T(8,128)(2,1)S(1)}, bf16[64,1536]{1,0:T(8,128)(2,1)S(1)}, u32[]{:S(2)}, u32[]{:S(2)}) collective-permute-start(bf16[64,1536]{1,0:T(8,128)(2,1)S(1)} %fusion.46.a0), channel_id=1, source_target_pairs={{0,2},{1,3},{2,0},{3,1},{4,6},{5,7},{6,4},{7,5},{8,10},{9,11},{10,... | collective-permute-start | bytes 589832 | tf_op jit(solution)/shard_map/ppermute | solution.py:28
  75.0 236.7 %all-gather.12.cloned.1.call-start = ((), (), s32[]{:S(2)}) async-start(), calls=%async_computation.2 | async-start | bytes 1966080 | tf_op jit(solution)/shard_map/all_gather | solution.py:321
  152.8 186.8 %all-gather.14.cloned.1.call-start = ((), (), s32[]{:S(2)}) async-start(), calls=%async_computation.3 | async-start | bytes 1474560 | tf_op jit(solution)/shard_map/all_gather | solution.py:322
  160.9 36.3 %collective-permute-start.13 = (bf16[64,1536]{1,0:T(8,128)(2,1)S(1)}, bf16[64,1536]{1,0:T(8,128)(2,1)S(1)}, u32[]{:S(2)}, u32[]{:S(2)}) collective-permute-start(bf16[64,1536]{1,0:T(8,128)(2,1)S(1)} %multiply_convert_fusion.2), channel_id=1, source_target_pairs={{0,8},{4,12},{8,0},{12,4},{1,9},{5,13},{9,1},{13,5},{2,10},{6,14},... | collective-permute-start | bytes 589832 | tf_op jit(solution)/shard_map/ppermute | solution.py:33
  175.0 28.8 %collective-permute-start.20 = (bf16[2,64,1536]{2,1,0:T(8,128)(2,1)}, bf16[2,64,1536]{2,1,0:T(8,128)(2,1)S(1)}, u32[]{:S(2)}, u32[]{:S(2)}) collective-permute-start(bf16[2,64,1536]{2,1,0:T(8,128)(2,1)} %pad_maximum_fusion.1.refs_0_), channel_id=1, source_target_pairs={{16,0},{17,1},{18,2},{19,3},{20,4},{21,5},{22,6},{23,7},{24,8},{25... | collective-permute-start | bytes 1179656 | tf_op jit(solution)/shard_map/ppermute | solution.py:41
  176.3 27.6 %collective-permute-start.11 = (bf16[2,64,1536]{2,1,0:T(8,128)(2,1)}, bf16[2,64,1536]{2,1,0:T(8,128)(2,1)}, u32[]{:S(2)}, u32[]{:S(2)}) collective-permute-start(bf16[2,64,1536]{2,1,0:T(8,128)(2,1)} %pad_maximum_fusion.1.refs_0_), channel_id=1, source_target_pairs={{0,2},{1,3},{2,0},{3,1},{4,6},{5,7},{6,4},{7,5},{8,10},{9,11},{10,... | collective-permute-start | bytes 1179656 | tf_op jit(solution)/shard_map/ppermute | solution.py:28
  210.6 23.5 %collective-permute-start.77 = (bf16[2,64,1536]{2,1,0:T(8,128)(2,1)}, bf16[2,64,1536]{2,1,0:T(8,128)(2,1)S(1)}, u32[]{:S(2)}, u32[]{:S(2)}) collective-permute-start(bf16[2,64,1536]{2,1,0:T(8,128)(2,1)} %convert_bitcast_fusion.1), channel_id=1, source_target_pairs={{0,4},{4,0},{8,12},{12,8},{1,5},{5,1},{9,13},{13,9},{2,6},{6,2},{1... | collective-permute-start | bytes 1179656 | tf_op jit(solution)/shard_map/ppermute | solution.py:33
  234.1 26.8 %collective-permute-start.33 = (bf16[2,2,64,1536]{3,2,1,0:T(8,128)(2,1)}, bf16[2,2,64,1536]{3,2,1,0:T(8,128)(2,1)S(1)}, u32[]{:S(2)}, u32[]{:S(2)}) collective-permute-start(bf16[2,2,64,1536]{3,2,1,0:T(8,128)(2,1)} %get-tuple-element.100), channel_id=1, source_target_pairs={{0,1},{1,0},{2,3},{3,2},{4,5},{5,4},{6,7},{7,6},{8,9},{9,8},{10,11... | collective-permute-start | bytes 2359304 | tf_op jit(solution)/shard_map/ppermute | solution.py:28
  238.3 23.6 %collective-permute-start.18 = (bf16[2,2,64,1536]{3,2,1,0:T(8,128)(2,1)}, bf16[2,2,64,1536]{3,2,1,0:T(8,128)(2,1)S(1)}, u32[]{:S(2)}, u32[]{:S(2)}) collective-permute-start(bf16[2,2,64,1536]{3,2,1,0:T(8,128)(2,1)} %get-tuple-element.96), channel_id=1, source_target_pairs={{0,1},{1,0},{2,3},{3,2},{4,5},{5,4},{6,7},{7,6},{8,9},{9,8},{10,11... | collective-permute-start | bytes 2359304 | tf_op jit(solution)/shard_map/ppermute | solution.py:28
  240.5 69.9 %collective-permute-start.82 = (bf16[2,64,1536]{2,1,0:T(8,128)(2,1)}, bf16[2,64,1536]{2,1,0:T(8,128)(2,1)S(1)}, u32[]{:S(2)}, u32[]{:S(2)}) collective-permute-start(bf16[2,64,1536]{2,1,0:T(8,128)(2,1)} %convert_bitcast_fusion.1), channel_id=1, source_target_pairs={{0,12},{4,8},{8,4},{12,0},{1,13},{5,9},{9,5},{13,1},{2,14},{6,10},... | collective-permute-start | bytes 1179656 | tf_op jit(solution)/shard_map/ppermute | solution.py:33
  241.3 90.1 %collective-permute-start.81 = (bf16[2,64,1536]{2,1,0:T(8,128)(2,1)}, bf16[2,64,1536]{2,1,0:T(8,128)(2,1)S(1)}, u32[]{:S(2)}, u32[]{:S(2)}) collective-permute-start(bf16[2,64,1536]{2,1,0:T(8,128)(2,1)} %convert_bitcast_fusion.1), channel_id=1, source_target_pairs={{0,8},{4,12},{8,0},{12,4},{1,9},{5,13},{9,1},{13,5},{2,10},{6,14},... | collective-permute-start | bytes 1179656 | tf_op jit(solution)/shard_map/ppermute | solution.py:33
  245.7 131.2 %collective-permute-start.88 = (bf16[2,64,1536]{2,1,0:T(8,128)(2,1)}, bf16[2,64,1536]{2,1,0:T(8,128)(2,1)}, u32[]{:S(2)}, u32[]{:S(2)}) collective-permute-start(bf16[2,64,1536]{2,1,0:T(8,128)(2,1)} %pad_maximum_fusion.7.refs_0_), channel_id=1, source_target_pairs={{0,1},{1,0},{2,3},{3,2},{4,5},{5,4},{6,7},{7,6},{8,9},{9,8},{10,11... | collective-permute-start | bytes 1179656 | tf_op jit(solution)/shard_map/ppermute | solution.py:28
  263.9 29.9 %collective-permute-start.34 = (bf16[2,64,1536]{2,1,0:T(8,128)(2,1)S(1)}, bf16[2,64,1536]{2,1,0:T(8,128)(2,1)S(1)}, u32[]{:S(2)}, u32[]{:S(2)}) collective-permute-start(bf16[2,64,1536]{2,1,0:T(8,128)(2,1)S(1)} %slice_bitcast_fusion.31), channel_id=1, source_target_pairs={{0,2},{1,3},{2,0},{3,1},{4,6},{5,7},{6,4},{7,5},{8,10},{9,11},{10,... | collective-permute-start | bytes 1179656 | tf_op jit(solution)/shard_map/ppermute | solution.py:28
  312.8 64.4 %collective-permute-start.89 = (bf16[2,64,1536]{2,1,0:T(8,128)(2,1)}, bf16[2,64,1536]{2,1,0:T(8,128)(2,1)}, u32[]{:S(2)}, u32[]{:S(2)}) collective-permute-start(bf16[2,64,1536]{2,1,0:T(8,128)(2,1)} %pad_maximum_fusion.7.refs_0_), channel_id=1, source_target_pairs={{0,2},{1,3},{2,0},{3,1},{4,6},{5,7},{6,4},{7,5},{8,10},{9,11},{10,... | collective-permute-start | bytes 1179656 | tf_op jit(solution)/shard_map/ppermute | solution.py:28
  347.8 34.3 %collective-permute-start.91 = (bf16[2,64,1536]{2,1,0:T(8,128)(2,1)S(1)}, bf16[2,64,1536]{2,1,0:T(8,128)(2,1)S(1)}, u32[]{:S(2)}, u32[]{:S(2)}) collective-permute-start(bf16[2,64,1536]{2,1,0:T(8,128)(2,1)S(1)} %pad_maximum_fusion.8.refs_4_), channel_id=1, source_target_pairs={{0,1},{1,0},{2,3},{3,2},{4,5},{5,4},{6,7},{7,6},{8,9},{9,8},{10,11... | collective-permute-start | bytes 1179656 | tf_op jit(solution)/shard_map/ppermute | solution.py:28
  383.3 27.6 %collective-permute-start.52 = (bf16[2,64,1536]{2,1,0:T(8,128)(2,1)S(1)}, bf16[2,64,1536]{2,1,0:T(8,128)(2,1)S(1)}, u32[]{:S(2)}, u32[]{:S(2)}) collective-permute-start(bf16[2,64,1536]{2,1,0:T(8,128)(2,1)S(1)} %pad_maximum_fusion.4.refs_4_), channel_id=1, source_target_pairs={{0,2},{1,3},{2,0},{3,1},{4,6},{5,7},{6,4},{7,5},{8,10},{9,11},{10,... | collective-permute-start | bytes 1179656 | tf_op jit(solution)/shard_map/ppermute | solution.py:28
  385.7 27.5 %collective-permute-start.60 = (bf16[2,64,1536]{2,1,0:T(8,128)(2,1)S(1)}, bf16[2,64,1536]{2,1,0:T(8,128)(2,1)S(1)}, u32[]{:S(2)}, u32[]{:S(2)}) collective-permute-start(bf16[2,64,1536]{2,1,0:T(8,128)(2,1)S(1)} %pad_maximum_fusion.4.refs_4_), channel_id=1, source_target_pairs={{0,16},{1,17},{2,18},{3,19},{4,20},{5,21},{6,22},{7,23},{8,24},{9,... | collective-permute-start | bytes 1179656 | tf_op jit(solution)/shard_map/ppermute | solution.py:41
  451.0 34.8 %collective-permute-start.99 = (bf16[2,2,64,1536]{3,2,1,0:T(8,128)(2,1)}, bf16[2,2,64,1536]{3,2,1,0:T(8,128)(2,1)}, u32[]{:S(2)}, u32[]{:S(2)}) collective-permute-start(bf16[2,2,64,1536]{3,2,1,0:T(8,128)(2,1)} %get-tuple-element.120), channel_id=1, source_target_pairs={{0,1},{1,0},{2,3},{3,2},{4,5},{5,4},{6,7},{7,6},{8,9},{9,8},{10,11... | collective-permute-start | bytes 2359304 | tf_op jit(solution)/shard_map/ppermute | solution.py:28
  451.7 35.6 %collective-permute-start.86 = (bf16[2,2,64,1536]{3,2,1,0:T(8,128)(2,1)}, bf16[2,2,64,1536]{3,2,1,0:T(8,128)(2,1)S(1)}, u32[]{:S(2)}, u32[]{:S(2)}) collective-permute-start(bf16[2,2,64,1536]{3,2,1,0:T(8,128)(2,1)} %get-tuple-element.115), channel_id=1, source_target_pairs={{0,1},{1,0},{2,3},{3,2},{4,5},{5,4},{6,7},{7,6},{8,9},{9,8},{10,11... | collective-permute-start | bytes 2359304 | tf_op jit(solution)/shard_map/ppermute | solution.py:28
  451.8 37.8 %collective-permute-start.69 = (bf16[2,2,64,1536]{3,2,1,0:T(8,128)(2,1)}, bf16[2,2,64,1536]{3,2,1,0:T(8,128)(2,1)}, u32[]{:S(2)}, u32[]{:S(2)}) collective-permute-start(bf16[2,2,64,1536]{3,2,1,0:T(8,128)(2,1)} %get-tuple-element.110), channel_id=1, source_target_pairs={{0,1},{1,0},{2,3},{3,2},{4,5},{5,4},{6,7},{7,6},{8,9},{9,8},{10,11... | collective-permute-start | bytes 2359304 | tf_op jit(solution)/shard_map/ppermute | solution.py:28
  466.6 120.6 %collective-permute-start.76 = (f32[64,1536]{1,0:T(8,128)}, f32[64,1536]{1,0:T(8,128)}, u32[]{:S(2)}, u32[]{:S(2)}) collective-permute-start(f32[64,1536]{1,0:T(8,128)} %select_bitcast_fusion), channel_id=1, source_target_pairs={{0,16},{16,0},{1,17},{17,1},{2,18},{18,2},{3,19},{19,3},{4,20},{20... | collective-permute-start | bytes 1179656 | tf_op jit(solution)/shard_map/ppermute | solution.py:37
  493.4 64.2 %collective-permute-start.100 = (bf16[2,64,1536]{2,1,0:T(8,128)(2,1)S(1)}, bf16[2,64,1536]{2,1,0:T(8,128)(2,1)S(1)}, u32[]{:S(2)}, u32[]{:S(2)}) collective-permute-start(bf16[2,64,1536]{2,1,0:T(8,128)(2,1)S(1)} %slice_bitcast_fusion.15), channel_id=1, source_target_pairs={{0,2},{1,3},{2,0},{3,1},{4,6},{5,7},{6,4},{7,5},{8,10},{9,11},{10,... | collective-permute-start | bytes 1179656 | tf_op jit(solution)/shard_map/ppermute | solution.py:28
  495.4 71.1 %collective-permute-start.87 = (bf16[2,64,1536]{2,1,0:T(8,128)(2,1)S(1)}, bf16[2,64,1536]{2,1,0:T(8,128)(2,1)S(1)}, u32[]{:S(2)}, u32[]{:S(2)}) collective-permute-start(bf16[2,64,1536]{2,1,0:T(8,128)(2,1)S(1)} %slice_bitcast_fusion.19), channel_id=1, source_target_pairs={{0,2},{1,3},{2,0},{3,1},{4,6},{5,7},{6,4},{7,5},{8,10},{9,11},{10,... | collective-permute-start | bytes 1179656 | tf_op jit(solution)/shard_map/ppermute | solution.py:28
  495.8 80.5 %collective-permute-start.70 = (bf16[2,64,1536]{2,1,0:T(8,128)(2,1)S(1)}, bf16[2,64,1536]{2,1,0:T(8,128)(2,1)S(1)}, u32[]{:S(2)}, u32[]{:S(2)}) collective-permute-start(bf16[2,64,1536]{2,1,0:T(8,128)(2,1)S(1)} %slice_bitcast_fusion.23), channel_id=1, source_target_pairs={{0,2},{1,3},{2,0},{3,1},{4,6},{5,7},{6,4},{7,5},{8,10},{9,11},{10,... | collective-permute-start | bytes 1179656 | tf_op jit(solution)/shard_map/ppermute | solution.py:28
  497.6 32.1 %collective-permute-start.102 = (bf16[2,64,1536]{2,1,0:T(8,128)(2,1)S(1)}, bf16[2,64,1536]{2,1,0:T(8,128)(2,1)S(1)}, u32[]{:S(2)}, u32[]{:S(2)}) collective-permute-start(bf16[2,64,1536]{2,1,0:T(8,128)(2,1)S(1)} %slice_bitcast_fusion.13), channel_id=1, source_target_pairs={{0,2},{1,3},{2,0},{3,1},{4,6},{5,7},{6,4},{7,5},{8,10},{9,11},{10,... | collective-permute-start | bytes 1179656 | tf_op jit(solution)/shard_map/ppermute | solution.py:28
  557.6 49.1 %collective-permute-start.55 = (bf16[2,64,1536]{2,1,0:T(8,128)(2,1)S(1)}, bf16[2,64,1536]{2,1,0:T(8,128)(2,1)S(1)}, u32[]{:S(2)}, u32[]{:S(2)}) collective-permute-start(bf16[2,64,1536]{2,1,0:T(8,128)(2,1)S(1)} %slice_bitcast_fusion.27), channel_id=1, source_target_pairs={{0,2},{1,3},{2,0},{3,1},{4,6},{5,7},{6,4},{7,5},{8,10},{9,11},{10,... | collective-permute-start | bytes 1179656 | tf_op jit(solution)/shard_map/ppermute | solution.py:28
  582.2 24.5 %collective-permute-start.66 = (bf16[2,64,1536]{2,1,0:T(8,128)(2,1)S(1)}, bf16[2,64,1536]{2,1,0:T(8,128)(2,1)S(1)}, u32[]{:S(2)}, u32[]{:S(2)}) collective-permute-start(bf16[2,64,1536]{2,1,0:T(8,128)(2,1)S(1)} %fusion.29), channel_id=1, source_target_pairs={{16,0},{17,1},{18,2},{19,3},{20,4},{21,5},{22,6},{23,7},{24,8},{25... | collective-permute-start | bytes 1179656 | tf_op jit(solution)/shard_map/ppermute | solution.py:521
  588.6 23.9 %collective-permute-start.74 = (bf16[64,1536]{1,0:T(8,128)(2,1)S(1)}, bf16[64,1536]{1,0:T(8,128)(2,1)S(1)}, u32[]{:S(2)}, u32[]{:S(2)}) collective-permute-start(bf16[64,1536]{1,0:T(8,128)(2,1)S(1)} %slice_bitcast_fusion.52), channel_id=1, source_target_pairs={{0,4},{4,0},{8,12},{12,8},{1,5},{5,1},{9,13},{13,9},{2,6},{6,2},{1... | collective-permute-start | bytes 589832 | tf_op jit(solution)/shard_map/ppermute | solution.py:33
  642.2 24.7 %collective-permute-start.121 = (bf16[2,64,1536]{2,1,0:T(8,128)(2,1)}, bf16[2,64,1536]{2,1,0:T(8,128)(2,1)}, u32[]{:S(2)}, u32[]{:S(2)}) collective-permute-start(bf16[2,64,1536]{2,1,0:T(8,128)(2,1)} %pad_maximum_fusion.9.refs_0_), channel_id=1, source_target_pairs={{16,0},{17,1},{18,2},{19,3},{20,4},{21,5},{22,6},{23,7},{24,8},{25... | collective-permute-start | bytes 1179656 | tf_op jit(solution)/shard_map/ppermute | solution.py:41
  643.5 23.5 %collective-permute-start.112 = (bf16[2,64,1536]{2,1,0:T(8,128)(2,1)}, bf16[2,64,1536]{2,1,0:T(8,128)(2,1)}, u32[]{:S(2)}, u32[]{:S(2)}) collective-permute-start(bf16[2,64,1536]{2,1,0:T(8,128)(2,1)} %pad_maximum_fusion.9.refs_0_), channel_id=1, source_target_pairs={{0,2},{1,3},{2,0},{3,1},{4,6},{5,7},{6,4},{7,5},{8,10},{9,11},{10,... | collective-permute-start | bytes 1179656 | tf_op jit(solution)/shard_map/ppermute | solution.py:28
  696.9 24.0 %collective-permute-start.134 = (bf16[2,2,64,1536]{3,2,1,0:T(8,128)(2,1)}, bf16[2,2,64,1536]{3,2,1,0:T(8,128)(2,1)S(1)}, u32[]{:S(2)}, u32[]{:S(2)}) collective-permute-start(bf16[2,2,64,1536]{3,2,1,0:T(8,128)(2,1)} %get-tuple-element.136), channel_id=1, source_target_pairs={{0,1},{1,0},{2,3},{3,2},{4,5},{5,4},{6,7},{7,6},{8,9},{9,8},{10,11... | collective-permute-start | bytes 2359304 | tf_op jit(solution)/shard_map/ppermute | solution.py:28
  699.6 143.9 %collective-permute-start.166 = (bf16[384,384]{1,0:T(8,128)(2,1)}, bf16[384,384]{1,0:T(8,128)(2,1)}, u32[]{:S(2)}, u32[]{:S(2)}) collective-permute-start(bf16[384,384]{1,0:T(8,128)(2,1)} %get-tuple-element.219), channel_id=1, source_target_pairs={{0,4},{4,0},{8,12},{12,8},{1,5},{5,1},{9,13},{13,9},{2,6},{6,2},{1... | collective-permute-start | bytes 884744 | tf_op jit(solution)/shard_map/ppermute | solution.py:33
  702.1 142.3 %collective-permute-start.165 = (bf16[384,384]{1,0:T(8,128)(2,1)}, bf16[384,384]{1,0:T(8,128)(2,1)}, u32[]{:S(2)}, u32[]{:S(2)}) collective-permute-start(bf16[384,384]{1,0:T(8,128)(2,1)} %get-tuple-element.220), channel_id=1, source_target_pairs={{0,8},{4,12},{8,0},{12,4},{1,9},{5,13},{9,1},{13,5},{2,10},{6,14},... | collective-permute-start | bytes 884744 | tf_op jit(solution)/shard_map/ppermute | solution.py:33
  721.3 38.1 %collective-permute-start.135 = (bf16[2,64,1536]{2,1,0:T(8,128)(2,1)S(1)}, bf16[2,64,1536]{2,1,0:T(8,128)(2,1)S(1)}, u32[]{:S(2)}, u32[]{:S(2)}) collective-permute-start(bf16[2,64,1536]{2,1,0:T(8,128)(2,1)S(1)} %slice_bitcast_fusion.7), channel_id=1, source_target_pairs={{0,2},{1,3},{2,0},{3,1},{4,6},{5,7},{6,4},{7,5},{8,10},{9,11},{10,... | collective-permute-start | bytes 1179656 | tf_op jit(solution)/shard_map/ppermute | solution.py:28
  724.4 42.8 %collective-permute-start.120 = (bf16[2,64,1536]{2,1,0:T(8,128)(2,1)S(1)}, bf16[2,64,1536]{2,1,0:T(8,128)(2,1)S(1)}, u32[]{:S(2)}, u32[]{:S(2)}) collective-permute-start(bf16[2,64,1536]{2,1,0:T(8,128)(2,1)S(1)} %slice_bitcast_fusion.11), channel_id=1, source_target_pairs={{0,2},{1,3},{2,0},{3,1},{4,6},{5,7},{6,4},{7,5},{8,10},{9,11},{10,... | collective-permute-start | bytes 1179656 | tf_op jit(solution)/shard_map/ppermute | solution.py:28
  775.9 25.0 %collective-permute-start.132 = (bf16[64,1536]{1,0:T(8,128)(2,1)S(1)}, bf16[64,1536]{1,0:T(8,128)(2,1)S(1)}, u32[]{:S(2)}, u32[]{:S(2)}) collective-permute-start(bf16[64,1536]{1,0:T(8,128)(2,1)S(1)} %get-tuple-element.234), channel_id=1, source_target_pairs={{0,12},{4,8},{8,4},{12,0},{1,13},{5,9},{9,5},{13,1},{2,14},{6,10},... | collective-permute-start | bytes 589832 | tf_op jit(solution)/shard_map/ppermute | solution.py:33
  776.8 68.9 %collective-permute-start.164 = (bf16[384,384]{1,0:T(8,128)(2,1)}, bf16[384,384]{1,0:T(8,128)(2,1)}, u32[]{:S(2)}, u32[]{:S(2)}) collective-permute-start(bf16[384,384]{1,0:T(8,128)(2,1)} %get-tuple-element.218), channel_id=1, source_target_pairs={{0,12},{4,8},{8,4},{12,0},{1,13},{5,9},{9,5},{13,1},{2,14},{6,10},... | collective-permute-start | bytes 884744 | tf_op jit(solution)/shard_map/ppermute | solution.py:33
  843.5 43.8 %collective-permute-start.161 = (bf16[384,384]{1,0:T(8,128)(2,1)S(1)}, bf16[384,384]{1,0:T(8,128)(2,1)S(1)}, u32[]{:S(2)}, u32[]{:S(2)}) collective-permute-start(bf16[384,384]{1,0:T(8,128)(2,1)S(1)} %get-tuple-element.221), channel_id=1, source_target_pairs={{0,12},{4,8},{8,4},{12,0},{1,13},{5,9},{9,5},{13,1},{2,14},{6,10},... | collective-permute-start | bytes 884744 | tf_op jit(solution)/shard_map/ppermute | solution.py:33
  844.4 61.8 %collective-permute-start.158 = (bf16[384,512]{1,0:T(8,128)(2,1)S(1)}, bf16[384,512]{1,0:T(8,128)(2,1)S(1)}, u32[]{:S(2)}, u32[]{:S(2)}) collective-permute-start(bf16[384,512]{1,0:T(8,128)(2,1)S(1)} %copy-done.100), channel_id=1, source_target_pairs={{0,4},{4,0},{8,12},{12,8},{1,5},{5,1},{9,13},{13,9},{2,6},{6,2},{1... | collective-permute-start | bytes 1179656 | tf_op jit(solution)/shard_map/ppermute | solution.py:33
  845.7 67.4 %collective-permute-start.157 = (bf16[384,512]{1,0:T(8,128)(2,1)S(1)}, bf16[384,512]{1,0:T(8,128)(2,1)S(1)}, u32[]{:S(2)}, u32[]{:S(2)}) collective-permute-start(bf16[384,512]{1,0:T(8,128)(2,1)S(1)} %copy-done.99), channel_id=1, source_target_pairs={{0,8},{4,12},{8,0},{12,4},{1,9},{5,13},{9,1},{13,5},{2,10},{6,14},... | collective-permute-start | bytes 1179656 | tf_op jit(solution)/shard_map/ppermute | solution.py:33
  846.3 66.9 %collective-permute-start.156 = (bf16[384,512]{1,0:T(8,128)(2,1)S(1)}, bf16[384,512]{1,0:T(8,128)(2,1)S(1)}, u32[]{:S(2)}, u32[]{:S(2)}) collective-permute-start(bf16[384,512]{1,0:T(8,128)(2,1)S(1)} %copy-done.98), channel_id=1, source_target_pairs={{0,12},{4,8},{8,4},{12,0},{1,13},{5,9},{9,5},{13,1},{2,14},{6,10},... | collective-permute-start | bytes 1179656 | tf_op jit(solution)/shard_map/ppermute | solution.py:33
  862.6 29.2 %collective-permute-start.151 = (bf16[1536,128]{1,0:T(8,128)(2,1)S(1)}, bf16[1536,128]{1,0:T(8,128)(2,1)S(1)}, u32[]{:S(2)}, u32[]{:S(2)}) collective-permute-start(bf16[1536,128]{1,0:T(8,128)(2,1)S(1)} %broadcast_select_fusion.1), channel_id=1, source_target_pairs={{0,1},{1,0},{2,3},{3,2},{4,5},{5,4},{6,7},{7,6},{8,9},{9,8},{10,11... | collective-permute-start | bytes 1179656 | tf_op jit(solution)/shard_map/ppermute | solution.py:28
  909.5 34.5 %collective-permute-start.152 = (bf16[384,512]{1,0:T(8,128)(2,1)S(1)}, bf16[384,512]{1,0:T(8,128)(2,1)S(1)}, u32[]{:S(2)}, u32[]{:S(2)}) collective-permute-start(bf16[384,512]{1,0:T(8,128)(2,1)S(1)} %get-tuple-element.215), channel_id=1, source_target_pairs={{0,12},{4,8},{8,4},{12,0},{1,13},{5,9},{9,5},{13,1},{2,14},{6,10},... | collective-permute-start | bytes 1179656 | tf_op jit(solution)/shard_map/ppermute | solution.py:33
  913.1 31.7 %collective-permute-start.145 = (bf16[64,1536]{1,0:T(8,128)(2,1)S(1)}, bf16[64,1536]{1,0:T(8,128)(2,1)S(1)}, u32[]{:S(2)}, u32[]{:S(2)}) collective-permute-start(bf16[64,1536]{1,0:T(8,128)(2,1)S(1)} %get-tuple-element.191), channel_id=1, source_target_pairs={{0,16},{16,0},{1,17},{17,1},{2,18},{18,2},{3,19},{19,3},{4,20},{20... | collective-permute-start | bytes 589832 | tf_op jit(solution)/shard_map/ppermute | solution.py:37
  (278 other events, 3209.2 us)
Sparse Core Ops, SparseCore 0:
  57.3 37.2 all-gather.7
  96.8 29.7 all-gather.9
  153.0 48.6 all-gather.11
  210.7 34.1 all-gather.13

commit v2 on v1

v2 whole, which is shorter than its diff:
```python
import functools

import jax
import jax.numpy as jnp
from jax import lax
from jax.experimental import pallas as pl
from jax.experimental.pallas import tpu as pltpu
from jax.sharding import PartitionSpec as P

H = 12
KVH = 2
HD = 128
E = 16

EPS = 1e-06
THETA = 10000.0
BF = jnp.bfloat16
F32 = jnp.float32
MIB = 1024 * 1024
COST = 4
IN_VMEM = 4


def dot(a, b, ca, cb):
    return lax.dot_general(a, b, (((ca,), (cb,)), ((), ())), preferred_element_type=F32)


def move(value, section=0, dp=0, tensor=0):
    n_dp, n_t = lax.axis_size("dp"), lax.axis_size("tensor")
    pairs = []
    for s in range(2):
        for d in range(n_dp):
            for t in range(n_t):
                here = (s * n_dp + d) * n_t + t
                pairs.append((here, ((s ^ section) * n_dp + (d ^ dp)) * n_t + (t ^ tensor)))
    return lax.ppermute(value, ("section", "dp", "tensor"), pairs)


def kv_turn(value):
    return lax.ppermute(value, "tensor", [(0, 0), (1, 2), (2, 1), (3, 3)])


def over_tensor(value):
    across = move(value, tensor=2)
    return [value, move(value, tensor=1), across, move(across, tensor=1)]


def after(value, *tokens):
    return jnp.where(there(*tokens), value, jnp.zeros_like(value))


def there(*tokens):
    marks = [token[(0,) * token.ndim].astype(F32) for token in tokens]
    total = functools.reduce(jnp.add, marks)
    return total == total


def sum_over_tensor(keep, send):
    total = keep + move(send, tensor=1)
    return total[0], move(total[1], tensor=2)


def rope(value, cosine, sine):
    return value * cosine + pltpu.roll(value, HD // 2, 1) * sine


def allowed_pairs(idx_row, idx_col, start_col):
    keys = idx_row[...]
    return (keys <= idx_col[...]) & (keys >= start_col[...])


def assemble(refs, weights):
    (blocks,) = refs
    n_dp, half = blocks.shape[1:3]
    for k in range(n_dp):
        for part in range(2):
            at = (2 * k + part) * half
            weights[at : at + half, :] = blocks[part, k]


def whole_sequence(blocks, into):
    rows = blocks[0].shape[0]
    for r, ref in enumerate(blocks):
        into[r * rows : (r + 1) * rows, :] = ref[...]


def attn_fwd_kernel(heads, n_w, me, *refs):
    w_refs, ins, outs, (a_all, weights) = take(refs, n_w, 9, 7, 2)
    a0, a1, a2, a3, cosine, sine, idx_row, idx_col, start_col = ins
    keep, send, q_out, k_out, v_out, lse_out, o_out = outs
    rows, qcols = a0.shape[0], heads * HD
    assemble(w_refs, weights)
    whole_sequence((a0, a1, a2, a3), a_all)
    qkv = dot(a_all[...], weights[:, : qcols + 2 * HD], 1, 0)
    co, si = cosine[...], sine[...]
    k = rope(qkv[:, qcols : qcols + HD], co, si).astype(BF)
    v = qkv[:, qcols + HD :].astype(BF)
    k_out[...] = k
    v_out[...] = v
    allowed = allowed_pairs(idx_row, idx_col, start_col)
    lane = lax.broadcasted_iota(jnp.int32, (k.shape[0], HD), 1)
    lse_all = jnp.zeros((k.shape[0], HD), F32)
    for h in range(heads):
        qh = rope(qkv[:, h * HD : (h + 1) * HD], co, si).astype(BF)
        q_out[:, h * HD : (h + 1) * HD] = qh
        s = jnp.where(allowed, HD ** (-0.5) * dot(qh, k, 1, 1), -1e30)
        top = jnp.max(s, axis=1, keepdims=True)
        lse = top + jnp.log(jnp.sum(jnp.exp(s - top), axis=1, keepdims=True))
        p = jnp.exp(s - lse).astype(BF)
        o_out[:, h * HD : (h + 1) * HD] = dot(p, v, 1, 0).astype(BF)
        lse_all = jnp.where(lane == h, lse, lse_all)
    lse_out[...] = lse_all
    part = dot(o_out[...], weights[:, qcols + 2 * HD :], 1, 1).astype(BF)
    for r in range(4):
        (send if r % 2 else keep)[r // 2] = part[r * rows : (r + 1) * rows, :]


def attn_bwd_kernel(heads, n_w, me, *refs):
    w_refs, ins, outs, (d_all, weights, dqkv) = take(refs, n_w, 13, 5, 3)
    d0, d1, d2, d3, q_in, k_in, v_in, lse_in, cosine, sine, idx_row, idx_col, start_col = ins
    keep, send, dq_out, kv_keep, kv_send = outs
    rows, qcols = d0.shape[0], heads * HD
    assemble(w_refs, weights)
    whole_sequence((d0, d1, d2, d3), d_all)
    do = dot(d_all[...], weights[:, qcols + 2 * HD :], 1, 0).astype(BF)
    co, si = cosine[...], -sine[...]
    k, v = k_in[...], v_in[...]
    allowed = allowed_pairs(idx_row, idx_col, start_col)
    dk = jnp.zeros((do.shape[0], HD), F32)
    dv = jnp.zeros((do.shape[0], HD), F32)
    for h in range(heads):
        qh = q_in[:, h * HD : (h + 1) * HD]
        doh = do[:, h * HD : (h + 1) * HD]
        s = jnp.where(allowed, HD ** (-0.5) * dot(qh, k, 1, 1), -1e30)
        p = jnp.exp(s - lse_in[:, h : h + 1])
        dv = dv + dot(p.astype(BF), doh, 0, 0)
        dp = dot(doh, v, 1, 1)
        ds = (p * (dp - jnp.sum(p * dp, axis=1, keepdims=True))).astype(BF)
        dq = HD ** (-0.5) * dot(ds, k, 1, 0)
        dk = dk + dot(ds, qh, 0, 0)
        dqkv[:, h * HD : (h + 1) * HD] = rope(dq, co, si).astype(BF)
    dk = rope(HD ** (-0.5) * dk, co, si).astype(BF)
    dv = dv.astype(BF)
    dqkv[:, qcols : qcols + HD] = dk
    dqkv[:, qcols + HD :] = dv
    dq_out[...] = dqkv[:, :qcols]
    core0 = me[2] == 0
    kv_keep[...] = jnp.where(core0, dk, dv)
    kv_send[...] = jnp.where(core0, dv, dk)
    part = dot(dqkv[...], weights[:, : qcols + 2 * HD], 1, 1).astype(BF)
    for r in range(4):
        (send if r % 2 else keep)[r // 2] = part[r * rows : (r + 1) * rows, :]


def total_of(terms, places):
    total = None
    for ref, place in zip(terms, places):
        term = (ref[...] if place is None else ref[place]).astype(F32)
        total = term if total is None else total + term
    return total


def finish_kernel(places, base, gain, *refs):
    terms, (out, normed) = refs[: len(places)], refs[len(places) :]
    total = base[...]
    if places:
        total = total + total_of(terms, places)
    out[...] = total
    r = lax.rsqrt(jnp.mean(total * total, axis=1, keepdims=True) + EPS)
    normed[...] = (total * r * gain[...]).astype(BF)


def norm_back_kernel(places, rows_in, gain, upper, *refs):
    terms, rest = refs[: len(places)], refs[len(places) :]
    grad = total_of(terms, places)
    x = rows_in[...]
    r = lax.rsqrt(jnp.mean(x * x, axis=1, keepdims=True) + EPS)
    weighted = grad * gain[...]
    projected = jnp.mean(weighted * x, axis=1, keepdims=True)
    total = upper[...] + (r * weighted - x * (r * r * r) * projected)
    if len(rest) == 3:
        out, low, gain_sum = rest
        low[...] = total.astype(BF)
    else:
        more, out, following, low, gain_sum = rest
        after = more[...] + total
        following[...] = after
        low[...] = after.astype(BF)
    out[...] = total
    gain_sum[...] = jnp.sum(grad * x * r, axis=0, keepdims=True)


def split_rows(me, n_dp, grad, mine, theirs, flipped):
    half = grad.shape[0] // (2 * n_dp)
    for k in range(n_dp):
        start = (me[0] ^ k if flipped else k) * (2 * half)
        near = pl.multiple_of(start + me[1] * half, 16)
        far = pl.multiple_of(start + (1 - me[1]) * half, 16)
        mine[k] = grad[pl.ds(near, half), :]
        theirs[k] = grad[pl.ds(far, half), :]


def out_grad(blocks, attended, d_all, into):
    whole_sequence(blocks, d_all)
    into[...] = dot(d_all[...], attended[...], 0, 0).astype(BF)


def qkv_grad(blocks, dq, kv_keep, kv_got, a_all, into):
    whole_sequence(blocks, a_all)
    a = a_all[...]
    qcols = dq.shape[1]
    into[:, :qcols] = dot(a, dq[...], 0, 0).astype(BF)
    rows = blocks[0].shape[0]
    got = [kv_got[r * rows : (r + 1) * rows, :] for r in (1, 0, 3, 2)]
    kv = (kv_keep[...].astype(F32) + jnp.concatenate(got, axis=0).astype(F32)).astype(BF)
    into[:, qcols : qcols + HD] = dot(a, kv, 0, 0).astype(BF)


def attn_wgrad_kernel(
    flipped, n_dp, me, a0, a1, a2, a3, dq, kv_keep, kv_got, d0, d1, d2, d3, attended, mine, theirs, tokens, grad
):
    cols = dq.shape[1] + HD
    qkv_grad((a0, a1, a2, a3), dq, kv_keep, kv_got, tokens, grad.at[:, :cols])
    out_grad((d0, d1, d2, d3), attended, tokens, grad.at[:, cols:])
    split_rows(me, n_dp, grad, mine, theirs, flipped)


def slot_rows(pos_row, s, experts, cap):
    slot = lax.broadcasted_iota(jnp.int32, (cap, pos_row.shape[2]), 0)
    hits = [(slot == pos_row[s, e : e + 1, :]).astype(F32) for e in range(experts)]
    return jnp.concatenate(hits, axis=0).astype(BF)


def start_all(*copies):
    for copy in copies:
        copy.start()
    return list(copies)


def wait_all(copies):
    for copy in copies:
        copy.wait()


def slot_gates(hit, gate_cols, s, experts, cap):
    both = dot(hit, gate_cols[s], 1, 0)
    lane = lax.broadcasted_iota(jnp.int32, both.shape, 1)
    own = lax.broadcasted_iota(jnp.int32, both.shape, 0) // cap
    return jnp.sum(jnp.where((lane == own) | (lane == own + experts), both, 0.0), axis=1, keepdims=True)


def gathered(me, ref, batch, count):
    return [[(ref, ((me[0] ^ s) * 4 + (me[3] ^ r), batch)) for r in range(4)] for s in range(count)]


def dispatch(blocks, tokens, pos_row, gate_cols, into, gates, experts, cap, scaled, fetched=None):
    for s, places in enumerate(blocks):
        for r, (ref, at) in enumerate(places):
            rows = ref.shape[-2]
            if fetched is not None:
                fetched[s][r].wait()
            elif len(blocks) > IN_VMEM:
                pltpu.sync_copy(ref.at[at], tokens.at[pl.ds(r * rows, rows)])
            else:
                tokens[s, r * rows : (r + 1) * rows, :] = ref[at]
        sequence = tokens if len(blocks) > IN_VMEM else tokens.at[s]
        hit = slot_rows(pos_row, s, experts, cap)
        picked = dot(hit, sequence[...], 1, 0)
        if scaled:
            picked = picked * slot_gates(hit, gate_cols, s, experts, cap)
        elif gates is not None:
            gates[s] = slot_gates(hit, gate_cols, s, experts, cap)
        picked = picked.astype(BF)
        for e in range(experts):
            into[e, s * cap : (s + 1) * cap, :] = picked[e * cap : (e + 1) * cap, :]


def place(out, result, e, cap, gates):
    for s in range(result.shape[0]):
        value = out[s * cap : (s + 1) * cap, :]
        if gates is not None:
            value = value * gates[s, e * cap : (e + 1) * cap, :]
        result[s, e * cap : (e + 1) * cap, :] = value.astype(BF)


def combine(values, pos_row, keep, send, experts, cap, rows):
    for s in range(values.shape[0]):
        total = dot(slot_rows(pos_row, s, experts, cap), values[s], 0, 0).astype(BF)
        for r in range(4):
            (send if r % 2 else keep)[r // 2, s] = total[r * rows : (r + 1) * rows, :]


def silu_parts(gu):
    half = gu.shape[1] // 2
    gate, up = gu[:, :half], gu[:, half:]
    sg = 1.0 / (1.0 + jnp.exp(-gate))
    return gate, up, sg


def gate_up_grad(dz, gu, out):
    half = gu.shape[1] // 2
    gate, up, sg = silu_parts(gu)
    out[:, :half] = (dz * up * sg * (1.0 + gate * (1.0 - sg))).astype(BF)
    out[:, half:] = (dz * gate * sg).astype(BF)


def take(refs, *counts):
    parts, at = [], 0
    for count in counts:
        parts.append(refs[at : at + count])
        at += count
    return parts


def sequences(refs, count):
    return [[(refs[r], s) for r in range(4)] for s in range(count)]


def expert_weights(w_in, w_out, wi, wo, sems):
    return [
        start_all(
            pltpu.make_async_copy(w_in.at[e], wi.at[e], sems.at[2 * e]),
            pltpu.make_async_copy(w_out.at[e], wo.at[e], sems.at[2 * e + 1]),
        )
        for e in range(w_in.shape[0])
    ]


def moe_fwd_kernel(experts, cap, rows, count, *refs):
    blocks, ins, outs, scratch = take(refs, 4, 4, 4, 8)
    pos_row, gate_cols, w_in, w_out = ins
    x_out, gu_out, keep, send = outs
    tokens, x_all, result, gates, gu_all, wi, wo, sems = scratch
    weights = expert_weights(w_in, w_out, wi, wo, sems)
    dispatch(sequences(blocks, count), tokens, pos_row, gate_cols, x_all, gates, experts, cap, False)
    done = start_all(pltpu.make_async_copy(x_all, x_out, sems.at[2 * experts]))
    for e in range(experts):
        wait_all(weights[e])
        gu = dot(x_all[e], wi[e], 1, 0)
        gu_all[e] = gu
        gate, up, sg = silu_parts(gu)
        z = (gate * sg * up).astype(BF)
        place(dot(z, wo[e], 1, 0), result, e, cap, gates)
    done += start_all(pltpu.make_async_copy(gu_all, gu_out, sems.at[2 * experts + 1]))
    combine(result, pos_row, keep, send, experts, cap, rows)
    wait_all(done)


def moe_bwd_kernel(experts, cap, rows, count, *refs):
    blocks, ins, outs, scratch = take(refs, 4, 5, 5, 9)
    pos_row, gate_cols, gu_in, w_in, w_out = ins
    dr_out, z_out, dgu_out, keep, send = outs
    tokens, dr_all, result, gu_all, z_all, dgu_all, wi, wo, sems = scratch
    fetched = start_all(pltpu.make_async_copy(gu_in, gu_all, sems.at[2 * experts + 3]))
    weights = expert_weights(w_in, w_out, wi, wo, sems)
    dispatch(sequences(blocks, count), tokens, pos_row, gate_cols, dr_all, None, experts, cap, True)
    done = start_all(pltpu.make_async_copy(dr_all, dr_out, sems.at[2 * experts]))
    wait_all(fetched)
    for e in range(experts):
        wait_all(weights[e])
        gu = gu_all[e]
        gate, up, sg = silu_parts(gu)
        z_all[e] = (gate * sg * up).astype(BF)
        gate_up_grad(dot(dr_all[e], wo[e], 1, 1), gu, dgu_all.at[e])
        place(dot(dgu_all[e], wi[e], 1, 1), result, e, cap, None)
    done += start_all(
        pltpu.make_async_copy(z_all, z_out, sems.at[2 * experts + 1]),
        pltpu.make_async_copy(dgu_all, dgu_out, sems.at[2 * experts + 2]),
    )
    combine(result, pos_row, keep, send, experts, cap, rows)
    wait_all(done)


def moe_turn_kernel(experts, cap, rows, count, batch, me, *refs):
    blocks, (grads,), ins, outs, scratch = take(refs, 4, 1, 4, 6, 11)
    pos_row, gate_cols, w_in, w_out = ins
    x_out, z_out, dr_out, dgu_out, keep, send = outs
    tokens, x_all, dr_all, result, z_all, dgu_all, wi, wo, sems, grad_tokens, block_sems = scratch
    weights = expert_weights(w_in, w_out, wi, wo, sems)
    places = gathered(me, grads, batch, count)
    if count <= IN_VMEM:
        copies = [
            start_all(*[
                pltpu.make_async_copy(
                    ref.at[at], grad_tokens.at[s, pl.ds(r * rows, rows)], block_sems.at[s, r]
                )
                for r, (ref, at) in enumerate(places[s])
            ])
            for s in range(count)
        ]
        routed = pos_row, gate_cols
        dispatch(sequences(blocks, count), tokens, *routed, x_all, None, experts, cap, False)
        done = start_all(pltpu.make_async_copy(x_all, x_out, sems.at[2 * experts + 1]))
        dispatch(places, grad_tokens, *routed, dr_all, None, experts, cap, True, copies)
    else:
        dispatch(sequences(blocks, count), tokens, pos_row, gate_cols, x_all, None, experts, cap, False)
        done = start_all(pltpu.make_async_copy(x_all, x_out, sems.at[2 * experts + 1]))
        dispatch(places, tokens, pos_row, gate_cols, dr_all, None, experts, cap, True)
    done += start_all(pltpu.make_async_copy(dr_all, dr_out, sems.at[2 * experts]))
    for e in range(experts):
        wait_all(weights[e])
        gu = dot(x_all[e], wi[e], 1, 0)
        gate, up, sg = silu_parts(gu)
        z_all[e] = (gate * sg * up).astype(BF)
        gate_up_grad(dot(dr_all[e], wo[e], 1, 1), gu, dgu_all.at[e])
        place(dot(dgu_all[e], wi[e], 1, 1), result, e, cap, None)
    done += start_all(
        pltpu.make_async_copy(z_all, z_out, sems.at[2 * experts + 2]),
        pltpu.make_async_copy(dgu_all, dgu_out, sems.at[2 * experts + 3]),
    )
    combine(result, pos_row, keep, send, experts, cap, rows)
    wait_all(done)


def moe_out_kernel(experts, cap, rows, count, me, z, pos_row, gate_cols, w_out, keep, send, result):
    gates = []
    for s in range(count):
        gates.append(slot_gates(slot_rows(pos_row, s, experts, cap), gate_cols, s, experts, cap))
    for e in range(experts):
        out = dot(z[e], w_out[e], 1, 0)
        for s in range(count):
            value = out[s * cap : (s + 1) * cap, :] * gates[s][e * cap : (e + 1) * cap, :]
            result[s, e * cap : (e + 1) * cap, :] = value.astype(BF)
    for s in range(count):
        total = dot(slot_rows(pos_row, s, experts, cap), result[s], 0, 0).astype(BF)
        for r in range(4):
            (send if r % 2 else keep)[r // 2, me[0] ^ s] = total[r * rows : (r + 1) * rows, :]


def moe_wgrad_kernel(sel, *refs):
    first, second, (_, dwin, dwout) = refs[:8], refs[8:16], refs[16:]

    def run(x0, x1, dg0, dg1, z0, z1, dr0, dr1):
        dwin[0] = dot(x0[0], dg0[0], 0, 0) + dot(x1[0], dg1[0], 0, 0)
        dwout[0] = dot(z0[0], dr0[0], 0, 0) + dot(z1[0], dr1[0], 0, 0)

    @pl.when(sel[0] == 0)
    def _():
        run(*first)

    @pl.when(sel[0] == 1)
    def _():
        run(*second)


def per_device(
    block_input, segments, expert_ids, gate_values, cotangent, attn_gain,
    query_weight, kv_weight, out_weight, moe_gain, w_in, w_out,
):
    sec = lax.axis_index("section")
    dp = lax.axis_index("dp")
    t = lax.axis_index("tensor")
    n_dp = lax.axis_size("dp")
    n_t = lax.axis_size("tensor")
    first = sec == 0
    core0 = t % 2 == 0
    me = jnp.stack([dp, sec, t % 2, t]).astype(jnp.int32)
    rows, width = block_input.shape[1], block_input.shape[2]
    seq = segments.shape[1]
    top = expert_ids.shape[3]
    heads = query_weight.shape[2] // HD
    qcols = heads * HD
    experts, ffn = w_in.shape[1], w_out.shape[2]
    cap = -(-(seq * top * 9 // (8 * E)) // 16) * 16
    slots = n_dp * cap
    dp_order = jnp.arange(n_dp, dtype=jnp.int32) ^ dp
    t_order = jnp.arange(n_t, dtype=jnp.int32) ^ t
    drows = width // n_dp
    half = drows // 2

    pair = jax.ShapeDtypeStruct((2, rows, width), BF)
    smem = pl.BlockSpec(memory_space=pltpu.SMEM)
    vmem = pl.BlockSpec(memory_space=pltpu.VMEM)
    any_space = pl.BlockSpec(memory_space=pl.ANY)
    hbm = pl.BlockSpec(memory_space=pltpu.HBM)
    seq_scratch = pltpu.VMEM((seq, width), BF)

    def shape(*dims, dtype=BF):
        return jax.ShapeDtypeStruct(dims, dtype)

    def call(
        kernel, name, ins, outs, scratch, limit, cost, in_specs=None, out_specs=None, hold=(), tokens=()
    ):
        n_ins, n_outs, n_hold, n_tok = len(ins), len(outs), len(hold), len(tokens)

        def body(*refs):
            given, results, rest = take(refs, n_ins + n_tok + n_hold, n_outs + n_hold, len(scratch))
            kernel(*given[:n_ins], *results[:n_outs], *rest)

        out = pl.pallas_call(
            body,
            out_shape=list(outs) + [jax.ShapeDtypeStruct(h.shape, h.dtype) for h in hold],
            in_specs=(in_specs or [smem] + [vmem] * (n_ins - 1)) + [any_space] * (n_tok + n_hold),
            out_specs=(out_specs or [vmem] * n_outs) + [any_space] * n_hold,
            scratch_shapes=scratch,
            input_output_aliases={n_ins + n_tok + i: n_outs + i for i in range(n_hold)},
            compiler_params=pltpu.CompilerParams(vmem_limit_bytes=limit * MIB),
            cost_estimate=pl.CostEstimate(flops=cost * 10**9, bytes_accessed=cost * 3 * MIB, transcendentals=0),
            name=name,
        )(*ins, *tokens, *hold)
        return out[:n_outs], out[n_outs:]

    acols = 2 * qcols + 2 * HD
    weights_scratch = pltpu.VMEM((width, acols), BF)

    def attn_fwd(a_blocks, weights, token=()):
        ins = (me, *weights, *a_blocks, *place_args)
        outs = [
            pair, pair, shape(seq, qcols), shape(seq, HD), shape(seq, HD),
            shape(seq, HD, dtype=F32), shape(seq, qcols),
        ]
        return call(
            functools.partial(attn_fwd_kernel, heads, len(weights)), "attn_fwd",
            ins, outs, [seq_scratch, weights_scratch], 20, 0, tokens=token,
        )

    def attn_bwd(d_blocks, saved, weights, tokens=()):
        ins = (me, *weights, *d_blocks, *saved, *place_args)
        return call(
            functools.partial(attn_bwd_kernel, heads, len(weights)), "attn_bwd",
            ins, [pair, pair, shape(seq, qcols), shape(seq, HD), shape(seq, HD)],
            [seq_scratch, weights_scratch, pltpu.VMEM((seq, qcols + 2 * HD), BF)], 20, 0, tokens=tokens,
        )

    tok_f32, tok_bf = shape(rows, width, dtype=F32), shape(rows, width)

    def finish(base, gain, terms, hold=()):
        (out, normed), held = call(
            functools.partial(finish_kernel, [at for _, at in terms]), "finish",
            (base, gain, *[value for value, _ in terms]), [tok_f32, tok_bf], [], 8, 0,
            [vmem] * (2 + len(terms)), hold=hold,
        )
        return out, normed, held

    def norm_back(x, gain, upper, terms, more=(), tokens=()):
        return call(
            functools.partial(norm_back_kernel, [at for _, at in terms]), "norm_back",
            (x, gain, upper, *[value for value, _ in terms], *more),
            [tok_f32] * (1 + len(more)) + [tok_bf, shape(1, width, dtype=F32)], [], 8, 0,
            [vmem] * (3 + len(terms) + len(more)), tokens=tokens,
        )

    def halves_grad(kernel, name, ins, cols):
        return call(
            functools.partial(kernel, n_dp), name, (me, *ins), [shape(n_dp, half, cols)] * 2,
            [seq_scratch, pltpu.VMEM((width, cols), BF)], 20, 1,
        )[0]

    slot_scratch = pltpu.VMEM((experts, slots, width), BF)
    token_scratch = pltpu.VMEM((n_dp, seq, width), BF) if n_dp <= IN_VMEM else seq_scratch
    result_scratch = pltpu.VMEM((n_dp, experts * cap, width), BF)
    weight_scratch = [pltpu.VMEM((experts, width, 2 * ffn), BF), pltpu.VMEM((experts, ffn, width), BF)]
    z_scratch = pltpu.VMEM((experts, slots, ffn), BF)
    dgu_scratch = pltpu.VMEM((experts, slots, 2 * ffn), BF)
    gu_scratch = pltpu.VMEM((experts, slots, 2 * ffn), F32)
    copy_sems = pltpu.SemaphoreType.DMA((2 * experts + 4,))
    row_shape = shape(experts, slots, width)
    gu_shape = shape(experts, slots, 2 * ffn, dtype=F32)
    z_shape = shape(experts, slots, ffn)
    dgu_shape = shape(experts, slots, 2 * ffn)
    sum_shapes = [shape(2, n_dp, rows, width)] * 2
    limit = 48
    block_space = vmem if n_dp <= IN_VMEM else hbm
    expert_args = (w_in[0], w_out[0])

    def moe_fwd(blocks, b, tokens=(), hold=()):
        (x, gu, keep, send), held = call(
            functools.partial(moe_fwd_kernel, experts, cap, rows, n_dp), "moe_fwd",
            (*blocks, *routes[b], *expert_args), [row_shape, gu_shape] + sum_shapes,
            [
                token_scratch, slot_scratch, result_scratch, pltpu.VMEM((n_dp, experts * cap, 1), F32),
                gu_scratch, *weight_scratch, copy_sems,
            ],
            limit, COST, [block_space] * 4 + [vmem] * 2 + [hbm] * 2, [hbm] * 2 + [vmem] * 2,
            hold, tokens,
        )
        return (x, gu), (keep, send), held

    def moe_bwd(blocks, gu, b, tokens=(), hold=()):
        (dr, z, dgu, keep, send), held = call(
            functools.partial(moe_bwd_kernel, experts, cap, rows, n_dp), "moe_bwd",
            (*blocks, *routes[b], gu, *expert_args), [row_shape, z_shape, dgu_shape] + sum_shapes,
            [
                token_scratch, slot_scratch, result_scratch, gu_scratch, z_scratch, dgu_scratch,
                *weight_scratch, copy_sems,
            ],
            limit, COST, [block_space] * 4 + [vmem] * 2 + [hbm] * 3, [hbm] * 3 + [vmem] * 2,
            hold, tokens,
        )
        return (dgu, z, dr), (keep, send), held

    def moe_turn(blocks, grads, b, tokens=()):
        (x, z, dr, dgu, keep, send), _ = call(
            functools.partial(moe_turn_kernel, experts, cap, rows, n_dp, b), "moe_turn",
            (me, *blocks, grads, *routes[b], *expert_args),
            [row_shape, z_shape, row_shape, dgu_shape] + sum_shapes,
            [
                token_scratch, slot_scratch, slot_scratch, result_scratch, z_scratch, dgu_scratch,
                *weight_scratch, copy_sems,
                token_scratch,
                pltpu.SemaphoreType.DMA((n_dp, 4)),
            ],
            limit + 4, COST * 2,
            [smem] + [block_space] * 4 + [hbm] + [vmem] * 2 + [hbm] * 2,
            [hbm] * 4 + [vmem] * 2, tokens=tokens,
        )
        return (x, dgu, z, dr), (keep, send)

    def moe_out(z, b, *tokens):
        return call(
            functools.partial(moe_out_kernel, experts, cap, rows, n_dp), "moe_out",
            (me, z, *routes[b], w_out[0]), sum_shapes, [result_scratch], 20, COST, tokens=tokens,
        )[0]

    def moe_wgrad(sets, token):
        def spec(which, *dims):
            return pl.BlockSpec((1,) + dims, lambda e, sel: (jnp.where(sel[0] == which, e, 0), 0, 0))

        in_specs = []
        for which in range(2):
            for dims in ((slots, width), (slots, 2 * ffn), (slots, ffn), (slots, width)):
                in_specs += [spec(which, *dims)] * 2
        flat = [value for which in range(2) for parts in zip(*sets[which]) for value in parts]
        return pl.pallas_call(
            moe_wgrad_kernel,
            grid_spec=pltpu.PrefetchScalarGridSpec(
                num_scalar_prefetch=1,
                grid=(experts,),
                in_specs=in_specs + [any_space],
                out_specs=[
                    pl.BlockSpec((1, width, 2 * ffn), lambda e, sel: (e, 0, 0)),
                    pl.BlockSpec((1, ffn, width), lambda e, sel: (e, 0, 0)),
                ],
            ),
            out_shape=[
                shape(experts, width, 2 * ffn, dtype=F32), shape(experts, ffn, width, dtype=F32),
            ],
            compiler_params=pltpu.CompilerParams(vmem_limit_bytes=48 * MIB),
            cost_estimate=pl.CostEstimate(flops=10**10, bytes_accessed=40 * MIB, transcendentals=0),
            name="moe_wgrad",
        )(sec.astype(jnp.int32)[None], *flat, token)

    gains = jnp.concatenate([attn_gain, moe_gain], axis=0)
    gains = jnp.stack(over_tensor(gains))[t_order].transpose(1, 0, 2).reshape(2, drows)
    gains = jnp.stack([gains] + [move(gains, dp=k) for k in range(1, n_dp)])[dp_order]
    gains = gains.transpose(1, 0, 2).reshape(2, 1, width)
    gains_far = move(gains, section=1)
    layer_gain = [jnp.where(sec == l, gains, gains_far).astype(F32) for l in range(2)]
    (gains0, gains1) = layer_gain

    def seeds_of(matrix):
        low, high = matrix[:half], matrix[half:]
        return jnp.where(first, low, high), move(jnp.where(first, high, low), section=1)

    def gather_weights(seed):
        return lax.all_gather(seed[None, None], ("section", "dp"), axis=0, tiled=True).reshape(
            2, n_dp, half, acols
        )

    kv_own = kv_turn(kv_weight[0])
    kv_core = move(kv_own, tensor=1)
    key_value = jnp.where(
        core0, jnp.concatenate([kv_own, kv_core], axis=1), jnp.concatenate([kv_core, kv_own], axis=1)
    )
    routing = jnp.concatenate([expert_ids[0].astype(F32), gate_values[0]], axis=2)
    routing = [routing] + [move(routing, dp=k) for k in range(1, n_dp)]
    seed_near, seed_far = seeds_of(
        jnp.concatenate([query_weight[0], key_value, out_weight[0].T], axis=1)
    )

    segment = jnp.where(first, segments[0], segments[1])
    ordinal = jnp.arange(seq, dtype=jnp.int32)
    start = jnp.sum((segment[None, :] < segment[:, None]).astype(jnp.int32), axis=1)
    places = (ordinal - start).astype(F32)

    def turned(vector):
        return vector.reshape(n_t, rows)[t_order].reshape(seq)

    idx = turned(ordinal)
    start_col = turned(start)[:, None]
    frequency = THETA ** (-2.0 * jnp.arange(HD // 2, dtype=F32) / HD)
    angles = turned(places)[:, None] * frequency[None, :]
    cosine = jnp.cos(angles)
    cosine = jnp.concatenate([cosine, cosine], axis=1)
    sine = jnp.sin(angles)
    sine = jnp.concatenate([-sine, sine], axis=1)
    place_args = (cosine, sine, idx[None, :], idx[:, None], start_col)

    def routes_of(routing):
        routing = jnp.stack(routing)
        routing = routing.reshape(n_dp, 2, n_t, rows, 2 * top)[:, :, t_order]
        routing = routing.reshape(n_dp, 2, seq, 2 * top)
        names = (dp * experts + jnp.arange(experts, dtype=jnp.int32)).astype(F32)
        chosen = routing[:, :, :, :top, None] == names
        member = jnp.sum(chosen.astype(F32), axis=3)
        gates = jnp.sum(jnp.where(chosen, routing[:, :, :, top:, None], 0.0), axis=3)
        lower = (ordinal[:, None] > ordinal[None, :]).astype(BF)
        rank = jnp.einsum("ij,smje->smei", lower, member.astype(BF), preferred_element_type=F32)
        slot = jnp.where(member.transpose(0, 1, 3, 2) > 0.5, rank, -1.0).astype(jnp.int32)
        gate_high = gates.astype(BF)
        gate_low = (gates - gate_high.astype(F32)).astype(BF)
        gate_cols = jnp.concatenate([gate_high, gate_low], axis=3)
        gate_cols = jnp.pad(gate_cols, ((0, 0), (0, 0), (0, 0), (0, HD - 2 * experts)))
        return [(slot[:, b], gate_cols[:, b]) for b in range(2)]

    def to_host(own, *tokens):
        parts = jnp.stack([own] + [move(own, dp=k) for k in range(1, n_dp)])
        if tokens:
            parts = after(parts, *tokens)
        across = move(parts, tensor=2)
        near = [parts, move(parts, tensor=1), across, move(across, tensor=1)]
        parts, across = move(parts, section=1), move(across, section=1)
        return near, [parts, move(parts, tensor=1), across, move(across, tensor=1)]

    def core_sum(sums):
        return sums[0] + move(sums[1], tensor=1)

    def dp_terms(parts):
        return [(parts, 0)] + [(move(parts[k], dp=k), None) for k in range(1, n_dp)]

    def from_host(near, far, host, *tokens):
        here = sec == host
        across = move(jnp.where(here, near[1], move(far[1], section=1)), tensor=2)
        if tokens:
            here = here & there(*tokens)
        total = jnp.where(here, near[0], move(far[0], section=1)) + across
        return dp_terms(total), total

    x0 = jnp.where(first, block_input[0], block_input[1])
    seed = jnp.where(first & there(*routing[1:]), seed_near, seed_far)
    weights0 = (gather_weights(seed),)
    _, a, _ = finish(x0, gains0[0], [])

    routes = routes_of(routing)
    a_blocks = over_tensor(a)
    (keep, send, *saved, attended), _ = attn_fwd(
        a_blocks, weights0, [part for route in routes for part in route]
    )
    part0, part1 = sum_over_tensor(keep, send)
    mid, m, _ = finish(x0, gains0[1], [(part0, None), (part1, None)])
    kept0 = (x0, a_blocks, saved, attended, mid, weights0)
    cot_far = move(jnp.where(first, cotangent[0, 1], cotangent[0, 0]), section=1)
    cot_near = jnp.where(first, cotangent[0, 0], cotangent[0, 1])
    cots = jnp.stack([jnp.where(first, cot_near, cot_far), jnp.where(first, cot_far, cot_near)])
    near, far = to_host(m, cots)
    seed = jnp.where(first & there(near[0]), seed_far, seed_near)
    weights1 = (gather_weights(seed),)
    cot_all = after(cotangent[0].astype(BF), near[2])
    cot_all = lax.all_gather(cot_all[None], ("dp", "tensor"), axis=0, tiled=True)
    kept_near, sums_near, _ = moe_fwd(near, 0)
    kept_far, sums_far, _ = moe_fwd(far, 1, (sums_near[1],))
    terms, total = from_host(core_sum(sums_near), core_sum(sums_far), 0)
    out0, a, _ = finish(mid, gains1[0], terms)

    a_blocks = over_tensor(a)
    (keep, send, *saved, attended), _ = attn_fwd(a_blocks, weights1)
    part0, part1 = sum_over_tensor(keep, send)
    mid, m, _ = finish(out0, gains1[1], [(part0, None), (part1, None)])
    kept1 = (out0, a_blocks, saved, attended, mid, weights1)
    near, far = to_host(m)
    set_near, sums_near = moe_turn(near, cot_all, 1)
    set_far, sums_far = moe_turn(far, cot_all, 0, (sums_near[1],))
    sets = [None, (set_near, set_far)]
    terms, total = from_host(core_sum(sums_near), core_sum(sums_far), 1)
    out_near, out_far = (
        core_sum(moe_out(part[2], b, sums_far[0])) for b, part in ((1, set_near), (0, set_far))
    )
    out_far = move(after(out_far, total), section=1)

    cot_far = move(jnp.where(first, cotangent[0, 1], cotangent[0, 0]), section=1)
    cot_near = jnp.where(first, cotangent[0, 0], cotangent[0, 1])
    cots = (jnp.where(first, cot_near, cot_far), jnp.where(first, cot_far, cot_near))

    def attention_back(kept, l, g, terms, more, *tokens):
        x, a_blocks, saved, attended, mid, weights = kept
        (dmid, d, moe_gain_sum), _ = norm_back(mid, layer_gain[l][1], g, terms, tokens=tokens)
        d_blocks = over_tensor(d)
        (keep, send, dq, kv_keep, kv_send), _ = attn_bwd(d_blocks, saved, weights)
        args = (*a_blocks, dq, kv_keep, move(kv_send, tensor=1), *d_blocks, attended)
        mine, theirs = halves_grad(
            functools.partial(attn_wgrad_kernel, l == 0), "attn_wgrad", args, 2 * qcols + HD
        )
        part0, part1 = sum_over_tensor(keep, send)
        (*outs, attn_gain_sum), _ = norm_back(
            x, layer_gain[l][0], dmid, [(part0, None), (part1, None)], more
        )
        return outs, jnp.concatenate([attn_gain_sum, moe_gain_sum]), mine, theirs

    (in_grad1, g, g_low), gain_sums1, mine, theirs = attention_back(
        kept1, 1, cots[1], terms, (cots[0],), out_far
    )
    out1 = jnp.where(first, out_far, out_near)
    out_across = move(out1[1], tensor=2)
    theirs = move(theirs, section=1)
    near, far = to_host(g_low, out_across, theirs)
    out1 = lax.psum_scatter(out1[0] + out_across, "dp", scatter_dimension=0, tiled=True)
    out1 = mid + out1[0].astype(F32)
    shard1 = lax.psum_scatter(mine + theirs, "dp", scatter_dimension=0, tiled=True)
    shard1 = shard1[0].astype(F32)
    grads_near, sums_near, _ = moe_bwd(near, kept_near[1], 0)
    grads_far, sums_far, _ = moe_bwd(far, kept_far[1], 1, (sums_near[1],))
    sets[0] = ((kept_near[0], *grads_near), (kept_far[0], *grads_far))
    terms, _ = from_host(core_sum(sums_near), core_sum(sums_far), 0)
    (in_grad0, _), gain_sums0, mine, theirs = attention_back(kept0, 0, g, terms, ())

    gain_sums = jnp.concatenate([gain_sums0, gain_sums1])
    gain_sums = gain_sums + move(gain_sums, tensor=1)
    gain_sums = gain_sums + move(gain_sums, tensor=2)
    gain_sums = gain_sums.astype(BF).reshape(4, n_dp, drows).transpose(1, 0, 2)[dp_order]
    gain_sums = jnp.pad(gain_sums, ((0, 0), (0, 12), (0, 2 * qcols + HD - drows)))
    parts = jnp.concatenate([mine + move(theirs, section=1), gain_sums], axis=1)
    parts = [parts[0]] + [move(parts[k], dp=k) for k in range(1, n_dp)]
    dw_in, dw_out = moe_wgrad(sets, parts[1])
    shard0 = sum(part.astype(F32) for part in parts)
    shard0 = jnp.where(there(dw_in), shard0, 0.0)

    gain0, gain1 = shard0[half : half + 2], shard0[half + 2 : half + 4]
    own = jnp.where(first, shard0[:half], shard1)
    own_gain = jnp.where(first, gain0, gain1)[:, :drows]
    far = jnp.concatenate([
        jnp.where(first, shard1, shard0[:half]),
        jnp.pad(jnp.where(first, gain1, gain0), ((0, 14), (0, 0))),
    ])
    far = move(far.astype(BF), section=1).astype(F32)
    grad_shard = jnp.where(
        first, jnp.concatenate([own, far[:half]]), jnp.concatenate([far[:half], own])
    )
    gains = own_gain + far[half : half + 2, :drows]
    gains = lax.dynamic_slice_in_dim(gains, t * attn_gain.shape[1], attn_gain.shape[1], 1)
    cols = qcols + HD
    grad_out = grad_shard[:, cols:].T
    grad_kv = kv_turn(grad_shard[:, qcols:cols])
    def both_batches(value0, value1):
        far = move(jnp.where(first, value1, value0).astype(BF), section=1).astype(F32)
        near = jnp.where(first, value0, value1)
        return jnp.stack([jnp.where(first, near, far), jnp.where(first, far, near)])[None]

    return (
        both_batches(out0, out1),
        both_batches(in_grad0, in_grad1),
        gains[0:1],
        grad_shard[None, :, :qcols],
        grad_kv[None],
        grad_out[None],
        gains[1:2],
        dw_in[None],
        dw_out[None],
    )


def solution(mesh):
    return jax.shard_map(
        per_device,
        mesh=mesh,
        in_specs=(
            P(None, ("dp", "tensor"), None),
            P(None, "dp"),
            P("section", None, "dp", None),
            P("section", None, "dp", None),
            P("section", None, ("dp", "tensor"), None),
            P("section", ("dp", "tensor")),
            P("section", "dp", "tensor"),
            P("section", "dp", "tensor"),
            P("section", "tensor", "dp"),
            P("section", ("dp", "tensor")),
            P("section", "dp", None, "tensor"),
            P("section", "dp", "tensor", None),
        ),
        out_specs=(
            P("section", None, ("dp", "tensor"), None),
            P("section", None, ("dp", "tensor"), None),
            P("section", ("dp", "tensor")),
            P("section", "dp", "tensor"),
            P("section", "dp", "tensor"),
            P("section", "tensor", "dp"),
            P("section", ("dp", "tensor")),
            P("section", "dp", None, "tensor"),
            P("section", "dp", "tensor", None),
        ),
        check_vma=False,
    )
```

time: 979 us -> 840 us (0.86)
  starting transfers between devices: 200 us -> 146 us
  blocking collectives: 49.1 us -> 0 us
  other arithmetic: 49.6 us -> 32.8 us
  Pallas kernels: 155 us -> 139 us
  local copies, waits for them, and re-layouts: 53.2 us -> 42.8 us
    ppermute x166 -> x103, starting transfers between devices: 190 us -> 135 us  [move(): return lax.ppermute(value, ('section', 'dp', 'tensor'), pairs)]
    all_gather x2 -> x0, blocking collectives: 49.1 us -> none  [the longest x1 37.3 us: per_device(): lax.all_gather(jnp.stack([attn_gain[0], moe_gain[0]])[None], ('section',...]
    pallas_call x14 -> x22, Pallas kernels: 138 us -> 123 us  [call(): pl.pallas_call(body, out_shape=list(outs) + [jax.ShapeDtypeStruct(h.shape...]
    all_gather x4 -> x3, waiting for transfers between devices: 39.1 us -> 34.5 us  [the longest x2 34.5 us: gather_weights(): lax.all_gather(seed[None, None], ('section', 'dp'), axis=0, tiled=True)]
    ppermute x166 -> x103, waiting for transfers between devices: 401 us -> 403 us  [move(): return lax.ppermute(value, ('section', 'dp', 'tensor'), pairs)]
    unnamed x309 -> x235, local copies, waits for them, and re-layouts: 26.9 us -> 26.1 us
  transfers between devices with their start and end apart: 172 -> 110, of which waited for: 61 -> 64; matrix products, arithmetic and copies ran while one was open for 8% -> 5% of each run, Pallas kernels for 16% -> 12%
where the time goes in v2:
time: 840 us; the launch traced here: 829 us
  waiting for transfers between devices  442 us (53%)
  starting transfers between devices  146 us (17%)
  Pallas kernels  139 us (17%)
  local copies, waits for them, and re-layouts  42.8 us (5%)
  other arithmetic  32.8 us (4%)
  between operations  25.8 us (3%)
    ppermute x103, waiting for transfers between devices, move(): return lax.ppermute(value, ('section', 'dp', 'tensor'), pairs)  403 us
    ppermute x103, starting transfers between devices, move(): return lax.ppermute(value, ('section', 'dp', 'tensor'), pairs)  135 us
    pallas_call x22, Pallas kernels, call(): pl.pallas_call(body, out_shape=list(outs) + [jax.ShapeDtypeStruct(h.shape...  123 us
    all_gather x2, waiting for transfers between devices, gather_weights(): lax.all_gather(seed[None, None], ('section', 'dp'), axis=0, tiled=True)  34.5 us
    unnamed x235, local copies, waits for them, and re-layouts  26.1 us
  transfers between devices with their start and end apart: 110, of which 64 were waited for; matrix products, arithmetic and copies ran while one was open for 5% of the time, Pallas kernels for 12%

profile of v2, /device:TPU:9, one launch (start us, length us, event | category | flops | bytes accessed | tf_op | source)
XLA Modules:
  0.0 828.9 jit_solution(4600279950023009388)
XLA Ops:
  7.2 3.7 collective-permute-start.10
  54.3 34.5 %all-gather.8.cloned.1.call-done = bf16[1536,1024]{1,0:T(8,128)(2,1)} async-done(((bf16[192,1024]{1,0:T(8,128)(2,1)}), bf16[1536,1024]{1,0:T(8,128)(2,1)}) %all-gather.8.cloned.1.call-update) | async-done | bytes 3145744 | tf_op jit(solution)/shard_map/all_gather | solution.py:656
  98.1 4.9 collective-permute-done.17.refs_3_
  108.7 8.8 %collective-permute-done.21 = bf16[64,1536]{1,0:T(8,128)(2,1)S(1)} collective-permute-done((bf16[64,1536]{1,0:T(8,128)(2,1)S(1)}, bf16[64,1536]{1,0:T(8,128)(2,1)S(1)}, u32[]{:S(2)}, u32[]{:S(2)}) %collective-permute-start.21) | collective-permute-done | bytes 196640 | tf_op jit(solution)/shard_map/ppermute | solution.py:36
  125.6 16.5 %collective-permute-done.23.refs_2_ = bf16[4,64,1536]{2,1,0:T(8,128)(2,1)} collective-permute-done((bf16[4,64,1536]{2,1,0:T(8,128)(2,1)S(1)}, bf16[4,64,1536]{2,1,0:T(8,128)(2,1)}, u32[]{:S(2)}, u32[]{:S(2)}) %collective-permute-start.23) | collective-permute-done | bytes 786464 | tf_op jit(solution)/shard_map/ppermute | solution.py:36
  151.5 18.1 %collective-permute-done.26.refs_0_ = bf16[4,64,1536]{2,1,0:T(8,128)(2,1)S(1)} collective-permute-done((bf16[4,64,1536]{2,1,0:T(8,128)(2,1)S(1)}, bf16[4,64,1536]{2,1,0:T(8,128)(2,1)S(1)}, u32[]{:S(2)}, u32[]{:S(2)}) %collective-permute-start.26) | collective-permute-done | bytes 786464 | tf_op jit(solution)/shard_map/ppermute | solution.py:36
  169.6 11.8 %collective-permute-start.27 = (bf16[4,64,1536]{2,1,0:T(8,128)(2,1)S(1)}, bf16[4,64,1536]{2,1,0:T(8,128)(2,1)S(1)}, u32[]{:S(2)}, u32[]{:S(2)}) collective-permute-start(bf16[4,64,1536]{2,1,0:T(8,128)(2,1)S(1)} %collective-permute-done.26.refs_0_), channel_id=1, source_target_pairs={{0,1},{1,0},{2,3},{3,2},{4,5},{5,4},{6,7},{7,6},{8,9},{9,8},{10,11... | collective-permute-start | bytes 2359304 | tf_op jit(solution)/shard_map/ppermute | solution.py:36
  181.4 16.2 %collective-permute-done.28.refs_2_ = bf16[4,64,1536]{2,1,0:T(8,128)(2,1)S(1)} collective-permute-done((bf16[4,64,1536]{2,1,0:T(8,128)(2,1)}, bf16[4,64,1536]{2,1,0:T(8,128)(2,1)S(1)}, u32[]{:S(2)}, u32[]{:S(2)}) %collective-permute-start.28) | collective-permute-done | bytes 786464 | tf_op jit(solution)/shard_map/ppermute | solution.py:36
  200.8 11.8 %moe_fwd.2 = (bf16[4,320,1536]{2,1,0:T(8,128)(2,1)}, f32[4,320,384]{2,1,0:T(8,128)}, bf16[2,4,64,1536]{3,2,1,0:T(8,128)(2,1)S(1)}, bf16[2,4,64,1536]{3,2,1,0:T(8,128)(2,1)}) custom-call(bf16[4,64,1536]{2,1,0:T(8,128)(2,1)S(1)} %maximum_select_fusion.1.refs_0_, bf16[4,64,1536]{2,1,0:T(8,128)(2,1)S(1)} %collective-permute-done.22.refs_1_, ...), custom_call_target="tpu_custom_call" | custom-call | flops 4000000000 | bytes 12582912 | tf_op jit(solution)/shard_map/moe_fwd/pallas_call | solution.py:490
  212.6 10.8 %moe_fwd.3 = (bf16[4,320,1536]{2,1,0:T(8,128)(2,1)}, f32[4,320,384]{2,1,0:T(8,128)}, bf16[2,4,64,1536]{3,2,1,0:T(8,128)(2,1)S(1)}, bf16[2,4,64,1536]{3,2,1,0:T(8,128)(2,1)}) custom-call(bf16[4,64,1536]{2,1,0:T(8,128)(2,1)S(1)} %collective-permute-done.26.refs_0_, bf16[4,64,1536]{2,1,0:T(8,128)(2,1)S(1)} %collective-permute-done.27.refs_1_, ...), custom_call_target="tpu_custom_call" | custom-call | flops 4000000000 | bytes 12582912 | tf_op jit(solution)/shard_map/moe_fwd/pallas_call | solution.py:490
  224.0 4.5 collective-permute-done.30
  231.2 17.1 %collective-permute-done.32 = bf16[4,64,1536]{2,1,0:T(8,128)(2,1)S(1)} collective-permute-done((bf16[4,64,1536]{2,1,0:T(8,128)(2,1)S(1)}, bf16[4,64,1536]{2,1,0:T(8,128)(2,1)S(1)}, u32[]{:S(2)}, u32[]{:S(2)}) %collective-permute-start.32) | collective-permute-done | bytes 786464 | tf_op jit(solution)/shard_map/ppermute | solution.py:36
  249.7 15.4 %collective-permute-done.31 = bf16[4,64,1536]{2,1,0:T(8,128)(2,1)S(1)} collective-permute-done((bf16[4,64,1536]{2,1,0:T(8,128)(2,1)S(1)}, bf16[4,64,1536]{2,1,0:T(8,128)(2,1)S(1)}, u32[]{:S(2)}, u32[]{:S(2)}) %collective-permute-start.31) | collective-permute-done | bytes 786464 | tf_op jit(solution)/shard_map/ppermute | solution.py:36
  265.1 4.6 collective-permute-done.33
  273.8 10.6 %collective-permute-done.36.refs_5_ = bf16[64,1536]{1,0:T(8,128)(2,1)S(1)} collective-permute-done((bf16[64,1536]{1,0:T(8,128)(2,1)S(1)}, bf16[64,1536]{1,0:T(8,128)(2,1)S(1)}, u32[]{:S(2)}, u32[]{:S(2)}) %collective-permute-start.36) | collective-permute-done | bytes 196640 | tf_op jit(solution)/shard_map/ppermute | solution.py:36
  306.2 5.7 collective-permute-done.41.refs_3_
  312.9 4.0 collective-permute-start.43
  317.3 12.1 %collective-permute-done.43 = bf16[64,1536]{1,0:T(8,128)(2,1)S(1)} collective-permute-done((bf16[64,1536]{1,0:T(8,128)(2,1)S(1)}, bf16[64,1536]{1,0:T(8,128)(2,1)S(1)}, u32[]{:S(2)}, u32[]{:S(2)}) %collective-permute-start.43) | collective-permute-done | bytes 196640 | tf_op jit(solution)/shard_map/ppermute | solution.py:36
  331.1 16.3 %collective-permute-done.46.refs_3_ = bf16[4,64,1536]{2,1,0:T(8,128)(2,1)S(1)} collective-permute-done((bf16[4,64,1536]{2,1,0:T(8,128)(2,1)S(1)}, bf16[4,64,1536]{2,1,0:T(8,128)(2,1)S(1)}, u32[]{:S(2)}, u32[]{:S(2)}) %collective-permute-start.46) | collective-permute-done | bytes 786464 | tf_op jit(solution)/shard_map/ppermute | solution.py:36
  352.5 12.0 %collective-permute-done.51.refs_3_ = bf16[4,64,1536]{2,1,0:T(8,128)(2,1)} collective-permute-done((bf16[4,64,1536]{2,1,0:T(8,128)(2,1)S(1)}, bf16[4,64,1536]{2,1,0:T(8,128)(2,1)}, u32[]{:S(2)}, u32[]{:S(2)}) %collective-permute-start.51) | collective-permute-done | bytes 786464 | tf_op jit(solution)/shard_map/ppermute | solution.py:36
  370.2 21.2 %moe_turn.2 = (bf16[4,320,1536]{2,1,0:T(8,128)(2,1)}, bf16[4,320,192]{2,1,0:T(8,128)(2,1)S(1)}, bf16[4,320,1536]{2,1,0:T(8,128)(2,1)}, bf16[4,320,384]{2,1,0:T(8...) custom-call(s32[4]{0:T(128)S(1)} %copy-done.85, bf16[4,64,1536]{2,1,0:T(8,128)(2,1)S(1)} %copy-done.27, ...), custom_call_target="tpu_custom_call" | custom-call | flops 8000000000 | bytes 25165824 | tf_op jit(solution)/shard_map/moe_turn/pallas_call | solution.py:490
  391.4 21.0 %moe_turn.3 = (bf16[4,320,1536]{2,1,0:T(8,128)(2,1)}, bf16[4,320,192]{2,1,0:T(8,128)(2,1)S(1)}, bf16[4,320,1536]{2,1,0:T(8,128)(2,1)}, bf16[4,320,384]{2,1,0:T(8...) custom-call(s32[4]{0:T(128)S(1)} %copy-done.85, ...), custom_call_target="tpu_custom_call" | custom-call | flops 8000000000 | bytes 25165824 | tf_op jit(solution)/shard_map/moe_turn/pallas_call | solution.py:490
  425.0 12.2 %collective-permute-done.55 = bf16[4,64,1536]{2,1,0:T(8,128)(2,1)S(1)} collective-permute-done((bf16[4,64,1536]{2,1,0:T(8,128)(2,1)S(1)}, bf16[4,64,1536]{2,1,0:T(8,128)(2,1)S(1)}, u32[]{:S(2)}, u32[]{:S(2)}) %collective-permute-start.55) | collective-permute-done | bytes 786464 | tf_op jit(solution)/shard_map/ppermute | solution.py:36
  437.9 16.2 %collective-permute-done.54 = bf16[4,64,1536]{2,1,0:T(8,128)(2,1)S(1)} collective-permute-done((bf16[4,64,1536]{2,1,0:T(8,128)(2,1)S(1)}, bf16[4,64,1536]{2,1,0:T(8,128)(2,1)S(1)}, u32[]{:S(2)}, u32[]{:S(2)}) %collective-permute-start.54) | collective-permute-done | bytes 786464 | tf_op jit(solution)/shard_map/ppermute | solution.py:36
  458.4 3.7 moe_out.3
  465.6 4.1 collective-permute-start.63
  469.7 10.2 %collective-permute-done.64.refs_6_ = bf16[64,1536]{1,0:T(8,128)(2,1)S(1)} collective-permute-done((bf16[64,1536]{1,0:T(8,128)(2,1)S(1)}, bf16[64,1536]{1,0:T(8,128)(2,1)S(1)}, u32[]{:S(2)}, u32[]{:S(2)}) %collective-permute-start.64) | collective-permute-done | bytes 196640 | tf_op jit(solution)/shard_map/ppermute | solution.py:36
  483.0 7.6 collective-permute-done.58.refs_7_
  495.7 4.5 collective-permute-start.67
  513.4 21.4 %collective-permute-done.69.refs_4_ = bf16[64,1536]{1,0:T(8,128)(2,1)S(1)} collective-permute-done((bf16[64,1536]{1,0:T(8,128)(2,1)S(1)}, bf16[64,1536]{1,0:T(8,128)(2,1)S(1)}, u32[]{:S(2)}, u32[]{:S(2)}) %collective-permute-start.69) | collective-permute-done | bytes 196640 | tf_op jit(solution)/shard_map/ppermute | solution.py:36
  536.6 4.1 collective-permute-start.73
  543.1 10.3 %collective-permute-done.73 = bf16[64,1536]{1,0:T(8,128)(2,1)S(1)} collective-permute-done((bf16[64,1536]{1,0:T(8,128)(2,1)S(1)}, bf16[64,1536]{1,0:T(8,128)(2,1)S(1)}, u32[]{:S(2)}, u32[]{:S(2)}) %collective-permute-start.73) | collective-permute-done | bytes 196640 | tf_op jit(solution)/shard_map/ppermute | solution.py:36
  554.3 17.1 %collective-permute-done.76.refs_2_ = bf16[4,64,1536]{2,1,0:T(8,128)(2,1)S(1)} collective-permute-done((bf16[4,64,1536]{2,1,0:T(8,128)(2,1)S(1)}, bf16[4,64,1536]{2,1,0:T(8,128)(2,1)S(1)}, u32[]{:S(2)}, u32[]{:S(2)}) %collective-permute-start.76) | collective-permute-done | bytes 786464 | tf_op jit(solution)/shard_map/ppermute | solution.py:36
  574.7 13.5 %collective-permute-done.81.refs_2_ = bf16[4,64,1536]{2,1,0:T(8,128)(2,1)S(1)} collective-permute-done((bf16[4,64,1536]{2,1,0:T(8,128)(2,1)S(1)}, bf16[4,64,1536]{2,1,0:T(8,128)(2,1)S(1)}, u32[]{:S(2)}, u32[]{:S(2)}) %collective-permute-start.81) | collective-permute-done | bytes 786464 | tf_op jit(solution)/shard_map/ppermute | solution.py:36
  591.3 15.0 %moe_bwd.2 = (bf16[4,320,1536]{2,1,0:T(8,128)(2,1)}, bf16[4,320,192]{2,1,0:T(8,128)(2,1)S(1)}, bf16[4,320,384]{2,1,0:T(8,128)(2,1)S(1)}, bf16[2,4,64,1536]{3,2,1,0:T(8,128)(2,1)}, bf16[2,4,64,1536]{3,2,1,0:T(8,128)(2,1)}) custom-call(bf16[4,64,1536]{2,1,0:T(8,128)(2,1)S(1)} %maximum_select_fusion.2.refs_0_, ...), custom_call_target="tpu_custom_call" | custom-call | flops 4000000000 | bytes 12582912 | tf_op jit(solution)/shard_map/moe_bwd/pallas_call | solution.py:490
  608.2 14.9 %moe_bwd.3 = (bf16[4,320,1536]{2,1,0:T(8,128)(2,1)}, bf16[4,320,192]{2,1,0:T(8,128)(2,1)S(1)}, bf16[4,320,384]{2,1,0:T(8,128)(2,1)S(1)}, bf16[2,4,64,1536]{3,2,1,0:T(8,128)(2,1)}, bf16[2,4,64,1536]{3,2,1,0:T(8,128)(2,1)}) custom-call(bf16[4,64,1536]{2,1,0:T(8,128)(2,1)S(1)} %collective-permute-done.79.refs_0_, ...), custom_call_target="tpu_custom_call" | custom-call | flops 4000000000 | bytes 12582912 | tf_op jit(solution)/shard_map/moe_bwd/pallas_call | solution.py:490
  623.7 4.5 collective-permute-done.83
  633.0 17.0 %collective-permute-done.85 = bf16[4,64,1536]{2,1,0:T(8,128)(2,1)S(1)} collective-permute-done((bf16[4,64,1536]{2,1,0:T(8,128)(2,1)S(1)}, bf16[4,64,1536]{2,1,0:T(8,128)(2,1)S(1)}, u32[]{:S(2)}, u32[]{:S(2)}) %collective-permute-start.85) | collective-permute-done | bytes 786464 | tf_op jit(solution)/shard_map/ppermute | solution.py:36
  652.9 14.0 %collective-permute-done.84 = bf16[4,64,1536]{2,1,0:T(8,128)(2,1)} collective-permute-done((bf16[4,64,1536]{2,1,0:T(8,128)(2,1)}, bf16[4,64,1536]{2,1,0:T(8,128)(2,1)}, u32[]{:S(2)}, u32[]{:S(2)}) %collective-permute-start.84) | collective-permute-done | bytes 786464 | tf_op jit(solution)/shard_map/ppermute | solution.py:36
  671.0 4.2 collective-permute-start.88
  675.2 12.9 %collective-permute-done.89.refs_6_ = bf16[64,1536]{1,0:T(8,128)(2,1)S(1)} collective-permute-done((bf16[64,1536]{1,0:T(8,128)(2,1)S(1)}, bf16[64,1536]{1,0:T(8,128)(2,1)S(1)}, u32[]{:S(2)}, u32[]{:S(2)}) %collective-permute-start.89) | collective-permute-done | bytes 196640 | tf_op jit(solution)/shard_map/ppermute | solution.py:36
  713.3 4.0 attn_bwd.3
  736.1 26.3 %collective-permute-done.97 = bf16[4,192,896]{2,1,0:T(8,128)(2,1)} collective-permute-done((bf16[4,192,896]{2,1,0:T(8,128)(2,1)S(1)}, bf16[4,192,896]{2,1,0:T(8,128)(2,1)}, u32[]{:S(2)}, u32[]{:S(2)}) %collective-permute-start.97) | collective-permute-done | bytes 1376288 | tf_op jit(solution)/shard_map/ppermute | solution.py:36
  769.9 4.0 collective-permute-start.101
  775.5 16.1 %moe_wgrad.1 = (f32[4,1536,384]{2,1,0:T(8,128)}, f32[4,192,1536]{2,1,0:T(8,128)}) custom-call(s32[1]{0:T(128)} %bitcast.16.sel, bf16[4,320,1536]{2,1,0:T(8,128)(2,1)} %get-tuple-element.148.refs_0_, bf16[4,320,1536]{2,1,0:T(8,128)(2,1)} %get-tuple-element.149.refs_1_, bf16[4,320,384]{2,1,0:T(8,128)(2,1)S(1)} %copy-done.23, ...), custom_call_target="tpu_custom_call" | custom-call | flops 10000000000 | bytes 41943040 | tf_op jit(solution)/shard_map/moe_wgrad/pallas_call | solution.py:624
  794.3 6.1 collective-permute-done.101
  802.2 7.5 collective-permute-done.103
  811.8 6.0 collective-permute-start.104
  (571 shorter events, 244.0 us)
Async XLA Ops:
  7.2 81.7 %all-gather.8.cloned.1.call-start = ((), (), s32[]{:S(2)}) async-start(), calls=%async_computation.5 | async-start | bytes 3538944 | tf_op jit(solution)/shard_map/all_gather | solution.py:656
  27.2 267.7 %all-gather.10.cloned.1.call-start = ((), (), s32[]{:S(2)}) async-start(), calls=%async_computation.6 | async-start | bytes 3538944 | tf_op jit(solution)/shard_map/all_gather | solution.py:656
  124.2 244.2 %all-gather.6.cloned.1.call-start = ((), (), s32[]{:S(2)}) async-start(), calls=%async_computation.2 | async-start | bytes 6684672 | tf_op jit(solution)/shard_map/all_gather | solution.py:749
  124.3 17.8 %collective-permute-start.23 = (bf16[4,64,1536]{2,1,0:T(8,128)(2,1)S(1)}, bf16[4,64,1536]{2,1,0:T(8,128)(2,1)}, u32[]{:S(2)}, u32[]{:S(2)}) collective-permute-start(bf16[4,64,1536]{2,1,0:T(8,128)(2,1)S(1)} %maximum_select_fusion.1.refs_0_), channel_id=1, source_target_pairs={{0,2},{1,3},{2,0},{3,1},{4,6},{5,7},{6,4},{7,5},{8,10},{9,11},{10,... | collective-permute-start | bytes 2359304 | tf_op jit(solution)/shard_map/ppermute | solution.py:36
  146.5 553.3 %reduce-scatter.3.cloned.1.call-start = ((), (), s32[]{:S(2)}) async-start(), calls=%async_computation.3 | async-start | bytes 983040 | tf_op jit(solution)/shard_map/reduce_scatter | solution.py:796
  147.1 22.5 %collective-permute-start.26 = (bf16[4,64,1536]{2,1,0:T(8,128)(2,1)S(1)}, bf16[4,64,1536]{2,1,0:T(8,128)(2,1)S(1)}, u32[]{:S(2)}, u32[]{:S(2)}) collective-permute-start(bf16[4,64,1536]{2,1,0:T(8,128)(2,1)S(1)} %maximum_select_fusion.1.refs_0_), channel_id=1, source_target_pairs={{0,16},{1,17},{2,18},{3,19},{4,20},{5,21},{6,22},{7,23},{8,24},{9,... | collective-permute-start | bytes 2359304 | tf_op jit(solution)/shard_map/ppermute | solution.py:36
  147.4 50.2 %collective-permute-start.28 = (bf16[4,64,1536]{2,1,0:T(8,128)(2,1)}, bf16[4,64,1536]{2,1,0:T(8,128)(2,1)S(1)}, u32[]{:S(2)}, u32[]{:S(2)}) collective-permute-start(bf16[4,64,1536]{2,1,0:T(8,128)(2,1)} %collective-permute-done.23.refs_2_), channel_id=1, source_target_pairs={{0,16},{1,17},{2,18},{3,19},{4,20},{5,21},{6,22},{7,23},{8,24},{9,... | collective-permute-start | bytes 2359304 | tf_op jit(solution)/shard_map/ppermute | solution.py:36
  148.6 52.2 %collective-permute-start.22 = (bf16[4,64,1536]{2,1,0:T(8,128)(2,1)S(1)}, bf16[4,64,1536]{2,1,0:T(8,128)(2,1)S(1)}, u32[]{:S(2)}, u32[]{:S(2)}) collective-permute-start(bf16[4,64,1536]{2,1,0:T(8,128)(2,1)S(1)} %maximum_select_fusion.1.refs_0_), channel_id=1, source_target_pairs={{0,1},{1,0},{2,3},{3,2},{4,5},{5,4},{6,7},{7,6},{8,9},{9,8},{10,11... | collective-permute-start | bytes 2359304 | tf_op jit(solution)/shard_map/ppermute | solution.py:36
  151.5 49.3 %collective-permute-start.24 = (bf16[4,64,1536]{2,1,0:T(8,128)(2,1)}, bf16[4,64,1536]{2,1,0:T(8,128)(2,1)S(1)}, u32[]{:S(2)}, u32[]{:S(2)}) collective-permute-start(bf16[4,64,1536]{2,1,0:T(8,128)(2,1)} %collective-permute-done.23.refs_2_), channel_id=1, source_target_pairs={{0,1},{1,0},{2,3},{3,2},{4,5},{5,4},{6,7},{7,6},{8,9},{9,8},{10,11... | collective-permute-start | bytes 2359304 | tf_op jit(solution)/shard_map/ppermute | solution.py:36
  169.6 43.0 %collective-permute-start.27 = (bf16[4,64,1536]{2,1,0:T(8,128)(2,1)S(1)}, bf16[4,64,1536]{2,1,0:T(8,128)(2,1)S(1)}, u32[]{:S(2)}, u32[]{:S(2)}) collective-permute-start(bf16[4,64,1536]{2,1,0:T(8,128)(2,1)S(1)} %collective-permute-done.26.refs_0_), channel_id=1, source_target_pairs={{0,1},{1,0},{2,3},{3,2},{4,5},{5,4},{6,7},{7,6},{8,9},{9,8},{10,11... | collective-permute-start | bytes 2359304 | tf_op jit(solution)/shard_map/ppermute | solution.py:36
  229.0 19.3 %collective-permute-start.32 = (bf16[4,64,1536]{2,1,0:T(8,128)(2,1)S(1)}, bf16[4,64,1536]{2,1,0:T(8,128)(2,1)S(1)}, u32[]{:S(2)}, u32[]{:S(2)}) collective-permute-start(bf16[4,64,1536]{2,1,0:T(8,128)(2,1)S(1)} %get-tuple-element.229), channel_id=1, source_target_pairs={{0,16},{1,17},{2,18},{3,19},{4,20},{5,21},{6,22},{7,23},{8,24},{9,... | collective-permute-start | bytes 2359304 | tf_op jit(solution)/shard_map/ppermute | solution.py:36
  229.9 35.2 %collective-permute-start.31 = (bf16[4,64,1536]{2,1,0:T(8,128)(2,1)S(1)}, bf16[4,64,1536]{2,1,0:T(8,128)(2,1)S(1)}, u32[]{:S(2)}, u32[]{:S(2)}) collective-permute-start(bf16[4,64,1536]{2,1,0:T(8,128)(2,1)S(1)} %get-tuple-element.228), channel_id=1, source_target_pairs={{0,16},{1,17},{2,18},{3,19},{4,20},{5,21},{6,22},{7,23},{8,24},{9,... | collective-permute-start | bytes 2359304 | tf_op jit(solution)/shard_map/ppermute | solution.py:36
  248.4 21.2 %collective-permute-start.33 = (bf16[4,64,1536]{2,1,0:T(8,128)(2,1)S(1)}, bf16[4,64,1536]{2,1,0:T(8,128)(2,1)S(1)}, u32[]{:S(2)}, u32[]{:S(2)}) collective-permute-start(bf16[4,64,1536]{2,1,0:T(8,128)(2,1)S(1)} %fusion.10), channel_id=1, source_target_pairs={{0,2},{1,3},{2,0},{3,1},{4,6},{5,7},{6,4},{7,5},{8,10},{9,11},{10,... | collective-permute-start | bytes 2359304 | tf_op jit(solution)/shard_map/ppermute | solution.py:36
  312.9 16.6 %collective-permute-start.43 = (bf16[64,1536]{1,0:T(8,128)(2,1)S(1)}, bf16[64,1536]{1,0:T(8,128)(2,1)S(1)}, u32[]{:S(2)}, u32[]{:S(2)}) collective-permute-start(bf16[64,1536]{1,0:T(8,128)(2,1)S(1)} %get-tuple-element.106), channel_id=1, source_target_pairs={{0,8},{1,9},{2,10},{3,11},{4,12},{5,13},{6,14},{7,15},{8,0},{9,1},... | collective-permute-start | bytes 589832 | tf_op jit(solution)/shard_map/ppermute | solution.py:36
  329.6 17.9 %collective-permute-start.46 = (bf16[4,64,1536]{2,1,0:T(8,128)(2,1)S(1)}, bf16[4,64,1536]{2,1,0:T(8,128)(2,1)S(1)}, u32[]{:S(2)}, u32[]{:S(2)}) collective-permute-start(bf16[4,64,1536]{2,1,0:T(8,128)(2,1)S(1)} %pad_maximum_fusion.1.refs_1_), channel_id=1, source_target_pairs={{0,2},{1,3},{2,0},{3,1},{4,6},{5,7},{6,4},{7,5},{8,10},{9,11},{10,... | collective-permute-start | bytes 2359304 | tf_op jit(solution)/shard_map/ppermute | solution.py:36
  330.1 21.9 %collective-permute-start.49 = (bf16[4,64,1536]{2,1,0:T(8,128)(2,1)S(1)}, bf16[4,64,1536]{2,1,0:T(8,128)(2,1)}, u32[]{:S(2)}, u32[]{:S(2)}) collective-permute-start(bf16[4,64,1536]{2,1,0:T(8,128)(2,1)S(1)} %pad_maximum_fusion.1.refs_1_), channel_id=1, source_target_pairs={{0,16},{1,17},{2,18},{3,19},{4,20},{5,21},{6,22},{7,23},{8,24},{9,... | collective-permute-start | bytes 2359304 | tf_op jit(solution)/shard_map/ppermute | solution.py:36
  347.5 17.0 %collective-permute-start.51 = (bf16[4,64,1536]{2,1,0:T(8,128)(2,1)S(1)}, bf16[4,64,1536]{2,1,0:T(8,128)(2,1)}, u32[]{:S(2)}, u32[]{:S(2)}) collective-permute-start(bf16[4,64,1536]{2,1,0:T(8,128)(2,1)S(1)} %collective-permute-done.46.refs_3_), channel_id=1, source_target_pairs={{0,16},{1,17},{2,18},{3,19},{4,20},{5,21},{6,22},{7,23},{8,24},{9,... | collective-permute-start | bytes 2359304 | tf_op jit(solution)/shard_map/ppermute | solution.py:36
  348.6 18.9 %collective-permute-start.45 = (bf16[4,64,1536]{2,1,0:T(8,128)(2,1)S(1)}, bf16[4,64,1536]{2,1,0:T(8,128)(2,1)S(1)}, u32[]{:S(2)}, u32[]{:S(2)}) collective-permute-start(bf16[4,64,1536]{2,1,0:T(8,128)(2,1)S(1)} %pad_maximum_fusion.1.refs_1_), channel_id=1, source_target_pairs={{0,1},{1,0},{2,3},{3,2},{4,5},{5,4},{6,7},{7,6},{8,9},{9,8},{10,11... | collective-permute-start | bytes 2359304 | tf_op jit(solution)/shard_map/ppermute | solution.py:36
  352.0 39.4 %collective-permute-start.50 = (bf16[4,64,1536]{2,1,0:T(8,128)(2,1)}, bf16[4,64,1536]{2,1,0:T(8,128)(2,1)}, u32[]{:S(2)}, u32[]{:S(2)}) collective-permute-start(bf16[4,64,1536]{2,1,0:T(8,128)(2,1)} %collective-permute-done.49.refs_1_), channel_id=1, source_target_pairs={{0,1},{1,0},{2,3},{3,2},{4,5},{5,4},{6,7},{7,6},{8,9},{9,8},{10,11... | collective-permute-start | bytes 2359304 | tf_op jit(solution)/shard_map/ppermute | solution.py:36
  364.4 26.9 %collective-permute-start.52 = (bf16[4,64,1536]{2,1,0:T(8,128)(2,1)}, bf16[4,64,1536]{2,1,0:T(8,128)(2,1)}, u32[]{:S(2)}, u32[]{:S(2)}) collective-permute-start(bf16[4,64,1536]{2,1,0:T(8,128)(2,1)} %collective-permute-done.51.refs_3_), channel_id=1, source_target_pairs={{0,1},{1,0},{2,3},{3,2},{4,5},{5,4},{6,7},{7,6},{8,9},{9,8},{10,11... | collective-permute-start | bytes 2359304 | tf_op jit(solution)/shard_map/ppermute | solution.py:36
  418.1 19.1 %collective-permute-start.55 = (bf16[4,64,1536]{2,1,0:T(8,128)(2,1)S(1)}, bf16[4,64,1536]{2,1,0:T(8,128)(2,1)S(1)}, u32[]{:S(2)}, u32[]{:S(2)}) collective-permute-start(bf16[4,64,1536]{2,1,0:T(8,128)(2,1)S(1)} %get-tuple-element.227), channel_id=1, source_target_pairs={{0,16},{1,17},{2,18},{3,19},{4,20},{5,21},{6,22},{7,23},{8,24},{9,... | collective-permute-start | bytes 2359304 | tf_op jit(solution)/shard_map/ppermute | solution.py:36
  423.2 33.8 %collective-permute-start.57 = (bf16[2,4,64,1536]{3,2,1,0:T(8,128)(2,1)S(1)}, bf16[2,4,64,1536]{3,2,1,0:T(8,128)(2,1)S(1)}, u32[]{:S(2)}, u32[]{:S(2)}) collective-permute-start(bf16[2,4,64,1536]{3,2,1,0:T(8,128)(2,1)S(1)} %get-tuple-element.113), channel_id=1, source_target_pairs={{0,1},{1,0},{2,3},{3,2},{4,5},{5,4},{6,7},{7,6},{8,9},{9,8},{10,11... | collective-permute-start | bytes 4718600 | tf_op jit(solution)/shard_map/ppermute | solution.py:36
  423.6 30.5 %collective-permute-start.54 = (bf16[4,64,1536]{2,1,0:T(8,128)(2,1)S(1)}, bf16[4,64,1536]{2,1,0:T(8,128)(2,1)S(1)}, u32[]{:S(2)}, u32[]{:S(2)}) collective-permute-start(bf16[4,64,1536]{2,1,0:T(8,128)(2,1)S(1)} %get-tuple-element.226), channel_id=1, source_target_pairs={{0,16},{1,17},{2,18},{3,19},{4,20},{5,21},{6,22},{7,23},{8,24},{9,... | collective-permute-start | bytes 2359304 | tf_op jit(solution)/shard_map/ppermute | solution.py:36
  437.3 17.6 %collective-permute-start.56 = (bf16[4,64,1536]{2,1,0:T(8,128)(2,1)S(1)}, bf16[4,64,1536]{2,1,0:T(8,128)(2,1)S(1)}, u32[]{:S(2)}, u32[]{:S(2)}) collective-permute-start(bf16[4,64,1536]{2,1,0:T(8,128)(2,1)S(1)} %fusion.7), channel_id=1, source_target_pairs={{0,2},{1,3},{2,0},{3,1},{4,6},{5,7},{6,4},{7,5},{8,10},{9,11},{10,... | collective-permute-start | bytes 2359304 | tf_op jit(solution)/shard_map/ppermute | solution.py:36
  457.1 33.5 %collective-permute-start.58 = (bf16[2,4,64,1536]{3,2,1,0:T(8,128)(2,1)S(1)}, bf16[2,4,64,1536]{3,2,1,0:T(8,128)(2,1)S(1)}, u32[]{:S(2)}, u32[]{:S(2)}) collective-permute-start(bf16[2,4,64,1536]{3,2,1,0:T(8,128)(2,1)S(1)} %add_select_fusion.1), channel_id=1, source_target_pairs={{0,16},{1,17},{2,18},{3,19},{4,20},{5,21},{6,22},{7,23},{8,24},{9,... | collective-permute-start | bytes 4718600 | tf_op jit(solution)/shard_map/ppermute | solution.py:36
  462.1 48.3 %collective-permute-start.59 = (bf16[2,4,64,1536]{3,2,1,0:T(8,128)(2,1)S(1)}, bf16[2,4,64,1536]{3,2,1,0:T(8,128)(2,1)S(1)}, u32[]{:S(2)}, u32[]{:S(2)}) collective-permute-start(bf16[2,4,64,1536]{3,2,1,0:T(8,128)(2,1)S(1)} %get-tuple-element.116), channel_id=1, source_target_pairs={{0,1},{1,0},{2,3},{3,2},{4,5},{5,4},{6,7},{7,6},{8,9},{9,8},{10,11... | collective-permute-start | bytes 4718600 | tf_op jit(solution)/shard_map/ppermute | solution.py:36
  465.6 17.0 %collective-permute-start.63 = (bf16[64,1536]{1,0:T(8,128)(2,1)S(1)}, bf16[64,1536]{1,0:T(8,128)(2,1)S(1)}, u32[]{:S(2)}, u32[]{:S(2)}) collective-permute-start(bf16[64,1536]{1,0:T(8,128)(2,1)S(1)} %get-tuple-element.245), channel_id=1, source_target_pairs={{0,8},{1,9},{2,10},{3,11},{4,12},{5,13},{6,14},{7,15},{8,0},{9,1},... | collective-permute-start | bytes 589832 | tf_op jit(solution)/shard_map/ppermute | solution.py:36
  509.2 32.1 %collective-permute-start.71 = (bf16[4,192,896]{2,1,0:T(8,128)(2,1)S(1)}, bf16[4,192,896]{2,1,0:T(8,128)(2,1)S(1)}, u32[]{:S(2)}, u32[]{:S(2)}) collective-permute-start(bf16[4,192,896]{2,1,0:T(8,128)(2,1)S(1)} %get-tuple-element.130), channel_id=1, source_target_pairs={{0,16},{1,17},{2,18},{3,19},{4,20},{5,21},{6,22},{7,23},{8,24},{9,... | collective-permute-start | bytes 4128776 | tf_op jit(solution)/shard_map/ppermute | solution.py:36
  511.4 29.3 %collective-permute-start.60 = (bf16[4,64,1536]{2,1,0:T(8,128)(2,1)S(1)}, bf16[4,64,1536]{2,1,0:T(8,128)(2,1)S(1)}, u32[]{:S(2)}, u32[]{:S(2)}) collective-permute-start(bf16[4,64,1536]{2,1,0:T(8,128)(2,1)S(1)} %slice_bitcast_fusion.4), channel_id=1, source_target_pairs={{0,2},{1,3},{2,0},{3,1},{4,6},{5,7},{6,4},{7,5},{8,10},{9,11},{10,... | collective-permute-start | bytes 2359304 | tf_op jit(solution)/shard_map/ppermute | solution.py:36
  512.8 22.0 %collective-permute-start.69 = (bf16[64,1536]{1,0:T(8,128)(2,1)S(1)}, bf16[64,1536]{1,0:T(8,128)(2,1)S(1)}, u32[]{:S(2)}, u32[]{:S(2)}) collective-permute-start(bf16[64,1536]{1,0:T(8,128)(2,1)S(1)} %get-tuple-element.256), channel_id=1, source_target_pairs={{0,2},{1,3},{2,0},{3,1},{4,6},{5,7},{6,4},{7,5},{8,10},{9,11},{10,... | collective-permute-start | bytes 589832 | tf_op jit(solution)/shard_map/ppermute | solution.py:36
  536.6 16.9 %collective-permute-start.73 = (bf16[64,1536]{1,0:T(8,128)(2,1)S(1)}, bf16[64,1536]{1,0:T(8,128)(2,1)S(1)}, u32[]{:S(2)}, u32[]{:S(2)}) collective-permute-start(bf16[64,1536]{1,0:T(8,128)(2,1)S(1)} %get-tuple-element.131), channel_id=1, source_target_pairs={{0,8},{1,9},{2,10},{3,11},{4,12},{5,13},{6,14},{7,15},{8,0},{9,1},... | collective-permute-start | bytes 589832 | tf_op jit(solution)/shard_map/ppermute | solution.py:36
  553.6 17.8 %collective-permute-start.76 = (bf16[4,64,1536]{2,1,0:T(8,128)(2,1)S(1)}, bf16[4,64,1536]{2,1,0:T(8,128)(2,1)S(1)}, u32[]{:S(2)}, u32[]{:S(2)}) collective-permute-start(bf16[4,64,1536]{2,1,0:T(8,128)(2,1)S(1)} %maximum_select_fusion.2.refs_0_), channel_id=1, source_target_pairs={{0,2},{1,3},{2,0},{3,1},{4,6},{5,7},{6,4},{7,5},{8,10},{9,11},{10,... | collective-permute-start | bytes 2359304 | tf_op jit(solution)/shard_map/ppermute | solution.py:36
  554.0 20.2 %collective-permute-start.79 = (bf16[4,64,1536]{2,1,0:T(8,128)(2,1)S(1)}, bf16[4,64,1536]{2,1,0:T(8,128)(2,1)S(1)}, u32[]{:S(2)}, u32[]{:S(2)}) collective-permute-start(bf16[4,64,1536]{2,1,0:T(8,128)(2,1)S(1)} %maximum_select_fusion.2.refs_0_), channel_id=1, source_target_pairs={{0,16},{1,17},{2,18},{3,19},{4,20},{5,21},{6,22},{7,23},{8,24},{9,... | collective-permute-start | bytes 2359304 | tf_op jit(solution)/shard_map/ppermute | solution.py:36
  571.4 16.8 %collective-permute-start.81 = (bf16[4,64,1536]{2,1,0:T(8,128)(2,1)S(1)}, bf16[4,64,1536]{2,1,0:T(8,128)(2,1)S(1)}, u32[]{:S(2)}, u32[]{:S(2)}) collective-permute-start(bf16[4,64,1536]{2,1,0:T(8,128)(2,1)S(1)} %collective-permute-done.76.refs_2_), channel_id=1, source_target_pairs={{0,16},{1,17},{2,18},{3,19},{4,20},{5,21},{6,22},{7,23},{8,24},{9,... | collective-permute-start | bytes 2359304 | tf_op jit(solution)/shard_map/ppermute | solution.py:36
  571.6 19.7 %collective-permute-start.75 = (bf16[4,64,1536]{2,1,0:T(8,128)(2,1)S(1)}, bf16[4,64,1536]{2,1,0:T(8,128)(2,1)S(1)}, u32[]{:S(2)}, u32[]{:S(2)}) collective-permute-start(bf16[4,64,1536]{2,1,0:T(8,128)(2,1)S(1)} %maximum_select_fusion.2.refs_0_), channel_id=1, source_target_pairs={{0,1},{1,0},{2,3},{3,2},{4,5},{5,4},{6,7},{7,6},{8,9},{9,8},{10,11... | collective-permute-start | bytes 2359304 | tf_op jit(solution)/shard_map/ppermute | solution.py:36
  574.1 17.2 %collective-permute-start.77 = (bf16[4,64,1536]{2,1,0:T(8,128)(2,1)S(1)}, bf16[4,64,1536]{2,1,0:T(8,128)(2,1)S(1)}, u32[]{:S(2)}, u32[]{:S(2)}) collective-permute-start(bf16[4,64,1536]{2,1,0:T(8,128)(2,1)S(1)} %collective-permute-done.76.refs_2_), channel_id=1, source_target_pairs={{0,1},{1,0},{2,3},{3,2},{4,5},{5,4},{6,7},{7,6},{8,9},{9,8},{10,11... | collective-permute-start | bytes 2359304 | tf_op jit(solution)/shard_map/ppermute | solution.py:36
  574.2 34.1 %collective-permute-start.80 = (bf16[4,64,1536]{2,1,0:T(8,128)(2,1)S(1)}, bf16[4,64,1536]{2,1,0:T(8,128)(2,1)S(1)}, u32[]{:S(2)}, u32[]{:S(2)}) collective-permute-start(bf16[4,64,1536]{2,1,0:T(8,128)(2,1)S(1)} %collective-permute-done.79.refs_0_), channel_id=1, source_target_pairs={{0,1},{1,0},{2,3},{3,2},{4,5},{5,4},{6,7},{7,6},{8,9},{9,8},{10,11... | collective-permute-start | bytes 2359304 | tf_op jit(solution)/shard_map/ppermute | solution.py:36
  588.1 20.1 %collective-permute-start.82 = (bf16[4,64,1536]{2,1,0:T(8,128)(2,1)S(1)}, bf16[4,64,1536]{2,1,0:T(8,128)(2,1)S(1)}, u32[]{:S(2)}, u32[]{:S(2)}) collective-permute-start(bf16[4,64,1536]{2,1,0:T(8,128)(2,1)S(1)} %collective-permute-done.81.refs_2_), channel_id=1, source_target_pairs={{0,1},{1,0},{2,3},{3,2},{4,5},{5,4},{6,7},{7,6},{8,9},{9,8},{10,11... | collective-permute-start | bytes 2359304 | tf_op jit(solution)/shard_map/ppermute | solution.py:36
  631.0 19.0 %collective-permute-start.85 = (bf16[4,64,1536]{2,1,0:T(8,128)(2,1)S(1)}, bf16[4,64,1536]{2,1,0:T(8,128)(2,1)S(1)}, u32[]{:S(2)}, u32[]{:S(2)}) collective-permute-start(bf16[4,64,1536]{2,1,0:T(8,128)(2,1)S(1)} %get-tuple-element.225), channel_id=1, source_target_pairs={{0,16},{1,17},{2,18},{3,19},{4,20},{5,21},{6,22},{7,23},{8,24},{9,... | collective-permute-start | bytes 2359304 | tf_op jit(solution)/shard_map/ppermute | solution.py:36
  632.2 34.8 %collective-permute-start.84 = (bf16[4,64,1536]{2,1,0:T(8,128)(2,1)}, bf16[4,64,1536]{2,1,0:T(8,128)(2,1)}, u32[]{:S(2)}, u32[]{:S(2)}) collective-permute-start(bf16[4,64,1536]{2,1,0:T(8,128)(2,1)} %get-tuple-element.224), channel_id=1, source_target_pairs={{0,16},{1,17},{2,18},{3,19},{4,20},{5,21},{6,22},{7,23},{8,24},{9,... | collective-permute-start | bytes 2359304 | tf_op jit(solution)/shard_map/ppermute | solution.py:36
  651.0 17.8 %collective-permute-start.86 = (bf16[4,64,1536]{2,1,0:T(8,128)(2,1)}, bf16[4,64,1536]{2,1,0:T(8,128)(2,1)}, u32[]{:S(2)}, u32[]{:S(2)}) collective-permute-start(bf16[4,64,1536]{2,1,0:T(8,128)(2,1)} %fusion.3), channel_id=1, source_target_pairs={{0,2},{1,3},{2,0},{3,1},{4,6},{5,7},{6,4},{7,5},{8,10},{9,11},{10,... | collective-permute-start | bytes 2359304 | tf_op jit(solution)/shard_map/ppermute | solution.py:36
  652.6 148.0 %reduce-scatter.5.cloned.1.call-start = ((), (), s32[]{:S(2)}) async-start(), calls=%async_computation.4 | async-start | bytes 1720320 | tf_op jit(solution)/shard_map/reduce_scatter | solution.py:798
  670.4 17.8 %collective-permute-start.89 = (bf16[64,1536]{1,0:T(8,128)(2,1)S(1)}, bf16[64,1536]{1,0:T(8,128)(2,1)S(1)}, u32[]{:S(2)}, u32[]{:S(2)}) collective-permute-start(bf16[64,1536]{1,0:T(8,128)(2,1)S(1)} %get-tuple-element.241), channel_id=1, source_target_pairs={{0,12},{1,13},{2,14},{3,15},{4,8},{5,9},{6,10},{7,11},{8,4},{9,5},... | collective-permute-start | bytes 589832 | tf_op jit(solution)/shard_map/ppermute | solution.py:36
  671.0 19.4 %collective-permute-start.88 = (bf16[64,1536]{1,0:T(8,128)(2,1)S(1)}, bf16[64,1536]{1,0:T(8,128)(2,1)S(1)}, u32[]{:S(2)}, u32[]{:S(2)}) collective-permute-start(bf16[64,1536]{1,0:T(8,128)(2,1)S(1)} %get-tuple-element.242), channel_id=1, source_target_pairs={{0,8},{1,9},{2,10},{3,11},{4,12},{5,13},{6,14},{7,15},{8,0},{9,1},... | collective-permute-start | bytes 589832 | tf_op jit(solution)/shard_map/ppermute | solution.py:36
  730.5 31.9 %collective-permute-start.97 = (bf16[4,192,896]{2,1,0:T(8,128)(2,1)S(1)}, bf16[4,192,896]{2,1,0:T(8,128)(2,1)}, u32[]{:S(2)}, u32[]{:S(2)}) collective-permute-start(bf16[4,192,896]{2,1,0:T(8,128)(2,1)S(1)} %get-tuple-element.167), channel_id=1, source_target_pairs={{0,16},{1,17},{2,18},{3,19},{4,20},{5,21},{6,22},{7,23},{8,24},{9,... | collective-permute-start | bytes 4128776 | tf_op jit(solution)/shard_map/ppermute | solution.py:36
  732.9 34.8 %collective-permute-start.95 = (bf16[64,1536]{1,0:T(8,128)(2,1)}, bf16[64,1536]{1,0:T(8,128)(2,1)}, u32[]{:S(2)}, u32[]{:S(2)}) collective-permute-start(bf16[64,1536]{1,0:T(8,128)(2,1)} %select_convert_fusion), channel_id=1, source_target_pairs={{0,16},{1,17},{2,18},{3,19},{4,20},{5,21},{6,22},{7,23},{8,24},{9,... | collective-permute-start | bytes 589832 | tf_op jit(solution)/shard_map/ppermute | solution.py:36
  769.6 24.6 %collective-permute-start.102 = (bf16[208,896]{1,0:T(8,128)(2,1)S(1)}, bf16[208,896]{1,0:T(8,128)(2,1)S(1)}, u32[]{:S(2)}, u32[]{:S(2)}) collective-permute-start(bf16[208,896]{1,0:T(8,128)(2,1)S(1)} %get-tuple-element.231), channel_id=1, source_target_pairs={{0,12},{1,13},{2,14},{3,15},{4,8},{5,9},{6,10},{7,11},{8,4},{9,5},... | collective-permute-start | bytes 1118216 | tf_op jit(solution)/shard_map/ppermute | solution.py:36
  769.9 30.5 %collective-permute-start.101 = (bf16[208,896]{1,0:T(8,128)(2,1)S(1)}, bf16[208,896]{1,0:T(8,128)(2,1)S(1)}, u32[]{:S(2)}, u32[]{:S(2)}) collective-permute-start(bf16[208,896]{1,0:T(8,128)(2,1)S(1)} %get-tuple-element.232), channel_id=1, source_target_pairs={{0,8},{1,9},{2,10},{3,11},{4,12},{5,13},{6,14},{7,15},{8,0},{9,1},... | collective-permute-start | bytes 1118216 | tf_op jit(solution)/shard_map/ppermute | solution.py:36
  (178 other events, 4572.2 us)
Sparse Core Ops, SparseCore 0:
  27.3 61.4 all-gather.7
  124.4 78.6 all-gather.9
  205.3 62.4 all-gather.5
  652.8 24.2 reduce-scatter.2
  706.3 30.8 reduce-scatter.4

commit v3 on v2

v3 whole, which is shorter than its diff:
```python
import functools

import jax
import jax.numpy as jnp
from jax import lax
from jax.experimental import pallas as pl
from jax.experimental.pallas import tpu as pltpu
from jax.sharding import PartitionSpec as P

H = 12
KVH = 2
HD = 128
E = 16

EPS = 1e-06
THETA = 10000.0
BF = jnp.bfloat16
F32 = jnp.float32
MIB = 1024 * 1024
COST = 4
TOGETHER = 4
DEPTH = 4


def dot(a, b, ca, cb):
    return lax.dot_general(a, b, (((ca,), (cb,)), ((), ())), preferred_element_type=F32)


def move(value, section=0, dp=0, tensor=0):
    n_dp, n_t = lax.axis_size("dp"), lax.axis_size("tensor")
    pairs = []
    for s in range(2):
        for d in range(n_dp):
            for t in range(n_t):
                here = (s * n_dp + d) * n_t + t
                pairs.append((here, ((s ^ section) * n_dp + (d ^ dp)) * n_t + (t ^ tensor)))
    return lax.ppermute(value, ("section", "dp", "tensor"), pairs)


def kv_turn(value):
    return lax.ppermute(value, "tensor", [(0, 0), (1, 2), (2, 1), (3, 3)])


def over_tensor(value):
    across = move(value, tensor=2)
    return [value, move(value, tensor=1), across, move(across, tensor=1)]


def after(value, *tokens):
    ready = functools.reduce(jnp.logical_and, [token == token for token in tokens])
    return jnp.where(ready, value, jnp.zeros_like(value))


def there(*tokens):
    marks = [token[(0,) * token.ndim].astype(F32) for token in tokens]
    total = functools.reduce(jnp.add, marks)
    return total == total


def sum_over_tensor(keep, send):
    total = keep + move(send, tensor=1)
    return total[0], move(total[1], tensor=2)


def rope(value, cosine, sine):
    return value * cosine + pltpu.roll(value, HD // 2, 1) * sine


def allowed_pairs(me, rows, start):
    def places(axis):
        at = lax.broadcasted_iota(jnp.int32, (4 * rows, 4 * rows), axis)
        return (me[3] ^ (at // rows)) * rows + at % rows

    keys = places(1)
    return (keys <= places(0)) & (keys >= start.astype(jnp.int32))


def assemble(blocks, weights, sems):
    halves, n_dp, half = blocks.shape[:3]
    return start_all(*[
        pltpu.make_async_copy(
            blocks.at[part, k], weights.at[pl.ds((2 * k + part) * half, half)], sems.at[part, k]
        )
        for part in range(halves)
        for k in range(n_dp)
    ])


def whole_sequence(blocks, into):
    rows = blocks[0].shape[0]
    for r, ref in enumerate(blocks):
        into[r * rows : (r + 1) * rows, :] = ref[...]


def attn_fwd_kernel(heads, me, blocks, a0, a1, a2, a3, table, keep, send, saved, a_all, weights, sems):
    rows, qcols = a0.shape[0], heads * HD
    copies = assemble(blocks, weights, sems)
    whole_sequence((a0, a1, a2, a3), a_all)
    wait_all(copies)
    qkv = dot(a_all[...], weights[:, : qcols + 2 * HD], 1, 0)
    co, si = table[:, :HD], table[:, HD : 2 * HD]
    k = rope(qkv[:, qcols : qcols + HD], co, si).astype(BF)
    v = qkv[:, qcols + HD :].astype(BF)
    saved[:, qcols : qcols + HD] = k
    saved[:, qcols + HD : qcols + 2 * HD] = v
    allowed = allowed_pairs(me, rows, table[:, 2 * HD : 2 * HD + 1])
    for h in range(heads):
        qh = rope(qkv[:, h * HD : (h + 1) * HD], co, si).astype(BF)
        saved[:, h * HD : (h + 1) * HD] = qh
        p = softmax(qh, k, allowed).astype(BF)
        at = qcols + 2 * HD + h * HD
        saved[:, at : at + HD] = dot(p, v, 1, 0).astype(BF)
    part = dot(saved[:, qcols + 2 * HD :], weights[:, qcols + 2 * HD :], 1, 1).astype(BF)
    for r in range(4):
        (send if r % 2 else keep)[r // 2] = part[r * rows : (r + 1) * rows, :]


def softmax(qh, k, allowed):
    s = jnp.where(allowed, HD ** (-0.5) * dot(qh, k, 1, 1), -1e30)
    e = jnp.exp(s - jnp.max(s, axis=1, keepdims=True))
    return e * (1.0 / jnp.sum(e, axis=1, keepdims=True))


def attn_bwd_kernel(
    heads, me, blocks, d0, d1, d2, d3, saved, table,
    keep, send, dq_out, kv_send, d_all, weights, sems, dqkv,
):
    rows, qcols = d0.shape[0], heads * HD
    copies = assemble(blocks, weights, sems)
    whole_sequence((d0, d1, d2, d3), d_all)
    wait_all(copies)
    do = dot(d_all[...], weights[:, qcols + 2 * HD :], 1, 0).astype(BF)
    co, si = table[:, :HD], -table[:, HD : 2 * HD]
    k, v = saved[:, qcols : qcols + HD], saved[:, qcols + HD : qcols + 2 * HD]
    allowed = allowed_pairs(me, rows, table[:, 2 * HD : 2 * HD + 1])
    dk = jnp.zeros((do.shape[0], HD), F32)
    dv = jnp.zeros((do.shape[0], HD), F32)
    for h in range(heads):
        qh = saved[:, h * HD : (h + 1) * HD]
        doh = do[:, h * HD : (h + 1) * HD]
        p = softmax(qh, k, allowed)
        dv = dv + dot(p.astype(BF), doh, 0, 0)
        dp = dot(doh, v, 1, 1)
        ds = (p * (dp - jnp.sum(p * dp, axis=1, keepdims=True))).astype(BF)
        dq = HD ** (-0.5) * dot(ds, k, 1, 0)
        dk = dk + dot(ds, qh, 0, 0)
        dqkv[:, h * HD : (h + 1) * HD] = rope(dq, co, si).astype(BF)
    dk = rope(HD ** (-0.5) * dk, co, si).astype(BF)
    dv = dv.astype(BF)
    dqkv[:, qcols : qcols + HD] = dk
    dqkv[:, qcols + HD :] = dv
    core0 = me[2] == 0
    dq_out[:, :qcols] = dqkv[:, :qcols]
    dq_out[:, qcols:] = jnp.where(core0, dk, dv)
    kv_send[...] = jnp.where(core0, dv, dk)
    part = dot(dqkv[...], weights[:, : qcols + 2 * HD], 1, 1).astype(BF)
    for r in range(4):
        (send if r % 2 else keep)[r // 2] = part[r * rows : (r + 1) * rows, :]


def total_of(terms, places):
    total = None
    for ref, place in zip(terms, places):
        term = (ref[...] if place is None else ref[place]).astype(F32)
        total = term if total is None else total + term
    return total


def finish_kernel(places, base, gain, *refs):
    terms, (out, normed) = refs[: len(places)], refs[len(places) :]
    total = base[...]
    if places:
        total = total + total_of(terms, places)
    out[...] = total
    r = lax.rsqrt(jnp.mean(total * total, axis=1, keepdims=True) + EPS)
    normed[...] = (total * r * gain[...]).astype(BF)


def norm_back_kernel(places, rows_in, gain, upper, *refs):
    terms, rest = refs[: len(places)], refs[len(places) :]
    grad = total_of(terms, places)
    x = rows_in[...]
    r = lax.rsqrt(jnp.mean(x * x, axis=1, keepdims=True) + EPS)
    weighted = grad * gain[...]
    projected = jnp.mean(weighted * x, axis=1, keepdims=True)
    total = upper[...] + (r * weighted - x * (r * r * r) * projected)
    if len(rest) == 3:
        out, low, gain_sum = rest
        low[...] = total.astype(BF)
    else:
        more, out, following, low, gain_sum = rest
        after = more[...] + total
        following[...] = after
        low[...] = after.astype(BF)
    out[...] = total
    gain_sum[...] = jnp.sum(grad * x * r, axis=0, keepdims=True)


def split_rows(me, n_dp, grad, mine, theirs, flipped):
    half = grad.shape[0] // (2 * n_dp)
    for k in range(n_dp):
        start = (me[0] ^ k if flipped else k) * (2 * half)
        near = pl.multiple_of(start + me[1] * half, 16)
        far = pl.multiple_of(start + (1 - me[1]) * half, 16)
        mine[k] = grad[pl.ds(near, half), :]
        theirs[k] = grad[pl.ds(far, half), :]


def attn_wgrad_kernel(flipped, n_dp, me, a_all, d_all, saved, dq, kv_got, mine, theirs, grad):
    cols = dq.shape[1]
    qcols = cols - HD
    rows = a_all.shape[0] // 4
    got = [kv_got[r * rows : (r + 1) * rows, :] for r in (1, 0, 3, 2)]
    kv = (dq[:, qcols:].astype(F32) + jnp.concatenate(got, axis=0).astype(F32)).astype(BF)
    a = a_all[...]
    grad[:, :qcols] = dot(a, dq[:, :qcols], 0, 0).astype(BF)
    grad[:, qcols:cols] = dot(a, kv, 0, 0).astype(BF)
    grad[:, cols:] = dot(d_all[...], saved[:, qcols + 2 * HD :], 0, 0).astype(BF)
    split_rows(me, n_dp, grad, mine, theirs, flipped)


def slot_rows(pos_row, s, experts, cap):
    slot = lax.broadcasted_iota(jnp.int32, (cap, pos_row.shape[2]), 0)
    hits = [(slot == pos_row[s, e : e + 1, :]).astype(F32) for e in range(experts)]
    return jnp.concatenate(hits, axis=0).astype(BF)


def start_all(*copies):
    for copy in copies:
        copy.start()
    return list(copies)


def wait_all(copies):
    for copy in copies:
        copy.wait()


def slot_gates(hit, gate_cols, s, experts, cap):
    both = dot(hit, gate_cols[s], 1, 0)
    lane = lax.broadcasted_iota(jnp.int32, both.shape, 1)
    own = lax.broadcasted_iota(jnp.int32, both.shape, 0) // cap
    return jnp.sum(jnp.where((lane == own) | (lane == own + experts), both, 0.0), axis=1, keepdims=True)


def gathered(me, ref, batch, count):
    return [[(ref, ((me[0] ^ s) * 4 + (me[3] ^ r), batch)) for r in range(4)] for s in range(count)]


def sequences(refs, count):
    out = []
    for at in range(0, len(refs), 8):
        out.append([(refs[at + r], None) for r in range(4)])
        out += [[(refs[at + 4 + r], s) for r in range(4)] for s in range(count - 1)]
    return out


def dispatch(tasks, ring, sems, pos_row, gate_cols, gates, experts, cap, following=()):
    def fetch(i):
        copies = []
        for r, (ref, at) in enumerate(tasks[i][0]):
            rows = ref.shape[-2]
            target = ring.at[i % DEPTH, pl.ds(r * rows, rows)]
            source = ref if at is None else ref.at[at]
            copies.append(pltpu.make_async_copy(source, target, sems.at[i % DEPTH, r]))
        return start_all(*copies)

    coming = [fetch(i) for i in range(min(DEPTH, len(tasks)))]
    following = list(following)
    for i, (_, s, into) in enumerate(tasks):
        wait_all(coming[i])
        hit = slot_rows(pos_row, s, experts, cap)
        picked = dot(hit, ring[i % DEPTH], 1, 0).astype(BF)
        for e in range(experts):
            into[e, s * cap : (s + 1) * cap, :] = picked[e * cap : (e + 1) * cap, :]
        if gates is not None and i < pos_row.shape[0]:
            gate = slot_gates(hit, gate_cols, s, experts, cap)
            for e in range(experts):
                gates[e, s * cap : (s + 1) * cap, :] = gate[e * cap : (e + 1) * cap, :]
        if i + DEPTH < len(tasks):
            coming.append(fetch(i + DEPTH))
        for copy in following[:2]:
            copy.start()
        following = following[2:]
    start_all(*following)


def place(out, result, e, cap):
    out = out.astype(BF)
    for s in range(result.shape[0]):
        result[s, e * cap : (e + 1) * cap, :] = out[s * cap : (s + 1) * cap, :]


def combine(values, pos_row, keep, send, experts, cap, rows, order=None):
    for s in range(values.shape[0]):
        total = dot(slot_rows(pos_row, s, experts, cap), values[s], 0, 0).astype(BF)
        at = s if order is None else order[s]
        for r in range(4):
            (send if r % 2 else keep)[r // 2, at] = total[r * rows : (r + 1) * rows, :]


def silu_parts(gu):
    half = gu.shape[1] // 2
    gate, up = gu[:, :half], gu[:, half:]
    sg = 1.0 / (1.0 + jnp.exp(-gate))
    return gate, up, sg


def gate_up_grad(dz, gate, up, sg, out):
    half = gate.shape[1]
    out[:, :half] = (dz * up * sg * (1.0 + gate * (1.0 - sg))).astype(BF)
    out[:, half:] = (dz * gate * sg).astype(BF)


def take(refs, *counts):
    parts, at = [], 0
    for count in counts:
        parts.append(refs[at : at + count])
        at += count
    return parts


def expert_weights(w_in, w_out, wi, wo, sems):
    copies = [
        [
            pltpu.make_async_copy(w_in.at[e], wi.at[e], sems.at[2 * e]),
            pltpu.make_async_copy(w_out.at[e], wo.at[e], sems.at[2 * e + 1]),
        ]
        for e in range(w_in.shape[0])
    ]
    return copies, [copy for pair in copies for copy in pair]


def moe_fwd_kernel(experts, cap, rows, count, n_blocks, *refs):
    blocks, ins, outs, scratch = take(refs, n_blocks, 4, 3, 9)
    pos_row, gate_cols, w_in, w_out = ins
    gu_out, keep, send = outs
    ring, x_all, result, gates, gu_all, wi, wo, sems, ring_sems = scratch
    weights, coming = expert_weights(w_in, w_out, wi, wo, sems)
    tasks = [(places, s, x_all) for s, places in enumerate(sequences(blocks, count))]
    dispatch(tasks, ring, ring_sems, pos_row, gate_cols, gates, experts, cap, coming)
    for e in range(experts):
        wait_all(weights[e])
        gu = dot(x_all[e], wi[e], 1, 0)
        gu_all[e] = gu
        gate, up, sg = silu_parts(gu)
        z = (gate * sg * up * gates[e]).astype(BF)
        place(dot(z, wo[e], 1, 0), result, e, cap)
    done = start_all(pltpu.make_async_copy(gu_all, gu_out, sems.at[2 * experts]))
    combine(result, pos_row, keep, send, experts, cap, rows)
    wait_all(done)


def moe_bwd_kernel(experts, cap, rows, count, n_blocks, *refs):
    blocks, ins, outs, scratch = take(refs, n_blocks, 5, 4, 11)
    pos_row, gate_cols, gu_in, w_in, w_out = ins
    z_out, dgu_out, keep, send = outs
    ring, dr_all, result, gates, gu_all, z_all, dgu_all, wi, wo, sems, ring_sems = scratch
    weights, coming = expert_weights(w_in, w_out, wi, wo, sems)
    fetched = pltpu.make_async_copy(gu_in, gu_all, sems.at[2 * experts])
    tasks = [(places, s, dr_all) for s, places in enumerate(sequences(blocks, count))]
    dispatch(tasks, ring, ring_sems, pos_row, gate_cols, gates, experts, cap, [fetched] + coming)
    fetched.wait()
    for e in range(experts):
        wait_all(weights[e])
        gate, up, sg = silu_parts(gu_all[e])
        z_all[e] = (gate * sg * up * gates[e]).astype(BF)
        gate_up_grad(dot(dr_all[e], wo[e], 1, 1) * gates[e], gate, up, sg, dgu_all.at[e])
        place(dot(dgu_all[e], wi[e], 1, 1), result, e, cap)
    done = start_all(
        pltpu.make_async_copy(z_all, z_out, sems.at[2 * experts + 1]),
        pltpu.make_async_copy(dgu_all, dgu_out, sems.at[2 * experts + 2]),
    )
    combine(result, pos_row, keep, send, experts, cap, rows)
    wait_all(done)


def moe_turn_kernel(experts, cap, rows, count, n_blocks, batches, me, *refs):
    blocks, ins, outs, scratch = take(refs, n_blocks, 5, 4, 11)
    grads, pos_row, gate_cols, w_in, w_out = ins
    z_out, dgu_out, keep, send = outs
    ring, x_all, dr_all, result, gates, z_all, dgu_all, wi, wo, sems, ring_sems = scratch
    weights, coming = expert_weights(w_in, w_out, wi, wo, sems)
    grad_places = [places for batch in batches for places in gathered(me, grads, batch, count)]
    tasks = [(places, s, x_all) for s, places in enumerate(sequences(blocks, count))]
    tasks += [(places, s, dr_all) for s, places in enumerate(grad_places)]
    dispatch(tasks, ring, ring_sems, pos_row, gate_cols, gates, experts, cap, coming)
    for e in range(experts):
        wait_all(weights[e])
        gu = dot(x_all[e], wi[e], 1, 0)
        gate, up, sg = silu_parts(gu)
        z_all[e] = (gate * sg * up * gates[e]).astype(BF)
        gate_up_grad(dot(dr_all[e], wo[e], 1, 1) * gates[e], gate, up, sg, dgu_all.at[e])
        place(dot(dgu_all[e], wi[e], 1, 1), result, e, cap)
    done = start_all(
        pltpu.make_async_copy(z_all, z_out, sems.at[2 * experts]),
        pltpu.make_async_copy(dgu_all, dgu_out, sems.at[2 * experts + 1]),
    )
    combine(result, pos_row, keep, send, experts, cap, rows)
    wait_all(done)


def moe_out_kernel(experts, cap, rows, count, me, z, pos_row, w_out, keep, send, result):
    for e in range(experts):
        place(dot(z[e], w_out[e], 1, 0), result, e, cap)
    order = [s // count * count + (me[0] ^ (s % count)) for s in range(pos_row.shape[0])]
    combine(result, pos_row, keep, send, experts, cap, rows, order)


def moe_wgrad_kernel(experts, cap, count, n_blocks, *refs):
    me, refs = refs[0], refs[1:]
    x0, g0, x1, ins, hidden, outs, scratch = take(refs, n_blocks, n_blocks, n_blocks, 2, 4, 2, 9)
    cots, pos_row = ins
    dwin, dwout = outs
    ring, x_all, dr_all, dgu, z, din, dout, sems, ring_sems = scratch

    def tokens(x_places, g_places, dgu_in, z_in):
        fetched = start_all(
            pltpu.make_async_copy(dgu_in, dgu, sems.at[4]), pltpu.make_async_copy(z_in, z, sems.at[5])
        )
        tasks = [(places, s, x_all) for s, places in enumerate(x_places)]
        tasks += [(places, s, dr_all) for s, places in enumerate(g_places)]
        dispatch(tasks, ring, ring_sems, pos_row, None, None, experts, cap)
        wait_all(fetched)

    @pl.when(me[1] == 0)
    def _():
        tokens(sequences(x0, count), sequences(g0, count), hidden[0], hidden[1])

    @pl.when(me[1] == 1)
    def _():
        places = [part for batch in (1, 0) for part in gathered(me, cots, batch, count)]
        tokens(sequences(x1, count), places, hidden[2], hidden[3])

    leaving = [[], []]
    for e in range(experts):
        slot = e % 2
        wait_all(leaving[slot])
        din[slot] = dot(x_all[e], dgu[e], 0, 0)
        dout[slot] = dot(z[e], dr_all[e], 0, 0)
        leaving[slot] = start_all(
            pltpu.make_async_copy(din.at[slot], dwin.at[e], sems.at[slot]),
            pltpu.make_async_copy(dout.at[slot], dwout.at[e], sems.at[2 + slot]),
        )
    wait_all(leaving[0] + leaving[1])


def per_device(
    block_input, segments, expert_ids, gate_values, cotangent, attn_gain,
    query_weight, kv_weight, out_weight, moe_gain, w_in, w_out,
):
    sec = lax.axis_index("section")
    dp = lax.axis_index("dp")
    t = lax.axis_index("tensor")
    n_dp = lax.axis_size("dp")
    n_t = lax.axis_size("tensor")
    first = sec == 0
    core0 = t % 2 == 0
    me = jnp.stack([dp, sec, t % 2, t]).astype(jnp.int32)
    rows, width = block_input.shape[1], block_input.shape[2]
    seq = segments.shape[1]
    top = expert_ids.shape[3]
    heads = query_weight.shape[2] // HD
    qcols = heads * HD
    experts, ffn = w_in.shape[1], w_out.shape[2]
    cap = -(-(seq * top * 9 // (8 * E)) // 16) * 16
    sides = 2 if n_dp <= TOGETHER else 1
    total = 2 * n_dp
    slots = total * cap
    dp_order = jnp.arange(n_dp, dtype=jnp.int32) ^ dp
    t_order = jnp.arange(n_t, dtype=jnp.int32) ^ t
    drows = width // n_dp
    half = drows // 2

    pair = jax.ShapeDtypeStruct((2, rows, width), BF)
    smem = pl.BlockSpec(memory_space=pltpu.SMEM)
    vmem = pl.BlockSpec(memory_space=pltpu.VMEM)
    any_space = pl.BlockSpec(memory_space=pl.ANY)
    hbm = pl.BlockSpec(memory_space=pltpu.HBM)
    seq_scratch = pltpu.VMEM((seq, width), BF)

    def me_after(*tokens):
        return jnp.where(there(*tokens), me, 0) if tokens else me

    def shape(*dims, dtype=BF):
        return jax.ShapeDtypeStruct(dims, dtype)

    def call(
        kernel, name, ins, outs, scratch, limit, cost, in_specs=None, out_specs=None, hold=(), tokens=()
    ):
        n_ins, n_outs, n_hold, n_tok = len(ins), len(outs), len(hold), len(tokens)

        def body(*refs):
            given, results, rest = take(refs, n_ins + n_tok + n_hold, n_outs + n_hold, len(scratch))
            kernel(*given[:n_ins], *results[:n_outs], *rest)

        out = pl.pallas_call(
            body,
            out_shape=list(outs) + [jax.ShapeDtypeStruct(h.shape, h.dtype) for h in hold],
            in_specs=(in_specs or [smem] + [vmem] * (n_ins - 1)) + [any_space] * (n_tok + n_hold),
            out_specs=(out_specs or [vmem] * n_outs) + [any_space] * n_hold,
            scratch_shapes=scratch,
            input_output_aliases={n_ins + n_tok + i: n_outs + i for i in range(n_hold)},
            compiler_params=pltpu.CompilerParams(vmem_limit_bytes=limit * MIB),
            cost_estimate=pl.CostEstimate(flops=cost * 10**9, bytes_accessed=cost * 3 * MIB, transcendentals=0),
            name=name,
        )(*ins, *tokens, *hold)
        return out[:n_outs], out[n_outs:]

    acols = 2 * qcols + 2 * HD
    weights_scratch = pltpu.VMEM((width, acols), BF)
    weights_sems = pltpu.SemaphoreType.DMA((2, n_dp))

    def attn_fwd(a_blocks, weights, tokens=()):
        return call(
            functools.partial(attn_fwd_kernel, heads), "attn_fwd",
            (me, weights, *a_blocks, table),
            [pair, pair, shape(seq, acols), shape(seq, width)],
            [weights_scratch, weights_sems], 20, 0, [smem, hbm] + [vmem] * 5, tokens=tokens,
        )[0]

    def attn_bwd(d_blocks, saved, weights):
        return call(
            functools.partial(attn_bwd_kernel, heads), "attn_bwd",
            (me, weights, *d_blocks, saved, table),
            [pair, pair, shape(seq, qcols + HD), shape(seq, HD), shape(seq, width)],
            [weights_scratch, weights_sems, pltpu.VMEM((seq, qcols + 2 * HD), BF)], 20, 0,
            [smem, hbm] + [vmem] * 6,
        )[0]

    tok_f32, tok_bf = shape(rows, width, dtype=F32), shape(rows, width)

    def finish(base, gain, terms, hold=()):
        (out, normed), held = call(
            functools.partial(finish_kernel, [at for _, at in terms]), "finish",
            (base, gain, *[value for value, _ in terms]), [tok_f32, tok_bf], [], 8, 0,
            [vmem] * (2 + len(terms)), hold=hold,
        )
        return out, normed, held

    def norm_back(x, gain, upper, terms, more=(), tokens=()):
        return call(
            functools.partial(norm_back_kernel, [at for _, at in terms]), "norm_back",
            (x, gain, upper, *[value for value, _ in terms], *more),
            [tok_f32] * (1 + len(more)) + [tok_bf, shape(1, width, dtype=F32)], [], 8, 0,
            [vmem] * (3 + len(terms) + len(more)), tokens=tokens,
        )

    def halves_grad(kernel, name, ins, cols):
        return call(
            functools.partial(kernel, n_dp), name, (me, *ins), [shape(n_dp, half, cols)] * 2,
            [pltpu.VMEM((width, cols), BF)], 20, 1,
        )[0]

    count = sides * n_dp
    part_slots = count * cap
    weight_scratch = [pltpu.VMEM((experts, width, 2 * ffn), BF), pltpu.VMEM((experts, ffn, width), BF)]
    ring_scratch = pltpu.VMEM((DEPTH, seq, width), BF)
    slot_scratch = pltpu.VMEM((experts, part_slots, width), BF)
    result_scratch = pltpu.VMEM((count, experts * cap, width), BF)
    z_scratch = pltpu.VMEM((experts, part_slots, ffn), BF)
    dgu_scratch = pltpu.VMEM((experts, part_slots, 2 * ffn), BF)
    gu_scratch = pltpu.VMEM((experts, part_slots, 2 * ffn), F32)
    gate_scratch = pltpu.VMEM((experts, part_slots, 1), F32)
    copy_sems = pltpu.SemaphoreType.DMA((2 * experts + 3,))
    ring_sems = pltpu.SemaphoreType.DMA((DEPTH, 4))
    gu_shape = shape(experts, part_slots, 2 * ffn, dtype=F32)
    z_shape = shape(experts, part_slots, ffn)
    dgu_shape = shape(experts, part_slots, 2 * ffn)
    sum_shapes = [shape(2, count, rows, width)] * 2
    expert_args = (w_in[0], w_out[0])

    def by_sides(run, arrays, axes):
        if sides == 2:
            return run(arrays, (0, 1))
        size = [value.shape[axis] // 2 for value, axis in zip(arrays, axes)]
        outs = []
        for side in range(2):
            parts = [
                lax.slice_in_dim(value, side * n, (side + 1) * n, axis=axis)
                for value, n, axis in zip(arrays, size, axes)
            ]
            outs.append(run(parts, (side,)))
        return [jnp.concatenate(both, axis=1) for both in zip(*outs)]

    def of_sides(blocks, which):
        return [part for side in which for part in blocks[side]]

    def moe_fwd(blocks, route):
        def run(arrays, which):
            parts = of_sides(blocks, which)
            return call(
                functools.partial(moe_fwd_kernel, experts, cap, rows, n_dp, len(parts)), "moe_fwd",
                (*parts, *arrays, *expert_args), [gu_shape] + sum_shapes,
                [
                    ring_scratch, slot_scratch, result_scratch, gate_scratch, gu_scratch, *weight_scratch, copy_sems, ring_sems,
                ],
                48, COST, [any_space] * len(parts) + [vmem] * 2 + [hbm] * 2, [hbm] + [vmem] * 2,
            )[0]

        gu, keep, send = by_sides(run, route, (0, 0))
        return gu, (keep, send)

    def moe_bwd(blocks, gu, route):
        def run(arrays, which):
            parts = of_sides(blocks, which)
            return call(
                functools.partial(moe_bwd_kernel, experts, cap, rows, n_dp, len(parts)), "moe_bwd",
                (*parts, *arrays, *expert_args), [z_shape, dgu_shape] + sum_shapes,
                [
                    ring_scratch, slot_scratch, result_scratch, gate_scratch, gu_scratch, z_scratch,
                    dgu_scratch,
                    *weight_scratch, copy_sems, ring_sems,
                ],
                50, COST, [any_space] * len(parts) + [vmem] * 2 + [hbm] * 3, [hbm] * 2 + [vmem] * 2,
            )[0]

        z, dgu, keep, send = by_sides(run, (*route, gu), (0, 0, 1))
        return (dgu, z), (keep, send)

    def moe_turn(blocks, grads, route):
        def run(arrays, which):
            parts = of_sides(blocks, which)
            batches = [1 - side for side in which]
            return call(
                functools.partial(
                    moe_turn_kernel, experts, cap, rows, n_dp, len(parts), batches
                ),
                "moe_turn", (me, *parts, grads, *arrays, *expert_args),
                [z_shape, dgu_shape] + sum_shapes,
                [
                    ring_scratch, slot_scratch, slot_scratch, result_scratch, gate_scratch, z_scratch,
                    dgu_scratch,
                    *weight_scratch, copy_sems, ring_sems,
                ],
                57, COST * 2, [smem] + [any_space] * (len(parts) + 1) + [vmem] * 2 + [hbm] * 2,
                [hbm] * 2 + [vmem] * 2,
            )[0]

        z, dgu, keep, send = by_sides(run, route, (0, 0))
        return (dgu, z), (keep, send)

    def moe_out(z, route, *tokens):
        def run(arrays, which):
            return call(
                functools.partial(moe_out_kernel, experts, cap, rows, n_dp), "moe_out",
                (me_after(*tokens), *arrays, w_out[0]), sum_shapes, [result_scratch], 32, COST,
            )[0]

        return by_sides(run, (z, route[0]), (1, 0))

    def moe_wgrad(blocks0, grads0, blocks1, hidden, route, *tokens):
        arrays = [of_sides(blocks, (0, 1)) for blocks in (blocks0, grads0, blocks1)]
        return call(
            functools.partial(moe_wgrad_kernel, experts, cap, n_dp, len(arrays[0])), "moe_wgrad",
            (me_after(*tokens), *arrays[0], *arrays[1], *arrays[2], cot_all, route, *hidden),
            [shape(experts, width, 2 * ffn, dtype=F32), shape(experts, ffn, width, dtype=F32)],
            [
                ring_scratch, pltpu.VMEM((experts, slots, width), BF), pltpu.VMEM((experts, slots, width), BF),
                pltpu.VMEM((experts, slots, 2 * ffn), BF), pltpu.VMEM((experts, slots, ffn), BF),
                pltpu.VMEM((2, width, 2 * ffn), F32), pltpu.VMEM((2, ffn, width), F32),
                pltpu.SemaphoreType.DMA((6,)), ring_sems,
            ],
            48, 10, [smem] + [hbm] * (3 * len(arrays[0]) + 1) + [vmem] + [hbm] * 4, [hbm] * 2,
        )[0]

    gains = jnp.concatenate([attn_gain, moe_gain], axis=0)
    gains = jnp.stack(over_tensor(gains))[t_order].transpose(1, 0, 2).reshape(2, drows)
    gains = jnp.stack([gains] + [move(gains, dp=k) for k in range(1, n_dp)])[dp_order]
    gains = gains.transpose(1, 0, 2).reshape(2, 1, width)
    gains_far = move(gains, section=1)
    layer_gain = [jnp.where(sec == l, gains, gains_far).astype(F32) for l in range(2)]
    (gains0, gains1) = layer_gain

    def seeds_of(matrix):
        low, high = matrix[:half], matrix[half:]
        return jnp.where(first, low, high), move(jnp.where(first, high, low), section=1)

    def gather_weights(seed):
        return lax.all_gather(seed[None, None], ("section", "dp"), axis=0, tiled=True).reshape(
            2, n_dp, half, acols
        )

    kv_own = kv_turn(kv_weight[0])
    kv_core = move(kv_own, tensor=1)
    key_value = jnp.where(
        core0, jnp.concatenate([kv_own, kv_core], axis=1), jnp.concatenate([kv_core, kv_own], axis=1)
    )
    routing = jnp.concatenate([expert_ids[0].astype(F32), gate_values[0]], axis=2)
    routing = [routing] + [move(routing, dp=k) for k in range(1, n_dp)]
    seed_near, seed_far = seeds_of(
        jnp.concatenate([query_weight[0], key_value, out_weight[0].T], axis=1)
    )

    segment = jnp.where(first, segments[0], segments[1])
    ordinal = jnp.arange(seq, dtype=jnp.int32)
    start = jnp.sum((segment[None, :] < segment[:, None]).astype(jnp.int32), axis=1)
    places = (ordinal - start).astype(F32)

    def turned(vector):
        return vector.reshape(n_t, rows)[t_order].reshape(seq)

    start_col = turned(start)[:, None]
    frequency = THETA ** (-2.0 * jnp.arange(HD // 2, dtype=F32) / HD)
    angles = turned(places)[:, None] * frequency[None, :]
    cosine = jnp.cos(angles)
    cosine = jnp.concatenate([cosine, cosine], axis=1)
    sine = jnp.sin(angles)
    sine = jnp.concatenate([-sine, sine], axis=1)
    table = jnp.concatenate([cosine, sine, jnp.pad(start_col.astype(F32), ((0, 0), (0, HD - 1)))], axis=1)

    def routes_of(routing):
        routing = jnp.stack(routing)
        routing = routing.reshape(n_dp, 2, n_t, rows, 2 * top)[:, :, t_order]
        routing = routing.reshape(n_dp, 2, seq, 2 * top)
        names = (dp * experts + jnp.arange(experts, dtype=jnp.int32)).astype(F32)
        chosen = routing[:, :, :, :top, None] == names
        member = jnp.sum(chosen.astype(F32), axis=3)
        gates = jnp.sum(jnp.where(chosen, routing[:, :, :, top:, None], 0.0), axis=3)
        lower = (ordinal[:, None] > ordinal[None, :]).astype(BF)
        rank = jnp.einsum("ij,smje->smei", lower, member.astype(BF), preferred_element_type=F32)
        slot = jnp.where(member.transpose(0, 1, 3, 2) > 0.5, rank, -1.0).astype(jnp.int32)
        gate_high = gates.astype(BF)
        gate_low = (gates - gate_high.astype(F32)).astype(BF)
        gate_cols = jnp.concatenate([gate_high, gate_low], axis=3)
        gate_cols = jnp.pad(gate_cols, ((0, 0), (0, 0), (0, 0), (0, HD - 2 * experts)))
        return [
            tuple(jnp.concatenate([part[:, b], part[:, 1 - b]]) for part in (slot, gate_cols))
            for b in range(2)
        ]

    def spread(value):
        near, far = [value, move(value, tensor=2)], [move(value, section=1), move(value, section=1, tensor=2)]
        return [[part[0], move(part[0], tensor=1), part[1], move(part[1], tensor=1)] for part in (near, far)]

    def to_host(own, *tokens):
        near_own, far_own = spread(own)
        others = jnp.stack([move(own, dp=k) for k in range(1, n_dp)])
        near, far = spread(after(others, near_own[2], far_own[0], far_own[2], *tokens))
        return near_own + near, far_own + far

    def core_sums(keep, send, *tokens):
        got = move(send, tensor=1)
        sums = [
            [keep[y, at : at + n_dp] + got[y, at : at + n_dp] for y in range(2)] for at in (0, n_dp)
        ]
        if tokens:
            sums[1][1] = after(sums[1][1], *tokens)
        return sums

    def gather_sums(near, far, host, *tokens):
        near = near[0] + move(near[1], tensor=2)
        far = move(far[0], section=1) + move(far[1], section=1, tensor=2)
        total = jnp.where(sec == host, near, far)
        return after(total, *tokens) if tokens else total

    def parts_of(near, far, which):
        return [[part[which] for part in side] for side in (near, far)]

    def others_sums(near, far, host, *tokens):
        return gather_sums(*parts_of(near, far, slice(1, None)), host, *tokens)

    def all_sums(near, far, others, host, *tokens):
        total = gather_sums(*parts_of(near, far, 0), host).astype(F32)
        for k in range(1, n_dp):
            total = total + move(others[k - 1], dp=k).astype(F32)
        return [(after(total, *tokens) if tokens else total, None)]

    def from_host(near, far, host):
        return all_sums(near, far, others_sums(near, far, host), host)

    x0 = jnp.where(first, block_input[0], block_input[1])
    seed = jnp.where(first & there(*routing[1:]), seed_near, seed_far)
    weights0 = gather_weights(seed)
    _, a, _ = finish(x0, gains0[0], [])

    routes = routes_of(routing)
    a_blocks = over_tensor(a)
    keep, send, saved, a_all = attn_fwd(
        a_blocks, weights0, routes[0]
    )
    part0, part1 = sum_over_tensor(keep, send)
    mid, m, _ = finish(x0, gains0[1], [(part0, None), (part1, None)])
    kept0 = (x0, a_all, saved, mid, weights0)
    cot_far = move(jnp.where(first, cotangent[0, 1], cotangent[0, 0]), section=1)
    cot_near = jnp.where(first, cotangent[0, 0], cotangent[0, 1])
    cots = jnp.stack([jnp.where(first, cot_near, cot_far), jnp.where(first, cot_far, cot_near)])
    near, far = to_host(m, cots[0])
    there_now = [part.reshape(-1, width)[:half, :acols] for part in (near[6], far[4], far[6])]
    weights1 = gather_weights(after(jnp.where(first, seed_far, seed_near), *there_now))
    cot_all = after(cotangent[0].astype(BF), *[part[:1] for part in (near[6], far[4], far[6])])
    cot_all = lax.all_gather(cot_all[None], ("dp", "tensor"), axis=0, tiled=True)
    blocks0 = (near, far)
    gu0, sums = moe_fwd(blocks0, routes[0])
    terms = from_host(*core_sums(*sums), 0)
    out0, a, _ = finish(mid, gains1[0], terms)

    a_blocks = over_tensor(a)
    keep, send, saved, a_all = attn_fwd(a_blocks, weights1)
    part0, part1 = sum_over_tensor(keep, send)
    mid, m, _ = finish(out0, gains1[1], [(part0, None), (part1, None)])
    kept1 = (out0, a_all, saved, mid, weights1)
    near, far = to_host(m)
    blocks1 = (near, far)
    hidden1, sums = moe_turn(blocks1, cot_all, routes[1])
    terms = from_host(*core_sums(*sums), 1)

    cot_far = move(jnp.where(first, cotangent[0, 1], cotangent[0, 0]), section=1)
    cot_near = jnp.where(first, cotangent[0, 0], cotangent[0, 1])
    cots = (jnp.where(first, cot_near, cot_far), jnp.where(first, cot_far, cot_near))

    def attention_back(kept, l, g, terms, more, beside=None):
        x, a_all, saved, mid, weights = kept
        (dmid, d, moe_gain_sum), _ = norm_back(mid, layer_gain[l][1], g, terms)
        d_blocks = over_tensor(d)
        extra = core_sums(*beside(d)) if beside is not None else None
        if extra is not None:
            d_blocks[3] = after(d_blocks[3], extra[1][0][0])
        keep, send, dq, kv_send, d_all = attn_bwd(d_blocks, saved, weights)
        args = (a_all, d_all, saved, dq, move(kv_send, tensor=1))
        mine, theirs = halves_grad(
            functools.partial(attn_wgrad_kernel, l == 0), "attn_wgrad", args, 2 * qcols + HD
        )
        part0, part1 = sum_over_tensor(keep, send)
        (*outs, attn_gain_sum), _ = norm_back(
            x, layer_gain[l][0], dmid, [(part0, None), (part1, None)], more
        )
        return outs, jnp.concatenate([attn_gain_sum, moe_gain_sum]), mine, theirs, extra

    (in_grad1, g, g_low), gain_sums1, mine, theirs, outs = attention_back(
        kept1, 1, cots[1], terms, (cots[0],), lambda d: moe_out(hidden1[1], routes[1], d)
    )
    out_near, out_far = (jnp.stack(side) for side in outs)
    out_far = move(out_far, section=1)
    grad1 = jnp.where(first, jnp.stack([mine, theirs]), jnp.stack([theirs, mine]))
    near, far = to_host(g_low, grad1[0, 0, :1, :1], out_far[0, :1])
    shard1_sum = lax.psum_scatter(
        grad1.reshape(2 * n_dp, half, acols - HD), ("section", "dp"), scatter_dimension=0, tiled=True
    )
    grads0 = (near, far)
    hidden0, sums = moe_bwd(grads0, gu0, routes[0])
    near_far = core_sums(*sums, shard1_sum[0, :1, :1])
    route = jnp.where(first, routes[0][0], routes[1][0])
    dw_in, dw_out = moe_wgrad(
        blocks0, grads0, blocks1, (*hidden0, *hidden1), route, near_far[1][1]
    )
    others = others_sums(*near_far, 0, dw_out[0, :rows])
    out1 = after(jnp.where(first, out_far, out_near), others[:1])
    out_across = move(out1[1], tensor=2)
    terms = all_sums(*near_far, others, 0, out_across[0])
    out1_sum = lax.psum_scatter(out1[0] + out_across, "dp", scatter_dimension=0, tiled=True)
    (in_grad0, _), gain_sums0, mine, theirs, _ = attention_back(kept0, 0, g, terms, ())

    gain_sums = jnp.concatenate([gain_sums0, gain_sums1])
    gain_sums = gain_sums + move(gain_sums, tensor=1)
    gain_sums = gain_sums + move(gain_sums, tensor=2)
    gain_sums = gain_sums.astype(BF).reshape(4, n_dp, drows).transpose(1, 0, 2)[dp_order]
    gain_sums = jnp.pad(gain_sums, ((0, 0), (0, 12), (0, 2 * qcols + HD - drows)))
    parts = jnp.concatenate([mine + move(theirs, section=1), gain_sums], axis=1)
    parts = [parts[0]] + [move(parts[k], dp=k) for k in range(1, n_dp)]
    out1 = mid + out1_sum[0].astype(F32)
    shard1 = shard1_sum[0].astype(F32)
    shard0 = sum(part.astype(F32) for part in parts)

    gain0, gain1 = shard0[half : half + 2], shard0[half + 2 : half + 4]
    own = jnp.where(first, shard0[:half], shard1)
    own_gain = jnp.where(first, gain0, gain1)[:, :drows]
    far = jnp.concatenate([
        jnp.where(first, shard1, shard0[:half]),
        jnp.pad(jnp.where(first, gain1, gain0), ((0, 14), (0, 0))),
    ])
    far = move(far.astype(BF), section=1).astype(F32)
    grad_shard = jnp.where(
        first, jnp.concatenate([own, far[:half]]), jnp.concatenate([far[:half], own])
    )
    gains = own_gain + far[half : half + 2, :drows]
    gains = lax.dynamic_slice_in_dim(gains, t * attn_gain.shape[1], attn_gain.shape[1], 1)
    cols = qcols + HD
    grad_out = grad_shard[:, cols:].T
    grad_kv = kv_turn(grad_shard[:, qcols:cols])
    def mine_and_theirs(value0, value1):
        return jnp.where(first, value0, value1), jnp.where(first, value1, value0)

    out_near, out_far = mine_and_theirs(out0, out1)
    grad_near, grad_far = mine_and_theirs(in_grad0, in_grad1)
    theirs = move(jnp.stack([out_far, grad_far]).astype(BF), section=1).astype(F32)

    def both_batches(near, far):
        return jnp.where(first, jnp.stack([near, far]), jnp.stack([far, near]))[None]

    return (
        both_batches(out_near, theirs[0]),
        both_batches(grad_near, theirs[1]),
        gains[0:1],
        grad_shard[None, :, :qcols],
        grad_kv[None],
        grad_out[None],
        gains[1:2],
        dw_in[None],
        dw_out[None],
    )


def solution(mesh):
    return jax.shard_map(
        per_device,
        mesh=mesh,
        in_specs=(
            P(None, ("dp", "tensor"), None),
            P(None, "dp"),
            P("section", None, "dp", None),
            P("section", None, "dp", None),
            P("section", None, ("dp", "tensor"), None),
            P("section", ("dp", "tensor")),
            P("section", "dp", "tensor"),
            P("section", "dp", "tensor"),
            P("section", "tensor", "dp"),
            P("section", ("dp", "tensor")),
            P("section", "dp", None, "tensor"),
            P("section", "dp", "tensor", None),
        ),
        out_specs=(
            P("section", None, ("dp", "tensor"), None),
            P("section", None, ("dp", "tensor"), None),
            P("section", ("dp", "tensor")),
            P("section", "dp", "tensor"),
            P("section", "dp", "tensor"),
            P("section", "tensor", "dp"),
            P("section", ("dp", "tensor")),
            P("section", "dp", None, "tensor"),
            P("section", "dp", "tensor", None),
        ),
        check_vma=False,
    )
```

time: 840 us -> 807 us (0.961)
  waiting for transfers between devices: 442 us -> 396 us
  starting transfers between devices: 146 us -> 162 us
    ppermute x103 -> x127, waiting for transfers between devices: 403 us -> 347 us  [move(): return lax.ppermute(value, ('section', 'dp', 'tensor'), pairs)]
    pallas_call x22 -> x19, Pallas kernels: 123 us -> 141 us  [call(): pl.pallas_call(body, out_shape=list(outs) + [jax.ShapeDtypeStruct(h.shape...]
    ppermute x103 -> x127, starting transfers between devices: 135 us -> 151 us  [move(): return lax.ppermute(value, ('section', 'dp', 'tensor'), pairs)]
    pallas_call x1 -> x0, Pallas kernels: 16.1 us -> none  [moe_wgrad(): pl.pallas_call(moe_wgrad_kernel, grid_spec=pltpu.PrefetchScalarGridSpec(n...]
    reduce_scatter x1, waiting for transfers between devices: 0.01 us -> 9.67 us  [per_device(): lax.psum_scatter(out1[0] + out_across, 'dp', scatter_dimension=0, tiled=T...]
    unnamed x235 -> x257, local copies, waits for them, and re-layouts: 26.1 us -> 24.1 us
  transfers between devices with their start and end apart: 110 -> 134, of which waited for: 64 -> 81; matrix products, arithmetic and copies ran while one was open for 5% -> 4% of each run, Pallas kernels for 12% -> 12%
where the time goes in v3:
time: 807 us; the launch traced here: 796 us
  waiting for transfers between devices  396 us (49%)
  starting transfers between devices  162 us (20%)
  Pallas kernels  141 us (17%)
  other arithmetic  36.3 us (4%)
  local copies, waits for them, and re-layouts  35.9 us (4%)
  between operations  23.9 us (3%)
    ppermute x127, waiting for transfers between devices, move(): return lax.ppermute(value, ('section', 'dp', 'tensor'), pairs)  347 us
    ppermute x127, starting transfers between devices, move(): return lax.ppermute(value, ('section', 'dp', 'tensor'), pairs)  151 us
    pallas_call x19, Pallas kernels, call(): pl.pallas_call(body, out_shape=list(outs) + [jax.ShapeDtypeStruct(h.shape...  141 us
    all_gather x2, waiting for transfers between devices, gather_weights(): lax.all_gather(seed[None, None], ('section', 'dp'), axis=0, tiled=True)  34.2 us
    unnamed x257, local copies, waits for them, and re-layouts  24.1 us
  transfers between devices with their start and end apart: 134, of which 81 were waited for; matrix products, arithmetic and copies ran while one was open for 4% of the time, Pallas kernels for 12%

profile of v3, /device:TPU:9, one launch (start us, length us, event | category | flops | bytes accessed | tf_op | source)
XLA Modules:
  0.0 796.2 jit_solution(5648027690177313269)
XLA Ops:
  54.7 34.2 %all-gather.8.cloned.1.call-done = bf16[1536,1024]{1,0:T(8,128)(2,1)} async-done(((bf16[192,1024]{1,0:T(8,128)(2,1)}), bf16[1536,1024]{1,0:T(8,128)(2,1)}) %all-gather.8.cloned.1.call-update) | async-done | bytes 3145744 | tf_op jit(solution)/shard_map/all_gather | solution.py:680
  90.8 4.1 attn_fwd.2
  100.0 4.5 collective-permute-done.17.refs_3_
  114.3 3.9 collective-permute-done.21.refs_8_.refs_9_
  127.4 11.7 %collective-permute-done.34.refs_14_.refs_15_ = bf16[3,64,1536]{2,1,0:T(8,128)(2,1)S(1)} collective-permute-done((bf16[3,64,1536]{2,1,0:T(8,128)(2,1)S(1)}, bf16[3,64,1536]{2,1,0:T(8,128)(2,1)S(1)}, u32[]{:S(2)}, u32[]{:S(2)}) %collective-permute-start.34) | collective-permute-done | bytes 589856 | tf_op jit(solution)/shard_map/ppermute | solution.py:37
  139.1 12.8 %collective-permute-done.32.refs_12_.refs_13_ = bf16[3,64,1536]{2,1,0:T(8,128)(2,1)S(1)} collective-permute-done((bf16[3,64,1536]{2,1,0:T(8,128)(2,1)S(1)}, bf16[3,64,1536]{2,1,0:T(8,128)(2,1)S(1)}, u32[]{:S(2)}, u32[]{:S(2)}) %collective-permute-start.32) | collective-permute-done | bytes 589856 | tf_op jit(solution)/shard_map/ppermute | solution.py:37
  164.6 25.6 %moe_fwd.1 = (f32[4,640,384]{2,1,0:T(8,128)}, bf16[2,8,64,1536]{3,2,1,0:T(8,128)(2,1)}, bf16[2,8,64,1536]{3,2,1,0:T(8,128)(2,1)}) custom-call(bf16[64,1536]{1,0:T(8,128)(2,1)S(1)} %copy-done.68, bf16[64,1536]{1,0:T(8,128)(2,1)S(1)} %collective-permute-done.18.refs_1_.refs_2_, bf16[64,1536]{1,0:T(8,128)(2,1)S(1)} %collective-permute-done.19.refs_2_.refs_3_, ...), custom_call_target="tpu_custom_call" | custom-call | flops 4000000000 | bytes 12582912 | tf_op jit(solution)/shard_map/moe_fwd/pallas_call | solution.py:497
  203.9 10.4 %collective-permute-done.40 = bf16[3,64,1536]{2,1,0:T(8,128)(2,1)S(1)} collective-permute-done((bf16[3,64,1536]{2,1,0:T(8,128)(2,1)S(1)}, bf16[3,64,1536]{2,1,0:T(8,128)(2,1)S(1)}, u32[]{:S(2)}, u32[]{:S(2)}) %collective-permute-start.40) | collective-permute-done | bytes 589856 | tf_op jit(solution)/shard_map/ppermute | solution.py:37
  217.8 13.6 %collective-permute-done.42 = bf16[3,64,1536]{2,1,0:T(8,128)(2,1)S(1)} collective-permute-done((bf16[3,64,1536]{2,1,0:T(8,128)(2,1)S(1)}, bf16[3,64,1536]{2,1,0:T(8,128)(2,1)S(1)}, u32[]{:S(2)}, u32[]{:S(2)}) %collective-permute-start.42) | collective-permute-done | bytes 589856 | tf_op jit(solution)/shard_map/ppermute | solution.py:37
  235.2 4.7 collective-permute-done.39
  239.9 5.3 collective-permute-done.43
  245.2 7.3 collective-permute-done.45
  252.5 6.7 collective-permute-done.44
  269.9 4.6 attn_fwd.3
  277.2 10.2 %collective-permute-done.50.refs_3_ = bf16[64,1536]{1,0:T(8,128)(2,1)S(1)} collective-permute-done((bf16[64,1536]{1,0:T(8,128)(2,1)S(1)}, bf16[64,1536]{1,0:T(8,128)(2,1)S(1)}, u32[]{:S(2)}, u32[]{:S(2)}) %collective-permute-start.50) | collective-permute-done | bytes 196640 | tf_op jit(solution)/shard_map/ppermute | solution.py:37
  291.3 3.8 collective-permute-start.57
  299.9 11.1 %collective-permute-done.58 = bf16[64,1536]{1,0:T(8,128)(2,1)S(1)} collective-permute-done((bf16[64,1536]{1,0:T(8,128)(2,1)S(1)}, bf16[64,1536]{1,0:T(8,128)(2,1)S(1)}, u32[]{:S(2)}, u32[]{:S(2)}) %collective-permute-start.58) | collective-permute-done | bytes 196640 | tf_op jit(solution)/shard_map/ppermute | solution.py:37
  318.2 9.4 %collective-permute-done.66.refs_15_.refs_47_ = bf16[3,64,1536]{2,1,0:T(8,128)(2,1)S(1)} collective-permute-done((bf16[3,64,1536]{2,1,0:T(8,128)(2,1)S(1)}, bf16[3,64,1536]{2,1,0:T(8,128)(2,1)S(1)}, u32[]{:S(2)}, u32[]{:S(2)}) %collective-permute-start.66) | collective-permute-done | bytes 589856 | tf_op jit(solution)/shard_map/ppermute | solution.py:37
  330.4 9.2 %collective-permute-done.64.refs_13_.refs_45_ = bf16[3,64,1536]{2,1,0:T(8,128)(2,1)S(1)} collective-permute-done((bf16[3,64,1536]{2,1,0:T(8,128)(2,1)S(1)}, bf16[3,64,1536]{2,1,0:T(8,128)(2,1)S(1)}, u32[]{:S(2)}, u32[]{:S(2)}) %collective-permute-start.64) | collective-permute-done | bytes 589856 | tf_op jit(solution)/shard_map/ppermute | solution.py:37
  347.6 31.7 %moe_turn.1 = (bf16[4,640,192]{2,1,0:T(8,128)(2,1)}, bf16[4,640,384]{2,1,0:T(8,128)(2,1)}, bf16[2,8,64,1536]{3,2,1,0:T(8,128)(2,1)}, bf16[2,8,64,1536]{3,2,1,0:T(8,128)(2,1)}) custom-call(s32[4]{0:T(128)} %copy-done.53, bf16[64,1536]{1,0:T(8,128)(2,1)} %copy-done.78, bf16[64,1536]{1,0:T(8,128)(2,1)} %copy-done.80, bf16[64,1536]{1,0:T(8,128)(2,1)} %copy-done.43, ...), custom_call_target="tpu_custom_call" | custom-call | flops 8000000000 | bytes 25165824 | tf_op jit(solution)/shard_map/moe_turn/pallas_call | solution.py:497
  379.6 5.7 collective-permute-done.68
  392.8 9.8 %collective-permute-done.72 = bf16[3,64,1536]{2,1,0:T(8,128)(2,1)S(1)} collective-permute-done((bf16[3,64,1536]{2,1,0:T(8,128)(2,1)S(1)}, bf16[3,64,1536]{2,1,0:T(8,128)(2,1)S(1)}, u32[]{:S(2)}, u32[]{:S(2)}) %collective-permute-start.72) | collective-permute-done | bytes 589856 | tf_op jit(solution)/shard_map/ppermute | solution.py:37
  403.9 12.2 %collective-permute-done.74 = bf16[3,64,1536]{2,1,0:T(8,128)(2,1)S(1)} collective-permute-done((bf16[3,64,1536]{2,1,0:T(8,128)(2,1)S(1)}, bf16[3,64,1536]{2,1,0:T(8,128)(2,1)S(1)}, u32[]{:S(2)}, u32[]{:S(2)}) %collective-permute-start.74) | collective-permute-done | bytes 589856 | tf_op jit(solution)/shard_map/ppermute | solution.py:37
  416.3 3.8 collective-permute-start.75
  426.8 8.6 %collective-permute-done.76 = bf16[64,1536]{1,0:T(8,128)(2,1)S(1)} collective-permute-done((bf16[64,1536]{1,0:T(8,128)(2,1)S(1)}, bf16[64,1536]{1,0:T(8,128)(2,1)S(1)}, u32[]{:S(2)}, u32[]{:S(2)}) %collective-permute-start.76) | collective-permute-done | bytes 196640 | tf_op jit(solution)/shard_map/ppermute | solution.py:37
  437.7 6.0 moe_out.1
  447.3 5.5 collective-permute-done.79.refs_4_
  457.8 5.1 attn_bwd.2
  481.1 19.9 %collective-permute-done.89.refs_10_.refs_27_ = bf16[64,1536]{1,0:T(8,128)(2,1)S(1)} collective-permute-done((bf16[64,1536]{1,0:T(8,128)(2,1)}, bf16[64,1536]{1,0:T(8,128)(2,1)S(1)}, u32[]{:S(2)}, u32[]{:S(2)}) %collective-permute-start.89) | collective-permute-done | bytes 196640 | tf_op jit(solution)/shard_map/ppermute | solution.py:37
  504.9 5.0 collective-permute-start.91
  511.2 9.3 %collective-permute-done.92 = bf16[64,1536]{1,0:T(8,128)(2,1)S(1)} collective-permute-done((bf16[64,1536]{1,0:T(8,128)(2,1)}, bf16[64,1536]{1,0:T(8,128)(2,1)S(1)}, u32[]{:S(2)}, u32[]{:S(2)}) %collective-permute-start.92) | collective-permute-done | bytes 196640 | tf_op jit(solution)/shard_map/ppermute | solution.py:37
  526.0 5.1 collective-permute-start.85
  532.7 11.4 %collective-permute-done.101.refs_14_.refs_31_ = bf16[3,64,1536]{2,1,0:T(8,128)(2,1)S(1)} collective-permute-done((bf16[3,64,1536]{2,1,0:T(8,128)(2,1)S(1)}, bf16[3,64,1536]{2,1,0:T(8,128)(2,1)S(1)}, u32[]{:S(2)}, u32[]{:S(2)}) %collective-permute-start.101) | collective-permute-done | bytes 589856 | tf_op jit(solution)/shard_map/ppermute | solution.py:37
  544.1 4.5 collective-permute-start.102
  548.7 5.7 collective-permute-done.99.refs_12_.refs_29_
  566.1 27.7 %moe_bwd.1 = (bf16[4,640,192]{2,1,0:T(8,128)(2,1)}, bf16[4,640,384]{2,1,0:T(8,128)(2,1)}, bf16[2,8,64,1536]{3,2,1,0:T(8,128)(2,1)}, bf16[2,8,64,1536]{3,2,1,0:T(8,128)(2,1)}) custom-call(bf16[64,1536]{1,0:T(8,128)(2,1)} %get-tuple-element.94.refs_0_.refs_17_, bf16[64,1536]{1,0:T(8,128)(2,1)S(1)} %collective-permute-done.85.refs_1_.refs_18_, ...), custom_call_target="tpu_custom_call" | custom-call | flops 4000000000 | bytes 12582912 | tf_op jit(solution)/shard_map/moe_bwd/pallas_call | solution.py:497
  609.9 22.3 %moe_wgrad.1 = (f32[4,1536,384]{2,1,0:T(8,128)}, f32[4,192,1536]{2,1,0:T(8,128)}) custom-call(s32[4]{0:T(128)S(1)} %broadcast_select_fusion.7.refs_0_, bf16[64,1536]{1,0:T(8,128)(2,1)S(1)} %copy-done.69, bf16[64,1536]{1,0:T(8,128)(2,1)S(1)} %copy-done.71, bf16[64,1536]{1,0:T(8,128)(2,1)S(1)} %copy-done.50, bf16[64,1536]{1,0:T(8,128)(2,1)S(1)} %copy-done.77, ...), custom_call_target="tpu_custom_call" | custom-call | flops 10000000000 | bytes 31457280 | tf_op jit(solution)/shard_map/moe_wgrad/pallas_call | solution.py:497
  643.3 5.5 collective-permute-start.111
  648.8 16.8 %collective-permute-done.108 = bf16[64,1536]{1,0:T(8,128)(2,1)S(1)} collective-permute-done((bf16[64,1536]{1,0:T(8,128)(2,1)S(1)}, bf16[64,1536]{1,0:T(8,128)(2,1)S(1)}, u32[]{:S(2)}, u32[]{:S(2)}) %collective-permute-start.108) | collective-permute-done | bytes 196640 | tf_op jit(solution)/shard_map/ppermute | solution.py:37
  668.6 3.8 collective-permute-done.112
  675.0 5.8 collective-permute-start.114
  680.8 4.4 collective-permute-start.116
  686.3 5.2 attn_bwd.3
  710.1 9.7 %reduce-scatter.5.cloned.1.call-done = bf16[1,64,1536]{2,1,0:T(8,128)(2,1)} async-done(((bf16[4,64,1536]{2,1,0:T(8,128)(2,1)}), bf16[1,64,1536]{2,1,0:T(8,128)(2,1)}) %reduce-scatter.5.cloned.1.call-update) | async-done | bytes 196624 | tf_op jit(solution)/shard_map/reduce_scatter | solution.py:851
  722.1 12.8 %collective-permute-done.121 = bf16[4,192,896]{2,1,0:T(8,128)(2,1)} collective-permute-done((bf16[4,192,896]{2,1,0:T(8,128)(2,1)}, bf16[4,192,896]{2,1,0:T(8,128)(2,1)}, u32[]{:S(2)}, u32[]{:S(2)}) %collective-permute-start.121) | collective-permute-done | bytes 1376288 | tf_op jit(solution)/shard_map/ppermute | solution.py:37
  746.5 22.8 %collective-permute-done.125 = bf16[208,896]{1,0:T(8,128)(2,1)S(1)} collective-permute-done((bf16[208,896]{1,0:T(8,128)(2,1)S(1)}, bf16[208,896]{1,0:T(8,128)(2,1)S(1)}, u32[]{:S(2)}, u32[]{:S(2)}) %collective-permute-start.125) | collective-permute-done | bytes 372768 | tf_op jit(solution)/shard_map/ppermute | solution.py:37
  770.7 5.4 collective-permute-done.127
  778.2 7.3 collective-permute-start.128
  (659 shorter events, 280.3 us)
Async XLA Ops:
  7.2 81.7 %all-gather.8.cloned.1.call-start = ((), (), s32[]{:S(2)}) async-start(), calls=%async_computation.5 | async-start | bytes 3538944 | tf_op jit(solution)/shard_map/all_gather | solution.py:680
  27.2 240.8 %all-gather.10.cloned.1.call-start = ((), (), s32[]{:S(2)}) async-start(), calls=%async_computation.6 | async-start | bytes 3538944 | tf_op jit(solution)/shard_map/all_gather | solution.py:680
  125.9 25.9 %collective-permute-start.32 = (bf16[3,64,1536]{2,1,0:T(8,128)(2,1)S(1)}, bf16[3,64,1536]{2,1,0:T(8,128)(2,1)S(1)}, u32[]{:S(2)}, u32[]{:S(2)}) collective-permute-start(bf16[3,64,1536]{2,1,0:T(8,128)(2,1)S(1)} %maximum_select_fusion.5.refs_4_.refs_5_), channel_id=1, source_target_pairs={{0,16},{1,17},{2,18},{3,19},{4,20},{5,21},{6,22},{7,23},{8,24},{9,... | collective-permute-start | bytes 1769480 | tf_op jit(solution)/shard_map/ppermute | solution.py:37
  127.1 26.5 %collective-permute-start.28 = (bf16[3,64,1536]{2,1,0:T(8,128)(2,1)S(1)}, bf16[3,64,1536]{2,1,0:T(8,128)(2,1)}, u32[]{:S(2)}, u32[]{:S(2)}) collective-permute-start(bf16[3,64,1536]{2,1,0:T(8,128)(2,1)S(1)} %maximum_select_fusion.5.refs_4_.refs_5_), channel_id=1, source_target_pairs={{0,2},{1,3},{2,0},{3,1},{4,6},{5,7},{6,4},{7,5},{8,10},{9,11},{10,... | collective-permute-start | bytes 1769480 | tf_op jit(solution)/shard_map/ppermute | solution.py:37
  155.8 191.7 %all-gather.6.cloned.1.call-start = ((), (), s32[]{:S(2)}) async-start(), calls=%async_computation.2 | async-start | bytes 6684672 | tf_op jit(solution)/shard_map/all_gather | solution.py:792
  192.7 401.6 %reduce-scatter.3.cloned.1.call-start = ((), (), s32[]{:S(2)}) async-start(), calls=%async_computation.3 | async-start | bytes 3096576 | tf_op jit(solution)/shard_map/reduce_scatter | solution.py:837
  201.1 30.3 %collective-permute-start.42 = (bf16[3,64,1536]{2,1,0:T(8,128)(2,1)S(1)}, bf16[3,64,1536]{2,1,0:T(8,128)(2,1)S(1)}, u32[]{:S(2)}, u32[]{:S(2)}) collective-permute-start(bf16[3,64,1536]{2,1,0:T(8,128)(2,1)S(1)} %slice_bitcast_fusion.12), channel_id=1, source_target_pairs={{0,18},{1,19},{2,16},{3,17},{4,22},{5,23},{6,20},{7,21},{8,26},{9,... | collective-permute-start | bytes 1769480 | tf_op jit(solution)/shard_map/ppermute | solution.py:37
  202.5 31.6 %collective-permute-start.37 = (bf16[64,1536]{1,0:T(8,128)(2,1)S(1)}, bf16[64,1536]{1,0:T(8,128)(2,1)S(1)}, u32[]{:S(2)}, u32[]{:S(2)}) collective-permute-start(bf16[64,1536]{1,0:T(8,128)(2,1)S(1)} %slice_bitcast_fusion.46), channel_id=1, source_target_pairs={{0,2},{1,3},{2,0},{3,1},{4,6},{5,7},{6,4},{7,5},{8,10},{9,11},{10,... | collective-permute-start | bytes 589832 | tf_op jit(solution)/shard_map/ppermute | solution.py:37
  203.6 31.6 %collective-permute-start.38 = (bf16[64,1536]{1,0:T(8,128)(2,1)S(1)}, bf16[64,1536]{1,0:T(8,128)(2,1)S(1)}, u32[]{:S(2)}, u32[]{:S(2)}) collective-permute-start(bf16[64,1536]{1,0:T(8,128)(2,1)S(1)} %slice_bitcast_fusion.45), channel_id=1, source_target_pairs={{0,16},{1,17},{2,18},{3,19},{4,20},{5,21},{6,22},{7,23},{8,24},{9,... | collective-permute-start | bytes 589832 | tf_op jit(solution)/shard_map/ppermute | solution.py:37
  214.3 25.5 %collective-permute-start.39 = (bf16[64,1536]{1,0:T(8,128)(2,1)S(1)}, bf16[64,1536]{1,0:T(8,128)(2,1)S(1)}, u32[]{:S(2)}, u32[]{:S(2)}) collective-permute-start(bf16[64,1536]{1,0:T(8,128)(2,1)S(1)} %slice_bitcast_fusion.44), channel_id=1, source_target_pairs={{0,18},{1,19},{2,16},{3,17},{4,22},{5,23},{6,20},{7,21},{8,26},{9,... | collective-permute-start | bytes 589832 | tf_op jit(solution)/shard_map/ppermute | solution.py:37
  231.7 20.7 %collective-permute-start.45 = (bf16[64,1536]{1,0:T(8,128)(2,1)S(1)}, bf16[64,1536]{1,0:T(8,128)(2,1)S(1)}, u32[]{:S(2)}, u32[]{:S(2)}) collective-permute-start(bf16[64,1536]{1,0:T(8,128)(2,1)S(1)} %get-tuple-element.213), channel_id=1, source_target_pairs={{0,12},{1,13},{2,14},{3,15},{4,8},{5,9},{6,10},{7,11},{8,4},{9,5},... | collective-permute-start | bytes 589832 | tf_op jit(solution)/shard_map/ppermute | solution.py:37
  234.2 25.0 %collective-permute-start.44 = (bf16[64,1536]{1,0:T(8,128)(2,1)S(1)}, bf16[64,1536]{1,0:T(8,128)(2,1)S(1)}, u32[]{:S(2)}, u32[]{:S(2)}) collective-permute-start(bf16[64,1536]{1,0:T(8,128)(2,1)S(1)} %get-tuple-element.214), channel_id=1, source_target_pairs={{0,8},{1,9},{2,10},{3,11},{4,12},{5,13},{6,14},{7,15},{8,0},{9,1},... | collective-permute-start | bytes 589832 | tf_op jit(solution)/shard_map/ppermute | solution.py:37
  290.4 20.7 %collective-permute-start.58 = (bf16[64,1536]{1,0:T(8,128)(2,1)S(1)}, bf16[64,1536]{1,0:T(8,128)(2,1)S(1)}, u32[]{:S(2)}, u32[]{:S(2)}) collective-permute-start(bf16[64,1536]{1,0:T(8,128)(2,1)S(1)} %get-tuple-element.78.refs_1_.refs_33_), channel_id=1, source_target_pairs={{0,12},{1,13},{2,14},{3,15},{4,8},{5,9},{6,10},{7,11},{8,4},{9,5},... | collective-permute-start | bytes 589832 | tf_op jit(solution)/shard_map/ppermute | solution.py:37
  291.3 21.0 %collective-permute-start.57 = (bf16[64,1536]{1,0:T(8,128)(2,1)S(1)}, bf16[64,1536]{1,0:T(8,128)(2,1)S(1)}, u32[]{:S(2)}, u32[]{:S(2)}) collective-permute-start(bf16[64,1536]{1,0:T(8,128)(2,1)S(1)} %get-tuple-element.78.refs_1_.refs_33_), channel_id=1, source_target_pairs={{0,8},{1,9},{2,10},{3,11},{4,12},{5,13},{6,14},{7,15},{8,0},{9,1},... | collective-permute-start | bytes 589832 | tf_op jit(solution)/shard_map/ppermute | solution.py:37
  314.1 25.5 %collective-permute-start.64 = (bf16[3,64,1536]{2,1,0:T(8,128)(2,1)S(1)}, bf16[3,64,1536]{2,1,0:T(8,128)(2,1)S(1)}, u32[]{:S(2)}, u32[]{:S(2)}) collective-permute-start(bf16[3,64,1536]{2,1,0:T(8,128)(2,1)S(1)} %maximum_select_fusion.6.refs_5_.refs_37_), channel_id=1, source_target_pairs={{0,16},{1,17},{2,18},{3,19},{4,20},{5,21},{6,22},{7,23},{8,24},{9,... | collective-permute-start | bytes 1769480 | tf_op jit(solution)/shard_map/ppermute | solution.py:37
  314.2 27.0 %collective-permute-start.60 = (bf16[3,64,1536]{2,1,0:T(8,128)(2,1)S(1)}, bf16[3,64,1536]{2,1,0:T(8,128)(2,1)S(1)}, u32[]{:S(2)}, u32[]{:S(2)}) collective-permute-start(bf16[3,64,1536]{2,1,0:T(8,128)(2,1)S(1)} %maximum_select_fusion.6.refs_5_.refs_37_), channel_id=1, source_target_pairs={{0,2},{1,3},{2,0},{3,1},{4,6},{5,7},{6,4},{7,5},{8,10},{9,11},{10,... | collective-permute-start | bytes 1769480 | tf_op jit(solution)/shard_map/ppermute | solution.py:37
  316.7 25.1 %collective-permute-start.63 = (bf16[64,1536]{1,0:T(8,128)(2,1)S(1)}, bf16[64,1536]{1,0:T(8,128)(2,1)S(1)}, u32[]{:S(2)}, u32[]{:S(2)}) collective-permute-start(bf16[64,1536]{1,0:T(8,128)(2,1)S(1)} %collective-permute-done.55.refs_11_.refs_43_), channel_id=1, source_target_pairs={{0,1},{1,0},{2,3},{3,2},{4,5},{5,4},{6,7},{7,6},{8,9},{9,8},{10,11... | collective-permute-start | bytes 589832 | tf_op jit(solution)/shard_map/ppermute | solution.py:37
  317.8 27.5 %collective-permute-start.59 = (bf16[3,64,1536]{2,1,0:T(8,128)(2,1)S(1)}, bf16[3,64,1536]{2,1,0:T(8,128)(2,1)S(1)}, u32[]{:S(2)}, u32[]{:S(2)}) collective-permute-start(bf16[3,64,1536]{2,1,0:T(8,128)(2,1)S(1)} %maximum_select_fusion.6.refs_5_.refs_37_), channel_id=1, source_target_pairs={{0,1},{1,0},{2,3},{3,2},{4,5},{5,4},{6,7},{7,6},{8,9},{9,8},{10,11... | collective-permute-start | bytes 1769480 | tf_op jit(solution)/shard_map/ppermute | solution.py:37
  327.5 17.8 %collective-permute-start.67 = (bf16[3,64,1536]{2,1,0:T(8,128)(2,1)S(1)}, bf16[3,64,1536]{2,1,0:T(8,128)(2,1)S(1)}, u32[]{:S(2)}, u32[]{:S(2)}) collective-permute-start(bf16[3,64,1536]{2,1,0:T(8,128)(2,1)S(1)} %collective-permute-done.66.refs_15_.refs_47_), channel_id=1, source_target_pairs={{0,1},{1,0},{2,3},{3,2},{4,5},{5,4},{6,7},{7,6},{8,9},{9,8},{10,11... | collective-permute-start | bytes 1769480 | tf_op jit(solution)/shard_map/ppermute | solution.py:37
  389.7 26.5 %collective-permute-start.74 = (bf16[3,64,1536]{2,1,0:T(8,128)(2,1)S(1)}, bf16[3,64,1536]{2,1,0:T(8,128)(2,1)S(1)}, u32[]{:S(2)}, u32[]{:S(2)}) collective-permute-start(bf16[3,64,1536]{2,1,0:T(8,128)(2,1)S(1)} %slice_bitcast_fusion.8), channel_id=1, source_target_pairs={{0,18},{1,19},{2,16},{3,17},{4,22},{5,23},{6,20},{7,21},{8,26},{9,... | collective-permute-start | bytes 1769480 | tf_op jit(solution)/shard_map/ppermute | solution.py:37
  390.9 29.3 %collective-permute-start.69 = (bf16[64,1536]{1,0:T(8,128)(2,1)S(1)}, bf16[64,1536]{1,0:T(8,128)(2,1)S(1)}, u32[]{:S(2)}, u32[]{:S(2)}) collective-permute-start(bf16[64,1536]{1,0:T(8,128)(2,1)S(1)} %slice_bitcast_fusion.37), channel_id=1, source_target_pairs={{0,2},{1,3},{2,0},{3,1},{4,6},{5,7},{6,4},{7,5},{8,10},{9,11},{10,... | collective-permute-start | bytes 589832 | tf_op jit(solution)/shard_map/ppermute | solution.py:37
  391.4 31.3 %collective-permute-start.70 = (bf16[64,1536]{1,0:T(8,128)(2,1)S(1)}, bf16[64,1536]{1,0:T(8,128)(2,1)S(1)}, u32[]{:S(2)}, u32[]{:S(2)}) collective-permute-start(bf16[64,1536]{1,0:T(8,128)(2,1)S(1)} %slice_bitcast_fusion.36), channel_id=1, source_target_pairs={{0,16},{1,17},{2,18},{3,19},{4,20},{5,21},{6,22},{7,23},{8,24},{9,... | collective-permute-start | bytes 589832 | tf_op jit(solution)/shard_map/ppermute | solution.py:37
  402.6 22.0 %collective-permute-start.71 = (bf16[64,1536]{1,0:T(8,128)(2,1)S(1)}, bf16[64,1536]{1,0:T(8,128)(2,1)S(1)}, u32[]{:S(2)}, u32[]{:S(2)}) collective-permute-start(bf16[64,1536]{1,0:T(8,128)(2,1)S(1)} %slice_bitcast_fusion.35), channel_id=1, source_target_pairs={{0,18},{1,19},{2,16},{3,17},{4,22},{5,23},{6,20},{7,21},{8,26},{9,... | collective-permute-start | bytes 589832 | tf_op jit(solution)/shard_map/ppermute | solution.py:37
  456.5 53.4 %collective-permute-start.90 = (bf16[2,4,64,1536]{3,2,1,0:T(8,128)(2,1)}, bf16[2,4,64,1536]{3,2,1,0:T(8,128)(2,1)}, u32[]{:S(2)}, u32[]{:S(2)}) collective-permute-start(bf16[2,4,64,1536]{3,2,1,0:T(8,128)(2,1)} %pad_maximum_fusion), channel_id=1, source_target_pairs={{0,16},{1,17},{2,18},{3,19},{4,20},{5,21},{6,22},{7,23},{8,24},{9,... | collective-permute-start | bytes 4718600 | tf_op jit(solution)/shard_map/ppermute | solution.py:37
  473.0 27.9 %collective-permute-start.89 = (bf16[64,1536]{1,0:T(8,128)(2,1)}, bf16[64,1536]{1,0:T(8,128)(2,1)S(1)}, u32[]{:S(2)}, u32[]{:S(2)}) collective-permute-start(bf16[64,1536]{1,0:T(8,128)(2,1)} %get-tuple-element.94.refs_0_.refs_17_), channel_id=1, source_target_pairs={{0,18},{1,19},{2,16},{3,17},{4,22},{5,23},{6,20},{7,21},{8,26},{9,... | collective-permute-start | bytes 589832 | tf_op jit(solution)/shard_map/ppermute | solution.py:37
  474.5 30.4 %collective-permute-start.88 = (bf16[64,1536]{1,0:T(8,128)(2,1)}, bf16[64,1536]{1,0:T(8,128)(2,1)S(1)}, u32[]{:S(2)}, u32[]{:S(2)}) collective-permute-start(bf16[64,1536]{1,0:T(8,128)(2,1)} %get-tuple-element.94.refs_0_.refs_17_), channel_id=1, source_target_pairs={{0,16},{1,17},{2,18},{3,19},{4,20},{5,21},{6,22},{7,23},{8,24},{9,... | collective-permute-start | bytes 589832 | tf_op jit(solution)/shard_map/ppermute | solution.py:37
  474.7 35.2 %collective-permute-start.86 = (bf16[64,1536]{1,0:T(8,128)(2,1)}, bf16[64,1536]{1,0:T(8,128)(2,1)S(1)}, u32[]{:S(2)}, u32[]{:S(2)}) collective-permute-start(bf16[64,1536]{1,0:T(8,128)(2,1)} %get-tuple-element.94.refs_0_.refs_17_), channel_id=1, source_target_pairs={{0,2},{1,3},{2,0},{3,1},{4,6},{5,7},{6,4},{7,5},{8,10},{9,11},{10,... | collective-permute-start | bytes 589832 | tf_op jit(solution)/shard_map/ppermute | solution.py:37
  479.5 240.2 %reduce-scatter.5.cloned.1.call-start = ((), (), s32[]{:S(2)}) async-start(), calls=%async_computation.4 | async-start | bytes 983040 | tf_op jit(solution)/shard_map/reduce_scatter | solution.py:851
  479.6 31.6 %collective-permute-start.93 = (bf16[64,1536]{1,0:T(8,128)(2,1)}, bf16[64,1536]{1,0:T(8,128)(2,1)S(1)}, u32[]{:S(2)}, u32[]{:S(2)}) collective-permute-start(bf16[64,1536]{1,0:T(8,128)(2,1)} %get-tuple-element.94.refs_0_.refs_17_), channel_id=1, source_target_pairs={{0,12},{1,13},{2,14},{3,15},{4,8},{5,9},{6,10},{7,11},{8,4},{9,5},... | collective-permute-start | bytes 589832 | tf_op jit(solution)/shard_map/ppermute | solution.py:37
  501.0 19.5 %collective-permute-start.92 = (bf16[64,1536]{1,0:T(8,128)(2,1)}, bf16[64,1536]{1,0:T(8,128)(2,1)S(1)}, u32[]{:S(2)}, u32[]{:S(2)}) collective-permute-start(bf16[64,1536]{1,0:T(8,128)(2,1)} %get-tuple-element.94.refs_0_.refs_17_), channel_id=1, source_target_pairs={{0,8},{1,9},{2,10},{3,11},{4,12},{5,13},{6,14},{7,15},{8,0},{9,1},... | collective-permute-start | bytes 589832 | tf_op jit(solution)/shard_map/ppermute | solution.py:37
  504.9 18.2 %collective-permute-start.91 = (bf16[64,1536]{1,0:T(8,128)(2,1)}, bf16[64,1536]{1,0:T(8,128)(2,1)S(1)}, u32[]{:S(2)}, u32[]{:S(2)}) collective-permute-start(bf16[64,1536]{1,0:T(8,128)(2,1)} %get-tuple-element.94.refs_0_.refs_17_), channel_id=1, source_target_pairs={{0,4},{1,5},{2,6},{3,7},{4,0},{5,1},{6,2},{7,3},{8,12},{9,13},{10,... | collective-permute-start | bytes 589832 | tf_op jit(solution)/shard_map/ppermute | solution.py:37
  523.2 20.9 %collective-permute-start.101 = (bf16[3,64,1536]{2,1,0:T(8,128)(2,1)S(1)}, bf16[3,64,1536]{2,1,0:T(8,128)(2,1)S(1)}, u32[]{:S(2)}, u32[]{:S(2)}) collective-permute-start(bf16[3,64,1536]{2,1,0:T(8,128)(2,1)S(1)} %maximum_select_fusion.7.refs_4_.refs_21_), channel_id=1, source_target_pairs={{0,18},{1,19},{2,16},{3,17},{4,22},{5,23},{6,20},{7,21},{8,26},{9,... | collective-permute-start | bytes 1769480 | tf_op jit(solution)/shard_map/ppermute | solution.py:37
  523.3 31.0 %collective-permute-start.99 = (bf16[3,64,1536]{2,1,0:T(8,128)(2,1)S(1)}, bf16[3,64,1536]{2,1,0:T(8,128)(2,1)S(1)}, u32[]{:S(2)}, u32[]{:S(2)}) collective-permute-start(bf16[3,64,1536]{2,1,0:T(8,128)(2,1)S(1)} %maximum_select_fusion.7.refs_4_.refs_21_), channel_id=1, source_target_pairs={{0,16},{1,17},{2,18},{3,19},{4,20},{5,21},{6,22},{7,23},{8,24},{9,... | collective-permute-start | bytes 1769480 | tf_op jit(solution)/shard_map/ppermute | solution.py:37
  523.4 34.5 %collective-permute-start.95 = (bf16[3,64,1536]{2,1,0:T(8,128)(2,1)S(1)}, bf16[3,64,1536]{2,1,0:T(8,128)(2,1)S(1)}, u32[]{:S(2)}, u32[]{:S(2)}) collective-permute-start(bf16[3,64,1536]{2,1,0:T(8,128)(2,1)S(1)} %maximum_select_fusion.7.refs_4_.refs_21_), channel_id=1, source_target_pairs={{0,2},{1,3},{2,0},{3,1},{4,6},{5,7},{6,4},{7,5},{8,10},{9,11},{10,... | collective-permute-start | bytes 1769480 | tf_op jit(solution)/shard_map/ppermute | solution.py:37
  531.1 26.9 %collective-permute-start.98 = (bf16[64,1536]{1,0:T(8,128)(2,1)}, bf16[64,1536]{1,0:T(8,128)(2,1)S(1)}, u32[]{:S(2)}, u32[]{:S(2)}) collective-permute-start(bf16[64,1536]{1,0:T(8,128)(2,1)} %copy-done.9), channel_id=1, source_target_pairs={{0,1},{1,0},{2,3},{3,2},{4,5},{5,4},{6,7},{7,6},{8,9},{9,8},{10,11... | collective-permute-start | bytes 589832 | tf_op jit(solution)/shard_map/ppermute | solution.py:37
  532.4 29.6 %collective-permute-start.94 = (bf16[3,64,1536]{2,1,0:T(8,128)(2,1)S(1)}, bf16[3,64,1536]{2,1,0:T(8,128)(2,1)S(1)}, u32[]{:S(2)}, u32[]{:S(2)}) collective-permute-start(bf16[3,64,1536]{2,1,0:T(8,128)(2,1)S(1)} %maximum_select_fusion.7.refs_4_.refs_21_), channel_id=1, source_target_pairs={{0,1},{1,0},{2,3},{3,2},{4,5},{5,4},{6,7},{7,6},{8,9},{9,8},{10,11... | collective-permute-start | bytes 1769480 | tf_op jit(solution)/shard_map/ppermute | solution.py:37
  544.1 17.9 %collective-permute-start.102 = (bf16[3,64,1536]{2,1,0:T(8,128)(2,1)S(1)}, bf16[3,64,1536]{2,1,0:T(8,128)(2,1)S(1)}, u32[]{:S(2)}, u32[]{:S(2)}) collective-permute-start(bf16[3,64,1536]{2,1,0:T(8,128)(2,1)S(1)} %collective-permute-done.101.refs_14_.refs_31_), channel_id=1, source_target_pairs={{0,1},{1,0},{2,3},{3,2},{4,5},{5,4},{6,7},{7,6},{8,9},{9,8},{10,11... | collective-permute-start | bytes 1769480 | tf_op jit(solution)/shard_map/ppermute | solution.py:37
  605.9 27.4 %collective-permute-start.106 = (bf16[3,64,1536]{2,1,0:T(8,128)(2,1)S(1)}, bf16[3,64,1536]{2,1,0:T(8,128)(2,1)S(1)}, u32[]{:S(2)}, u32[]{:S(2)}) collective-permute-start(bf16[3,64,1536]{2,1,0:T(8,128)(2,1)S(1)} %slice_bitcast_fusion.4), channel_id=1, source_target_pairs={{0,18},{1,19},{2,16},{3,17},{4,22},{5,23},{6,20},{7,21},{8,26},{9,... | collective-permute-start | bytes 1769480 | tf_op jit(solution)/shard_map/ppermute | solution.py:37
  607.4 27.5 %collective-permute-start.104 = (bf16[3,64,1536]{2,1,0:T(8,128)(2,1)S(1)}, bf16[3,64,1536]{2,1,0:T(8,128)(2,1)S(1)}, u32[]{:S(2)}, u32[]{:S(2)}) collective-permute-start(bf16[3,64,1536]{2,1,0:T(8,128)(2,1)S(1)} %slice_bitcast_fusion.6), channel_id=1, source_target_pairs={{0,2},{1,3},{2,0},{3,1},{4,6},{5,7},{6,4},{7,5},{8,10},{9,11},{10,... | collective-permute-start | bytes 1769480 | tf_op jit(solution)/shard_map/ppermute | solution.py:37
  609.3 26.1 %collective-permute-start.105 = (bf16[3,64,1536]{2,1,0:T(8,128)(2,1)S(1)}, bf16[3,64,1536]{2,1,0:T(8,128)(2,1)S(1)}, u32[]{:S(2)}, u32[]{:S(2)}) collective-permute-start(bf16[3,64,1536]{2,1,0:T(8,128)(2,1)S(1)} %slice_bitcast_fusion.5), channel_id=1, source_target_pairs={{0,16},{1,17},{2,18},{3,19},{4,20},{5,21},{6,22},{7,23},{8,24},{9,... | collective-permute-start | bytes 1769480 | tf_op jit(solution)/shard_map/ppermute | solution.py:37
  638.6 33.8 %collective-permute-start.107 = (bf16[4,64,1536]{2,1,0:T(8,128)(2,1)S(1)}, bf16[4,64,1536]{2,1,0:T(8,128)(2,1)S(1)}, u32[]{:S(2)}, u32[]{:S(2)}) collective-permute-start(bf16[4,64,1536]{2,1,0:T(8,128)(2,1)S(1)} %slice_bitcast_fusion), channel_id=1, source_target_pairs={{0,2},{1,3},{2,0},{3,1},{4,6},{5,7},{6,4},{7,5},{8,10},{9,11},{10,... | collective-permute-start | bytes 2359304 | tf_op jit(solution)/shard_map/ppermute | solution.py:37
  640.6 25.0 %collective-permute-start.108 = (bf16[64,1536]{1,0:T(8,128)(2,1)S(1)}, bf16[64,1536]{1,0:T(8,128)(2,1)S(1)}, u32[]{:S(2)}, u32[]{:S(2)}) collective-permute-start(bf16[64,1536]{1,0:T(8,128)(2,1)S(1)} %slice_bitcast_fusion.28), channel_id=1, source_target_pairs={{0,2},{1,3},{2,0},{3,1},{4,6},{5,7},{6,4},{7,5},{8,10},{9,11},{10,... | collective-permute-start | bytes 589832 | tf_op jit(solution)/shard_map/ppermute | solution.py:37
  640.7 28.0 %collective-permute-start.109 = (bf16[64,1536]{1,0:T(8,128)(2,1)S(1)}, bf16[64,1536]{1,0:T(8,128)(2,1)S(1)}, u32[]{:S(2)}, u32[]{:S(2)}) collective-permute-start(bf16[64,1536]{1,0:T(8,128)(2,1)S(1)} %slice_bitcast_fusion.27), channel_id=1, source_target_pairs={{0,16},{1,17},{2,18},{3,19},{4,20},{5,21},{6,22},{7,23},{8,24},{9,... | collective-permute-start | bytes 589832 | tf_op jit(solution)/shard_map/ppermute | solution.py:37
  643.3 25.4 %collective-permute-start.111 = (bf16[64,1536]{1,0:T(8,128)(2,1)S(1)}, bf16[64,1536]{1,0:T(8,128)(2,1)S(1)}, u32[]{:S(2)}, u32[]{:S(2)}) collective-permute-start(bf16[64,1536]{1,0:T(8,128)(2,1)S(1)} %get-tuple-element.206), channel_id=1, source_target_pairs={{0,4},{1,5},{2,6},{3,7},{4,0},{5,1},{6,2},{7,3},{8,12},{9,13},{10,... | collective-permute-start | bytes 589832 | tf_op jit(solution)/shard_map/ppermute | solution.py:37
  648.8 19.8 %collective-permute-start.113 = (bf16[64,1536]{1,0:T(8,128)(2,1)S(1)}, bf16[64,1536]{1,0:T(8,128)(2,1)S(1)}, u32[]{:S(2)}, u32[]{:S(2)}) collective-permute-start(bf16[64,1536]{1,0:T(8,128)(2,1)S(1)} %get-tuple-element.207), channel_id=1, source_target_pairs={{0,12},{1,13},{2,14},{3,15},{4,8},{5,9},{6,10},{7,11},{8,4},{9,5},... | collective-permute-start | bytes 589832 | tf_op jit(solution)/shard_map/ppermute | solution.py:37
  703.5 31.4 %collective-permute-start.121 = (bf16[4,192,896]{2,1,0:T(8,128)(2,1)}, bf16[4,192,896]{2,1,0:T(8,128)(2,1)}, u32[]{:S(2)}, u32[]{:S(2)}) collective-permute-start(bf16[4,192,896]{2,1,0:T(8,128)(2,1)} %get-tuple-element.115), channel_id=1, source_target_pairs={{0,16},{1,17},{2,18},{3,19},{4,20},{5,21},{6,22},{7,23},{8,24},{9,... | collective-permute-start | bytes 4128776 | tf_op jit(solution)/shard_map/ppermute | solution.py:37
  720.8 22.4 %collective-permute-start.119 = (bf16[2,64,1536]{2,1,0:T(8,128)(2,1)S(1)}, bf16[2,64,1536]{2,1,0:T(8,128)(2,1)S(1)}, u32[]{:S(2)}, u32[]{:S(2)}) collective-permute-start(bf16[2,64,1536]{2,1,0:T(8,128)(2,1)S(1)} %pad_maximum_fusion.4), channel_id=1, source_target_pairs={{0,16},{1,17},{2,18},{3,19},{4,20},{5,21},{6,22},{7,23},{8,24},{9,... | collective-permute-start | bytes 1179656 | tf_op jit(solution)/shard_map/ppermute | solution.py:37
  740.3 29.0 %collective-permute-start.125 = (bf16[208,896]{1,0:T(8,128)(2,1)S(1)}, bf16[208,896]{1,0:T(8,128)(2,1)S(1)}, u32[]{:S(2)}, u32[]{:S(2)}) collective-permute-start(bf16[208,896]{1,0:T(8,128)(2,1)S(1)} %get-tuple-element.199), channel_id=1, source_target_pairs={{0,8},{1,9},{2,10},{3,11},{4,12},{5,13},{6,14},{7,15},{8,0},{9,1},... | collective-permute-start | bytes 1118216 | tf_op jit(solution)/shard_map/ppermute | solution.py:37
  (213 other events, 2704.0 us)
Sparse Core Ops, SparseCore 0:
  27.3 61.5 all-gather.7
  156.0 60.1 all-gather.9
  218.5 85.4 all-gather.5
  479.7 90.5 reduce-scatter.2
  698.3 21.4 reduce-scatter.4

commit v4 on v3

--- a/solution.py
+++ b/solution.py
@@ -830,10 +830,9 @@
     (in_grad1, g, g_low), gain_sums1, mine, theirs, outs = attention_back(
         kept1, 1, cots[1], terms, (cots[0],), lambda d: moe_out(hidden1[1], routes[1], d)
     )
-    out_near, out_far = (jnp.stack(side) for side in outs)
-    out_far = move(out_far, section=1)
+    out_first, out_second = (jnp.stack([side[y] for side in outs]) for y in range(2))
     grad1 = jnp.where(first, jnp.stack([mine, theirs]), jnp.stack([theirs, mine]))
-    near, far = to_host(g_low, grad1[0, 0, :1, :1], out_far[0, :1])
+    near, far = to_host(g_low, grad1[0, 0, :1, :1])
     shard1_sum = lax.psum_scatter(
         grad1.reshape(2 * n_dp, half, acols - HD), ("section", "dp"), scatter_dimension=0, tiled=True
     )
@@ -845,20 +844,20 @@
         blocks0, grads0, blocks1, (*hidden0, *hidden1), route, near_far[1][1]
     )
     others = others_sums(*near_far, 0, dw_out[0, :rows])
-    out1 = after(jnp.where(first, out_far, out_near), others[:1])
-    out_across = move(out1[1], tensor=2)
-    terms = all_sums(*near_far, others, 0, out_across[0])
-    out1_sum = lax.psum_scatter(out1[0] + out_across, "dp", scatter_dimension=0, tiled=True)
+    terms = all_sums(*near_far, others, 0)
     (in_grad0, _), gain_sums0, mine, theirs, _ = attention_back(kept0, 0, g, terms, ())
+    out_across = move(after(out_second, in_grad0[None, None]), tensor=2)
+    out1_sum = lax.psum_scatter(
+        (out_first + out_across).swapaxes(0, 1), "dp", scatter_dimension=0, tiled=True
+    )[0].astype(F32)
 
     gain_sums = jnp.concatenate([gain_sums0, gain_sums1])
     gain_sums = gain_sums + move(gain_sums, tensor=1)
-    gain_sums = gain_sums + move(gain_sums, tensor=2)
+    gain_sums = after(gain_sums + move(gain_sums, tensor=2), out_across[0, 0, :4])
     gain_sums = gain_sums.astype(BF).reshape(4, n_dp, drows).transpose(1, 0, 2)[dp_order]
     gain_sums = jnp.pad(gain_sums, ((0, 0), (0, 12), (0, 2 * qcols + HD - drows)))
     parts = jnp.concatenate([mine + move(theirs, section=1), gain_sums], axis=1)
     parts = [parts[0]] + [move(parts[k], dp=k) for k in range(1, n_dp)]
-    out1 = mid + out1_sum[0].astype(F32)
     shard1 = shard1_sum[0].astype(F32)
     shard0 = sum(part.astype(F32) for part in parts)
 
@@ -881,15 +880,17 @@
     def mine_and_theirs(value0, value1):
         return jnp.where(first, value0, value1), jnp.where(first, value1, value0)
 
-    out_near, out_far = mine_and_theirs(out0, out1)
     grad_near, grad_far = mine_and_theirs(in_grad0, in_grad1)
-    theirs = move(jnp.stack([out_far, grad_far]).astype(BF), section=1).astype(F32)
+    out_swap = jnp.where(first, mid, out0)
+    theirs = move(jnp.stack([out_swap, grad_far]).astype(BF), section=1).astype(F32)
+    out_near = jnp.where(first, out0, mid + out1_sum[0])
+    out_far = jnp.where(first, theirs[0], theirs[0] + out1_sum[1])
 
     def both_batches(near, far):
         return jnp.where(first, jnp.stack([near, far]), jnp.stack([far, near]))[None]
 
     return (
-        both_batches(out_near, theirs[0]),
+        both_batches(out_near, out_far),
         both_batches(grad_near, theirs[1]),
         gains[0:1],
         grad_shard[None, :, :qcols],

time: 807 us -> 804 us (level)
  waiting for transfers between devices: 396 us -> 408 us
    ppermute x127 -> x126, waiting for transfers between devices: 347 us -> 367 us  [move(): return lax.ppermute(value, ('section', 'dp', 'tensor'), pairs)]
    reduce_scatter x1, waiting for transfers between devices: 9.67 us -> 0.01 us  [per_device(): lax.psum_scatter((out_first + out_across).swapaxes(0, 1), 'dp', scatter_d...]
    ppermute x127 -> x126, starting transfers between devices: 151 us -> 146 us  [move(): return lax.ppermute(value, ('section', 'dp', 'tensor'), pairs)]
    unnamed x257 -> x235, local copies, waits for them, and re-layouts: 24.1 us -> 20.3 us
  transfers between devices with their start and end apart: 134 -> 133, of which waited for: 81 -> 77; matrix products, arithmetic and copies ran while one was open for 4% -> 4% of each run, Pallas kernels for 12% -> 11%
where the time goes in v4:
time: 804 us; the launch traced here: 796 us
  waiting for transfers between devices  408 us (51%)
  starting transfers between devices  157 us (20%)
  Pallas kernels  141 us (18%)
  other arithmetic  33 us (4%)
  local copies, waits for them, and re-layouts  32.4 us (4%)
  between operations  23.8 us (3%)
    ppermute x126, waiting for transfers between devices, move(): return lax.ppermute(value, ('section', 'dp', 'tensor'), pairs)  367 us
    ppermute x126, starting transfers between devices, move(): return lax.ppermute(value, ('section', 'dp', 'tensor'), pairs)  146 us
    pallas_call x19, Pallas kernels, call(): pl.pallas_call(body, out_shape=list(outs) + [jax.ShapeDtypeStruct(h.shape...  141 us
    all_gather x2, waiting for transfers between devices, gather_weights(): lax.all_gather(seed[None, None], ('section', 'dp'), axis=0, tiled=True)  35.5 us
    unnamed x235, local copies, waits for them, and re-layouts  20.3 us
  transfers between devices with their start and end apart: 133, of which 77 were waited for; matrix products, arithmetic and copies ran while one was open for 4% of the time, Pallas kernels for 11%

profile of v4, /device:TPU:9, one launch (start us, length us, event | category | flops | bytes accessed | tf_op | source)
XLA Modules:
  0.0 795.6 jit_solution(6376053778226750762)
XLA Ops:
  53.4 35.5 %all-gather.8.cloned.1.call-done = bf16[1536,1024]{1,0:T(8,128)(2,1)} async-done(((bf16[192,1024]{1,0:T(8,128)(2,1)}), bf16[1536,1024]{1,0:T(8,128)(2,1)}) %all-gather.8.cloned.1.call-update) | async-done | bytes 3145744 | tf_op jit(solution)/shard_map/all_gather | solution.py:680
  90.8 4.1 attn_fwd.2
  100.9 4.5 collective-permute-done.17.refs_3_
  114.8 4.2 collective-permute-done.22.refs_10_.refs_11_
  120.0 8.1 %collective-permute-done.26 = bf16[64,1536]{1,0:T(8,128)(2,1)S(1)} collective-permute-done((bf16[64,1536]{1,0:T(8,128)(2,1)S(1)}, bf16[64,1536]{1,0:T(8,128)(2,1)S(1)}, u32[]{:S(2)}, u32[]{:S(2)}) %collective-permute-start.26) | collective-permute-done | bytes 196640 | tf_op jit(solution)/shard_map/ppermute | solution.py:37
  130.9 9.7 %collective-permute-done.28.refs_6_.refs_7_ = bf16[3,64,1536]{2,1,0:T(8,128)(2,1)S(1)} collective-permute-done((bf16[3,64,1536]{2,1,0:T(8,128)(2,1)S(1)}, bf16[3,64,1536]{2,1,0:T(8,128)(2,1)S(1)}, u32[]{:S(2)}, u32[]{:S(2)}) %collective-permute-start.28) | collective-permute-done | bytes 589856 | tf_op jit(solution)/shard_map/ppermute | solution.py:37
  140.8 13.4 %collective-permute-done.34.refs_14_.refs_15_ = bf16[3,64,1536]{2,1,0:T(8,128)(2,1)S(1)} collective-permute-done((bf16[3,64,1536]{2,1,0:T(8,128)(2,1)S(1)}, bf16[3,64,1536]{2,1,0:T(8,128)(2,1)S(1)}, u32[]{:S(2)}, u32[]{:S(2)}) %collective-permute-start.34) | collective-permute-done | bytes 589856 | tf_op jit(solution)/shard_map/ppermute | solution.py:37
  156.3 3.7 collective-permute-start.18
  168.5 26.5 %moe_fwd.1 = (f32[4,640,384]{2,1,0:T(8,128)}, bf16[2,8,64,1536]{3,2,1,0:T(8,128)(2,1)}, bf16[2,8,64,1536]{3,2,1,0:T(8,128)(2,1)}) custom-call(bf16[64,1536]{1,0:T(8,128)(2,1)S(1)} %get-tuple-element.69.refs_0_.refs_1_, bf16[64,1536]{1,0:T(8,128)(2,1)S(1)} %collective-permute-done.18.refs_1_.refs_2_, ...), custom_call_target="tpu_custom_call" | custom-call | flops 4000000000 | bytes 12582912 | tf_op jit(solution)/shard_map/moe_fwd/pallas_call | solution.py:497
  197.5 3.8 collective-permute-done.36
  208.0 11.2 %collective-permute-done.40 = bf16[3,64,1536]{2,1,0:T(8,128)(2,1)S(1)} collective-permute-done((bf16[3,64,1536]{2,1,0:T(8,128)(2,1)S(1)}, bf16[3,64,1536]{2,1,0:T(8,128)(2,1)S(1)}, u32[]{:S(2)}, u32[]{:S(2)}) %collective-permute-start.40) | collective-permute-done | bytes 589856 | tf_op jit(solution)/shard_map/ppermute | solution.py:37
  219.5 13.2 %collective-permute-done.42 = bf16[3,64,1536]{2,1,0:T(8,128)(2,1)S(1)} collective-permute-done((bf16[3,64,1536]{2,1,0:T(8,128)(2,1)S(1)}, bf16[3,64,1536]{2,1,0:T(8,128)(2,1)S(1)}, u32[]{:S(2)}, u32[]{:S(2)}) %collective-permute-start.42) | collective-permute-done | bytes 589856 | tf_op jit(solution)/shard_map/ppermute | solution.py:37
  241.3 4.2 collective-permute-done.43
  245.6 6.4 collective-permute-done.44
  252.0 8.2 %collective-permute-done.45 = bf16[64,1536]{1,0:T(8,128)(2,1)S(1)} collective-permute-done((bf16[64,1536]{1,0:T(8,128)(2,1)S(1)}, bf16[64,1536]{1,0:T(8,128)(2,1)S(1)}, u32[]{:S(2)}, u32[]{:S(2)}) %collective-permute-start.45) | collective-permute-done | bytes 196640 | tf_op jit(solution)/shard_map/ppermute | solution.py:37
  272.7 4.5 attn_fwd.3
  280.5 9.7 %collective-permute-done.50.refs_3_ = bf16[64,1536]{1,0:T(8,128)(2,1)S(1)} collective-permute-done((bf16[64,1536]{1,0:T(8,128)(2,1)S(1)}, bf16[64,1536]{1,0:T(8,128)(2,1)S(1)}, u32[]{:S(2)}, u32[]{:S(2)}) %collective-permute-start.50) | collective-permute-done | bytes 196640 | tf_op jit(solution)/shard_map/ppermute | solution.py:37
  297.1 3.7 collective-permute-done.55.refs_11_.refs_43_
  301.0 9.6 %collective-permute-done.56 = bf16[64,1536]{1,0:T(8,128)(2,1)S(1)} collective-permute-done((bf16[64,1536]{1,0:T(8,128)(2,1)S(1)}, bf16[64,1536]{1,0:T(8,128)(2,1)S(1)}, u32[]{:S(2)}, u32[]{:S(2)}) %collective-permute-start.56) | collective-permute-done | bytes 196640 | tf_op jit(solution)/shard_map/ppermute | solution.py:37
  310.6 7.8 collective-permute-done.58
  324.7 7.4 collective-permute-done.60.refs_7_.refs_39_
  336.6 9.1 %collective-permute-done.66.refs_15_.refs_47_ = bf16[3,64,1536]{2,1,0:T(8,128)(2,1)S(1)} collective-permute-done((bf16[3,64,1536]{2,1,0:T(8,128)(2,1)S(1)}, bf16[3,64,1536]{2,1,0:T(8,128)(2,1)S(1)}, u32[]{:S(2)}, u32[]{:S(2)}) %collective-permute-start.66) | collective-permute-done | bytes 589856 | tf_op jit(solution)/shard_map/ppermute | solution.py:37
  353.4 31.7 %moe_turn.1 = (bf16[4,640,192]{2,1,0:T(8,128)(2,1)}, bf16[4,640,384]{2,1,0:T(8,128)(2,1)}, bf16[2,8,64,1536]{3,2,1,0:T(8,128)(2,1)}, bf16[2,8,64,1536]{3,2,1,0:T(8,128)(2,1)}) custom-call(s32[4]{0:T(128)} %copy-done.43, bf16[64,1536]{1,0:T(8,128)(2,1)} %copy-done.67, bf16[64,1536]{1,0:T(8,128)(2,1)} %copy-done.69, bf16[64,1536]{1,0:T(8,128)(2,1)} %copy-done.29, ...), custom_call_target="tpu_custom_call" | custom-call | flops 8000000000 | bytes 25165824 | tf_op jit(solution)/shard_map/moe_turn/pallas_call | solution.py:497
  385.6 5.5 collective-permute-done.68
  398.2 9.8 %collective-permute-done.72 = bf16[3,64,1536]{2,1,0:T(8,128)(2,1)S(1)} collective-permute-done((bf16[3,64,1536]{2,1,0:T(8,128)(2,1)S(1)}, bf16[3,64,1536]{2,1,0:T(8,128)(2,1)S(1)}, u32[]{:S(2)}, u32[]{:S(2)}) %collective-permute-start.72) | collective-permute-done | bytes 589856 | tf_op jit(solution)/shard_map/ppermute | solution.py:37
  409.1 12.6 %collective-permute-done.74 = bf16[3,64,1536]{2,1,0:T(8,128)(2,1)S(1)} collective-permute-done((bf16[3,64,1536]{2,1,0:T(8,128)(2,1)S(1)}, bf16[3,64,1536]{2,1,0:T(8,128)(2,1)S(1)}, u32[]{:S(2)}, u32[]{:S(2)}) %collective-permute-start.74) | collective-permute-done | bytes 589856 | tf_op jit(solution)/shard_map/ppermute | solution.py:37
  425.6 4.5 collective-permute-done.71
  430.3 10.5 %collective-permute-done.77 = bf16[64,1536]{1,0:T(8,128)(2,1)S(1)} collective-permute-done((bf16[64,1536]{1,0:T(8,128)(2,1)S(1)}, bf16[64,1536]{1,0:T(8,128)(2,1)S(1)}, u32[]{:S(2)}, u32[]{:S(2)}) %collective-permute-start.77) | collective-permute-done | bytes 196640 | tf_op jit(solution)/shard_map/ppermute | solution.py:37
  443.1 6.0 moe_out.1
  452.2 6.0 collective-permute-done.80.refs_4_
  461.9 5.0 attn_bwd.2
  488.6 4.1 collective-permute-done.91
  492.7 17.9 %collective-permute-done.92 = bf16[64,1536]{1,0:T(8,128)(2,1)S(1)} collective-permute-done((bf16[64,1536]{1,0:T(8,128)(2,1)}, bf16[64,1536]{1,0:T(8,128)(2,1)S(1)}, u32[]{:S(2)}, u32[]{:S(2)}) %collective-permute-start.92) | collective-permute-done | bytes 196640 | tf_op jit(solution)/shard_map/ppermute | solution.py:37
  513.5 9.9 %collective-permute-start.84 = (bf16[64,1536]{1,0:T(8,128)(2,1)}, bf16[64,1536]{1,0:T(8,128)(2,1)S(1)}, u32[]{:S(2)}, u32[]{:S(2)}) collective-permute-start(bf16[64,1536]{1,0:T(8,128)(2,1)} %get-tuple-element.89.refs_0_.refs_17_), channel_id=1, source_target_pairs={{0,1},{1,0},{2,3},{3,2},{4,5},{5,4},{6,7},{7,6},{8,9},{9,8},{10,11... | collective-permute-start | bytes 589832 | tf_op jit(solution)/shard_map/ppermute | solution.py:37
  525.4 15.2 %collective-permute-start.101 = (bf16[3,64,1536]{2,1,0:T(8,128)(2,1)S(1)}, bf16[3,64,1536]{2,1,0:T(8,128)(2,1)S(1)}, u32[]{:S(2)}, u32[]{:S(2)}) collective-permute-start(bf16[3,64,1536]{2,1,0:T(8,128)(2,1)S(1)} %collective-permute-done.100.refs_14_.refs_31_), channel_id=1, source_target_pairs={{0,1},{1,0},{2,3},{3,2},{4,5},{5,4},{6,7},{7,6},{8,9},{9,8},{10,11... | collective-permute-start | bytes 1769480 | tf_op jit(solution)/shard_map/ppermute | solution.py:37
  540.6 9.6 %collective-permute-start.99 = (bf16[3,64,1536]{2,1,0:T(8,128)(2,1)S(1)}, bf16[3,64,1536]{2,1,0:T(8,128)(2,1)S(1)}, u32[]{:S(2)}, u32[]{:S(2)}) collective-permute-start(bf16[3,64,1536]{2,1,0:T(8,128)(2,1)S(1)} %collective-permute-done.98.refs_12_.refs_29_), channel_id=1, source_target_pairs={{0,1},{1,0},{2,3},{3,2},{4,5},{5,4},{6,7},{7,6},{8,9},{9,8},{10,11... | collective-permute-start | bytes 1769480 | tf_op jit(solution)/shard_map/ppermute | solution.py:37
  554.9 27.9 %moe_bwd.1 = (bf16[4,640,192]{2,1,0:T(8,128)(2,1)}, bf16[4,640,384]{2,1,0:T(8,128)(2,1)}, bf16[2,8,64,1536]{3,2,1,0:T(8,128)(2,1)}, bf16[2,8,64,1536]{3,2,1,0:T(8,128)(2,1)}) custom-call(bf16[64,1536]{1,0:T(8,128)(2,1)} %get-tuple-element.89.refs_0_.refs_17_, bf16[64,1536]{1,0:T(8,128)(2,1)S(1)} %collective-permute-done.84.refs_1_.refs_18_, ...), custom_call_target="tpu_custom_call" | custom-call | flops 4000000000 | bytes 12582912 | tf_op jit(solution)/shard_map/moe_bwd/pallas_call | solution.py:497
  598.8 22.3 %moe_wgrad.1 = (f32[4,1536,384]{2,1,0:T(8,128)}, f32[4,192,1536]{2,1,0:T(8,128)}) custom-call(s32[4]{0:T(128)S(1)} %broadcast_select_fusion.7.refs_0_, bf16[64,1536]{1,0:T(8,128)(2,1)S(1)} %copy-done.58, bf16[64,1536]{1,0:T(8,128)(2,1)S(1)} %copy-done.60, bf16[64,1536]{1,0:T(8,128)(2,1)S(1)} %copy-done.36, bf16[64,1536]{1,0:T(8,128)(2,1)S(1)} %copy-done.62, ...), custom_call_target="tpu_custom_call" | custom-call | flops 10000000000 | bytes 31457280 | tf_op jit(solution)/shard_map/moe_wgrad/pallas_call | solution.py:497
  626.7 4.9 collective-permute-done.105
  631.6 11.0 %collective-permute-done.111 = bf16[64,1536]{1,0:T(8,128)(2,1)S(1)} collective-permute-done((bf16[64,1536]{1,0:T(8,128)(2,1)S(1)}, bf16[64,1536]{1,0:T(8,128)(2,1)S(1)}, u32[]{:S(2)}, u32[]{:S(2)}) %collective-permute-start.111) | collective-permute-done | bytes 196640 | tf_op jit(solution)/shard_map/ppermute | solution.py:37
  652.5 5.2 attn_bwd.3
  660.9 4.9 collective-permute-done.116.refs_4_
  675.0 25.8 %collective-permute-done.120 = bf16[4,192,896]{2,1,0:T(8,128)(2,1)S(1)} collective-permute-done((bf16[4,192,896]{2,1,0:T(8,128)(2,1)S(1)}, bf16[4,192,896]{2,1,0:T(8,128)(2,1)S(1)}, u32[]{:S(2)}, u32[]{:S(2)}) %collective-permute-start.120) | collective-permute-done | bytes 1376288 | tf_op jit(solution)/shard_map/ppermute | solution.py:37
  710.7 12.1 %collective-permute-done.123 = bf16[208,896]{1,0:T(8,128)(2,1)S(1)} collective-permute-done((bf16[208,896]{1,0:T(8,128)(2,1)S(1)}, bf16[208,896]{1,0:T(8,128)(2,1)S(1)}, u32[]{:S(2)}, u32[]{:S(2)}) %collective-permute-start.123) | collective-permute-done | bytes 372768 | tf_op jit(solution)/shard_map/ppermute | solution.py:37
  722.8 4.0 collective-permute-done.124
  726.8 38.6 %collective-permute-done.125 = bf16[208,896]{1,0:T(8,128)(2,1)S(1)} collective-permute-done((bf16[208,896]{1,0:T(8,128)(2,1)S(1)}, bf16[208,896]{1,0:T(8,128)(2,1)S(1)}, u32[]{:S(2)}, u32[]{:S(2)}) %collective-permute-start.125) | collective-permute-done | bytes 372768 | tf_op jit(solution)/shard_map/ppermute | solution.py:37
  767.6 4.9 collective-permute-done.126
  774.6 7.1 collective-permute-start.127
  (635 shorter events, 246.0 us)
Async XLA Ops:
  7.2 81.7 %all-gather.8.cloned.1.call-start = ((), (), s32[]{:S(2)}) async-start(), calls=%async_computation.5 | async-start | bytes 3538944 | tf_op jit(solution)/shard_map/all_gather | solution.py:680
  27.2 243.6 %all-gather.10.cloned.1.call-start = ((), (), s32[]{:S(2)}) async-start(), calls=%async_computation.6 | async-start | bytes 3538944 | tf_op jit(solution)/shard_map/all_gather | solution.py:680
  111.4 16.7 %collective-permute-start.26 = (bf16[64,1536]{1,0:T(8,128)(2,1)S(1)}, bf16[64,1536]{1,0:T(8,128)(2,1)S(1)}, u32[]{:S(2)}, u32[]{:S(2)}) collective-permute-start(bf16[64,1536]{1,0:T(8,128)(2,1)S(1)} %get-tuple-element.69.refs_0_.refs_1_), channel_id=1, source_target_pairs={{0,12},{1,13},{2,14},{3,15},{4,8},{5,9},{6,10},{7,11},{8,4},{9,5},... | collective-permute-start | bytes 589832 | tf_op jit(solution)/shard_map/ppermute | solution.py:37
  128.9 25.3 %collective-permute-start.34 = (bf16[3,64,1536]{2,1,0:T(8,128)(2,1)S(1)}, bf16[3,64,1536]{2,1,0:T(8,128)(2,1)S(1)}, u32[]{:S(2)}, u32[]{:S(2)}) collective-permute-start(bf16[3,64,1536]{2,1,0:T(8,128)(2,1)S(1)} %maximum_select_fusion.5.refs_4_.refs_5_), channel_id=1, source_target_pairs={{0,18},{1,19},{2,16},{3,17},{4,22},{5,23},{6,20},{7,21},{8,26},{9,... | collective-permute-start | bytes 1769480 | tf_op jit(solution)/shard_map/ppermute | solution.py:37
  156.2 197.2 %all-gather.6.cloned.1.call-start = ((), (), s32[]{:S(2)}) async-start(), calls=%async_computation.2 | async-start | bytes 6684672 | tf_op jit(solution)/shard_map/all_gather | solution.py:792
  197.4 385.9 %reduce-scatter.3.cloned.1.call-start = ((), (), s32[]{:S(2)}) async-start(), calls=%async_computation.3 | async-start | bytes 3096576 | tf_op jit(solution)/shard_map/reduce_scatter | solution.py:836
  204.4 14.8 %collective-permute-start.40 = (bf16[3,64,1536]{2,1,0:T(8,128)(2,1)S(1)}, bf16[3,64,1536]{2,1,0:T(8,128)(2,1)S(1)}, u32[]{:S(2)}, u32[]{:S(2)}) collective-permute-start(bf16[3,64,1536]{2,1,0:T(8,128)(2,1)S(1)} %slice_bitcast_fusion.12), channel_id=1, source_target_pairs={{0,2},{1,3},{2,0},{3,1},{4,6},{5,7},{6,4},{7,5},{8,10},{9,11},{10,... | collective-permute-start | bytes 1769480 | tf_op jit(solution)/shard_map/ppermute | solution.py:37
  205.2 27.6 %collective-permute-start.42 = (bf16[3,64,1536]{2,1,0:T(8,128)(2,1)S(1)}, bf16[3,64,1536]{2,1,0:T(8,128)(2,1)S(1)}, u32[]{:S(2)}, u32[]{:S(2)}) collective-permute-start(bf16[3,64,1536]{2,1,0:T(8,128)(2,1)S(1)} %slice_bitcast_fusion.10), channel_id=1, source_target_pairs={{0,18},{1,19},{2,16},{3,17},{4,22},{5,23},{6,20},{7,21},{8,26},{9,... | collective-permute-start | bytes 1769480 | tf_op jit(solution)/shard_map/ppermute | solution.py:37
  207.4 31.0 %collective-permute-start.37 = (bf16[64,1536]{1,0:T(8,128)(2,1)S(1)}, bf16[64,1536]{1,0:T(8,128)(2,1)S(1)}, u32[]{:S(2)}, u32[]{:S(2)}) collective-permute-start(bf16[64,1536]{1,0:T(8,128)(2,1)S(1)} %slice_bitcast_fusion.46), channel_id=1, source_target_pairs={{0,2},{1,3},{2,0},{3,1},{4,6},{5,7},{6,4},{7,5},{8,10},{9,11},{10,... | collective-permute-start | bytes 589832 | tf_op jit(solution)/shard_map/ppermute | solution.py:37
  207.8 31.0 %collective-permute-start.38 = (bf16[64,1536]{1,0:T(8,128)(2,1)S(1)}, bf16[64,1536]{1,0:T(8,128)(2,1)S(1)}, u32[]{:S(2)}, u32[]{:S(2)}) collective-permute-start(bf16[64,1536]{1,0:T(8,128)(2,1)S(1)} %slice_bitcast_fusion.45), channel_id=1, source_target_pairs={{0,16},{1,17},{2,18},{3,19},{4,20},{5,21},{6,22},{7,23},{8,24},{9,... | collective-permute-start | bytes 589832 | tf_op jit(solution)/shard_map/ppermute | solution.py:37
  219.2 22.1 %collective-permute-start.39 = (bf16[64,1536]{1,0:T(8,128)(2,1)S(1)}, bf16[64,1536]{1,0:T(8,128)(2,1)S(1)}, u32[]{:S(2)}, u32[]{:S(2)}) collective-permute-start(bf16[64,1536]{1,0:T(8,128)(2,1)S(1)} %slice_bitcast_fusion.44), channel_id=1, source_target_pairs={{0,18},{1,19},{2,16},{3,17},{4,22},{5,23},{6,20},{7,21},{8,26},{9,... | collective-permute-start | bytes 589832 | tf_op jit(solution)/shard_map/ppermute | solution.py:37
  233.0 19.0 %collective-permute-start.44 = (bf16[64,1536]{1,0:T(8,128)(2,1)S(1)}, bf16[64,1536]{1,0:T(8,128)(2,1)S(1)}, u32[]{:S(2)}, u32[]{:S(2)}) collective-permute-start(bf16[64,1536]{1,0:T(8,128)(2,1)S(1)} %get-tuple-element.214), channel_id=1, source_target_pairs={{0,8},{1,9},{2,10},{3,11},{4,12},{5,13},{6,14},{7,15},{8,0},{9,1},... | collective-permute-start | bytes 589832 | tf_op jit(solution)/shard_map/ppermute | solution.py:37
  238.4 21.7 %collective-permute-start.45 = (bf16[64,1536]{1,0:T(8,128)(2,1)S(1)}, bf16[64,1536]{1,0:T(8,128)(2,1)S(1)}, u32[]{:S(2)}, u32[]{:S(2)}) collective-permute-start(bf16[64,1536]{1,0:T(8,128)(2,1)S(1)} %get-tuple-element.213), channel_id=1, source_target_pairs={{0,12},{1,13},{2,14},{3,15},{4,8},{5,9},{6,10},{7,11},{8,4},{9,5},... | collective-permute-start | bytes 589832 | tf_op jit(solution)/shard_map/ppermute | solution.py:37
  293.1 17.5 %collective-permute-start.56 = (bf16[64,1536]{1,0:T(8,128)(2,1)S(1)}, bf16[64,1536]{1,0:T(8,128)(2,1)S(1)}, u32[]{:S(2)}, u32[]{:S(2)}) collective-permute-start(bf16[64,1536]{1,0:T(8,128)(2,1)S(1)} %get-tuple-element.77.refs_1_.refs_33_), channel_id=1, source_target_pairs={{0,4},{1,5},{2,6},{3,7},{4,0},{5,1},{6,2},{7,3},{8,12},{9,13},{10,... | collective-permute-start | bytes 589832 | tf_op jit(solution)/shard_map/ppermute | solution.py:37
  293.1 17.5 %collective-permute-start.57 = (bf16[64,1536]{1,0:T(8,128)(2,1)S(1)}, bf16[64,1536]{1,0:T(8,128)(2,1)S(1)}, u32[]{:S(2)}, u32[]{:S(2)}) collective-permute-start(bf16[64,1536]{1,0:T(8,128)(2,1)S(1)} %get-tuple-element.77.refs_1_.refs_33_), channel_id=1, source_target_pairs={{0,8},{1,9},{2,10},{3,11},{4,12},{5,13},{6,14},{7,15},{8,0},{9,1},... | collective-permute-start | bytes 589832 | tf_op jit(solution)/shard_map/ppermute | solution.py:37
  295.8 22.6 %collective-permute-start.58 = (bf16[64,1536]{1,0:T(8,128)(2,1)S(1)}, bf16[64,1536]{1,0:T(8,128)(2,1)S(1)}, u32[]{:S(2)}, u32[]{:S(2)}) collective-permute-start(bf16[64,1536]{1,0:T(8,128)(2,1)S(1)} %get-tuple-element.77.refs_1_.refs_33_), channel_id=1, source_target_pairs={{0,12},{1,13},{2,14},{3,15},{4,8},{5,9},{6,10},{7,11},{8,4},{9,5},... | collective-permute-start | bytes 589832 | tf_op jit(solution)/shard_map/ppermute | solution.py:37
  318.6 16.6 %collective-permute-start.64 = (bf16[3,64,1536]{2,1,0:T(8,128)(2,1)S(1)}, bf16[3,64,1536]{2,1,0:T(8,128)(2,1)S(1)}, u32[]{:S(2)}, u32[]{:S(2)}) collective-permute-start(bf16[3,64,1536]{2,1,0:T(8,128)(2,1)S(1)} %maximum_select_fusion.6.refs_5_.refs_37_), channel_id=1, source_target_pairs={{0,16},{1,17},{2,18},{3,19},{4,20},{5,21},{6,22},{7,23},{8,24},{9,... | collective-permute-start | bytes 1769480 | tf_op jit(solution)/shard_map/ppermute | solution.py:37
  319.9 25.8 %collective-permute-start.66 = (bf16[3,64,1536]{2,1,0:T(8,128)(2,1)S(1)}, bf16[3,64,1536]{2,1,0:T(8,128)(2,1)S(1)}, u32[]{:S(2)}, u32[]{:S(2)}) collective-permute-start(bf16[3,64,1536]{2,1,0:T(8,128)(2,1)S(1)} %maximum_select_fusion.6.refs_5_.refs_37_), channel_id=1, source_target_pairs={{0,18},{1,19},{2,16},{3,17},{4,22},{5,23},{6,20},{7,21},{8,26},{9,... | collective-permute-start | bytes 1769480 | tf_op jit(solution)/shard_map/ppermute | solution.py:37
  323.3 24.9 %collective-permute-start.53 = (bf16[64,1536]{1,0:T(8,128)(2,1)S(1)}, bf16[64,1536]{1,0:T(8,128)(2,1)S(1)}, u32[]{:S(2)}, u32[]{:S(2)}) collective-permute-start(bf16[64,1536]{1,0:T(8,128)(2,1)S(1)} %collective-permute-done.52.refs_3_.refs_35_), channel_id=1, source_target_pairs={{0,1},{1,0},{2,3},{3,2},{4,5},{5,4},{6,7},{7,6},{8,9},{9,8},{10,11... | collective-permute-start | bytes 589832 | tf_op jit(solution)/shard_map/ppermute | solution.py:37
  324.3 27.1 %collective-permute-start.59 = (bf16[3,64,1536]{2,1,0:T(8,128)(2,1)S(1)}, bf16[3,64,1536]{2,1,0:T(8,128)(2,1)S(1)}, u32[]{:S(2)}, u32[]{:S(2)}) collective-permute-start(bf16[3,64,1536]{2,1,0:T(8,128)(2,1)S(1)} %maximum_select_fusion.6.refs_5_.refs_37_), channel_id=1, source_target_pairs={{0,1},{1,0},{2,3},{3,2},{4,5},{5,4},{6,7},{7,6},{8,9},{9,8},{10,11... | collective-permute-start | bytes 1769480 | tf_op jit(solution)/shard_map/ppermute | solution.py:37
  332.1 19.4 %collective-permute-start.61 = (bf16[3,64,1536]{2,1,0:T(8,128)(2,1)S(1)}, bf16[3,64,1536]{2,1,0:T(8,128)(2,1)S(1)}, u32[]{:S(2)}, u32[]{:S(2)}) collective-permute-start(bf16[3,64,1536]{2,1,0:T(8,128)(2,1)S(1)} %collective-permute-done.60.refs_7_.refs_39_), channel_id=1, source_target_pairs={{0,1},{1,0},{2,3},{3,2},{4,5},{5,4},{6,7},{7,6},{8,9},{9,8},{10,11... | collective-permute-start | bytes 1769480 | tf_op jit(solution)/shard_map/ppermute | solution.py:37
  335.1 16.4 %collective-permute-start.65 = (bf16[3,64,1536]{2,1,0:T(8,128)(2,1)S(1)}, bf16[3,64,1536]{2,1,0:T(8,128)(2,1)S(1)}, u32[]{:S(2)}, u32[]{:S(2)}) collective-permute-start(bf16[3,64,1536]{2,1,0:T(8,128)(2,1)S(1)} %collective-permute-done.64.refs_13_.refs_45_), channel_id=1, source_target_pairs={{0,1},{1,0},{2,3},{3,2},{4,5},{5,4},{6,7},{7,6},{8,9},{9,8},{10,11... | collective-permute-start | bytes 1769480 | tf_op jit(solution)/shard_map/ppermute | solution.py:37
  393.6 15.5 %collective-permute-start.73 = (bf16[3,64,1536]{2,1,0:T(8,128)(2,1)S(1)}, bf16[3,64,1536]{2,1,0:T(8,128)(2,1)S(1)}, u32[]{:S(2)}, u32[]{:S(2)}) collective-permute-start(bf16[3,64,1536]{2,1,0:T(8,128)(2,1)S(1)} %slice_bitcast_fusion.7), channel_id=1, source_target_pairs={{0,16},{1,17},{2,18},{3,19},{4,20},{5,21},{6,22},{7,23},{8,24},{9,... | collective-permute-start | bytes 1769480 | tf_op jit(solution)/shard_map/ppermute | solution.py:37
  395.0 26.7 %collective-permute-start.74 = (bf16[3,64,1536]{2,1,0:T(8,128)(2,1)S(1)}, bf16[3,64,1536]{2,1,0:T(8,128)(2,1)S(1)}, u32[]{:S(2)}, u32[]{:S(2)}) collective-permute-start(bf16[3,64,1536]{2,1,0:T(8,128)(2,1)S(1)} %slice_bitcast_fusion.6), channel_id=1, source_target_pairs={{0,18},{1,19},{2,16},{3,17},{4,22},{5,23},{6,20},{7,21},{8,26},{9,... | collective-permute-start | bytes 1769480 | tf_op jit(solution)/shard_map/ppermute | solution.py:37
  396.4 28.5 %collective-permute-start.69 = (bf16[64,1536]{1,0:T(8,128)(2,1)S(1)}, bf16[64,1536]{1,0:T(8,128)(2,1)S(1)}, u32[]{:S(2)}, u32[]{:S(2)}) collective-permute-start(bf16[64,1536]{1,0:T(8,128)(2,1)S(1)} %slice_bitcast_fusion.37), channel_id=1, source_target_pairs={{0,2},{1,3},{2,0},{3,1},{4,6},{5,7},{6,4},{7,5},{8,10},{9,11},{10,... | collective-permute-start | bytes 589832 | tf_op jit(solution)/shard_map/ppermute | solution.py:37
  396.9 28.7 %collective-permute-start.70 = (bf16[64,1536]{1,0:T(8,128)(2,1)S(1)}, bf16[64,1536]{1,0:T(8,128)(2,1)S(1)}, u32[]{:S(2)}, u32[]{:S(2)}) collective-permute-start(bf16[64,1536]{1,0:T(8,128)(2,1)S(1)} %slice_bitcast_fusion.36), channel_id=1, source_target_pairs={{0,16},{1,17},{2,18},{3,19},{4,20},{5,21},{6,22},{7,23},{8,24},{9,... | collective-permute-start | bytes 589832 | tf_op jit(solution)/shard_map/ppermute | solution.py:37
  408.0 22.1 %collective-permute-start.71 = (bf16[64,1536]{1,0:T(8,128)(2,1)S(1)}, bf16[64,1536]{1,0:T(8,128)(2,1)S(1)}, u32[]{:S(2)}, u32[]{:S(2)}) collective-permute-start(bf16[64,1536]{1,0:T(8,128)(2,1)S(1)} %slice_bitcast_fusion.35), channel_id=1, source_target_pairs={{0,18},{1,19},{2,16},{3,17},{4,22},{5,23},{6,20},{7,21},{8,26},{9,... | collective-permute-start | bytes 589832 | tf_op jit(solution)/shard_map/ppermute | solution.py:37
  424.9 15.9 %collective-permute-start.77 = (bf16[64,1536]{1,0:T(8,128)(2,1)S(1)}, bf16[64,1536]{1,0:T(8,128)(2,1)S(1)}, u32[]{:S(2)}, u32[]{:S(2)}) collective-permute-start(bf16[64,1536]{1,0:T(8,128)(2,1)S(1)} %get-tuple-element.210), channel_id=1, source_target_pairs={{0,12},{1,13},{2,14},{3,15},{4,8},{5,9},{6,10},{7,11},{8,4},{9,5},... | collective-permute-start | bytes 589832 | tf_op jit(solution)/shard_map/ppermute | solution.py:37
  483.5 301.6 %reduce-scatter.5.cloned.1.call-start = ((), (), s32[]{:S(2)}) async-start(), calls=%async_computation.4 | async-start | bytes 1966080 | tf_op jit(solution)/shard_map/reduce_scatter | solution.py:850
  485.4 25.2 %collective-permute-start.92 = (bf16[64,1536]{1,0:T(8,128)(2,1)}, bf16[64,1536]{1,0:T(8,128)(2,1)S(1)}, u32[]{:S(2)}, u32[]{:S(2)}) collective-permute-start(bf16[64,1536]{1,0:T(8,128)(2,1)} %get-tuple-element.89.refs_0_.refs_17_), channel_id=1, source_target_pairs={{0,12},{1,13},{2,14},{3,15},{4,8},{5,9},{6,10},{7,11},{8,4},{9,5},... | collective-permute-start | bytes 589832 | tf_op jit(solution)/shard_map/ppermute | solution.py:37
  511.3 29.2 %collective-permute-start.94 = (bf16[3,64,1536]{2,1,0:T(8,128)(2,1)S(1)}, bf16[3,64,1536]{2,1,0:T(8,128)(2,1)S(1)}, u32[]{:S(2)}, u32[]{:S(2)}) collective-permute-start(bf16[3,64,1536]{2,1,0:T(8,128)(2,1)S(1)} %maximum_select_fusion.7.refs_4_.refs_21_), channel_id=1, source_target_pairs={{0,2},{1,3},{2,0},{3,1},{4,6},{5,7},{6,4},{7,5},{8,10},{9,11},{10,... | collective-permute-start | bytes 1769480 | tf_op jit(solution)/shard_map/ppermute | solution.py:37
  513.5 27.1 %collective-permute-start.98 = (bf16[3,64,1536]{2,1,0:T(8,128)(2,1)S(1)}, bf16[3,64,1536]{2,1,0:T(8,128)(2,1)S(1)}, u32[]{:S(2)}, u32[]{:S(2)}) collective-permute-start(bf16[3,64,1536]{2,1,0:T(8,128)(2,1)S(1)} %maximum_select_fusion.7.refs_4_.refs_21_), channel_id=1, source_target_pairs={{0,16},{1,17},{2,18},{3,19},{4,20},{5,21},{6,22},{7,23},{8,24},{9,... | collective-permute-start | bytes 1769480 | tf_op jit(solution)/shard_map/ppermute | solution.py:37
  523.5 30.2 %collective-permute-start.93 = (bf16[3,64,1536]{2,1,0:T(8,128)(2,1)S(1)}, bf16[3,64,1536]{2,1,0:T(8,128)(2,1)S(1)}, u32[]{:S(2)}, u32[]{:S(2)}) collective-permute-start(bf16[3,64,1536]{2,1,0:T(8,128)(2,1)S(1)} %maximum_select_fusion.7.refs_4_.refs_21_), channel_id=1, source_target_pairs={{0,1},{1,0},{2,3},{3,2},{4,5},{5,4},{6,7},{7,6},{8,9},{9,8},{10,11... | collective-permute-start | bytes 1769480 | tf_op jit(solution)/shard_map/ppermute | solution.py:37
  525.0 25.3 %collective-permute-start.86 = (bf16[64,1536]{1,0:T(8,128)(2,1)S(1)}, bf16[64,1536]{1,0:T(8,128)(2,1)S(1)}, u32[]{:S(2)}, u32[]{:S(2)}) collective-permute-start(bf16[64,1536]{1,0:T(8,128)(2,1)S(1)} %collective-permute-done.85.refs_2_.refs_19_), channel_id=1, source_target_pairs={{0,1},{1,0},{2,3},{3,2},{4,5},{5,4},{6,7},{7,6},{8,9},{9,8},{10,11... | collective-permute-start | bytes 589832 | tf_op jit(solution)/shard_map/ppermute | solution.py:37
  525.4 28.3 %collective-permute-start.101 = (bf16[3,64,1536]{2,1,0:T(8,128)(2,1)S(1)}, bf16[3,64,1536]{2,1,0:T(8,128)(2,1)S(1)}, u32[]{:S(2)}, u32[]{:S(2)}) collective-permute-start(bf16[3,64,1536]{2,1,0:T(8,128)(2,1)S(1)} %collective-permute-done.100.refs_14_.refs_31_), channel_id=1, source_target_pairs={{0,1},{1,0},{2,3},{3,2},{4,5},{5,4},{6,7},{7,6},{8,9},{9,8},{10,11... | collective-permute-start | bytes 1769480 | tf_op jit(solution)/shard_map/ppermute | solution.py:37
  595.0 27.2 %collective-permute-start.106 = (bf16[3,64,1536]{2,1,0:T(8,128)(2,1)S(1)}, bf16[3,64,1536]{2,1,0:T(8,128)(2,1)S(1)}, u32[]{:S(2)}, u32[]{:S(2)}) collective-permute-start(bf16[3,64,1536]{2,1,0:T(8,128)(2,1)S(1)} %slice_bitcast_fusion.4), channel_id=1, source_target_pairs={{0,2},{1,3},{2,0},{3,1},{4,6},{5,7},{6,4},{7,5},{8,10},{9,11},{10,... | collective-permute-start | bytes 1769480 | tf_op jit(solution)/shard_map/ppermute | solution.py:37
  595.5 26.7 %collective-permute-start.107 = (bf16[3,64,1536]{2,1,0:T(8,128)(2,1)S(1)}, bf16[3,64,1536]{2,1,0:T(8,128)(2,1)S(1)}, u32[]{:S(2)}, u32[]{:S(2)}) collective-permute-start(bf16[3,64,1536]{2,1,0:T(8,128)(2,1)S(1)} %slice_bitcast_fusion.3), channel_id=1, source_target_pairs={{0,16},{1,17},{2,18},{3,19},{4,20},{5,21},{6,22},{7,23},{8,24},{9,... | collective-permute-start | bytes 1769480 | tf_op jit(solution)/shard_map/ppermute | solution.py:37
  595.9 27.2 %collective-permute-start.108 = (bf16[3,64,1536]{2,1,0:T(8,128)(2,1)S(1)}, bf16[3,64,1536]{2,1,0:T(8,128)(2,1)S(1)}, u32[]{:S(2)}, u32[]{:S(2)}) collective-permute-start(bf16[3,64,1536]{2,1,0:T(8,128)(2,1)S(1)} %slice_bitcast_fusion.2), channel_id=1, source_target_pairs={{0,18},{1,19},{2,16},{3,17},{4,22},{5,23},{6,20},{7,21},{8,26},{9,... | collective-permute-start | bytes 1769480 | tf_op jit(solution)/shard_map/ppermute | solution.py:37
  597.7 28.8 %collective-permute-start.103 = (bf16[64,1536]{1,0:T(8,128)(2,1)S(1)}, bf16[64,1536]{1,0:T(8,128)(2,1)S(1)}, u32[]{:S(2)}, u32[]{:S(2)}) collective-permute-start(bf16[64,1536]{1,0:T(8,128)(2,1)S(1)} %slice_bitcast_fusion.28), channel_id=1, source_target_pairs={{0,2},{1,3},{2,0},{3,1},{4,6},{5,7},{6,4},{7,5},{8,10},{9,11},{10,... | collective-permute-start | bytes 589832 | tf_op jit(solution)/shard_map/ppermute | solution.py:37
  598.2 28.5 %collective-permute-start.104 = (bf16[64,1536]{1,0:T(8,128)(2,1)S(1)}, bf16[64,1536]{1,0:T(8,128)(2,1)S(1)}, u32[]{:S(2)}, u32[]{:S(2)}) collective-permute-start(bf16[64,1536]{1,0:T(8,128)(2,1)S(1)} %slice_bitcast_fusion.27), channel_id=1, source_target_pairs={{0,16},{1,17},{2,18},{3,19},{4,20},{5,21},{6,22},{7,23},{8,24},{9,... | collective-permute-start | bytes 589832 | tf_op jit(solution)/shard_map/ppermute | solution.py:37
  626.4 16.1 %collective-permute-start.111 = (bf16[64,1536]{1,0:T(8,128)(2,1)S(1)}, bf16[64,1536]{1,0:T(8,128)(2,1)S(1)}, u32[]{:S(2)}, u32[]{:S(2)}) collective-permute-start(bf16[64,1536]{1,0:T(8,128)(2,1)S(1)} %get-tuple-element.207), channel_id=1, source_target_pairs={{0,12},{1,13},{2,14},{3,15},{4,8},{5,9},{6,10},{7,11},{8,4},{9,5},... | collective-permute-start | bytes 589832 | tf_op jit(solution)/shard_map/ppermute | solution.py:37
  667.1 35.2 %collective-permute-start.117 = (bf16[2,4,64,1536]{3,2,0,1:T(8,128)(2,1)S(1)}, bf16[2,4,64,1536]{3,2,0,1:T(8,128)(2,1)S(1)}, u32[]{:S(2)}, u32[]{:S(2)}) collective-permute-start(bf16[2,4,64,1536]{3,2,0,1:T(8,128)(2,1)S(1)} %maximum_select_fusion.1), channel_id=1, source_target_pairs={{0,2},{1,3},{2,0},{3,1},{4,6},{5,7},{6,4},{7,5},{8,10},{9,11},{10,... | collective-permute-start | bytes 4718600 | tf_op jit(solution)/shard_map/ppermute | solution.py:37
  670.3 30.5 %collective-permute-start.120 = (bf16[4,192,896]{2,1,0:T(8,128)(2,1)S(1)}, bf16[4,192,896]{2,1,0:T(8,128)(2,1)S(1)}, u32[]{:S(2)}, u32[]{:S(2)}) collective-permute-start(bf16[4,192,896]{2,1,0:T(8,128)(2,1)S(1)} %get-tuple-element.115), channel_id=1, source_target_pairs={{0,16},{1,17},{2,18},{3,19},{4,20},{5,21},{6,22},{7,23},{8,24},{9,... | collective-permute-start | bytes 4128776 | tf_op jit(solution)/shard_map/ppermute | solution.py:37
  673.8 36.9 %collective-permute-start.118 = (bf16[2,64,1536]{2,1,0:T(8,128)(2,1)}, bf16[2,64,1536]{2,1,0:T(8,128)(2,1)S(1)}, u32[]{:S(2)}, u32[]{:S(2)}) collective-permute-start(bf16[2,64,1536]{2,1,0:T(8,128)(2,1)} %pad_maximum_fusion.3), channel_id=1, source_target_pairs={{0,16},{1,17},{2,18},{3,19},{4,20},{5,21},{6,22},{7,23},{8,24},{9,... | collective-permute-start | bytes 1179656 | tf_op jit(solution)/shard_map/ppermute | solution.py:37
  674.2 30.6 %collective-permute-start.122 = (f32[4,1536]{1,0:T(4,128)S(1)}, f32[4,1536]{1,0:T(4,128)S(1)}, u32[]{:S(2)}, u32[]{:S(2)}) collective-permute-start(f32[4,1536]{1,0:T(4,128)S(1)} %fusion.43), channel_id=1, source_target_pairs={{0,2},{1,3},{2,0},{3,1},{4,6},{5,7},{6,4},{7,5},{8,10},{9,11},{10,... | collective-permute-start | bytes 73736 | tf_op jit(solution)/shard_map/ppermute | solution.py:37
  707.9 15.0 %collective-permute-start.123 = (bf16[208,896]{1,0:T(8,128)(2,1)S(1)}, bf16[208,896]{1,0:T(8,128)(2,1)S(1)}, u32[]{:S(2)}, u32[]{:S(2)}) collective-permute-start(bf16[208,896]{1,0:T(8,128)(2,1)S(1)} %get-tuple-element.197), channel_id=1, source_target_pairs={{0,4},{1,5},{2,6},{3,7},{4,0},{5,1},{6,2},{7,3},{8,12},{9,13},{10,... | collective-permute-start | bytes 1118216 | tf_op jit(solution)/shard_map/ppermute | solution.py:37
  708.0 18.8 %collective-permute-start.124 = (bf16[208,896]{1,0:T(8,128)(2,1)S(1)}, bf16[208,896]{1,0:T(8,128)(2,1)S(1)}, u32[]{:S(2)}, u32[]{:S(2)}) collective-permute-start(bf16[208,896]{1,0:T(8,128)(2,1)S(1)} %get-tuple-element.199), channel_id=1, source_target_pairs={{0,8},{1,9},{2,10},{3,11},{4,12},{5,13},{6,14},{7,15},{8,0},{9,1},... | collective-permute-start | bytes 1118216 | tf_op jit(solution)/shard_map/ppermute | solution.py:37
  708.8 56.6 %collective-permute-start.125 = (bf16[208,896]{1,0:T(8,128)(2,1)S(1)}, bf16[208,896]{1,0:T(8,128)(2,1)S(1)}, u32[]{:S(2)}, u32[]{:S(2)}) collective-permute-start(bf16[208,896]{1,0:T(8,128)(2,1)S(1)} %get-tuple-element.198), channel_id=1, source_target_pairs={{0,12},{1,13},{2,14},{3,15},{4,8},{5,9},{6,10},{7,11},{8,4},{9,5},... | collective-permute-start | bytes 1118216 | tf_op jit(solution)/shard_map/ppermute | solution.py:37
  (201 other events, 2627.8 us)
Sparse Core Ops, SparseCore 0:
  27.3 61.5 all-gather.7
  156.3 63.8 all-gather.9
  222.5 95.4 all-gather.5
  483.6 86.0 reduce-scatter.2
  705.0 63.3 reduce-scatter.4

commit v5 on v4

--- a/solution.py
+++ b/solution.py
@@ -814,8 +814,6 @@
         (dmid, d, moe_gain_sum), _ = norm_back(mid, layer_gain[l][1], g, terms)
         d_blocks = over_tensor(d)
         extra = core_sums(*beside(d)) if beside is not None else None
-        if extra is not None:
-            d_blocks[3] = after(d_blocks[3], extra[1][0][0])
         keep, send, dq, kv_send, d_all = attn_bwd(d_blocks, saved, weights)
         args = (a_all, d_all, saved, dq, move(kv_send, tensor=1))
         mine, theirs = halves_grad(

time: 804 us -> 810 us (level)
    unnamed x235 -> x231, local copies, waits for them, and re-layouts: 20.3 us -> 20 us
  transfers between devices with their start and end apart: 133 -> 133, of which waited for: 77 -> 78; matrix products, arithmetic and copies ran while one was open for 4% -> 5% of each run, Pallas kernels for 11% -> 12%
where the time goes in v5:
time: 810 us; the launch traced here: 803 us
  waiting for transfers between devices  402 us (50%)
  starting transfers between devices  164 us (20%)
  Pallas kernels  141 us (17%)
  local copies, waits for them, and re-layouts  37.2 us (5%)
  other arithmetic  35 us (4%)
  between operations  23.5 us (3%)
    ppermute x126, waiting for transfers between devices, move(): return lax.ppermute(value, ('section', 'dp', 'tensor'), pairs)  361 us
    ppermute x126, starting transfers between devices, move(): return lax.ppermute(value, ('section', 'dp', 'tensor'), pairs)  153 us
    pallas_call x19, Pallas kernels, call(): pl.pallas_call(body, out_shape=list(outs) + [jax.ShapeDtypeStruct(h.shape...  141 us
    all_gather x2, waiting for transfers between devices, gather_weights(): lax.all_gather(seed[None, None], ('section', 'dp'), axis=0, tiled=True)  35.5 us
    unnamed x231, local copies, waits for them, and re-layouts  20 us
  transfers between devices with their start and end apart: 133, of which 78 were waited for; matrix products, arithmetic and copies ran while one was open for 5% of the time, Pallas kernels for 12%

profile of v5, /device:TPU:9, one launch (start us, length us, event | category | flops | bytes accessed | tf_op | source)
XLA Modules:
  0.0 802.9 jit_solution(10544941189902448219)
XLA Ops:
  7.2 3.7 collective-permute-start.10
  53.4 35.5 %all-gather.8.cloned.1.call-done = bf16[1536,1024]{1,0:T(8,128)(2,1)} async-done(((bf16[192,1024]{1,0:T(8,128)(2,1)}), bf16[1536,1024]{1,0:T(8,128)(2,1)}) %all-gather.8.cloned.1.call-update) | async-done | bytes 3145744 | tf_op jit(solution)/shard_map/all_gather | solution.py:680
  90.8 4.1 attn_fwd.2
  100.8 4.5 collective-permute-done.17.refs_3_
  114.7 4.2 collective-permute-done.22.refs_10_.refs_11_
  119.9 8.2 %collective-permute-done.26 = bf16[64,1536]{1,0:T(8,128)(2,1)S(1)} collective-permute-done((bf16[64,1536]{1,0:T(8,128)(2,1)S(1)}, bf16[64,1536]{1,0:T(8,128)(2,1)S(1)}, u32[]{:S(2)}, u32[]{:S(2)}) %collective-permute-start.26) | collective-permute-done | bytes 196640 | tf_op jit(solution)/shard_map/ppermute | solution.py:37
  130.9 9.7 %collective-permute-done.28.refs_6_.refs_7_ = bf16[3,64,1536]{2,1,0:T(8,128)(2,1)S(1)} collective-permute-done((bf16[3,64,1536]{2,1,0:T(8,128)(2,1)S(1)}, bf16[3,64,1536]{2,1,0:T(8,128)(2,1)S(1)}, u32[]{:S(2)}, u32[]{:S(2)}) %collective-permute-start.28) | collective-permute-done | bytes 589856 | tf_op jit(solution)/shard_map/ppermute | solution.py:37
  140.7 13.4 %collective-permute-done.34.refs_14_.refs_15_ = bf16[3,64,1536]{2,1,0:T(8,128)(2,1)S(1)} collective-permute-done((bf16[3,64,1536]{2,1,0:T(8,128)(2,1)S(1)}, bf16[3,64,1536]{2,1,0:T(8,128)(2,1)S(1)}, u32[]{:S(2)}, u32[]{:S(2)}) %collective-permute-start.34) | collective-permute-done | bytes 589856 | tf_op jit(solution)/shard_map/ppermute | solution.py:37
  156.2 3.7 collective-permute-start.18
  168.5 26.5 %moe_fwd.1 = (f32[4,640,384]{2,1,0:T(8,128)}, bf16[2,8,64,1536]{3,2,1,0:T(8,128)(2,1)}, bf16[2,8,64,1536]{3,2,1,0:T(8,128)(2,1)}) custom-call(bf16[64,1536]{1,0:T(8,128)(2,1)S(1)} %get-tuple-element.69.refs_0_.refs_1_, bf16[64,1536]{1,0:T(8,128)(2,1)S(1)} %collective-permute-done.18.refs_1_.refs_2_, ...), custom_call_target="tpu_custom_call" | custom-call | flops 4000000000 | bytes 12582912 | tf_op jit(solution)/shard_map/moe_fwd/pallas_call | solution.py:497
  197.4 3.8 collective-permute-done.36
  208.0 11.2 %collective-permute-done.40 = bf16[3,64,1536]{2,1,0:T(8,128)(2,1)S(1)} collective-permute-done((bf16[3,64,1536]{2,1,0:T(8,128)(2,1)S(1)}, bf16[3,64,1536]{2,1,0:T(8,128)(2,1)S(1)}, u32[]{:S(2)}, u32[]{:S(2)}) %collective-permute-start.40) | collective-permute-done | bytes 589856 | tf_op jit(solution)/shard_map/ppermute | solution.py:37
  219.5 13.2 %collective-permute-done.42 = bf16[3,64,1536]{2,1,0:T(8,128)(2,1)S(1)} collective-permute-done((bf16[3,64,1536]{2,1,0:T(8,128)(2,1)S(1)}, bf16[3,64,1536]{2,1,0:T(8,128)(2,1)S(1)}, u32[]{:S(2)}, u32[]{:S(2)}) %collective-permute-start.42) | collective-permute-done | bytes 589856 | tf_op jit(solution)/shard_map/ppermute | solution.py:37
  241.2 4.6 collective-permute-done.43
  245.8 6.0 collective-permute-done.44
  251.8 8.5 %collective-permute-done.45 = bf16[64,1536]{1,0:T(8,128)(2,1)S(1)} collective-permute-done((bf16[64,1536]{1,0:T(8,128)(2,1)S(1)}, bf16[64,1536]{1,0:T(8,128)(2,1)S(1)}, u32[]{:S(2)}, u32[]{:S(2)}) %collective-permute-start.45) | collective-permute-done | bytes 196640 | tf_op jit(solution)/shard_map/ppermute | solution.py:37
  272.8 4.5 attn_fwd.3
  280.6 9.7 %collective-permute-done.50.refs_3_ = bf16[64,1536]{1,0:T(8,128)(2,1)S(1)} collective-permute-done((bf16[64,1536]{1,0:T(8,128)(2,1)S(1)}, bf16[64,1536]{1,0:T(8,128)(2,1)S(1)}, u32[]{:S(2)}, u32[]{:S(2)}) %collective-permute-start.50) | collective-permute-done | bytes 196640 | tf_op jit(solution)/shard_map/ppermute | solution.py:37
  301.0 9.5 %collective-permute-done.56 = bf16[64,1536]{1,0:T(8,128)(2,1)S(1)} collective-permute-done((bf16[64,1536]{1,0:T(8,128)(2,1)S(1)}, bf16[64,1536]{1,0:T(8,128)(2,1)S(1)}, u32[]{:S(2)}, u32[]{:S(2)}) %collective-permute-start.56) | collective-permute-done | bytes 196640 | tf_op jit(solution)/shard_map/ppermute | solution.py:37
  310.6 7.8 collective-permute-done.58
  324.7 7.4 collective-permute-done.60.refs_7_.refs_39_
  336.6 9.1 %collective-permute-done.66.refs_15_.refs_47_ = bf16[3,64,1536]{2,1,0:T(8,128)(2,1)S(1)} collective-permute-done((bf16[3,64,1536]{2,1,0:T(8,128)(2,1)S(1)}, bf16[3,64,1536]{2,1,0:T(8,128)(2,1)S(1)}, u32[]{:S(2)}, u32[]{:S(2)}) %collective-permute-start.66) | collective-permute-done | bytes 589856 | tf_op jit(solution)/shard_map/ppermute | solution.py:37
  353.4 31.7 %moe_turn.1 = (bf16[4,640,192]{2,1,0:T(8,128)(2,1)}, bf16[4,640,384]{2,1,0:T(8,128)(2,1)}, bf16[2,8,64,1536]{3,2,1,0:T(8,128)(2,1)}, bf16[2,8,64,1536]{3,2,1,0:T(8,128)(2,1)}) custom-call(s32[4]{0:T(128)} %copy-done.45, bf16[64,1536]{1,0:T(8,128)(2,1)} %copy-done.69, bf16[64,1536]{1,0:T(8,128)(2,1)} %copy-done.71, bf16[64,1536]{1,0:T(8,128)(2,1)} %copy-done.31, ...), custom_call_target="tpu_custom_call" | custom-call | flops 8000000000 | bytes 25165824 | tf_op jit(solution)/shard_map/moe_turn/pallas_call | solution.py:497
  385.6 5.5 collective-permute-done.68
  398.1 10.0 %collective-permute-done.72 = bf16[3,64,1536]{2,1,0:T(8,128)(2,1)S(1)} collective-permute-done((bf16[3,64,1536]{2,1,0:T(8,128)(2,1)S(1)}, bf16[3,64,1536]{2,1,0:T(8,128)(2,1)S(1)}, u32[]{:S(2)}, u32[]{:S(2)}) %collective-permute-start.72) | collective-permute-done | bytes 589856 | tf_op jit(solution)/shard_map/ppermute | solution.py:37
  409.1 12.6 %collective-permute-done.74 = bf16[3,64,1536]{2,1,0:T(8,128)(2,1)S(1)} collective-permute-done((bf16[3,64,1536]{2,1,0:T(8,128)(2,1)S(1)}, bf16[3,64,1536]{2,1,0:T(8,128)(2,1)S(1)}, u32[]{:S(2)}, u32[]{:S(2)}) %collective-permute-start.74) | collective-permute-done | bytes 589856 | tf_op jit(solution)/shard_map/ppermute | solution.py:37
  425.7 4.5 collective-permute-done.71
  430.4 10.4 %collective-permute-done.77 = bf16[64,1536]{1,0:T(8,128)(2,1)S(1)} collective-permute-done((bf16[64,1536]{1,0:T(8,128)(2,1)S(1)}, bf16[64,1536]{1,0:T(8,128)(2,1)S(1)}, u32[]{:S(2)}, u32[]{:S(2)}) %collective-permute-start.77) | collective-permute-done | bytes 196640 | tf_op jit(solution)/shard_map/ppermute | solution.py:37
  450.3 5.1 attn_bwd.2
  476.9 3.8 collective-permute-done.91
  480.7 17.9 %collective-permute-done.92 = bf16[64,1536]{1,0:T(8,128)(2,1)S(1)} collective-permute-done((bf16[64,1536]{1,0:T(8,128)(2,1)}, bf16[64,1536]{1,0:T(8,128)(2,1)S(1)}, u32[]{:S(2)}, u32[]{:S(2)}) %collective-permute-start.92) | collective-permute-done | bytes 196640 | tf_op jit(solution)/shard_map/ppermute | solution.py:37
  501.8 9.7 %collective-permute-start.84 = (bf16[64,1536]{1,0:T(8,128)(2,1)}, bf16[64,1536]{1,0:T(8,128)(2,1)S(1)}, u32[]{:S(2)}, u32[]{:S(2)}) collective-permute-start(bf16[64,1536]{1,0:T(8,128)(2,1)} %get-tuple-element.89.refs_0_.refs_17_), channel_id=1, source_target_pairs={{0,1},{1,0},{2,3},{3,2},{4,5},{5,4},{6,7},{7,6},{8,9},{9,8},{10,11... | collective-permute-start | bytes 589832 | tf_op jit(solution)/shard_map/ppermute | solution.py:37
  513.4 15.3 %collective-permute-start.101 = (bf16[3,64,1536]{2,1,0:T(8,128)(2,1)S(1)}, bf16[3,64,1536]{2,1,0:T(8,128)(2,1)S(1)}, u32[]{:S(2)}, u32[]{:S(2)}) collective-permute-start(bf16[3,64,1536]{2,1,0:T(8,128)(2,1)S(1)} %collective-permute-done.100.refs_14_.refs_31_), channel_id=1, source_target_pairs={{0,1},{1,0},{2,3},{3,2},{4,5},{5,4},{6,7},{7,6},{8,9},{9,8},{10,11... | collective-permute-start | bytes 1769480 | tf_op jit(solution)/shard_map/ppermute | solution.py:37
  528.8 9.7 %collective-permute-start.99 = (bf16[3,64,1536]{2,1,0:T(8,128)(2,1)S(1)}, bf16[3,64,1536]{2,1,0:T(8,128)(2,1)S(1)}, u32[]{:S(2)}, u32[]{:S(2)}) collective-permute-start(bf16[3,64,1536]{2,1,0:T(8,128)(2,1)S(1)} %collective-permute-done.98.refs_12_.refs_29_), channel_id=1, source_target_pairs={{0,1},{1,0},{2,3},{3,2},{4,5},{5,4},{6,7},{7,6},{8,9},{9,8},{10,11... | collective-permute-start | bytes 1769480 | tf_op jit(solution)/shard_map/ppermute | solution.py:37
  543.2 28.1 %moe_bwd.1 = (bf16[4,640,192]{2,1,0:T(8,128)(2,1)}, bf16[4,640,384]{2,1,0:T(8,128)(2,1)}, bf16[2,8,64,1536]{3,2,1,0:T(8,128)(2,1)}, bf16[2,8,64,1536]{3,2,1,0:T(8,128)(2,1)}) custom-call(bf16[64,1536]{1,0:T(8,128)(2,1)} %get-tuple-element.89.refs_0_.refs_17_, bf16[64,1536]{1,0:T(8,128)(2,1)S(1)} %collective-permute-done.84.refs_1_.refs_18_, ...), custom_call_target="tpu_custom_call" | custom-call | flops 4000000000 | bytes 12582912 | tf_op jit(solution)/shard_map/moe_bwd/pallas_call | solution.py:497
  588.8 22.1 %moe_wgrad.1 = (f32[4,1536,384]{2,1,0:T(8,128)}, f32[4,192,1536]{2,1,0:T(8,128)}) custom-call(s32[4]{0:T(128)S(1)} %get-tuple-element.247.refs_0_, bf16[64,1536]{1,0:T(8,128)(2,1)S(1)} %copy-done.60, bf16[64,1536]{1,0:T(8,128)(2,1)S(1)} %copy-done.62, bf16[64,1536]{1,0:T(8,128)(2,1)S(1)} %copy-done.38, bf16[64,1536]{1,0:T(8,128)(2,1)S(1)} %copy-done.64, ...), custom_call_target="tpu_custom_call" | custom-call | flops 10000000000 | bytes 31457280 | tf_op jit(solution)/shard_map/moe_wgrad/pallas_call | solution.py:497
  610.9 6.0 moe_out.1
  626.2 4.0 collective-permute-done.109
  633.4 9.6 %collective-permute-done.111 = bf16[64,1536]{1,0:T(8,128)(2,1)S(1)} collective-permute-done((bf16[64,1536]{1,0:T(8,128)(2,1)S(1)}, bf16[64,1536]{1,0:T(8,128)(2,1)S(1)}, u32[]{:S(2)}, u32[]{:S(2)}) %collective-permute-start.111) | collective-permute-done | bytes 196640 | tf_op jit(solution)/shard_map/ppermute | solution.py:37
  653.8 5.0 attn_bwd.3
  662.9 4.9 collective-permute-done.116.refs_4_
  668.8 3.7 slice_add_fusion.7
  681.5 26.1 %collective-permute-done.120 = bf16[4,192,896]{2,1,0:T(8,128)(2,1)S(1)} collective-permute-done((bf16[4,192,896]{2,1,0:T(8,128)(2,1)S(1)}, bf16[4,192,896]{2,1,0:T(8,128)(2,1)S(1)}, u32[]{:S(2)}, u32[]{:S(2)}) %collective-permute-start.120) | collective-permute-done | bytes 1376288 | tf_op jit(solution)/shard_map/ppermute | solution.py:37
  717.5 11.9 %collective-permute-done.123 = bf16[208,896]{1,0:T(8,128)(2,1)S(1)} collective-permute-done((bf16[208,896]{1,0:T(8,128)(2,1)S(1)}, bf16[208,896]{1,0:T(8,128)(2,1)S(1)}, u32[]{:S(2)}, u32[]{:S(2)}) %collective-permute-start.123) | collective-permute-done | bytes 372768 | tf_op jit(solution)/shard_map/ppermute | solution.py:37
  729.4 3.7 collective-permute-done.124
  733.1 39.3 %collective-permute-done.125 = bf16[208,896]{1,0:T(8,128)(2,1)S(1)} collective-permute-done((bf16[208,896]{1,0:T(8,128)(2,1)S(1)}, bf16[208,896]{1,0:T(8,128)(2,1)S(1)}, u32[]{:S(2)}, u32[]{:S(2)}) %collective-permute-start.125) | collective-permute-done | bytes 372768 | tf_op jit(solution)/shard_map/ppermute | solution.py:37
  774.7 4.9 collective-permute-done.126
  781.7 7.1 collective-permute-start.127
  (629 shorter events, 257.9 us)
Async XLA Ops:
  7.2 81.7 %all-gather.8.cloned.1.call-start = ((), (), s32[]{:S(2)}) async-start(), calls=%async_computation.5 | async-start | bytes 3538944 | tf_op jit(solution)/shard_map/all_gather | solution.py:680
  27.2 243.6 %all-gather.10.cloned.1.call-start = ((), (), s32[]{:S(2)}) async-start(), calls=%async_computation.6 | async-start | bytes 3538944 | tf_op jit(solution)/shard_map/all_gather | solution.py:680
  111.3 16.7 %collective-permute-start.26 = (bf16[64,1536]{1,0:T(8,128)(2,1)S(1)}, bf16[64,1536]{1,0:T(8,128)(2,1)S(1)}, u32[]{:S(2)}, u32[]{:S(2)}) collective-permute-start(bf16[64,1536]{1,0:T(8,128)(2,1)S(1)} %get-tuple-element.69.refs_0_.refs_1_), channel_id=1, source_target_pairs={{0,12},{1,13},{2,14},{3,15},{4,8},{5,9},{6,10},{7,11},{8,4},{9,5},... | collective-permute-start | bytes 589832 | tf_op jit(solution)/shard_map/ppermute | solution.py:37
  128.8 25.3 %collective-permute-start.34 = (bf16[3,64,1536]{2,1,0:T(8,128)(2,1)S(1)}, bf16[3,64,1536]{2,1,0:T(8,128)(2,1)S(1)}, u32[]{:S(2)}, u32[]{:S(2)}) collective-permute-start(bf16[3,64,1536]{2,1,0:T(8,128)(2,1)S(1)} %maximum_select_fusion.5.refs_4_.refs_5_), channel_id=1, source_target_pairs={{0,18},{1,19},{2,16},{3,17},{4,22},{5,23},{6,20},{7,21},{8,26},{9,... | collective-permute-start | bytes 1769480 | tf_op jit(solution)/shard_map/ppermute | solution.py:37
  156.2 197.2 %all-gather.6.cloned.1.call-start = ((), (), s32[]{:S(2)}) async-start(), calls=%async_computation.2 | async-start | bytes 6684672 | tf_op jit(solution)/shard_map/all_gather | solution.py:792
  197.4 376.9 %reduce-scatter.3.cloned.1.call-start = ((), (), s32[]{:S(2)}) async-start(), calls=%async_computation.3 | async-start | bytes 3096576 | tf_op jit(solution)/shard_map/reduce_scatter | solution.py:834
  204.4 14.8 %collective-permute-start.40 = (bf16[3,64,1536]{2,1,0:T(8,128)(2,1)S(1)}, bf16[3,64,1536]{2,1,0:T(8,128)(2,1)S(1)}, u32[]{:S(2)}, u32[]{:S(2)}) collective-permute-start(bf16[3,64,1536]{2,1,0:T(8,128)(2,1)S(1)} %slice_bitcast_fusion.12), channel_id=1, source_target_pairs={{0,2},{1,3},{2,0},{3,1},{4,6},{5,7},{6,4},{7,5},{8,10},{9,11},{10,... | collective-permute-start | bytes 1769480 | tf_op jit(solution)/shard_map/ppermute | solution.py:37
  205.1 27.6 %collective-permute-start.42 = (bf16[3,64,1536]{2,1,0:T(8,128)(2,1)S(1)}, bf16[3,64,1536]{2,1,0:T(8,128)(2,1)S(1)}, u32[]{:S(2)}, u32[]{:S(2)}) collective-permute-start(bf16[3,64,1536]{2,1,0:T(8,128)(2,1)S(1)} %slice_bitcast_fusion.10), channel_id=1, source_target_pairs={{0,18},{1,19},{2,16},{3,17},{4,22},{5,23},{6,20},{7,21},{8,26},{9,... | collective-permute-start | bytes 1769480 | tf_op jit(solution)/shard_map/ppermute | solution.py:37
  207.3 30.9 %collective-permute-start.37 = (bf16[64,1536]{1,0:T(8,128)(2,1)S(1)}, bf16[64,1536]{1,0:T(8,128)(2,1)S(1)}, u32[]{:S(2)}, u32[]{:S(2)}) collective-permute-start(bf16[64,1536]{1,0:T(8,128)(2,1)S(1)} %slice_bitcast_fusion.46), channel_id=1, source_target_pairs={{0,2},{1,3},{2,0},{3,1},{4,6},{5,7},{6,4},{7,5},{8,10},{9,11},{10,... | collective-permute-start | bytes 589832 | tf_op jit(solution)/shard_map/ppermute | solution.py:37
  207.7 30.9 %collective-permute-start.38 = (bf16[64,1536]{1,0:T(8,128)(2,1)S(1)}, bf16[64,1536]{1,0:T(8,128)(2,1)S(1)}, u32[]{:S(2)}, u32[]{:S(2)}) collective-permute-start(bf16[64,1536]{1,0:T(8,128)(2,1)S(1)} %slice_bitcast_fusion.45), channel_id=1, source_target_pairs={{0,16},{1,17},{2,18},{3,19},{4,20},{5,21},{6,22},{7,23},{8,24},{9,... | collective-permute-start | bytes 589832 | tf_op jit(solution)/shard_map/ppermute | solution.py:37
  219.2 22.0 %collective-permute-start.39 = (bf16[64,1536]{1,0:T(8,128)(2,1)S(1)}, bf16[64,1536]{1,0:T(8,128)(2,1)S(1)}, u32[]{:S(2)}, u32[]{:S(2)}) collective-permute-start(bf16[64,1536]{1,0:T(8,128)(2,1)S(1)} %slice_bitcast_fusion.44), channel_id=1, source_target_pairs={{0,18},{1,19},{2,16},{3,17},{4,22},{5,23},{6,20},{7,21},{8,26},{9,... | collective-permute-start | bytes 589832 | tf_op jit(solution)/shard_map/ppermute | solution.py:37
  233.0 18.8 %collective-permute-start.44 = (bf16[64,1536]{1,0:T(8,128)(2,1)S(1)}, bf16[64,1536]{1,0:T(8,128)(2,1)S(1)}, u32[]{:S(2)}, u32[]{:S(2)}) collective-permute-start(bf16[64,1536]{1,0:T(8,128)(2,1)S(1)} %get-tuple-element.214), channel_id=1, source_target_pairs={{0,8},{1,9},{2,10},{3,11},{4,12},{5,13},{6,14},{7,15},{8,0},{9,1},... | collective-permute-start | bytes 589832 | tf_op jit(solution)/shard_map/ppermute | solution.py:37
  238.3 22.0 %collective-permute-start.45 = (bf16[64,1536]{1,0:T(8,128)(2,1)S(1)}, bf16[64,1536]{1,0:T(8,128)(2,1)S(1)}, u32[]{:S(2)}, u32[]{:S(2)}) collective-permute-start(bf16[64,1536]{1,0:T(8,128)(2,1)S(1)} %get-tuple-element.213), channel_id=1, source_target_pairs={{0,12},{1,13},{2,14},{3,15},{4,8},{5,9},{6,10},{7,11},{8,4},{9,5},... | collective-permute-start | bytes 589832 | tf_op jit(solution)/shard_map/ppermute | solution.py:37
  293.1 17.4 %collective-permute-start.56 = (bf16[64,1536]{1,0:T(8,128)(2,1)S(1)}, bf16[64,1536]{1,0:T(8,128)(2,1)S(1)}, u32[]{:S(2)}, u32[]{:S(2)}) collective-permute-start(bf16[64,1536]{1,0:T(8,128)(2,1)S(1)} %get-tuple-element.77.refs_1_.refs_33_), channel_id=1, source_target_pairs={{0,4},{1,5},{2,6},{3,7},{4,0},{5,1},{6,2},{7,3},{8,12},{9,13},{10,... | collective-permute-start | bytes 589832 | tf_op jit(solution)/shard_map/ppermute | solution.py:37
  293.1 17.4 %collective-permute-start.57 = (bf16[64,1536]{1,0:T(8,128)(2,1)S(1)}, bf16[64,1536]{1,0:T(8,128)(2,1)S(1)}, u32[]{:S(2)}, u32[]{:S(2)}) collective-permute-start(bf16[64,1536]{1,0:T(8,128)(2,1)S(1)} %get-tuple-element.77.refs_1_.refs_33_), channel_id=1, source_target_pairs={{0,8},{1,9},{2,10},{3,11},{4,12},{5,13},{6,14},{7,15},{8,0},{9,1},... | collective-permute-start | bytes 589832 | tf_op jit(solution)/shard_map/ppermute | solution.py:37
  295.9 22.5 %collective-permute-start.58 = (bf16[64,1536]{1,0:T(8,128)(2,1)S(1)}, bf16[64,1536]{1,0:T(8,128)(2,1)S(1)}, u32[]{:S(2)}, u32[]{:S(2)}) collective-permute-start(bf16[64,1536]{1,0:T(8,128)(2,1)S(1)} %get-tuple-element.77.refs_1_.refs_33_), channel_id=1, source_target_pairs={{0,12},{1,13},{2,14},{3,15},{4,8},{5,9},{6,10},{7,11},{8,4},{9,5},... | collective-permute-start | bytes 589832 | tf_op jit(solution)/shard_map/ppermute | solution.py:37
  318.6 16.6 %collective-permute-start.64 = (bf16[3,64,1536]{2,1,0:T(8,128)(2,1)S(1)}, bf16[3,64,1536]{2,1,0:T(8,128)(2,1)S(1)}, u32[]{:S(2)}, u32[]{:S(2)}) collective-permute-start(bf16[3,64,1536]{2,1,0:T(8,128)(2,1)S(1)} %maximum_select_fusion.6.refs_5_.refs_37_), channel_id=1, source_target_pairs={{0,16},{1,17},{2,18},{3,19},{4,20},{5,21},{6,22},{7,23},{8,24},{9,... | collective-permute-start | bytes 1769480 | tf_op jit(solution)/shard_map/ppermute | solution.py:37
  319.9 25.8 %collective-permute-start.66 = (bf16[3,64,1536]{2,1,0:T(8,128)(2,1)S(1)}, bf16[3,64,1536]{2,1,0:T(8,128)(2,1)S(1)}, u32[]{:S(2)}, u32[]{:S(2)}) collective-permute-start(bf16[3,64,1536]{2,1,0:T(8,128)(2,1)S(1)} %maximum_select_fusion.6.refs_5_.refs_37_), channel_id=1, source_target_pairs={{0,18},{1,19},{2,16},{3,17},{4,22},{5,23},{6,20},{7,21},{8,26},{9,... | collective-permute-start | bytes 1769480 | tf_op jit(solution)/shard_map/ppermute | solution.py:37
  323.3 24.8 %collective-permute-start.53 = (bf16[64,1536]{1,0:T(8,128)(2,1)S(1)}, bf16[64,1536]{1,0:T(8,128)(2,1)S(1)}, u32[]{:S(2)}, u32[]{:S(2)}) collective-permute-start(bf16[64,1536]{1,0:T(8,128)(2,1)S(1)} %collective-permute-done.52.refs_3_.refs_35_), channel_id=1, source_target_pairs={{0,1},{1,0},{2,3},{3,2},{4,5},{5,4},{6,7},{7,6},{8,9},{9,8},{10,11... | collective-permute-start | bytes 589832 | tf_op jit(solution)/shard_map/ppermute | solution.py:37
  324.4 27.1 %collective-permute-start.59 = (bf16[3,64,1536]{2,1,0:T(8,128)(2,1)S(1)}, bf16[3,64,1536]{2,1,0:T(8,128)(2,1)S(1)}, u32[]{:S(2)}, u32[]{:S(2)}) collective-permute-start(bf16[3,64,1536]{2,1,0:T(8,128)(2,1)S(1)} %maximum_select_fusion.6.refs_5_.refs_37_), channel_id=1, source_target_pairs={{0,1},{1,0},{2,3},{3,2},{4,5},{5,4},{6,7},{7,6},{8,9},{9,8},{10,11... | collective-permute-start | bytes 1769480 | tf_op jit(solution)/shard_map/ppermute | solution.py:37
  332.1 19.4 %collective-permute-start.61 = (bf16[3,64,1536]{2,1,0:T(8,128)(2,1)S(1)}, bf16[3,64,1536]{2,1,0:T(8,128)(2,1)S(1)}, u32[]{:S(2)}, u32[]{:S(2)}) collective-permute-start(bf16[3,64,1536]{2,1,0:T(8,128)(2,1)S(1)} %collective-permute-done.60.refs_7_.refs_39_), channel_id=1, source_target_pairs={{0,1},{1,0},{2,3},{3,2},{4,5},{5,4},{6,7},{7,6},{8,9},{9,8},{10,11... | collective-permute-start | bytes 1769480 | tf_op jit(solution)/shard_map/ppermute | solution.py:37
  335.2 16.4 %collective-permute-start.65 = (bf16[3,64,1536]{2,1,0:T(8,128)(2,1)S(1)}, bf16[3,64,1536]{2,1,0:T(8,128)(2,1)S(1)}, u32[]{:S(2)}, u32[]{:S(2)}) collective-permute-start(bf16[3,64,1536]{2,1,0:T(8,128)(2,1)S(1)} %collective-permute-done.64.refs_13_.refs_45_), channel_id=1, source_target_pairs={{0,1},{1,0},{2,3},{3,2},{4,5},{5,4},{6,7},{7,6},{8,9},{9,8},{10,11... | collective-permute-start | bytes 1769480 | tf_op jit(solution)/shard_map/ppermute | solution.py:37
  393.7 15.5 %collective-permute-start.73 = (bf16[3,64,1536]{2,1,0:T(8,128)(2,1)S(1)}, bf16[3,64,1536]{2,1,0:T(8,128)(2,1)S(1)}, u32[]{:S(2)}, u32[]{:S(2)}) collective-permute-start(bf16[3,64,1536]{2,1,0:T(8,128)(2,1)S(1)} %slice_bitcast_fusion.7), channel_id=1, source_target_pairs={{0,16},{1,17},{2,18},{3,19},{4,20},{5,21},{6,22},{7,23},{8,24},{9,... | collective-permute-start | bytes 1769480 | tf_op jit(solution)/shard_map/ppermute | solution.py:37
  395.0 26.7 %collective-permute-start.74 = (bf16[3,64,1536]{2,1,0:T(8,128)(2,1)S(1)}, bf16[3,64,1536]{2,1,0:T(8,128)(2,1)S(1)}, u32[]{:S(2)}, u32[]{:S(2)}) collective-permute-start(bf16[3,64,1536]{2,1,0:T(8,128)(2,1)S(1)} %slice_bitcast_fusion.6), channel_id=1, source_target_pairs={{0,18},{1,19},{2,16},{3,17},{4,22},{5,23},{6,20},{7,21},{8,26},{9,... | collective-permute-start | bytes 1769480 | tf_op jit(solution)/shard_map/ppermute | solution.py:37
  396.4 28.5 %collective-permute-start.69 = (bf16[64,1536]{1,0:T(8,128)(2,1)S(1)}, bf16[64,1536]{1,0:T(8,128)(2,1)S(1)}, u32[]{:S(2)}, u32[]{:S(2)}) collective-permute-start(bf16[64,1536]{1,0:T(8,128)(2,1)S(1)} %slice_bitcast_fusion.37), channel_id=1, source_target_pairs={{0,2},{1,3},{2,0},{3,1},{4,6},{5,7},{6,4},{7,5},{8,10},{9,11},{10,... | collective-permute-start | bytes 589832 | tf_op jit(solution)/shard_map/ppermute | solution.py:37
  396.8 28.9 %collective-permute-start.70 = (bf16[64,1536]{1,0:T(8,128)(2,1)S(1)}, bf16[64,1536]{1,0:T(8,128)(2,1)S(1)}, u32[]{:S(2)}, u32[]{:S(2)}) collective-permute-start(bf16[64,1536]{1,0:T(8,128)(2,1)S(1)} %slice_bitcast_fusion.36), channel_id=1, source_target_pairs={{0,16},{1,17},{2,18},{3,19},{4,20},{5,21},{6,22},{7,23},{8,24},{9,... | collective-permute-start | bytes 589832 | tf_op jit(solution)/shard_map/ppermute | solution.py:37
  408.1 22.1 %collective-permute-start.71 = (bf16[64,1536]{1,0:T(8,128)(2,1)S(1)}, bf16[64,1536]{1,0:T(8,128)(2,1)S(1)}, u32[]{:S(2)}, u32[]{:S(2)}) collective-permute-start(bf16[64,1536]{1,0:T(8,128)(2,1)S(1)} %slice_bitcast_fusion.35), channel_id=1, source_target_pairs={{0,18},{1,19},{2,16},{3,17},{4,22},{5,23},{6,20},{7,21},{8,26},{9,... | collective-permute-start | bytes 589832 | tf_op jit(solution)/shard_map/ppermute | solution.py:37
  424.9 15.9 %collective-permute-start.77 = (bf16[64,1536]{1,0:T(8,128)(2,1)S(1)}, bf16[64,1536]{1,0:T(8,128)(2,1)S(1)}, u32[]{:S(2)}, u32[]{:S(2)}) collective-permute-start(bf16[64,1536]{1,0:T(8,128)(2,1)S(1)} %get-tuple-element.210), channel_id=1, source_target_pairs={{0,12},{1,13},{2,14},{3,15},{4,8},{5,9},{6,10},{7,11},{8,4},{9,5},... | collective-permute-start | bytes 589832 | tf_op jit(solution)/shard_map/ppermute | solution.py:37
  471.8 320.4 %reduce-scatter.5.cloned.1.call-start = ((), (), s32[]{:S(2)}) async-start(), calls=%async_computation.4 | async-start | bytes 1966080 | tf_op jit(solution)/shard_map/reduce_scatter | solution.py:848
  473.7 24.9 %collective-permute-start.92 = (bf16[64,1536]{1,0:T(8,128)(2,1)}, bf16[64,1536]{1,0:T(8,128)(2,1)S(1)}, u32[]{:S(2)}, u32[]{:S(2)}) collective-permute-start(bf16[64,1536]{1,0:T(8,128)(2,1)} %get-tuple-element.89.refs_0_.refs_17_), channel_id=1, source_target_pairs={{0,12},{1,13},{2,14},{3,15},{4,8},{5,9},{6,10},{7,11},{8,4},{9,5},... | collective-permute-start | bytes 589832 | tf_op jit(solution)/shard_map/ppermute | solution.py:37
  499.5 29.3 %collective-permute-start.94 = (bf16[3,64,1536]{2,1,0:T(8,128)(2,1)S(1)}, bf16[3,64,1536]{2,1,0:T(8,128)(2,1)S(1)}, u32[]{:S(2)}, u32[]{:S(2)}) collective-permute-start(bf16[3,64,1536]{2,1,0:T(8,128)(2,1)S(1)} %maximum_select_fusion.7.refs_4_.refs_21_), channel_id=1, source_target_pairs={{0,2},{1,3},{2,0},{3,1},{4,6},{5,7},{6,4},{7,5},{8,10},{9,11},{10,... | collective-permute-start | bytes 1769480 | tf_op jit(solution)/shard_map/ppermute | solution.py:37
  501.8 27.0 %collective-permute-start.98 = (bf16[3,64,1536]{2,1,0:T(8,128)(2,1)S(1)}, bf16[3,64,1536]{2,1,0:T(8,128)(2,1)S(1)}, u32[]{:S(2)}, u32[]{:S(2)}) collective-permute-start(bf16[3,64,1536]{2,1,0:T(8,128)(2,1)S(1)} %maximum_select_fusion.7.refs_4_.refs_21_), channel_id=1, source_target_pairs={{0,16},{1,17},{2,18},{3,19},{4,20},{5,21},{6,22},{7,23},{8,24},{9,... | collective-permute-start | bytes 1769480 | tf_op jit(solution)/shard_map/ppermute | solution.py:37
  511.5 30.4 %collective-permute-start.93 = (bf16[3,64,1536]{2,1,0:T(8,128)(2,1)S(1)}, bf16[3,64,1536]{2,1,0:T(8,128)(2,1)S(1)}, u32[]{:S(2)}, u32[]{:S(2)}) collective-permute-start(bf16[3,64,1536]{2,1,0:T(8,128)(2,1)S(1)} %maximum_select_fusion.7.refs_4_.refs_21_), channel_id=1, source_target_pairs={{0,1},{1,0},{2,3},{3,2},{4,5},{5,4},{6,7},{7,6},{8,9},{9,8},{10,11... | collective-permute-start | bytes 1769480 | tf_op jit(solution)/shard_map/ppermute | solution.py:37
  513.0 25.5 %collective-permute-start.86 = (bf16[64,1536]{1,0:T(8,128)(2,1)S(1)}, bf16[64,1536]{1,0:T(8,128)(2,1)S(1)}, u32[]{:S(2)}, u32[]{:S(2)}) collective-permute-start(bf16[64,1536]{1,0:T(8,128)(2,1)S(1)} %collective-permute-done.85.refs_2_.refs_19_), channel_id=1, source_target_pairs={{0,1},{1,0},{2,3},{3,2},{4,5},{5,4},{6,7},{7,6},{8,9},{9,8},{10,11... | collective-permute-start | bytes 589832 | tf_op jit(solution)/shard_map/ppermute | solution.py:37
  513.4 28.5 %collective-permute-start.101 = (bf16[3,64,1536]{2,1,0:T(8,128)(2,1)S(1)}, bf16[3,64,1536]{2,1,0:T(8,128)(2,1)S(1)}, u32[]{:S(2)}, u32[]{:S(2)}) collective-permute-start(bf16[3,64,1536]{2,1,0:T(8,128)(2,1)S(1)} %collective-permute-done.100.refs_14_.refs_31_), channel_id=1, source_target_pairs={{0,1},{1,0},{2,3},{3,2},{4,5},{5,4},{6,7},{7,6},{8,9},{9,8},{10,11... | collective-permute-start | bytes 1769480 | tf_op jit(solution)/shard_map/ppermute | solution.py:37
  584.8 35.9 %collective-permute-start.106 = (bf16[3,64,1536]{2,1,0:T(8,128)(2,1)S(1)}, bf16[3,64,1536]{2,1,0:T(8,128)(2,1)S(1)}, u32[]{:S(2)}, u32[]{:S(2)}) collective-permute-start(bf16[3,64,1536]{2,1,0:T(8,128)(2,1)S(1)} %slice_bitcast_fusion.4), channel_id=1, source_target_pairs={{0,2},{1,3},{2,0},{3,1},{4,6},{5,7},{6,4},{7,5},{8,10},{9,11},{10,... | collective-permute-start | bytes 1769480 | tf_op jit(solution)/shard_map/ppermute | solution.py:37
  585.3 35.5 %collective-permute-start.107 = (bf16[3,64,1536]{2,1,0:T(8,128)(2,1)S(1)}, bf16[3,64,1536]{2,1,0:T(8,128)(2,1)S(1)}, u32[]{:S(2)}, u32[]{:S(2)}) collective-permute-start(bf16[3,64,1536]{2,1,0:T(8,128)(2,1)S(1)} %slice_bitcast_fusion.3), channel_id=1, source_target_pairs={{0,16},{1,17},{2,18},{3,19},{4,20},{5,21},{6,22},{7,23},{8,24},{9,... | collective-permute-start | bytes 1769480 | tf_op jit(solution)/shard_map/ppermute | solution.py:37
  585.8 36.8 %collective-permute-start.108 = (bf16[3,64,1536]{2,1,0:T(8,128)(2,1)S(1)}, bf16[3,64,1536]{2,1,0:T(8,128)(2,1)S(1)}, u32[]{:S(2)}, u32[]{:S(2)}) collective-permute-start(bf16[3,64,1536]{2,1,0:T(8,128)(2,1)S(1)} %slice_bitcast_fusion.2), channel_id=1, source_target_pairs={{0,18},{1,19},{2,16},{3,17},{4,22},{5,23},{6,20},{7,21},{8,26},{9,... | collective-permute-start | bytes 1769480 | tf_op jit(solution)/shard_map/ppermute | solution.py:37
  587.5 35.4 %collective-permute-start.103 = (bf16[64,1536]{1,0:T(8,128)(2,1)}, bf16[64,1536]{1,0:T(8,128)(2,1)}, u32[]{:S(2)}, u32[]{:S(2)}) collective-permute-start(bf16[64,1536]{1,0:T(8,128)(2,1)} %slice_bitcast_fusion.28), channel_id=1, source_target_pairs={{0,2},{1,3},{2,0},{3,1},{4,6},{5,7},{6,4},{7,5},{8,10},{9,11},{10,... | collective-permute-start | bytes 589832 | tf_op jit(solution)/shard_map/ppermute | solution.py:37
  588.0 36.1 %collective-permute-start.104 = (bf16[64,1536]{1,0:T(8,128)(2,1)}, bf16[64,1536]{1,0:T(8,128)(2,1)}, u32[]{:S(2)}, u32[]{:S(2)}) collective-permute-start(bf16[64,1536]{1,0:T(8,128)(2,1)} %slice_bitcast_fusion.27), channel_id=1, source_target_pairs={{0,16},{1,17},{2,18},{3,19},{4,20},{5,21},{6,22},{7,23},{8,24},{9,... | collective-permute-start | bytes 589832 | tf_op jit(solution)/shard_map/ppermute | solution.py:37
  620.8 48.0 %collective-permute-start.78 = (bf16[2,8,64,1536]{3,2,0,1:T(8,128)(2,1)}, bf16[2,8,64,1536]{3,2,0,1:T(8,128)(2,1)}, u32[]{:S(2)}, u32[]{:S(2)}) collective-permute-start(bf16[2,8,64,1536]{3,2,0,1:T(8,128)(2,1)} %copy.141), channel_id=1, source_target_pairs={{0,1},{1,0},{2,3},{3,2},{4,5},{5,4},{6,7},{7,6},{8,9},{9,8},{10,11... | collective-permute-start | bytes 9437192 | tf_op jit(solution)/shard_map/ppermute | solution.py:37
  624.1 18.9 %collective-permute-start.111 = (bf16[64,1536]{1,0:T(8,128)(2,1)S(1)}, bf16[64,1536]{1,0:T(8,128)(2,1)S(1)}, u32[]{:S(2)}, u32[]{:S(2)}) collective-permute-start(bf16[64,1536]{1,0:T(8,128)(2,1)S(1)} %get-tuple-element.207), channel_id=1, source_target_pairs={{0,12},{1,13},{2,14},{3,15},{4,8},{5,9},{6,10},{7,11},{8,4},{9,5},... | collective-permute-start | bytes 589832 | tf_op jit(solution)/shard_map/ppermute | solution.py:37
  672.8 36.2 %collective-permute-start.117 = (bf16[2,4,64,1536]{3,2,0,1:T(8,128)(2,1)S(1)}, bf16[2,4,64,1536]{3,2,0,1:T(8,128)(2,1)S(1)}, u32[]{:S(2)}, u32[]{:S(2)}) collective-permute-start(bf16[2,4,64,1536]{3,2,0,1:T(8,128)(2,1)S(1)} %maximum_select_fusion.1), channel_id=1, source_target_pairs={{0,2},{1,3},{2,0},{3,1},{4,6},{5,7},{6,4},{7,5},{8,10},{9,11},{10,... | collective-permute-start | bytes 4718600 | tf_op jit(solution)/shard_map/ppermute | solution.py:37
  676.0 31.6 %collective-permute-start.120 = (bf16[4,192,896]{2,1,0:T(8,128)(2,1)S(1)}, bf16[4,192,896]{2,1,0:T(8,128)(2,1)S(1)}, u32[]{:S(2)}, u32[]{:S(2)}) collective-permute-start(bf16[4,192,896]{2,1,0:T(8,128)(2,1)S(1)} %get-tuple-element.115), channel_id=1, source_target_pairs={{0,16},{1,17},{2,18},{3,19},{4,20},{5,21},{6,22},{7,23},{8,24},{9,... | collective-permute-start | bytes 4128776 | tf_op jit(solution)/shard_map/ppermute | solution.py:37
  679.9 37.6 %collective-permute-start.118 = (bf16[2,64,1536]{2,1,0:T(8,128)(2,1)S(1)}, bf16[2,64,1536]{2,1,0:T(8,128)(2,1)S(1)}, u32[]{:S(2)}, u32[]{:S(2)}) collective-permute-start(bf16[2,64,1536]{2,1,0:T(8,128)(2,1)S(1)} %pad_maximum_fusion.3), channel_id=1, source_target_pairs={{0,16},{1,17},{2,18},{3,19},{4,20},{5,21},{6,22},{7,23},{8,24},{9,... | collective-permute-start | bytes 1179656 | tf_op jit(solution)/shard_map/ppermute | solution.py:37
  680.7 30.9 %collective-permute-start.122 = (f32[4,1536]{1,0:T(4,128)S(1)}, f32[4,1536]{1,0:T(4,128)S(1)}, u32[]{:S(2)}, u32[]{:S(2)}) collective-permute-start(f32[4,1536]{1,0:T(4,128)S(1)} %fusion.43), channel_id=1, source_target_pairs={{0,2},{1,3},{2,0},{3,1},{4,6},{5,7},{6,4},{7,5},{8,10},{9,11},{10,... | collective-permute-start | bytes 73736 | tf_op jit(solution)/shard_map/ppermute | solution.py:37
  714.8 18.4 %collective-permute-start.124 = (bf16[208,896]{1,0:T(8,128)(2,1)S(1)}, bf16[208,896]{1,0:T(8,128)(2,1)S(1)}, u32[]{:S(2)}, u32[]{:S(2)}) collective-permute-start(bf16[208,896]{1,0:T(8,128)(2,1)S(1)} %get-tuple-element.199), channel_id=1, source_target_pairs={{0,8},{1,9},{2,10},{3,11},{4,12},{5,13},{6,14},{7,15},{8,0},{9,1},... | collective-permute-start | bytes 1118216 | tf_op jit(solution)/shard_map/ppermute | solution.py:37
  715.3 57.1 %collective-permute-start.125 = (bf16[208,896]{1,0:T(8,128)(2,1)S(1)}, bf16[208,896]{1,0:T(8,128)(2,1)S(1)}, u32[]{:S(2)}, u32[]{:S(2)}) collective-permute-start(bf16[208,896]{1,0:T(8,128)(2,1)S(1)} %get-tuple-element.198), channel_id=1, source_target_pairs={{0,12},{1,13},{2,14},{3,15},{4,8},{5,9},{6,10},{7,11},{8,4},{9,5},... | collective-permute-start | bytes 1118216 | tf_op jit(solution)/shard_map/ppermute | solution.py:37
  (199 other events, 2721.5 us)
Sparse Core Ops, SparseCore 0:
  27.3 61.5 all-gather.7
  156.3 63.9 all-gather.9
  222.6 95.4 all-gather.5
  471.9 86.0 reduce-scatter.2
  711.7 63.4 reduce-scatter.4
